TPU v7x, 32 devices: a whole 2x2x4 slice. The times are simulated.
32 devices in a mesh: seq: 16 (over z, x, core), head: 2 (over y).
Axes of the slice: x: 2, y: 2, z: 4, core: 2. Of those that a mesh axis runs over, the one named last changes fastest.
Arguments:
- span_query: bfloat16 [2048, 8192], P('seq', 'head'), may hold values from -8 to 8
- span_kv: bfloat16 [2048, 2048], P('seq', 'head'), may hold values from -6 to 6
- prefix_cache: bfloat16 [32, 64, 2048], P('seq', None, 'head'), may hold values from -6 to 6
- prefix_len: int32 [2], replicated, may hold values from 256 to 1024, as said below
- block_owner: int32 [2, 16], replicated, may hold values from 0 to 15, as said below
Outputs:
- attended: bfloat16 [2048, 8192], P(('seq', 'head'))
Inputs may be any that keep to these rules, and one draw needn't show every extreme that they name: `prefix_len`: some request's prefix has exactly 1024 tokens in every draw. `block_owner`: each row is a permutation of the seq devices: every device holds one page slot for each request, used or not.
All inputs are finite; a program needn't handle non-finite values.
Results may differ from a plain program's by a relative error of at most 0.0065.
Values may be sent and summed in bfloat16 or wider, within the bound.
No kernel may reach another device: no remote copies, remote signals or barrier semaphores. Data moves between devices by JAX's collectives and lax.ppermute only.
A program may use at most 64 MiB of HBM per device.

v0:
```python
import jax
import jax.numpy as jnp
from jax import lax
from jax.sharding import PartitionSpec as P

QH = 64
KVH = 8
HD = 128
REQS = 2


key_block = 512


def from_behind(value, axis, steps):
    count = lax.axis_size(axis)
    leading, last = (max(0, -steps), min(count, count - steps))
    return lax.ppermute(value, axis, [(source, source + steps) for source in range(leading, last)])


def attend(attn_state, queries, kv_rows, visible, score_scale):
    running_max, running_sum, weighted = attn_state
    key_rows = kv_rows[:, :, 0]
    value_rows = kv_rows[:, :, 1]
    scores = (
        jnp.einsum("tgqd,kgd->tgqk", queries, key_rows, preferred_element_type=jnp.float32)
        * score_scale
    )
    live = visible[:, None, None, :]
    scores = jnp.where(live, scores, jnp.float32(-1e30))
    new_max = jnp.maximum(running_max, jnp.max(scores, axis=-1))
    weights = jnp.where(live, jnp.exp(scores - new_max[..., None]), jnp.float32(0.0))
    rescale = jnp.exp(running_max - new_max)
    running_sum = running_sum * rescale + jnp.sum(weights, axis=-1)
    update = jnp.einsum(
        "tgqk,kgd->tgqd",
        weights.astype(jnp.bfloat16),
        value_rows,
        preferred_element_type=jnp.float32,
    )
    weighted = weighted * rescale[..., None] + update
    return (new_max, running_sum, weighted)


def attend_blocks(attn_state, queries, kv_rows, visible, score_scale):
    key_count = kv_rows.shape[0]
    if key_count > key_block and key_count % key_block == 0:
        block_count = key_count // key_block
        row_blocks = kv_rows.reshape((block_count, key_block) + kv_rows.shape[1:])
        vis_blocks = visible.reshape(visible.shape[0], block_count, key_block).transpose(1, 0, 2)

        def one_block(carried, block_pair):
            return (attend(carried, queries, block_pair[0], block_pair[1], score_scale), None)

        attn_state, unused = lax.scan(one_block, attn_state, (row_blocks, vis_blocks))
        return attn_state
    return attend(attn_state, queries, kv_rows, visible, score_scale)


def body(span_query, span_kv, prefix_cache, prefix_len, block_owner):
    tok_rows = span_query.shape[0]
    head_groups = span_kv.shape[1] // (2 * HD)
    per_group = QH // KVH
    score_scale = HD ** (-0.5)
    queries = span_query.reshape(tok_rows, head_groups, per_group, HD)
    seq_size = lax.axis_size("seq")
    group_size = seq_size // REQS
    my_index = lax.axis_index("seq")
    my_request = my_index // group_size
    group_place = my_index % group_size
    attn_state = (
        jnp.full((tok_rows, head_groups, per_group), -1e30, jnp.float32),
        jnp.zeros((tok_rows, head_groups, per_group), jnp.float32),
        jnp.zeros((tok_rows, head_groups, per_group, HD), jnp.float32),
    )
    own_keys = span_kv.reshape(tok_rows, head_groups, 2, HD)
    causal = jnp.arange(tok_rows)[None, :] <= jnp.arange(tok_rows)[:, None]
    attn_state = attend_blocks(attn_state, queries, own_keys, causal, score_scale)

    def cycle_step(turn, carried):
        travelling, carried_state = carried
        travelling = from_behind(travelling, "seq", 1)
        earlier = jnp.broadcast_to(group_place >= turn, (tok_rows, tok_rows))
        carried_state = attend_blocks(
            carried_state,
            queries,
            travelling.reshape(tok_rows, head_groups, 2, HD),
            earlier,
            score_scale,
        )
        return (travelling, carried_state)

    unused_rows, attn_state = lax.fori_loop(1, group_size, cycle_step, (span_kv, attn_state))
    owners_row = lax.dynamic_index_in_dim(block_owner, my_request, 0, keepdims=False)
    prefix_limit = lax.dynamic_index_in_dim(prefix_len, my_request, 0, keepdims=False)
    block_len = prefix_cache.shape[1]
    slot_count = prefix_cache.shape[0]
    shard_rows = lax.all_gather(prefix_cache, "seq", axis=0, tiled=True)
    source_count = shard_rows.shape[0] // slot_count
    split_rows = shard_rows.reshape((source_count, slot_count) + shard_rows.shape[1:])
    own_blocks = lax.dynamic_index_in_dim(split_rows, my_request, 1, keepdims=False)
    source_ids = jnp.arange(source_count, dtype=jnp.int32)
    source_count = own_blocks.shape[0]
    matches = owners_row[:, None] == source_ids[None, :]
    block_index = jnp.sum(
        jnp.arange(owners_row.shape[0], dtype=jnp.int32)[:, None] * matches, axis=0
    )
    positions = (
        block_index[:, None] * block_len + jnp.arange(block_len, dtype=jnp.int32)[None, :]
    ).reshape(-1)
    visible = jnp.broadcast_to(
        (positions < prefix_limit)[None, :], (tok_rows, source_count * block_len)
    )
    page_rows = own_blocks.reshape(source_count * block_len, head_groups, 2, HD)
    attn_state = attend_blocks(attn_state, queries, page_rows, visible, score_scale)
    running_max, running_sum, weighted = attn_state
    result = (
        (weighted / running_sum[..., None])
        .reshape(tok_rows, head_groups * per_group * HD)
        .astype(jnp.bfloat16)
    )
    return lax.all_to_all(result, "head", split_axis=0, concat_axis=1, tiled=True)


def solution(mesh):
    placed = (P("seq", "head"), P("seq", "head"), P("seq", None, "head"), P(), P())
    return jax.shard_map(
        body, mesh=mesh, in_specs=placed, out_specs=P(("seq", "head"), None), check_vma=False
    )
```

profile of v0, /device:TPU:16, one launch (start us, length us, event | category | flops | bytes accessed | tf_op | source)
XLA Modules:
  0.0 167.1 jit_solution(15694144151333093725)
XLA Ops:
  6.5 0.7 all-gather.2.cloned.1.call-update
  7.3 1.2 dynamic_slice.21
  9.0 1.8 %copy.79 = bf16[128,1024]{0,1:T(8,128)(2,1)} copy(bf16[128,1024]{1,0:T(8,128)(2,1)} %param.10) | data formatting | bytes 524288 | tf_op jit(solution)/shard_map/while | solution.py:93
  10.8 1.6 copy.75
  13.1 1.4 fusion.27
  15.1 2.1 %bitcast_add_fusion.2 = f32[128,4,8,128]{3,0,2,1:T(8,128)S(1)} fusion(f32[4,128,128,8]{2,1,3,0:T(8,128)S(1)} %get-tuple-element.276, f32[128,4,8]{0,2,1:T(8,128)S(1)} %get-tuple-element.273, f32[128,4,8]{0,2,1:T(8,128)S(1)} %broadcast_maximum_fusion, pred[128,128]{0,1:T(8,128)(4,1)S(1)} %iota_compare_fusion, bf16[128,4,2,128]{0,3,2,1:T(8,128)(2,1)} %bitcast.18), kind=kOutput, calls=%fused_computation.41 | convolution fusion | flops 137363456 | bytes 4374528 | tf_op jit(solution)/shard_map/tgqk,kgd->tgqd/dot_general | solution.py:35
  17.3 101.3 %while.33 = (s32[]{:T(128)}, bf16[128,1024]{0,1:T(8,128)(2,1)}, f32[128,4,8]{0,2,1:T(8,128)S(1)}, f32[128,4,8]{0,2,1:T(8,128)S(1)}, f32[128,4,8,128]{3,0,2,1:T(8...) while((s32[]{:T(128)}, bf16[128,1024]{0,1:T(8,128)(2,1)}, ...), condition=%wide.region_5.6_spmd, body=%wide.region_2.5_spmd.sunk | while | flops 276307968 | bytes 13632648 | solution.py:93
  17.3 1.9 %collective-permute-start = (bf16[128,1024]{0,1:T(8,128)(2,1)}, bf16[128,1024]{0,1:T(8,128)(2,1)S(1)}, u32[]{:S(2)}, u32[]{:S(2)}) collective-permute-start(bf16[128,1024]{0,1:T(8,128)(2,1)} %get-tuple-element.388), channel_id=1, source_target_pairs={{0,2},{2,4},{4,6},{6,8},{8,10},{10,12},{12,14},{14,16},{16,18},{18... | collective-permute-start | bytes 786440 | tf_op jit(solution)/shard_map/while/body/eval_jaxpr/ppermute | solution.py:18
  19.2 13.0 %collective-permute-done = bf16[128,1024]{0,1:T(8,128)(2,1)S(1)} collective-permute-done((bf16[128,1024]{0,1:T(8,128)(2,1)}, bf16[128,1024]{0,1:T(8,128)(2,1)S(1)}, u32[]{:S(2)}, u32[]{:S(2)}) %collective-permute-start) | collective-permute-done | bytes 262176 | tf_op jit(solution)/shard_map/while/body/eval_jaxpr/ppermute | solution.py:18
  33.4 1.5 bitcast_add_fusion.5
  34.9 0.7 copy.121
  35.6 1.9 %collective-permute-start = (bf16[128,1024]{0,1:T(8,128)(2,1)}, bf16[128,1024]{0,1:T(8,128)(2,1)S(1)}, u32[]{:S(2)}, u32[]{:S(2)}) collective-permute-start(bf16[128,1024]{0,1:T(8,128)(2,1)} %get-tuple-element.388), channel_id=1, source_target_pairs={{0,2},{2,4},{4,6},{6,8},{8,10},{10,12},{12,14},{14,16},{16,18},{18... | collective-permute-start | bytes 786440 | tf_op jit(solution)/shard_map/while/body/eval_jaxpr/ppermute | solution.py:18
  37.5 16.9 %collective-permute-done = bf16[128,1024]{0,1:T(8,128)(2,1)S(1)} collective-permute-done((bf16[128,1024]{0,1:T(8,128)(2,1)}, bf16[128,1024]{0,1:T(8,128)(2,1)S(1)}, u32[]{:S(2)}, u32[]{:S(2)}) %collective-permute-start) | collective-permute-done | bytes 262176 | tf_op jit(solution)/shard_map/while/body/eval_jaxpr/ppermute | solution.py:18
  55.6 1.5 bitcast_add_fusion.5
  57.8 1.9 %collective-permute-start = (bf16[128,1024]{0,1:T(8,128)(2,1)}, bf16[128,1024]{0,1:T(8,128)(2,1)S(1)}, u32[]{:S(2)}, u32[]{:S(2)}) collective-permute-start(bf16[128,1024]{0,1:T(8,128)(2,1)} %get-tuple-element.388), channel_id=1, source_target_pairs={{0,2},{2,4},{4,6},{6,8},{8,10},{10,12},{12,14},{14,16},{16,18},{18... | collective-permute-start | bytes 786440 | tf_op jit(solution)/shard_map/while/body/eval_jaxpr/ppermute | solution.py:18
  59.7 6.9 %collective-permute-done = bf16[128,1024]{0,1:T(8,128)(2,1)S(1)} collective-permute-done((bf16[128,1024]{0,1:T(8,128)(2,1)}, bf16[128,1024]{0,1:T(8,128)(2,1)S(1)}, u32[]{:S(2)}, u32[]{:S(2)}) %collective-permute-start) | collective-permute-done | bytes 262176 | tf_op jit(solution)/shard_map/while/body/eval_jaxpr/ppermute | solution.py:18
  67.7 1.5 bitcast_add_fusion.5
  70.0 1.9 %collective-permute-start = (bf16[128,1024]{0,1:T(8,128)(2,1)}, bf16[128,1024]{0,1:T(8,128)(2,1)S(1)}, u32[]{:S(2)}, u32[]{:S(2)}) collective-permute-start(bf16[128,1024]{0,1:T(8,128)(2,1)} %get-tuple-element.388), channel_id=1, source_target_pairs={{0,2},{2,4},{4,6},{6,8},{8,10},{10,12},{12,14},{14,16},{16,18},{18... | collective-permute-start | bytes 786440 | tf_op jit(solution)/shard_map/while/body/eval_jaxpr/ppermute | solution.py:18
  71.9 6.9 %collective-permute-done = bf16[128,1024]{0,1:T(8,128)(2,1)S(1)} collective-permute-done((bf16[128,1024]{0,1:T(8,128)(2,1)}, bf16[128,1024]{0,1:T(8,128)(2,1)S(1)}, u32[]{:S(2)}, u32[]{:S(2)}) %collective-permute-start) | collective-permute-done | bytes 262176 | tf_op jit(solution)/shard_map/while/body/eval_jaxpr/ppermute | solution.py:18
  79.9 1.5 bitcast_add_fusion.5
  82.1 1.9 %collective-permute-start = (bf16[128,1024]{0,1:T(8,128)(2,1)}, bf16[128,1024]{0,1:T(8,128)(2,1)S(1)}, u32[]{:S(2)}, u32[]{:S(2)}) collective-permute-start(bf16[128,1024]{0,1:T(8,128)(2,1)} %get-tuple-element.388), channel_id=1, source_target_pairs={{0,2},{2,4},{4,6},{6,8},{8,10},{10,12},{12,14},{14,16},{16,18},{18... | collective-permute-start | bytes 786440 | tf_op jit(solution)/shard_map/while/body/eval_jaxpr/ppermute | solution.py:18
  84.0 6.9 %collective-permute-done = bf16[128,1024]{0,1:T(8,128)(2,1)S(1)} collective-permute-done((bf16[128,1024]{0,1:T(8,128)(2,1)}, bf16[128,1024]{0,1:T(8,128)(2,1)S(1)}, u32[]{:S(2)}, u32[]{:S(2)}) %collective-permute-start) | collective-permute-done | bytes 262176 | tf_op jit(solution)/shard_map/while/body/eval_jaxpr/ppermute | solution.py:18
  92.0 1.5 bitcast_add_fusion.5
  94.3 1.9 %collective-permute-start = (bf16[128,1024]{0,1:T(8,128)(2,1)}, bf16[128,1024]{0,1:T(8,128)(2,1)S(1)}, u32[]{:S(2)}, u32[]{:S(2)}) collective-permute-start(bf16[128,1024]{0,1:T(8,128)(2,1)} %get-tuple-element.388), channel_id=1, source_target_pairs={{0,2},{2,4},{4,6},{6,8},{8,10},{10,12},{12,14},{14,16},{16,18},{18... | collective-permute-start | bytes 786440 | tf_op jit(solution)/shard_map/while/body/eval_jaxpr/ppermute | solution.py:18
  96.2 6.9 %collective-permute-done = bf16[128,1024]{0,1:T(8,128)(2,1)S(1)} collective-permute-done((bf16[128,1024]{0,1:T(8,128)(2,1)}, bf16[128,1024]{0,1:T(8,128)(2,1)S(1)}, u32[]{:S(2)}, u32[]{:S(2)}) %collective-permute-start) | collective-permute-done | bytes 262176 | tf_op jit(solution)/shard_map/while/body/eval_jaxpr/ppermute | solution.py:18
  104.2 1.5 bitcast_add_fusion.5
  106.4 1.9 %collective-permute-start = (bf16[128,1024]{0,1:T(8,128)(2,1)}, bf16[128,1024]{0,1:T(8,128)(2,1)S(1)}, u32[]{:S(2)}, u32[]{:S(2)}) collective-permute-start(bf16[128,1024]{0,1:T(8,128)(2,1)} %get-tuple-element.388), channel_id=1, source_target_pairs={{0,2},{2,4},{4,6},{6,8},{8,10},{10,12},{12,14},{14,16},{16,18},{18... | collective-permute-start | bytes 786440 | tf_op jit(solution)/shard_map/while/body/eval_jaxpr/ppermute | solution.py:18
  108.3 6.9 %collective-permute-done = bf16[128,1024]{0,1:T(8,128)(2,1)S(1)} collective-permute-done((bf16[128,1024]{0,1:T(8,128)(2,1)}, bf16[128,1024]{0,1:T(8,128)(2,1)S(1)}, u32[]{:S(2)}, u32[]{:S(2)}) %collective-permute-start) | collective-permute-done | bytes 262176 | tf_op jit(solution)/shard_map/while/body/eval_jaxpr/ppermute | solution.py:18
  116.3 1.5 bitcast_add_fusion.5
  117.9 0.7 copy.121
  118.6 1.9 %copy.82 = f32[128,4,8,128]{0,3,2,1:T(8,128)} copy(f32[128,4,8,128]{3,0,2,1:T(8,128)S(1)} %get-tuple-element.233) | data formatting | bytes 4194304 | tf_op jit(solution)/shard_map/while | solution.py:55
  121.0 3.2 %dynamic-slice_bitcast_fusion.1 = bf16[16,1,64,1024]{3,2,0,1:T(8,128)(2,1)} fusion(bf16[16,2,64,1024]{3,2,1,0:T(8,128)(2,1)} %bitcast.156, s32[]{:T(128)S(6)} %select_n.54), kind=kLoop, calls=%fused_computation.44 | loop fusion | bytes 4194308
  124.2 3.2 %reshape_reshape.3 = bf16[2,512,4,2,128]{4,3,2,1,0:T(2,128)(2,1)S(1)} reshape(bf16[16,1,64,1024]{3,2,0,1:T(8,128)(2,1)} %dynamic-slice_bitcast_fusion.1) | data formatting | bytes 4194304 | tf_op jit(solution)/shard_map/reshape;reshape | solution.py:49
  127.7 16.3 %while.34 = (s32[]{:T(128)}, f32[128,4,8]{0,2,1:T(8,128)S(1)}, f32[128,4,8]{0,2,1:T(8,128)S(1)}, f32[128,4,8,128]{0,3,2,1:T(8,128)}, pred[2,128,512]{1,2,0:T(8,1...) while((s32[]{:T(128)}, f32[128,4,8]{0,2,1:T(8,128)S(1)}, ...), condition=%wide.region_10.11_spmd, body=%wide.region_7.10_spmd.sunk | while | flops 1102061568 | bytes 53018780 | solution.py:55
  127.7 0.7 constant_dynamic-slice_fusion.2
  128.6 1.3 fusion.56
  129.9 2.1 %fusion.57 = f32[128,4,8]{0,2,1:T(8,128)S(1)} fusion(f32[4,512,128,8]{2,1,3,0:T(8,128)S(1)} %get-tuple-element.376, f32[128,4,8]{0,2,1:T(8,128)S(1)} %max.13, pred[128,512]{0,1:T(8,128)(4,1)S(1)} %dynamic-slice_bitcast_fusion.4), kind=kLoop, calls=%fused_computation.26.clone.1 | loop fusion | flops 10481664 | bytes 8486912 | tf_op jit(solution)/shard_map/while/body/eval_jaxpr/reduce_sum | solution.py:34
  132.0 2.5 %bitcast_add_fusion.6 = f32[128,4,8,128]{0,3,2,1:T(8,128)S(1)} fusion(f32[128,4,8,128]{0,3,2,1:T(8,128)S(1)} %copy-done.1, f32[4,512,128,8]{2,1,3,0:T(8,128)S(1)} %get-tuple-element.376, f32[128,4,8]{0,2,1:T(8,128)S(1)} %max.13, pred[128,512]{0,1:T(8,128)(4,1)S(1)} %dynamic-slice_bitcast_fusion.4, f32[128,4,8]{0,2,1:T(8,128)S(1)} %get-tuple-element.378, ...), kind=kOutput, calls=%fused_computation.29.clone.1 | convolution fusion | flops 548405248 | bytes 13205504 | tf_op jit(solution)/shard_map/while/body/eval_jaxpr/tgqk,kgd->tgqd/dot_general | solution.py:35
  134.5 1.3 copy-done.2
  135.8 0.7 constant_dynamic-slice_fusion.2
  136.7 1.3 fusion.56
  138.0 2.1 %fusion.57 = f32[128,4,8]{0,2,1:T(8,128)S(1)} fusion(f32[4,512,128,8]{2,1,3,0:T(8,128)S(1)} %get-tuple-element.376, f32[128,4,8]{0,2,1:T(8,128)S(1)} %max.13, pred[128,512]{0,1:T(8,128)(4,1)S(1)} %dynamic-slice_bitcast_fusion.4), kind=kLoop, calls=%fused_computation.26.clone.1 | loop fusion | flops 10481664 | bytes 8486912 | tf_op jit(solution)/shard_map/while/body/eval_jaxpr/reduce_sum | solution.py:34
  140.1 2.5 %bitcast_add_fusion.6 = f32[128,4,8,128]{0,3,2,1:T(8,128)S(1)} fusion(f32[128,4,8,128]{0,3,2,1:T(8,128)S(1)} %copy-done.1, f32[4,512,128,8]{2,1,3,0:T(8,128)S(1)} %get-tuple-element.376, f32[128,4,8]{0,2,1:T(8,128)S(1)} %max.13, pred[128,512]{0,1:T(8,128)(4,1)S(1)} %dynamic-slice_bitcast_fusion.4, f32[128,4,8]{0,2,1:T(8,128)S(1)} %get-tuple-element.378, ...), kind=kOutput, calls=%fused_computation.29.clone.1 | convolution fusion | flops 548405248 | bytes 13205504 | tf_op jit(solution)/shard_map/while/body/eval_jaxpr/tgqk,kgd->tgqd/dot_general | solution.py:35
  142.6 1.3 copy-done.2
  143.9 1.9 %divide_convert_fusion = bf16[128,4,8,128]{0,3,2,1:T(8,128)(2,1)S(1)} fusion(f32[128,4,8,128]{0,3,2,1:T(8,128)} %get-tuple-element.172, f32[128,4,8]{0,2,1:T(8,128)S(1)} %get-tuple-element.173), kind=kLoop, calls=%fused_computation.43 | loop fusion | flops 1048576 | bytes 3162112 | tf_op jit(solution)/shard_map/convert_element_type | solution.py:120
  145.8 1.0 copy.85
  147.3 11.9 %all_to_all.16 = bf16[2,64,4096]{2,1,0:T(8,128)(2,1)S(1)} all-to-all(bf16[2,64,4096]{2,1,0:T(8,128)(2,1)S(1)} %convert_element_type.23), channel_id=1, replica_groups=mesh['seq'=16,'head'=2] {'head'}, dimensions={0} | all-to-all | bytes 2097152 | tf_op jit(solution)/shard_map/all_to_all | solution.py:122
  159.2 1.0 copy.105
  (76 shorter events, 14.4 us)
Async XLA Ops:
  6.5 2.0 %copy-start = (s32[2,16]{1,0:T(2,128)S(1)}, s32[2,16]{1,0:T(2,128)}, u32[]{:S(2)}) copy-start(s32[2,16]{1,0:T(2,128)} %param.13) | copy-start | bytes 388
  6.5 114.5 %all-gather.2.cloned.1.call-start = ((), (), s32[]{:S(2)}) async-start(), calls=%async_computation.1 | async-start | bytes 4456448 | tf_op jit(solution)/shard_map/all_gather | solution.py:98
  17.3 15.0 %collective-permute-start = (bf16[128,1024]{0,1:T(8,128)(2,1)}, bf16[128,1024]{0,1:T(8,128)(2,1)S(1)}, u32[]{:S(2)}, u32[]{:S(2)}) collective-permute-start(bf16[128,1024]{0,1:T(8,128)(2,1)} %get-tuple-element.388), channel_id=1, source_target_pairs={{0,2},{2,4},{4,6},{6,8},{8,10},{10,12},{12,14},{14,16},{16,18},{18... | collective-permute-start | bytes 786440 | tf_op jit(solution)/shard_map/while/body/eval_jaxpr/ppermute | solution.py:18
  35.6 18.8 %collective-permute-start = (bf16[128,1024]{0,1:T(8,128)(2,1)}, bf16[128,1024]{0,1:T(8,128)(2,1)S(1)}, u32[]{:S(2)}, u32[]{:S(2)}) collective-permute-start(bf16[128,1024]{0,1:T(8,128)(2,1)} %get-tuple-element.388), channel_id=1, source_target_pairs={{0,2},{2,4},{4,6},{6,8},{8,10},{10,12},{12,14},{14,16},{16,18},{18... | collective-permute-start | bytes 786440 | tf_op jit(solution)/shard_map/while/body/eval_jaxpr/ppermute | solution.py:18
  57.8 8.8 %collective-permute-start = (bf16[128,1024]{0,1:T(8,128)(2,1)}, bf16[128,1024]{0,1:T(8,128)(2,1)S(1)}, u32[]{:S(2)}, u32[]{:S(2)}) collective-permute-start(bf16[128,1024]{0,1:T(8,128)(2,1)} %get-tuple-element.388), channel_id=1, source_target_pairs={{0,2},{2,4},{4,6},{6,8},{8,10},{10,12},{12,14},{14,16},{16,18},{18... | collective-permute-start | bytes 786440 | tf_op jit(solution)/shard_map/while/body/eval_jaxpr/ppermute | solution.py:18
  70.0 8.8 %collective-permute-start = (bf16[128,1024]{0,1:T(8,128)(2,1)}, bf16[128,1024]{0,1:T(8,128)(2,1)S(1)}, u32[]{:S(2)}, u32[]{:S(2)}) collective-permute-start(bf16[128,1024]{0,1:T(8,128)(2,1)} %get-tuple-element.388), channel_id=1, source_target_pairs={{0,2},{2,4},{4,6},{6,8},{8,10},{10,12},{12,14},{14,16},{16,18},{18... | collective-permute-start | bytes 786440 | tf_op jit(solution)/shard_map/while/body/eval_jaxpr/ppermute | solution.py:18
  82.1 8.8 %collective-permute-start = (bf16[128,1024]{0,1:T(8,128)(2,1)}, bf16[128,1024]{0,1:T(8,128)(2,1)S(1)}, u32[]{:S(2)}, u32[]{:S(2)}) collective-permute-start(bf16[128,1024]{0,1:T(8,128)(2,1)} %get-tuple-element.388), channel_id=1, source_target_pairs={{0,2},{2,4},{4,6},{6,8},{8,10},{10,12},{12,14},{14,16},{16,18},{18... | collective-permute-start | bytes 786440 | tf_op jit(solution)/shard_map/while/body/eval_jaxpr/ppermute | solution.py:18
  94.3 8.8 %collective-permute-start = (bf16[128,1024]{0,1:T(8,128)(2,1)}, bf16[128,1024]{0,1:T(8,128)(2,1)S(1)}, u32[]{:S(2)}, u32[]{:S(2)}) collective-permute-start(bf16[128,1024]{0,1:T(8,128)(2,1)} %get-tuple-element.388), channel_id=1, source_target_pairs={{0,2},{2,4},{4,6},{6,8},{8,10},{10,12},{12,14},{14,16},{16,18},{18... | collective-permute-start | bytes 786440 | tf_op jit(solution)/shard_map/while/body/eval_jaxpr/ppermute | solution.py:18
  106.4 8.8 %collective-permute-start = (bf16[128,1024]{0,1:T(8,128)(2,1)}, bf16[128,1024]{0,1:T(8,128)(2,1)S(1)}, u32[]{:S(2)}, u32[]{:S(2)}) collective-permute-start(bf16[128,1024]{0,1:T(8,128)(2,1)} %get-tuple-element.388), channel_id=1, source_target_pairs={{0,2},{2,4},{4,6},{6,8},{8,10},{10,12},{12,14},{14,16},{16,18},{18... | collective-permute-start | bytes 786440 | tf_op jit(solution)/shard_map/while/body/eval_jaxpr/ppermute | solution.py:18
  129.9 2.1 %copy-start.1 = (f32[128,4,8,128]{0,3,2,1:T(8,128)S(1)}, f32[128,4,8,128]{0,3,2,1:T(8,128)}, u32[]{:S(2)}) copy-start(f32[128,4,8,128]{0,3,2,1:T(8,128)} %get-tuple-element.414) | copy-start | bytes 6291460 | tf_op jit(solution)/shard_map/while
  134.5 1.3 copy-start.2
  138.0 2.1 %copy-start.1 = (f32[128,4,8,128]{0,3,2,1:T(8,128)S(1)}, f32[128,4,8,128]{0,3,2,1:T(8,128)}, u32[]{:S(2)}) copy-start(f32[128,4,8,128]{0,3,2,1:T(8,128)} %get-tuple-element.414) | copy-start | bytes 6291460 | tf_op jit(solution)/shard_map/while
  142.6 1.3 copy-start.2
Sparse Core Ops, SparseCore 0:
  9.5 54.7 all-gather.1
where the time goes:
time: 168 us; the launch traced here: 167 us
  waiting for transfers between devices  65 us (39%)
  local copies, waits for them, and re-layouts  26 us (15%)
  matrix products  25.4 us (15%)
  between operations  13.6 us (8%)
  starting transfers between devices  13.4 us (8%)
  blocking collectives  11.9 us (7%)
  other arithmetic  11.3 us (7%)
    ppermute x7, waiting for transfers between devices, from_behind(): lax.ppermute(value, axis, [(source, source + steps) for source in range(l...  64.3 us
    dot_general x10, matrix products, attend(): jnp.einsum('tgqk,kgd->tgqd', weights.astype(jnp.bfloat16), value_rows, pr...  17.8 us
    ppermute x7, starting transfers between devices, from_behind(): lax.ppermute(value, axis, [(source, source + steps) for source in range(l...  13.4 us
    all_to_all x1, blocking collectives, body(): lax.all_to_all(result, 'head', split_axis=0, concat_axis=1, tiled=True)  11.9 us
    reduce_sum x10, other arithmetic, attend(): running_sum = running_sum * rescale + jnp.sum(weights, axis=-1)  8.55 us
    dot_general x10, matrix products, attend(): jnp.einsum('tgqd,kgd->tgqk', queries, key_rows, preferred_element_type=jn...  7.6 us
    while x24, local copies, waits for them, and re-layouts  7.6 us
    unnamed x4, local copies, waits for them, and re-layouts  4.8 us
  transfers between devices with their start and end apart: 8, of which 7 were waited for; matrix products, arithmetic and copies ran while one was open for 21% of the time, Pallas kernels for 0%

commit v1 on v0

v1 whole, which is shorter than its diff:
```python
import functools
import math

import jax
import jax.numpy as jnp
from jax import lax
from jax.experimental import pallas as pl
from jax.experimental.pallas import tpu as pltpu
from jax.sharding import PartitionSpec as P

QH = 64
KVH = 8
HD = 128
REQS = 2
PER_GROUP = QH // KVH
EXP2_SCALE = HD ** (-0.5) * math.log2(math.e)
MASKED = -1e30


def swap(value, bit):
    count = lax.axis_size("seq")
    return lax.ppermute(value, "seq", [(source, source ^ bit) for source in range(count)])


def hypercube_order(bits):
    order = [0]
    for bit in bits:
        order = order + [offset ^ bit for offset in order]
    return order


def gather_half(own, bits):
    pieces = [own]
    for bit in bits:
        pieces.append(swap(pieces[0] if len(pieces) == 1 else jnp.concatenate(pieces, axis=0), bit))
    return pieces


def attend_kernel(spec, place_ref, limit_ref, owner_ref, q_ref, *refs):
    tokens, page, chunk, groups, piece_sizes, orders, group_size = spec
    piece_count = len(piece_sizes)
    halves = [refs[:piece_count], refs[piece_count : 2 * piece_count]]
    out_ref = refs[2 * piece_count]
    page_seen, keys, values, scores, weights = refs[2 * piece_count + 1 :]
    half_cols = groups * HD
    chunks = len(orders[0])
    total_keys = chunks * chunk
    me = place_ref[0]
    request = me // group_size

    def note_page(index, carry):
        page_seen[owner_ref[request, index]] = jnp.clip(limit_ref[request] - index * page, 0, page)
        return carry

    lax.fori_loop(0, owner_ref.shape[1], note_page, 0)

    row = lax.broadcasted_iota(jnp.int32, (chunk, HD), 0)
    lane = lax.broadcasted_iota(jnp.int32, (chunk, HD), 1)
    for at, offset in enumerate(orders[0]):
        source = me ^ offset
        span_seen = jnp.where(source <= me, tokens, 0)
        seen = row < span_seen
        for which in range((chunk - tokens) // page):
            start = tokens + which * page
            count = page_seen[source ^ (which * group_size)]
            seen = seen | ((row >= start) & (row < start + count))
        bias = jnp.where(seen | (lane > 0), jnp.float32(0.0), jnp.float32(MASKED))
        keys[pl.ds(at * chunk, chunk), HD:] = bias.astype(jnp.bfloat16)
    values[:, HD:] = jnp.ones((total_keys, HD), jnp.bfloat16)

    pair = 2 * tokens
    ones = (lax.broadcasted_iota(jnp.int32, (pair, HD), 1) == 0).astype(jnp.bfloat16)
    causal = lax.broadcasted_iota(jnp.int32, (pair, tokens), 1) <= (
        lax.broadcasted_iota(jnp.int32, (pair, tokens), 0) % tokens
    )

    def fill(target, column):
        half, start = divmod(column, half_cols)
        order = orders[half]
        at = 0
        for piece, size in zip(halves[half], piece_sizes):
            for inner in range(size):
                slot = orders[0].index(order[at])
                target[pl.ds(slot * chunk, chunk), :HD] = piece[
                    pl.ds(inner * chunk, chunk), pl.ds(start, HD)
                ]
                at += 1

    for group in range(groups):
        fill(keys, group * 2 * HD)
        fill(values, group * 2 * HD + HD)

        def one_pair(index, carry):
            first = pl.multiple_of((group * PER_GROUP + index * 2) * HD, HD)
            second = pl.multiple_of(first + HD, HD)
            both = jnp.concatenate([q_ref[:, pl.ds(first, HD)], q_ref[:, pl.ds(second, HD)]], axis=0)
            query = jnp.concatenate([both, ones], axis=1)
            top = jnp.full((pair, HD), MASKED, jnp.float32)
            for at in range(chunks):
                part = lax.dot_general(
                    query,
                    keys[pl.ds(at * chunk, chunk), :],
                    (((1,), (1,)), ((), ())),
                    preferred_element_type=jnp.float32,
                )
                if at == 0:
                    part = jnp.concatenate(
                        [jnp.where(causal, part[:, :tokens], MASKED), part[:, tokens:]], axis=1
                    )
                scores[:, pl.ds(at * chunk, chunk)] = part
                for lane_at in range(0, chunk, HD):
                    top = jnp.maximum(top, part[:, lane_at : lane_at + HD])
            top = jnp.max(top, axis=1, keepdims=True)
            for at in range(chunks):
                part = scores[:, pl.ds(at * chunk, chunk)]
                weights[:, pl.ds(at * chunk, chunk)] = jnp.exp2((part - top) * EXP2_SCALE).astype(
                    jnp.bfloat16
                )
            summed = jnp.dot(weights[...], values[...], preferred_element_type=jnp.float32)
            result = (summed[:, :HD] / summed[:, HD:]).astype(jnp.bfloat16)
            out_ref[:, pl.ds(first, HD)] = result[:tokens]
            out_ref[:, pl.ds(second, HD)] = result[tokens:]
            return carry

        lax.fori_loop(0, PER_GROUP // 2, one_pair, 0)


def attend(place, limits, owners, queries, halves, orders, tokens, page, group_size):
    columns = queries.shape[1]
    groups = columns // (PER_GROUP * HD)
    chunk = halves[0][0].shape[0]
    sizes = tuple(piece.shape[0] // chunk for piece in halves[0])
    total_keys = sum(sizes) * chunk
    spec = (tokens, page, chunk, groups, sizes, orders, group_size)
    whole = pl.BlockSpec(memory_space=pltpu.VMEM)
    scalars = pl.BlockSpec(memory_space=pltpu.SMEM)
    flops = 2 * tokens * columns * total_keys * 3
    return pl.pallas_call(
        functools.partial(attend_kernel, spec),
        out_shape=jax.ShapeDtypeStruct(queries.shape, jnp.bfloat16),
        in_specs=[scalars] * 3 + [whole] * (1 + 2 * len(sizes)),
        out_specs=whole,
        scratch_shapes=[
            pltpu.SMEM((owners.shape[1],), jnp.int32),
            pltpu.VMEM((total_keys, 2 * HD), jnp.bfloat16),
            pltpu.VMEM((total_keys, 2 * HD), jnp.bfloat16),
            pltpu.VMEM((2 * tokens, total_keys), jnp.float32),
            pltpu.VMEM((2 * tokens, total_keys), jnp.bfloat16),
        ],
        compiler_params=pltpu.CompilerParams(vmem_limit_bytes=48 * 1024 * 1024),
        cost_estimate=pl.CostEstimate(flops=flops, bytes_accessed=8 << 20, transcendentals=0),
    )(place, limits, owners, queries, *halves[0], *halves[1])


def body(span_query, span_kv, prefix_cache, prefix_len, block_owner):
    tokens = span_query.shape[0]
    seq_size = lax.axis_size("seq")
    group_size = seq_size // REQS
    me = lax.axis_index("seq").astype(jnp.int32)
    request = me // group_size
    page = prefix_cache.shape[1]
    own_page = lax.dynamic_index_in_dim(prefix_cache, request, 0, keepdims=False)
    other_page = lax.dynamic_index_in_dim(prefix_cache, 1 - request, 0, keepdims=False)
    crossed = swap(other_page, group_size)
    rows = jnp.concatenate([span_kv, own_page, crossed], axis=0)
    half_cols = rows.shape[1] // 2
    bits = [1 << at for at in range(group_size.bit_length() - 1)]
    bit_orders = (bits[1:] + bits[:1], bits[:0:-1] + bits[:1])
    halves = [
        gather_half(rows[:, :half_cols], bit_orders[0]),
        gather_half(rows[:, half_cols:], bit_orders[1]),
    ]
    orders = tuple(tuple(hypercube_order(order)) for order in bit_orders)
    result = attend(
        me.reshape(1), prefix_len, block_owner, span_query, halves, orders, tokens, page, group_size
    )
    return lax.all_to_all(result, "head", split_axis=0, concat_axis=1, tiled=True)


def solution(mesh):
    placed = (P("seq", "head"), P("seq", "head"), P("seq", None, "head"), P(), P())
    return jax.shard_map(
        body, mesh=mesh, in_specs=placed, out_specs=P(("seq", "head"), None), check_vma=False
    )
```

time: 168 us -> 79.9 us (0.48)
  the two profiles are of different devices: /device:TPU:16 before, /device:TPU:0 now
where the time goes in v1:
time: 79.9 us; the launch traced here: 79.7 us
  waiting for transfers between devices  25 us (31%)
  Pallas kernels  25 us (31%)
  blocking collectives  16.6 us (21%)
  starting transfers between devices  9.6 us (12%)
  local copies, waits for them, and re-layouts  2.09 us (3%)
  other arithmetic  1.19 us (1%)
    pallas_call x1, Pallas kernels, attend(): pl.pallas_call(functools.partial(attend_kernel, spec), out_shape=jax.Shap...  25 us
    ppermute x7, waiting for transfers between devices, swap(): lax.ppermute(value, 'seq', [(source, source ^ bit) for source in range(co...  25 us
    all_to_all x1, blocking collectives, body(): lax.all_to_all(result, 'head', split_axis=0, concat_axis=1, tiled=True)  16.6 us
    ppermute x7, starting transfers between devices, swap(): lax.ppermute(value, 'seq', [(source, source ^ bit) for source in range(co...  9.6 us
  transfers between devices with their start and end apart: 7, of which 6 were waited for; matrix products, arithmetic and copies ran while one was open for 0% of the time, Pallas kernels for 0%

profile of v1, /device:TPU:0, one launch (start us, length us, event | category | flops | bytes accessed | tf_op | source)
XLA Modules:
  0.0 79.7 jit_solution(5900103728127629896)
XLA Ops:
  0.0 1.0 %dynamic-slice_bitcast_fusion.1 = (bf16[64,1024]{1,0:T(8,128)(2,1)S(1)}, bf16[64,1024]{1,0:T(8,128)(2,1)S(1)}) fusion(bf16[2,64,1024]{2,1,0:T(8,128)(2,1)} %param.7, s32[]{:T(128)S(6)} %select_n.13, s32[]{:T(128)S(6)} %select_n.14), kind=kLoop, calls=%fused_computation.6 | loop fusion | bytes 524296 | tf_op jit(solution)/shard_map/jit(dynamic_index_in_dim)/squeeze | solution.py:162
  1.0 4.1 %collective-permute-start = (bf16[64,1024]{1,0:T(8,128)(2,1)S(1)}, bf16[64,1024]{1,0:T(8,128)(2,1)S(1)}, u32[]{:S(2)}, u32[]{:S(2)}) collective-permute-start(bf16[64,1024]{1,0:T(8,128)(2,1)S(1)} %get-tuple-element.8), channel_id=1, source_target_pairs={{0,16},{2,18},{4,20},{6,22},{8,24},{10,26},{12,28},{14,30},{16,0},... | collective-permute-start | bytes 393224 | tf_op jit(solution)/shard_map/ppermute | solution.py:22
  5.1 6.3 %collective-permute-done = bf16[64,1024]{1,0:T(8,128)(2,1)S(1)} collective-permute-done((bf16[64,1024]{1,0:T(8,128)(2,1)S(1)}, bf16[64,1024]{1,0:T(8,128)(2,1)S(1)}, u32[]{:S(2)}, u32[]{:S(2)}) %collective-permute-start) | collective-permute-done | bytes 131104 | tf_op jit(solution)/shard_map/ppermute | solution.py:22
  11.4 1.0 %pad_maximum_fusion.2 = bf16[256,1024]{1,0:T(8,128)(2,1)S(1)} fusion(bf16[64,1024]{1,0:T(8,128)(2,1)S(1)} %collective-permute-done, bf16[64,1024]{1,0:T(8,128)(2,1)S(1)} %get-tuple-element.7, bf16[128,1024]{1,0:T(8,128)(2,1)} %param.6), kind=kLoop, calls=%fused_computation.2 | loop fusion | flops 1572864 | bytes 1048576 | tf_op jit(solution)/shard_map/concatenate | solution.py:165
  12.4 0.8 collective-permute-start.4
  13.2 1.5 %collective-permute-start.1 = (bf16[256,512]{1,0:T(8,128)(2,1)S(1)}, bf16[256,512]{1,0:T(8,128)(2,1)S(1)}, u32[]{:S(2)}, u32[]{:S(2)}) collective-permute-start(bf16[256,512]{1,0:T(8,128)(2,1)S(1)} %get-tuple-element.6.refs_0_), channel_id=1, source_target_pairs={{0,4},{2,6},{4,0},{6,2},{8,12},{10,14},{12,8},{14,10},{16,20},{18,... | collective-permute-start | bytes 786440 | tf_op jit(solution)/shard_map/ppermute | solution.py:22
  14.7 5.3 %collective-permute-done.4.refs_5_ = bf16[256,512]{1,0:T(8,128)(2,1)S(1)} collective-permute-done((bf16[256,512]{1,0:T(8,128)(2,1)S(1)}, bf16[256,512]{1,0:T(8,128)(2,1)S(1)}, u32[]{:S(2)}, u32[]{:S(2)}) %collective-permute-start.4) | collective-permute-done | bytes 262176 | tf_op jit(solution)/shard_map/ppermute | solution.py:22
  20.0 1.3 %collective-permute-start.5 = (bf16[512,512]{1,0:T(8,128)(2,1)S(1)}, bf16[512,512]{1,0:T(8,128)(2,1)S(1)}, u32[]{:S(2)}, u32[]{:S(2)}) collective-permute-start(bf16[512,512]{1,0:T(8,128)(2,1)S(1)} %pad_maximum_fusion.4), channel_id=1, source_target_pairs={{0,4},{2,6},{4,0},{6,2},{8,12},{10,14},{12,8},{14,10},{16,20},{18,... | collective-permute-start | bytes 1572872 | tf_op jit(solution)/shard_map/ppermute | solution.py:22
  21.3 0.0 collective-permute-done.1.refs_1_
  21.4 1.8 %collective-permute-start.2 = (bf16[512,512]{1,0:T(8,128)(2,1)S(1)}, bf16[512,512]{1,0:T(8,128)(2,1)S(1)}, u32[]{:S(2)}, u32[]{:S(2)}) collective-permute-start(bf16[512,512]{1,0:T(8,128)(2,1)S(1)} %pad_maximum_fusion.3), channel_id=1, source_target_pairs={{0,8},{2,10},{4,12},{6,14},{8,0},{10,2},{12,4},{14,6},{16,24},{18,... | collective-permute-start | bytes 1572872 | tf_op jit(solution)/shard_map/ppermute | solution.py:22
  23.1 9.3 %collective-permute-done.5.refs_6_ = bf16[512,512]{1,0:T(8,128)(2,1)S(1)} collective-permute-done((bf16[512,512]{1,0:T(8,128)(2,1)S(1)}, bf16[512,512]{1,0:T(8,128)(2,1)S(1)}, u32[]{:S(2)}, u32[]{:S(2)}) %collective-permute-start.5) | collective-permute-done | bytes 524320 | tf_op jit(solution)/shard_map/ppermute | solution.py:22
  32.4 0.1 pad_maximum_fusion.1
  32.5 0.0 copy-start
  32.5 0.0 copy-start.1
  32.5 0.0 copy-start.2
  32.5 0.1 collective-permute-start.6
  32.6 1.5 %collective-permute-done.2.refs_2_ = bf16[512,512]{1,0:T(8,128)(2,1)S(1)} collective-permute-done((bf16[512,512]{1,0:T(8,128)(2,1)S(1)}, bf16[512,512]{1,0:T(8,128)(2,1)S(1)}, u32[]{:S(2)}, u32[]{:S(2)}) %collective-permute-start.2) | collective-permute-done | bytes 524320 | tf_op jit(solution)/shard_map/ppermute | solution.py:22
  34.1 0.1 pad_maximum_fusion
  34.2 0.1 collective-permute-start.3
  34.3 1.0 %collective-permute-done.6.refs_7_ = bf16[1024,512]{1,0:T(8,128)(2,1)S(1)} collective-permute-done((bf16[1024,512]{1,0:T(8,128)(2,1)S(1)}, bf16[1024,512]{1,0:T(8,128)(2,1)S(1)}, u32[]{:S(2)}, u32[]{:S(2)}) %collective-permute-start.6) | collective-permute-done | bytes 1048608 | tf_op jit(solution)/shard_map/ppermute | solution.py:22
  35.2 0.0 copy-start.3
  35.2 1.7 %collective-permute-done.3.refs_3_ = bf16[1024,512]{1,0:T(8,128)(2,1)S(1)} collective-permute-done((bf16[1024,512]{1,0:T(8,128)(2,1)S(1)}, bf16[1024,512]{1,0:T(8,128)(2,1)S(1)}, u32[]{:S(2)}, u32[]{:S(2)}) %collective-permute-start.3) | collective-permute-done | bytes 1048608 | tf_op jit(solution)/shard_map/ppermute | solution.py:22
  36.9 0.0 copy-done.3
  36.9 0.0 copy-done
  36.9 0.0 copy-done.1
  36.9 0.0 copy-done.2
  36.9 25.0 %shard_map.55 = bf16[128,4096]{1,0:T(8,128)(2,1)S(1)} custom-call(s32[1]{0:T(128)} %bitcast.place_ref, s32[2]{0:T(128)S(1)} %copy-done.2, s32[2,16]{1,0:T(2,128)S(1)} %copy-done.1, bf16[128,4096]{1,0:T(8,128)(2,1)S(1)} %copy-done, bf16[256,512]{1,0:T(8,128)(2,1)S(1)} %get-tuple-element.6.refs_0_, bf16[256,512]{1,0:T(8,128)(2,1)S(1)} %collective-permute-done.1.refs_1_, ...), custom_call_target="tpu_custom_call" | custom-call | flops 6442450944 | bytes 8388608 | tf_op jit(solution)/shard_map/pallas_call | solution.py:138
  62.0 16.6 %all_to_all.19 = bf16[2,64,4096]{2,1,0:T(8,128)(2,1)S(1)} all-to-all(bf16[2,64,4096]{2,1,0:T(8,128)(2,1)S(1)} %bitcast.9), channel_id=1, replica_groups=mesh['seq'=16,'head'=2] {'head'}, dimensions={0} | all-to-all | bytes 2097152 | tf_op jit(solution)/shard_map/all_to_all | solution.py:177
  78.6 1.0 %copy.7 = bf16[2,8,8,4096]{3,2,0,1:T(8,128)(2,1)} copy(bf16[2,8,8,4096]{3,2,1,0:T(8,128)(2,1)S(1)} %bitcast.10) | data formatting | bytes 2097152 | tf_op jit(solution)/shard_map/all_to_all | solution.py:177
  (3 shorter events, 0.1 us)
Async XLA Ops:
  1.0 10.4 %collective-permute-start = (bf16[64,1024]{1,0:T(8,128)(2,1)S(1)}, bf16[64,1024]{1,0:T(8,128)(2,1)S(1)}, u32[]{:S(2)}, u32[]{:S(2)}) collective-permute-start(bf16[64,1024]{1,0:T(8,128)(2,1)S(1)} %get-tuple-element.8), channel_id=1, source_target_pairs={{0,16},{2,18},{4,20},{6,22},{8,24},{10,26},{12,28},{14,30},{16,0},... | collective-permute-start | bytes 393224 | tf_op jit(solution)/shard_map/ppermute | solution.py:22
  12.4 7.6 %collective-permute-start.4 = (bf16[256,512]{1,0:T(8,128)(2,1)S(1)}, bf16[256,512]{1,0:T(8,128)(2,1)S(1)}, u32[]{:S(2)}, u32[]{:S(2)}) collective-permute-start(bf16[256,512]{1,0:T(8,128)(2,1)S(1)} %get-tuple-element.5.refs_4_), channel_id=1, source_target_pairs={{0,8},{2,10},{4,12},{6,14},{8,0},{10,2},{12,4},{14,6},{16,24},{18,... | collective-permute-start | bytes 786440 | tf_op jit(solution)/shard_map/ppermute | solution.py:22
  13.2 8.1 %collective-permute-start.1 = (bf16[256,512]{1,0:T(8,128)(2,1)S(1)}, bf16[256,512]{1,0:T(8,128)(2,1)S(1)}, u32[]{:S(2)}, u32[]{:S(2)}) collective-permute-start(bf16[256,512]{1,0:T(8,128)(2,1)S(1)} %get-tuple-element.6.refs_0_), channel_id=1, source_target_pairs={{0,4},{2,6},{4,0},{6,2},{8,12},{10,14},{12,8},{14,10},{16,20},{18,... | collective-permute-start | bytes 786440 | tf_op jit(solution)/shard_map/ppermute | solution.py:22
  20.0 12.4 %collective-permute-start.5 = (bf16[512,512]{1,0:T(8,128)(2,1)S(1)}, bf16[512,512]{1,0:T(8,128)(2,1)S(1)}, u32[]{:S(2)}, u32[]{:S(2)}) collective-permute-start(bf16[512,512]{1,0:T(8,128)(2,1)S(1)} %pad_maximum_fusion.4), channel_id=1, source_target_pairs={{0,4},{2,6},{4,0},{6,2},{8,12},{10,14},{12,8},{14,10},{16,20},{18,... | collective-permute-start | bytes 1572872 | tf_op jit(solution)/shard_map/ppermute | solution.py:22
  21.4 12.7 %collective-permute-start.2 = (bf16[512,512]{1,0:T(8,128)(2,1)S(1)}, bf16[512,512]{1,0:T(8,128)(2,1)S(1)}, u32[]{:S(2)}, u32[]{:S(2)}) collective-permute-start(bf16[512,512]{1,0:T(8,128)(2,1)S(1)} %pad_maximum_fusion.3), channel_id=1, source_target_pairs={{0,8},{2,10},{4,12},{6,14},{8,0},{10,2},{12,4},{14,6},{16,24},{18,... | collective-permute-start | bytes 1572872 | tf_op jit(solution)/shard_map/ppermute | solution.py:22
  32.5 4.5 %copy-start = (bf16[128,4096]{1,0:T(8,128)(2,1)S(1)}, bf16[128,4096]{1,0:T(8,128)(2,1)}, u32[]{:S(2)}) copy-start(bf16[128,4096]{1,0:T(8,128)(2,1)} %q_ref.1) | copy-start | bytes 3145732
  32.5 4.4 %copy-start.1 = (s32[2,16]{1,0:T(2,128)S(1)}, s32[2,16]{1,0:T(2,128)}, u32[]{:S(2)}) copy-start(s32[2,16]{1,0:T(2,128)} %owner_ref.1) | copy-start | bytes 388
  32.5 4.4 %copy-start.2 = (s32[2]{0:T(128)S(1)}, s32[2]{0:T(128)}, u32[]{:S(2)}) copy-start(s32[2]{0:T(128)} %limit_ref.1) | copy-start | bytes 28
  32.5 2.7 %collective-permute-start.6 = (bf16[1024,512]{1,0:T(8,128)(2,1)S(1)}, bf16[1024,512]{1,0:T(8,128)(2,1)S(1)}, u32[]{:S(2)}, u32[]{:S(2)}) collective-permute-start(bf16[1024,512]{1,0:T(8,128)(2,1)S(1)} %pad_maximum_fusion.1), channel_id=1, source_target_pairs={{0,2},{2,0},{4,6},{6,4},{8,10},{10,8},{12,14},{14,12},{16,18},{18,... | collective-permute-start | bytes 3145736 | tf_op jit(solution)/shard_map/ppermute | solution.py:22
  34.2 2.7 %collective-permute-start.3 = (bf16[1024,512]{1,0:T(8,128)(2,1)S(1)}, bf16[1024,512]{1,0:T(8,128)(2,1)S(1)}, u32[]{:S(2)}, u32[]{:S(2)}) collective-permute-start(bf16[1024,512]{1,0:T(8,128)(2,1)S(1)} %pad_maximum_fusion), channel_id=1, source_target_pairs={{0,2},{2,0},{4,6},{6,4},{8,10},{10,8},{12,14},{14,12},{16,18},{18,... | collective-permute-start | bytes 3145736 | tf_op jit(solution)/shard_map/ppermute | solution.py:22
  35.2 1.7 %copy-start.3 = (bf16[1024,512]{1,0:T(8,128)(2,1)}, bf16[1024,512]{1,0:T(8,128)(2,1)S(1)}, u32[]{:S(2)}) copy-start(bf16[1024,512]{1,0:T(8,128)(2,1)S(1)} %collective-permute-done.6.refs_7_) | copy-start | bytes 3145732

commit v2 on v1

v2 whole, which is shorter than its diff:
```python
import functools
import math

import jax
import jax.numpy as jnp
from jax import lax
from jax.experimental import pallas as pl
from jax.experimental.pallas import tpu as pltpu
from jax.sharding import PartitionSpec as P

QH = 64
KVH = 8
HD = 128
REQS = 2
PER_GROUP = QH // KVH
EXP2_SCALE = HD ** (-0.5) * math.log2(math.e)
MASKED = -1e30
SCORE_BYTES = 8 * 1024 * 1024


def swap(value, axis, bit):
    count = lax.axis_size(axis)
    return lax.ppermute(value, axis, [(source, source ^ bit) for source in range(count)])


def gather_strip(own, bits):
    pieces, offsets = [own], [0]
    places = [[0]]
    for bit in bits:
        sent = pieces[0] if len(pieces) == 1 else jnp.concatenate(pieces, axis=0)
        pieces.append(swap(sent, "seq", bit))
        places.append([offset ^ bit for offset in offsets])
        offsets = offsets + places[-1]
    return list(zip(pieces, places))


def attend_kernel(spec, place_ref, limit_ref, owner_ref, q_ref, *refs):
    tokens, page, chunk, groups, block_heads, group_size, head_size, strips, sources = spec
    piece_refs = refs[: sum(len(strip) for strip in strips)]
    refs = refs[len(piece_refs) :]
    outs, refs = refs[:2], refs[2:]
    page_seen, keys, values, scores_a, scores_b, top_a, top_b = refs
    chunks = group_size
    me = place_ref[0]
    my_head = place_ref[1]
    request = me // group_size

    def note_page(index, carry):
        page_seen[owner_ref[request, index]] = jnp.clip(limit_ref[request] - index * page, 0, page)
        return carry

    lax.fori_loop(0, owner_ref.shape[1], note_page, 0)

    row = lax.broadcasted_iota(jnp.int32, (chunk, HD), 0)
    lane = lax.broadcasted_iota(jnp.int32, (chunk, HD), 1)
    for offset in range(chunks):
        source = me ^ offset
        seen = row < jnp.where(source <= me, tokens, 0)
        for which in range((chunk - tokens) // page):
            start = tokens + which * page
            count = page_seen[source ^ (which * group_size)]
            seen = seen | ((row >= start) & (row < start + count))
        bias = jnp.where(seen | (lane > 0), jnp.float32(0.0), jnp.float32(MASKED))
        for group in range(groups):
            keys[group, pl.ds(offset * chunk, chunk), HD:] = bias.astype(jnp.bfloat16)
    values[:, :, HD:] = jnp.ones((groups, chunks * chunk, HD), jnp.bfloat16)

    def fill(target, group, strip_at, column):
        first = sum(len(strip) for strip in strips[:strip_at])
        for ref, places in zip(piece_refs[first:], strips[strip_at]):
            for inner, offset in enumerate(places):
                target[group, pl.ds(offset * chunk, chunk), :HD] = ref[
                    pl.ds(inner * chunk, chunk), pl.ds(column, HD)
                ]

    for group in range(groups):
        fill(keys, group, *sources[2 * group])
        fill(values, group, *sources[2 * group + 1])

    block = block_heads * tokens
    blocks_a_group = PER_GROUP // block_heads
    blocks = groups * blocks_a_group
    ones = (lax.broadcasted_iota(jnp.int32, (block, HD), 1) == 0).astype(jnp.bfloat16)
    causal = lax.broadcasted_iota(jnp.int32, (block, tokens), 1) <= (
        lax.broadcasted_iota(jnp.int32, (block, tokens), 0) % tokens
    )

    def columns(index):
        return [
            pl.ds(pl.multiple_of((index * block_heads + head) * HD, HD), HD)
            for head in range(block_heads)
        ]

    def score_steps(index, scores, top):
        group = index // blocks_a_group
        query = jnp.concatenate([q_ref[:, column] for column in columns(index)], axis=0)
        query = jnp.concatenate([query, ones], axis=1)
        best = jnp.full((block, HD), MASKED, jnp.float32)
        for at in range(chunks):
            part = lax.dot_general(
                query,
                keys[group, pl.ds(at * chunk, chunk), :],
                (((1,), (1,)), ((), ())),
                preferred_element_type=jnp.float32,
            )
            if at == 0:
                own = jnp.where(causal, part[:, :tokens], MASKED)
                part = jnp.concatenate([own, part[:, tokens:]], axis=1)
            scores[:, pl.ds(at * chunk, chunk)] = part
            for lane_at in range(0, chunk, HD):
                best = jnp.maximum(best, part[:, lane_at : lane_at + HD])
            yield
        top[...] = jnp.broadcast_to(jnp.max(best, axis=1, keepdims=True), (block, HD))

    def value_steps(index, scores, top):
        group = index // blocks_a_group
        summed = jnp.zeros((block, 2 * HD), jnp.float32)
        for at in range(chunks):
            weights = []
            for lane_at in range(at * chunk, (at + 1) * chunk, HD):
                shifted = scores[:, pl.ds(lane_at, HD)] - top[...]
                weights.append(jnp.exp2(shifted * EXP2_SCALE).astype(jnp.bfloat16))
            summed = summed + jnp.dot(
                jnp.concatenate(weights, axis=1),
                values[group, pl.ds(at * chunk, chunk), :],
                preferred_element_type=jnp.float32,
            )
            yield
        result = (summed[:, :HD] / summed[:, HD:]).astype(jnp.bfloat16)
        kept = tokens // head_size
        for head, column in enumerate(columns(index)):
            one = result[head * tokens : (head + 1) * tokens]
            if head_size == 2:
                low, high = one[:kept], one[kept:]
                outs[0][:, column] = jnp.where(my_head == 0, low, high)
                outs[1][:, column] = jnp.where(my_head == 0, high, low)
            else:
                outs[0][:, column] = one[:kept]
                outs[1][:, column] = one[kept:]

    def run(*steps):
        live = list(steps)
        while live:
            for step in list(live):
                if next(step, live) is live:
                    live.remove(step)

    run(score_steps(0, scores_a, top_a))

    def two_blocks(index, carry):
        run(score_steps(2 * index + 1, scores_b, top_b), value_steps(2 * index, scores_a, top_a))
        ahead = jnp.minimum(2 * index + 2, blocks - 1)
        run(score_steps(ahead, scores_a, top_a), value_steps(2 * index + 1, scores_b, top_b))
        return carry

    lax.fori_loop(0, blocks // 2, two_blocks, 0)


def attend(place, limits, owners, queries, part, strips, sources, page, group_size, head_size):
    tokens = queries.shape[0]
    columns = len(sources) // 2 * PER_GROUP * HD
    groups = columns // (PER_GROUP * HD)
    chunk = strips[0][0][0].shape[0]
    total_keys = group_size * chunk
    block_heads = 4
    while block_heads > 1 and block_heads * tokens * total_keys * 4 > SCORE_BYTES:
        block_heads //= 2
    block = block_heads * tokens
    offsets = tuple(tuple(tuple(places) for _, places in strip) for strip in strips)
    pieces = [piece for strip in strips for piece, _ in strip]
    spec = (tokens, page, chunk, groups, block_heads, group_size, head_size, offsets, sources)
    whole = pl.BlockSpec(memory_space=pltpu.VMEM)
    scalars = pl.BlockSpec(memory_space=pltpu.SMEM)
    kept = tokens // head_size
    return pl.pallas_call(
        functools.partial(attend_kernel, spec),
        grid=(1,),
        out_shape=[
            jax.ShapeDtypeStruct((kept, columns), jnp.bfloat16),
            jax.ShapeDtypeStruct((tokens - kept, columns), jnp.bfloat16),
        ],
        in_specs=[scalars] * 3
        + [pl.BlockSpec((tokens, columns), lambda step: (0, part))]
        + [whole] * len(pieces),
        out_specs=[whole] * 2,
        scratch_shapes=[
            pltpu.SMEM((owners.shape[1],), jnp.int32),
            pltpu.VMEM((groups, total_keys, 2 * HD), jnp.bfloat16),
            pltpu.VMEM((groups, total_keys, 2 * HD), jnp.bfloat16),
            pltpu.VMEM((block, total_keys), jnp.float32),
            pltpu.VMEM((block, total_keys), jnp.float32),
            pltpu.VMEM((block, HD), jnp.float32),
            pltpu.VMEM((block, HD), jnp.float32),
        ],
        compiler_params=pltpu.CompilerParams(vmem_limit_bytes=48 * 1024 * 1024),
        cost_estimate=pl.CostEstimate(
            flops=8 * tokens * columns * total_keys,
            bytes_accessed=4 * tokens * columns + 2 * total_keys * columns // PER_GROUP,
            transcendentals=0,
        ),
    )(place, limits, owners, queries, *pieces)


def body(span_query, span_kv, prefix_cache, prefix_len, block_owner):
    seq_size = lax.axis_size("seq")
    head_size = lax.axis_size("head")
    group_size = seq_size // REQS
    me = lax.axis_index("seq").astype(jnp.int32)
    my_head = lax.axis_index("head").astype(jnp.int32)
    request = me // group_size
    page = prefix_cache.shape[1]
    own_page = lax.dynamic_index_in_dim(prefix_cache, request, 0, keepdims=False)
    other_page = lax.dynamic_index_in_dim(prefix_cache, 1 - request, 0, keepdims=False)
    crossed = swap(other_page, "seq", group_size)
    rows = jnp.concatenate([span_kv, own_page, crossed], axis=0)
    half_cols = rows.shape[1] // 2
    bits = [1 << at for at in range(group_size.bit_length() - 1)]
    bit_orders = (bits[1:] + bits[:1], bits[:0:-1] + bits[:1])
    strips = [
        gather_strip(rows[:, :half_cols], bit_orders[0]),
        gather_strip(rows[:, half_cols:], bit_orders[1]),
    ]
    groups = rows.shape[1] // (2 * HD)
    place = jnp.stack([me, my_head])
    common = (page, group_size, head_size)
    if groups % 2 or head_size != 2:
        sources = tuple(divmod(column, half_cols) for column in range(0, 2 * half_cols, HD))
        results = [
            attend(place, prefix_len, block_owner, span_query, 0, strips, sources, *common)
        ]
    else:
        sources = tuple((0, column) for column in range(0, half_cols, HD))
        results = [
            attend(
                place,
                prefix_len,
                block_owner,
                span_query,
                at,
                [strips[at]],
                sources,
                *common,
            )
            for at in range(2)
        ]
    if head_size != 2:
        joined = jnp.concatenate([jnp.concatenate(pair, axis=0) for pair in results], axis=1)
        return lax.all_to_all(joined, "head", split_axis=0, concat_axis=1, tiled=True)
    kept = [pair[0] for pair in results]
    received = [swap(pair[1], "head", 1) for pair in results]
    joined = jnp.concatenate(kept + kept, axis=1)
    start = (1 - my_head) * span_query.shape[1]
    for one in received:
        joined = lax.dynamic_update_slice(joined, one, (0, start))
        start = start + one.shape[1]
    return joined


def solution(mesh):
    placed = (P("seq", "head"), P("seq", "head"), P("seq", None, "head"), P(), P())
    return jax.shard_map(
        body, mesh=mesh, in_specs=placed, out_specs=P(("seq", "head"), None), check_vma=False
    )
```

time: 79.9 us -> 78.7 us (0.985)
  waiting for transfers between devices: 25 us -> 45.8 us
  blocking collectives: 16.6 us -> 0 us
  Pallas kernels: 25 us -> 15.9 us
  other arithmetic: 1.19 us -> 3.32 us
  starting transfers between devices: 9.6 us -> 11.5 us
    ppermute x7 -> x9, waiting for transfers between devices: 25 us -> 45.8 us  [swap(): lax.ppermute(value, axis, [(source, source ^ bit) for source in range(cou...]
    all_to_all x1 -> x0, blocking collectives: 16.6 us -> none  [body(): lax.all_to_all(result, 'head', split_axis=0, concat_axis=1, tiled=True)]
    pallas_call x1 -> x2, Pallas kernels: 25 us -> 15.9 us  [attend(): pl.pallas_call(functools.partial(attend_kernel, spec), grid=(1,), out_sha...]
    concatenate x4 -> x5, other arithmetic: 0.21 us -> 2.26 us  [the longest x4 2.16 us: gather_strip(): sent = pieces[0] if len(pieces) == 1 else jnp.concatenate(pieces, axis=0)]
    ppermute x7 -> x9, starting transfers between devices: 9.6 us -> 11.5 us  [swap(): lax.ppermute(value, axis, [(source, source ^ bit) for source in range(cou...]
    all_to_all x1 -> x0, local copies, waits for them, and re-layouts: 1.04 us -> none  [body(): lax.all_to_all(result, 'head', split_axis=0, concat_axis=1, tiled=True)]
  transfers between devices with their start and end apart: 7 -> 9, of which waited for: 6 -> 5; matrix products, arithmetic and copies ran while one was open for 0% -> 3% of each run, Pallas kernels for 0% -> 20%
where the time goes in v2:
time: 78.7 us; the launch traced here: 78.5 us
  waiting for transfers between devices  45.8 us (58%)
  Pallas kernels  15.9 us (20%)
  starting transfers between devices  11.5 us (15%)
  other arithmetic  3.32 us (4%)
  local copies, waits for them, and re-layouts  1.78 us (2%)
    ppermute x9, waiting for transfers between devices, swap(): lax.ppermute(value, axis, [(source, source ^ bit) for source in range(cou...  45.8 us
    pallas_call x2, Pallas kernels, attend(): pl.pallas_call(functools.partial(attend_kernel, spec), grid=(1,), out_sha...  15.9 us
    ppermute x9, starting transfers between devices, swap(): lax.ppermute(value, axis, [(source, source ^ bit) for source in range(cou...  11.5 us
    concatenate x4, other arithmetic, gather_strip(): sent = pieces[0] if len(pieces) == 1 else jnp.concatenate(pieces, axis=0)  2.16 us
  transfers between devices with their start and end apart: 9, of which 5 were waited for; matrix products, arithmetic and copies ran while one was open for 3% of the time, Pallas kernels for 20%

profile of v2, /device:TPU:0, one launch (start us, length us, event | category | flops | bytes accessed | tf_op | source)
XLA Modules:
  0.0 78.5 jit_solution(12300299208886615625)
XLA Ops:
  0.0 1.0 %dynamic-slice_bitcast_fusion.1 = (bf16[64,1024]{1,0:T(8,128)(2,1)S(1)}, bf16[64,1024]{1,0:T(8,128)(2,1)S(1)}) fusion(bf16[2,64,1024]{2,1,0:T(8,128)(2,1)} %param.7, s32[]{:T(128)S(6)} %select_n.19, s32[]{:T(128)S(6)} %select_n.20), kind=kLoop, calls=%fused_computation.7 | loop fusion | bytes 524296 | tf_op jit(solution)/shard_map/jit(dynamic_index_in_dim)/squeeze | solution.py:212
  1.0 4.1 %collective-permute-start = (bf16[64,1024]{1,0:T(8,128)(2,1)S(1)}, bf16[64,1024]{1,0:T(8,128)(2,1)S(1)}, u32[]{:S(2)}, u32[]{:S(2)}) collective-permute-start(bf16[64,1024]{1,0:T(8,128)(2,1)S(1)} %get-tuple-element.16), channel_id=1, source_target_pairs={{0,16},{2,18},{4,20},{6,22},{8,24},{10,26},{12,28},{14,30},{16,0},... | collective-permute-start | bytes 393224 | tf_op jit(solution)/shard_map/ppermute | solution.py:23
  5.1 6.3 %collective-permute-done = bf16[64,1024]{1,0:T(8,128)(2,1)S(1)} collective-permute-done((bf16[64,1024]{1,0:T(8,128)(2,1)S(1)}, bf16[64,1024]{1,0:T(8,128)(2,1)S(1)}, u32[]{:S(2)}, u32[]{:S(2)}) %collective-permute-start) | collective-permute-done | bytes 131104 | tf_op jit(solution)/shard_map/ppermute | solution.py:23
  11.4 1.0 %pad_maximum_fusion.3 = bf16[256,1024]{1,0:T(8,128)(2,1)S(1)} fusion(bf16[64,1024]{1,0:T(8,128)(2,1)S(1)} %collective-permute-done, bf16[64,1024]{1,0:T(8,128)(2,1)S(1)} %get-tuple-element.15, bf16[128,1024]{1,0:T(8,128)(2,1)} %param.6), kind=kLoop, calls=%fused_computation.3 | loop fusion | flops 1572864 | bytes 1048576 | tf_op jit(solution)/shard_map/concatenate | solution.py:215
  12.4 1.6 %collective-permute-start.1 = (bf16[256,512]{1,0:T(8,128)(2,1)S(1)}, bf16[256,512]{1,0:T(8,128)(2,1)S(1)}, u32[]{:S(2)}, u32[]{:S(2)}) collective-permute-start(bf16[256,512]{1,0:T(8,128)(2,1)S(1)} %get-tuple-element.13.refs_0_), channel_id=1, source_target_pairs={{0,4},{2,6},{4,0},{6,2},{8,12},{10,14},{12,8},{14,10},{16,20},{18,... | collective-permute-start | bytes 786440 | tf_op jit(solution)/shard_map/ppermute | solution.py:23
  14.0 6.0 %collective-permute-done.1.refs_1_ = bf16[256,512]{1,0:T(8,128)(2,1)S(1)} collective-permute-done((bf16[256,512]{1,0:T(8,128)(2,1)S(1)}, bf16[256,512]{1,0:T(8,128)(2,1)S(1)}, u32[]{:S(2)}, u32[]{:S(2)}) %collective-permute-start.1) | collective-permute-done | bytes 262176 | tf_op jit(solution)/shard_map/ppermute | solution.py:23
  20.0 1.5 %collective-permute-start.2 = (bf16[512,512]{1,0:T(8,128)(2,1)S(1)}, bf16[512,512]{1,0:T(8,128)(2,1)S(1)}, u32[]{:S(2)}, u32[]{:S(2)}) collective-permute-start(bf16[512,512]{1,0:T(8,128)(2,1)S(1)} %pad_maximum_fusion.4), channel_id=1, source_target_pairs={{0,8},{2,10},{4,12},{6,14},{8,0},{10,2},{12,4},{14,6},{16,24},{18,... | collective-permute-start | bytes 1572872 | tf_op jit(solution)/shard_map/ppermute | solution.py:23
  21.5 0.6 collective-permute-start.4
  22.1 16.3 %collective-permute-done.4.refs_1_ = bf16[256,512]{1,0:T(8,128)(2,1)S(1)} collective-permute-done((bf16[256,512]{1,0:T(8,128)(2,1)S(1)}, bf16[256,512]{1,0:T(8,128)(2,1)S(1)}, u32[]{:S(2)}, u32[]{:S(2)}) %collective-permute-start.4) | collective-permute-done | bytes 262176 | tf_op jit(solution)/shard_map/ppermute | solution.py:23
  38.5 1.6 %collective-permute-start.5 = (bf16[512,512]{1,0:T(8,128)(2,1)S(1)}, bf16[512,512]{1,0:T(8,128)(2,1)S(1)}, u32[]{:S(2)}, u32[]{:S(2)}) collective-permute-start(bf16[512,512]{1,0:T(8,128)(2,1)S(1)} %pad_maximum_fusion.5), channel_id=1, source_target_pairs={{0,4},{2,6},{4,0},{6,2},{8,12},{10,14},{12,8},{14,10},{16,20},{18,... | collective-permute-start | bytes 1572872 | tf_op jit(solution)/shard_map/ppermute | solution.py:23
  40.0 0.0 collective-permute-done.2.refs_2_
  40.0 1.1 %pad_maximum_fusion = bf16[1024,512]{1,0:T(8,128)(2,1)} fusion(bf16[512,512]{1,0:T(8,128)(2,1)S(1)} %collective-permute-done.2.refs_2_, bf16[256,512]{1,0:T(8,128)(2,1)S(1)} %collective-permute-done.1.refs_1_, bf16[256,512]{1,0:T(8,128)(2,1)S(1)} %get-tuple-element.13.refs_0_), kind=kLoop, calls=%fused_computation | loop fusion | flops 3145728 | bytes 2097152 | tf_op jit(solution)/shard_map/concatenate | solution.py:30
  41.1 0.0 copy-start
  41.1 0.0 copy-start.1
  41.1 0.0 copy-start.2
  41.1 0.0 collective-permute-start.3
  41.1 9.2 %collective-permute-done.5.refs_2_ = bf16[512,512]{1,0:T(8,128)(2,1)S(1)} collective-permute-done((bf16[512,512]{1,0:T(8,128)(2,1)S(1)}, bf16[512,512]{1,0:T(8,128)(2,1)S(1)}, u32[]{:S(2)}, u32[]{:S(2)}) %collective-permute-start.5) | collective-permute-done | bytes 524320 | tf_op jit(solution)/shard_map/ppermute | solution.py:23
  50.3 1.0 %pad_maximum_fusion.1 = bf16[1024,512]{1,0:T(8,128)(2,1)} fusion(bf16[512,512]{1,0:T(8,128)(2,1)S(1)} %collective-permute-done.5.refs_2_, bf16[256,512]{1,0:T(8,128)(2,1)S(1)} %collective-permute-done.4.refs_1_, bf16[256,512]{1,0:T(8,128)(2,1)S(1)} %get-tuple-element.14.refs_0_), kind=kLoop, calls=%fused_computation.1 | loop fusion | flops 3145728 | bytes 2097152 | tf_op jit(solution)/shard_map/concatenate | solution.py:30
  51.4 0.0 collective-permute-start.6
  51.4 0.1 pad_add_fusion.place_ref
  51.4 0.0 collective-permute-done.3.refs_3_
  51.4 0.0 copy-done
  51.4 0.0 copy-done.1
  51.5 0.0 copy-done.2
  51.5 8.0 %shard_map.55 = (bf16[64,2048]{1,0:T(8,128)(2,1)S(1)}, bf16[64,2048]{1,0:T(8,128)(2,1)S(1)}) custom-call(s32[2]{0:T(128)S(1)} %pad_add_fusion.place_ref, s32[2]{0:T(128)S(1)} %copy-done.2, s32[2,16]{1,0:T(2,128)S(1)} %copy-done.1, bf16[128,4096]{1,0:T(8,128)(2,1)S(1)} %copy-done, bf16[256,512]{1,0:T(8,128)(2,1)S(1)} %get-tuple-element.13.refs_0_, ...), custom_call_target="tpu_custom_call" | custom-call | flops 4294967296 | bytes 2097152 | tf_op jit(solution)/shard_map/pallas_call | solution.py:175
  59.4 1.8 %collective-permute-start.7 = (bf16[64,2048]{1,0:T(8,128)(2,1)S(1)}, bf16[64,2048]{1,0:T(8,128)(2,1)S(1)}, u32[]{:S(2)}, u32[]{:S(2)}) collective-permute-start(bf16[64,2048]{1,0:T(8,128)(2,1)S(1)} %get-tuple-element.11), channel_id=1, source_target_pairs={{0,1},{1,0},{2,3},{3,2},{4,5},{5,4},{6,7},{7,6},{8,9},{9,8},{10,11... | collective-permute-start | bytes 786440 | tf_op jit(solution)/shard_map/ppermute | solution.py:23
  61.3 0.0 collective-permute-done.6.refs_3_
  61.3 8.0 %shard_map.56 = (bf16[64,2048]{1,0:T(8,128)(2,1)S(1)}, bf16[64,2048]{1,0:T(8,128)(2,1)S(1)}) custom-call(s32[2]{0:T(128)S(1)} %pad_add_fusion.place_ref, s32[2]{0:T(128)S(1)} %copy-done.2, s32[2,16]{1,0:T(2,128)S(1)} %copy-done.1, bf16[128,4096]{1,0:T(8,128)(2,1)S(1)} %copy-done, bf16[256,512]{1,0:T(8,128)(2,1)S(1)} %get-tuple-element.14.refs_0_, ...), custom_call_target="tpu_custom_call" | custom-call | flops 4294967296 | bytes 2097152 | tf_op jit(solution)/shard_map/pallas_call | solution.py:175
  69.2 0.3 collective-permute-start.8
  69.6 0.1 pad_maximum_fusion.2
  69.7 0.0 collective-permute-done.7
  69.7 0.0 copy-start.3
  69.7 8.0 %collective-permute-done.8 = bf16[64,2048]{1,0:T(8,128)(2,1)S(1)} collective-permute-done((bf16[64,2048]{1,0:T(8,128)(2,1)S(1)}, bf16[64,2048]{1,0:T(8,128)(2,1)S(1)}, u32[]{:S(2)}, u32[]{:S(2)}) %collective-permute-start.8) | collective-permute-done | bytes 262176 | tf_op jit(solution)/shard_map/ppermute | solution.py:23
  77.8 0.0 copy-done.3
  77.8 0.7 constant_dynamic-update-slice_fusion
  (4 shorter events, 0.1 us)
Async XLA Ops:
  1.0 10.4 %collective-permute-start = (bf16[64,1024]{1,0:T(8,128)(2,1)S(1)}, bf16[64,1024]{1,0:T(8,128)(2,1)S(1)}, u32[]{:S(2)}, u32[]{:S(2)}) collective-permute-start(bf16[64,1024]{1,0:T(8,128)(2,1)S(1)} %get-tuple-element.16), channel_id=1, source_target_pairs={{0,16},{2,18},{4,20},{6,22},{8,24},{10,26},{12,28},{14,30},{16,0},... | collective-permute-start | bytes 393224 | tf_op jit(solution)/shard_map/ppermute | solution.py:23
  12.4 7.6 %collective-permute-start.1 = (bf16[256,512]{1,0:T(8,128)(2,1)S(1)}, bf16[256,512]{1,0:T(8,128)(2,1)S(1)}, u32[]{:S(2)}, u32[]{:S(2)}) collective-permute-start(bf16[256,512]{1,0:T(8,128)(2,1)S(1)} %get-tuple-element.13.refs_0_), channel_id=1, source_target_pairs={{0,4},{2,6},{4,0},{6,2},{8,12},{10,14},{12,8},{14,10},{16,20},{18,... | collective-permute-start | bytes 786440 | tf_op jit(solution)/shard_map/ppermute | solution.py:23
  20.0 20.0 %collective-permute-start.2 = (bf16[512,512]{1,0:T(8,128)(2,1)S(1)}, bf16[512,512]{1,0:T(8,128)(2,1)S(1)}, u32[]{:S(2)}, u32[]{:S(2)}) collective-permute-start(bf16[512,512]{1,0:T(8,128)(2,1)S(1)} %pad_maximum_fusion.4), channel_id=1, source_target_pairs={{0,8},{2,10},{4,12},{6,14},{8,0},{10,2},{12,4},{14,6},{16,24},{18,... | collective-permute-start | bytes 1572872 | tf_op jit(solution)/shard_map/ppermute | solution.py:23
  21.5 16.9 %collective-permute-start.4 = (bf16[256,512]{1,0:T(8,128)(2,1)S(1)}, bf16[256,512]{1,0:T(8,128)(2,1)S(1)}, u32[]{:S(2)}, u32[]{:S(2)}) collective-permute-start(bf16[256,512]{1,0:T(8,128)(2,1)S(1)} %get-tuple-element.14.refs_0_), channel_id=1, source_target_pairs={{0,8},{2,10},{4,12},{6,14},{8,0},{10,2},{12,4},{14,6},{16,24},{18,... | collective-permute-start | bytes 786440 | tf_op jit(solution)/shard_map/ppermute | solution.py:23
  38.5 11.9 %collective-permute-start.5 = (bf16[512,512]{1,0:T(8,128)(2,1)S(1)}, bf16[512,512]{1,0:T(8,128)(2,1)S(1)}, u32[]{:S(2)}, u32[]{:S(2)}) collective-permute-start(bf16[512,512]{1,0:T(8,128)(2,1)S(1)} %pad_maximum_fusion.5), channel_id=1, source_target_pairs={{0,4},{2,6},{4,0},{6,2},{8,12},{10,14},{12,8},{14,10},{16,20},{18,... | collective-permute-start | bytes 1572872 | tf_op jit(solution)/shard_map/ppermute | solution.py:23
  41.1 10.4 %copy-start = (bf16[128,4096]{1,0:T(8,128)(2,1)S(1)}, bf16[128,4096]{1,0:T(8,128)(2,1)}, u32[]{:S(2)}) copy-start(bf16[128,4096]{1,0:T(8,128)(2,1)} %q_ref.3) | copy-start | bytes 3145732
  41.1 10.4 %copy-start.1 = (s32[2,16]{1,0:T(2,128)S(1)}, s32[2,16]{1,0:T(2,128)}, u32[]{:S(2)}) copy-start(s32[2,16]{1,0:T(2,128)} %owner_ref.3) | copy-start | bytes 388
  41.1 10.4 %copy-start.2 = (s32[2]{0:T(128)S(1)}, s32[2]{0:T(128)}, u32[]{:S(2)}) copy-start(s32[2]{0:T(128)} %limit_ref.3) | copy-start | bytes 28
  41.1 10.4 %collective-permute-start.3 = (bf16[1024,512]{1,0:T(8,128)(2,1)}, bf16[1024,512]{1,0:T(8,128)(2,1)}, u32[]{:S(2)}, u32[]{:S(2)}) collective-permute-start(bf16[1024,512]{1,0:T(8,128)(2,1)} %pad_maximum_fusion), channel_id=1, source_target_pairs={{0,2},{2,0},{4,6},{6,4},{8,10},{10,8},{12,14},{14,12},{16,18},{18,... | collective-permute-start | bytes 3145736 | tf_op jit(solution)/shard_map/ppermute | solution.py:23
  51.4 9.9 %collective-permute-start.6 = (bf16[1024,512]{1,0:T(8,128)(2,1)}, bf16[1024,512]{1,0:T(8,128)(2,1)}, u32[]{:S(2)}, u32[]{:S(2)}) collective-permute-start(bf16[1024,512]{1,0:T(8,128)(2,1)} %pad_maximum_fusion.1), channel_id=1, source_target_pairs={{0,2},{2,0},{4,6},{6,4},{8,10},{10,8},{12,14},{14,12},{16,18},{18,... | collective-permute-start | bytes 3145736 | tf_op jit(solution)/shard_map/ppermute | solution.py:23
  59.4 10.2 %collective-permute-start.7 = (bf16[64,2048]{1,0:T(8,128)(2,1)S(1)}, bf16[64,2048]{1,0:T(8,128)(2,1)S(1)}, u32[]{:S(2)}, u32[]{:S(2)}) collective-permute-start(bf16[64,2048]{1,0:T(8,128)(2,1)S(1)} %get-tuple-element.11), channel_id=1, source_target_pairs={{0,1},{1,0},{2,3},{3,2},{4,5},{5,4},{6,7},{7,6},{8,9},{9,8},{10,11... | collective-permute-start | bytes 786440 | tf_op jit(solution)/shard_map/ppermute | solution.py:23
  69.2 8.5 %collective-permute-start.8 = (bf16[64,2048]{1,0:T(8,128)(2,1)S(1)}, bf16[64,2048]{1,0:T(8,128)(2,1)S(1)}, u32[]{:S(2)}, u32[]{:S(2)}) collective-permute-start(bf16[64,2048]{1,0:T(8,128)(2,1)S(1)} %get-tuple-element.12), channel_id=1, source_target_pairs={{0,1},{1,0},{2,3},{3,2},{4,5},{5,4},{6,7},{7,6},{8,9},{9,8},{10,11... | collective-permute-start | bytes 786440 | tf_op jit(solution)/shard_map/ppermute | solution.py:23
  69.7 8.0 %copy-start.3 = (bf16[64,8192]{1,0:T(8,128)(2,1)}, bf16[64,8192]{1,0:T(8,128)(2,1)S(1)}, u32[]{:S(2)}) copy-start(bf16[64,8192]{1,0:T(8,128)(2,1)S(1)} %constant_dynamic-update-slice_fusion.1) | copy-start | bytes 3145732

commit v3 on v2

--- a/solution.py
+++ b/solution.py
@@ -16,31 +16,35 @@
 EXP2_SCALE = HD ** (-0.5) * math.log2(math.e)
 MASKED = -1e30
 SCORE_BYTES = 8 * 1024 * 1024
-
-
-def swap(value, axis, bit):
-    count = lax.axis_size(axis)
-    return lax.ppermute(value, axis, [(source, source ^ bit) for source in range(count)])
-
-
-def gather_strip(own, bits):
-    pieces, offsets = [own], [0]
-    places = [[0]]
+KEY_CHUNK = 256
+SPAN_ROWS, OWN_PAGE, CROSSED_PAGE = range(3)
+
+
+def hop(value, bit_of_core):
+    count = lax.axis_size("seq")
+    return lax.ppermute(
+        value, "seq", [(source, source ^ bit_of_core[source % 2]) for source in range(count)]
+    )
+
+
+def shifted(layout, slots):
+    return [(slot + slots, kind, rows) for slot, kind, rows in layout]
+
+
+def hypercube_order(bits):
+    order = [0]
     for bit in bits:
-        sent = pieces[0] if len(pieces) == 1 else jnp.concatenate(pieces, axis=0)
-        pieces.append(swap(sent, "seq", bit))
-        places.append([offset ^ bit for offset in offsets])
-        offsets = offsets + places[-1]
-    return list(zip(pieces, places))
-
-
-def attend_kernel(spec, place_ref, limit_ref, owner_ref, q_ref, *refs):
-    tokens, page, chunk, groups, block_heads, group_size, head_size, strips, sources = spec
-    piece_refs = refs[: sum(len(strip) for strip in strips)]
-    refs = refs[len(piece_refs) :]
-    outs, refs = refs[:2], refs[2:]
+        order = order + [offset ^ bit for offset in order]
+    return order
+
+
+def attend_kernel(spec, block_heads, groups, place_ref, limit_ref, owner_ref, q_ref, *refs):
+    tokens, page, group_size, head_size, orders, layout = spec
+    halves, outs, refs = refs[:2], refs[2:4], refs[4:]
     page_seen, keys, values, scores_a, scores_b, top_a, top_b = refs
-    chunks = group_size
+    half_keys = halves[0].shape[0]
+    chunk = min(KEY_CHUNK, 2 * half_keys)
+    chunks = 2 * half_keys // chunk
     me = place_ref[0]
     my_head = place_ref[1]
     request = me // group_size
@@ -51,31 +55,31 @@
 
     lax.fori_loop(0, owner_ref.shape[1], note_page, 0)
 
-    row = lax.broadcasted_iota(jnp.int32, (chunk, HD), 0)
-    lane = lax.broadcasted_iota(jnp.int32, (chunk, HD), 1)
-    for offset in range(chunks):
-        source = me ^ offset
-        seen = row < jnp.where(source <= me, tokens, 0)
-        for which in range((chunk - tokens) // page):
-            start = tokens + which * page
-            count = page_seen[source ^ (which * group_size)]
-            seen = seen | ((row >= start) & (row < start + count))
-        bias = jnp.where(seen | (lane > 0), jnp.float32(0.0), jnp.float32(MASKED))
-        for group in range(groups):
-            keys[group, pl.ds(offset * chunk, chunk), HD:] = bias.astype(jnp.bfloat16)
-    values[:, :, HD:] = jnp.ones((groups, chunks * chunk, HD), jnp.bfloat16)
-
-    def fill(target, group, strip_at, column):
-        first = sum(len(strip) for strip in strips[:strip_at])
-        for ref, places in zip(piece_refs[first:], strips[strip_at]):
-            for inner, offset in enumerate(places):
-                target[group, pl.ds(offset * chunk, chunk), :HD] = ref[
-                    pl.ds(inner * chunk, chunk), pl.ds(column, HD)
-                ]
+    offsets = [hypercube_order(order) for order in orders]
+    for half in range(2):
+        holder = me ^ half
+        start = half * half_keys
+        for slot, kind, rows in layout:
+            source = holder ^ jnp.where(holder % 2 == 0, offsets[0][slot], offsets[1][slot])
+            if kind == SPAN_ROWS:
+                count = jnp.where(source <= me, tokens, 0)
+            elif kind == OWN_PAGE:
+                count = page_seen[source]
+            else:
+                count = page_seen[source ^ group_size]
+            row = lax.broadcasted_iota(jnp.int32, (rows, HD), 0)
+            lane = lax.broadcasted_iota(jnp.int32, (rows, HD), 1)
+            bias = jnp.where((row < count) | (lane > 0), jnp.float32(0.0), jnp.float32(MASKED))
+            for group in range(groups):
+                keys[group, pl.ds(start, rows), HD:] = bias.astype(jnp.bfloat16)
+            start += rows
+    values[:, :, HD:] = jnp.ones((groups, 2 * half_keys, HD), jnp.bfloat16)
 
     for group in range(groups):
-        fill(keys, group, *sources[2 * group])
-        fill(values, group, *sources[2 * group + 1])
+        for half, ref in enumerate(halves):
+            at = pl.ds(half * half_keys, half_keys)
+            keys[group, at, :HD] = ref[:, pl.ds(2 * group * HD, HD)]
+            values[group, at, :HD] = ref[:, pl.ds((2 * group + 1) * HD, HD)]
 
     block = block_heads * tokens
     blocks_a_group = PER_GROUP // block_heads
@@ -156,24 +160,19 @@
     lax.fori_loop(0, blocks // 2, two_blocks, 0)
 
 
-def attend(place, limits, owners, queries, part, strips, sources, page, group_size, head_size):
-    tokens = queries.shape[0]
-    columns = len(sources) // 2 * PER_GROUP * HD
+def attend(place, limits, owners, queries, part, mine, theirs, spec):
+    tokens, _, _, head_size = spec[:4]
+    total_keys, columns = 2 * mine.shape[0], mine.shape[1] // 2 * PER_GROUP
     groups = columns // (PER_GROUP * HD)
-    chunk = strips[0][0][0].shape[0]
-    total_keys = group_size * chunk
     block_heads = 4
     while block_heads > 1 and block_heads * tokens * total_keys * 4 > SCORE_BYTES:
         block_heads //= 2
     block = block_heads * tokens
-    offsets = tuple(tuple(tuple(places) for _, places in strip) for strip in strips)
-    pieces = [piece for strip in strips for piece, _ in strip]
-    spec = (tokens, page, chunk, groups, block_heads, group_size, head_size, offsets, sources)
     whole = pl.BlockSpec(memory_space=pltpu.VMEM)
     scalars = pl.BlockSpec(memory_space=pltpu.SMEM)
     kept = tokens // head_size
     return pl.pallas_call(
-        functools.partial(attend_kernel, spec),
+        functools.partial(attend_kernel, spec, block_heads, groups),
         grid=(1,),
         out_shape=[
             jax.ShapeDtypeStruct((kept, columns), jnp.bfloat16),
@@ -181,7 +180,7 @@
         ],
         in_specs=[scalars] * 3
         + [pl.BlockSpec((tokens, columns), lambda step: (0, part))]
-        + [whole] * len(pieces),
+        + [whole] * 2,
         out_specs=[whole] * 2,
         scratch_shapes=[
             pltpu.SMEM((owners.shape[1],), jnp.int32),
@@ -198,7 +197,7 @@
             bytes_accessed=4 * tokens * columns + 2 * total_keys * columns // PER_GROUP,
             transcendentals=0,
         ),
-    )(place, limits, owners, queries, *pieces)
+    )(place, limits, owners, queries, mine, theirs)
 
 
 def body(span_query, span_kv, prefix_cache, prefix_len, block_owner):
@@ -208,46 +207,53 @@
     me = lax.axis_index("seq").astype(jnp.int32)
     my_head = lax.axis_index("head").astype(jnp.int32)
     request = me // group_size
+    tokens = span_kv.shape[0]
     page = prefix_cache.shape[1]
+    columns = span_kv.shape[1]
+    groups = columns // (2 * HD)
+    parts = 2 if groups % 2 == 0 else 1
+    part_columns = columns // parts
+    bits = [1 << at for at in range(1, group_size.bit_length() - 1)]
+    orders = (bits, bits[::-1])
+
+    other_page = lax.dynamic_index_in_dim(prefix_cache, 1 - request, 0, keepdims=False)
     own_page = lax.dynamic_index_in_dim(prefix_cache, request, 0, keepdims=False)
-    other_page = lax.dynamic_index_in_dim(prefix_cache, 1 - request, 0, keepdims=False)
-    crossed = swap(other_page, "seq", group_size)
-    rows = jnp.concatenate([span_kv, own_page, crossed], axis=0)
-    half_cols = rows.shape[1] // 2
-    bits = [1 << at for at in range(group_size.bit_length() - 1)]
-    bit_orders = (bits[1:] + bits[:1], bits[:0:-1] + bits[:1])
-    strips = [
-        gather_strip(rows[:, :half_cols], bit_orders[0]),
-        gather_strip(rows[:, half_cols:], bit_orders[1]),
+    early = [jnp.concatenate([span_kv, own_page], axis=0)]
+    early_rows = [[(0, SPAN_ROWS, tokens), (0, OWN_PAGE, page)]]
+    late = [hop(other_page, (group_size, group_size))]
+    late_rows = [[(0, CROSSED_PAGE, page)]]
+    slots = 1
+    first = (orders[0][0], orders[1][0])
+    early.append(hop(early[0], first))
+    late.append(hop(late[0], first))
+    early_rows.append(shifted(early_rows[0], slots))
+    late_rows.append(shifted(late_rows[0], slots))
+    slots *= 2
+    layout = sum(early_rows + late_rows, [])
+
+    held = []
+    for part in range(parts):
+        cut = slice(part * part_columns, (part + 1) * part_columns)
+        held.append(jnp.concatenate([piece[:, cut] for piece in early + late], axis=0))
+    for pair in list(zip(*orders))[1:]:
+        held = [jnp.concatenate([rows, hop(rows, pair)], axis=0) for rows in held]
+        layout = layout + shifted(layout, slots)
+        slots *= 2
+    swapped = [hop(rows, (1, 1)) for rows in held]
+
+    place = jnp.stack([me, my_head])
+    spec = (tokens, page, group_size, head_size, orders, tuple(layout))
+    results = [
+        attend(place, prefix_len, block_owner, span_query, part, held[part], swapped[part], spec)
+        for part in range(parts)
     ]
-    groups = rows.shape[1] // (2 * HD)
-    place = jnp.stack([me, my_head])
-    common = (page, group_size, head_size)
-    if groups % 2 or head_size != 2:
-        sources = tuple(divmod(column, half_cols) for column in range(0, 2 * half_cols, HD))
-        results = [
-            attend(place, prefix_len, block_owner, span_query, 0, strips, sources, *common)
-        ]
-    else:
-        sources = tuple((0, column) for column in range(0, half_cols, HD))
-        results = [
-            attend(
-                place,
-                prefix_len,
-                block_owner,
-                span_query,
-                at,
-                [strips[at]],
-                sources,
-                *common,
-            )
-            for at in range(2)
-        ]
     if head_size != 2:
         joined = jnp.concatenate([jnp.concatenate(pair, axis=0) for pair in results], axis=1)
         return lax.all_to_all(joined, "head", split_axis=0, concat_axis=1, tiled=True)
     kept = [pair[0] for pair in results]
-    received = [swap(pair[1], "head", 1) for pair in results]
+    received = [
+        lax.ppermute(pair[1], "head", [(0, 1), (1, 0)]) for pair in results
+    ]
     joined = jnp.concatenate(kept + kept, axis=1)
     start = (1 - my_head) * span_query.shape[1]
     for one in received:

time: 78.7 us -> 59.8 us (0.76)
  waiting for transfers between devices: 45.8 us -> 27.1 us
  other arithmetic: 3.32 us -> 1.28 us
  starting transfers between devices: 11.5 us -> 12.9 us
    ppermute x9, waiting for transfers between devices: 45.8 us -> 27.1 us  [the longest x7 19.3 us: hop(): lax.ppermute(value, 'seq', [(source, source ^ bit_of_core[source % 2]) fo...]
    concatenate x5 -> x3, other arithmetic: 3.15 us -> 1.05 us  [the longest x1 0.98 us: body(): early = [jnp.concatenate([span_kv, own_page], axis=0)]]
    ppermute x9, starting transfers between devices: 11.5 us -> 12.9 us  [the longest x7 10.8 us: hop(): lax.ppermute(value, 'seq', [(source, source ^ bit_of_core[source % 2]) fo...]
  transfers between devices with their start and end apart: 9 -> 9, of which waited for: 5 -> 5; matrix products, arithmetic and copies ran while one was open for 3% -> 1% of each run, Pallas kernels for 20% -> 27%
where the time goes in v3:
time: 59.8 us; the launch traced here: 59.1 us
  waiting for transfers between devices  27.1 us (45%)
  Pallas kernels  15.7 us (26%)
  starting transfers between devices  12.9 us (22%)
  local copies, waits for them, and re-layouts  1.96 us (3%)
  other arithmetic  1.28 us (2%)
    ppermute x7, waiting for transfers between devices, hop(): lax.ppermute(value, 'seq', [(source, source ^ bit_of_core[source % 2]) fo...  19.3 us
    pallas_call x2, Pallas kernels, attend(): pl.pallas_call(functools.partial(attend_kernel, spec, block_heads, groups...  15.7 us
    ppermute x7, starting transfers between devices, hop(): lax.ppermute(value, 'seq', [(source, source ^ bit_of_core[source % 2]) fo...  10.8 us
    ppermute x2, waiting for transfers between devices, body(): lax.ppermute(pair[1], 'head', [(0, 1), (1, 0)])  7.75 us
    ppermute x2, starting transfers between devices, body(): lax.ppermute(pair[1], 'head', [(0, 1), (1, 0)])  2.16 us
  transfers between devices with their start and end apart: 9, of which 5 were waited for; matrix products, arithmetic and copies ran while one was open for 1% of the time, Pallas kernels for 27%

profile of v3, /device:TPU:0, one launch (start us, length us, event | category | flops | bytes accessed | tf_op | source)
XLA Modules:
  0.0 59.1 jit_solution(1126597975286410044)
XLA Ops:
  0.0 0.0 copy-start.4
  0.0 1.0 %dynamic-slice_bitcast_fusion = (bf16[64,1024]{1,0:T(8,128)(2,1)S(1)}, bf16[64,1024]{1,0:T(8,128)(2,1)S(1)}) fusion(bf16[2,64,1024]{2,1,0:T(8,128)(2,1)} %param.7, s32[]{:T(128)S(6)} %select_n.20, s32[]{:T(128)S(6)} %select_n.19), kind=kLoop, calls=%fused_computation.10 | loop fusion | bytes 524296 | tf_op jit(solution)/shard_map/jit(dynamic_index_in_dim)/squeeze | solution.py:219
  1.0 1.0 %pad_maximum_fusion.1 = bf16[192,1024]{1,0:T(8,128)(2,1)S(1)} fusion(bf16[64,1024]{1,0:T(8,128)(2,1)S(1)} %get-tuple-element.24, bf16[128,1024]{1,0:T(8,128)(2,1)} %param.6), kind=kLoop, calls=%fused_computation.3 | loop fusion | flops 786432 | bytes 786432 | tf_op jit(solution)/shard_map/concatenate | solution.py:221
  2.0 3.0 %collective-permute-start = (bf16[192,1024]{1,0:T(8,128)(2,1)S(1)}, bf16[192,1024]{1,0:T(8,128)(2,1)S(1)}, u32[]{:S(2)}, u32[]{:S(2)}) collective-permute-start(bf16[192,1024]{1,0:T(8,128)(2,1)S(1)} %pad_maximum_fusion.1), channel_id=1, source_target_pairs={{0,4},{2,10},{4,0},{6,14},{8,12},{10,2},{12,8},{14,6},{16,20},{18,... | collective-permute-start | bytes 1179656 | tf_op jit(solution)/shard_map/ppermute | solution.py:25
  5.0 2.6 %collective-permute-start.1 = (bf16[64,1024]{1,0:T(8,128)(2,1)S(1)}, bf16[64,1024]{1,0:T(8,128)(2,1)S(1)}, u32[]{:S(2)}, u32[]{:S(2)}) collective-permute-start(bf16[64,1024]{1,0:T(8,128)(2,1)S(1)} %get-tuple-element.23), channel_id=1, source_target_pairs={{0,16},{2,18},{4,20},{6,22},{8,24},{10,26},{12,28},{14,30},{16,0},... | collective-permute-start | bytes 393224 | tf_op jit(solution)/shard_map/ppermute | solution.py:25
  7.6 0.0 copy-done.4
  7.6 0.1 constant_dynamic-update-slice_fusion.4
  7.7 3.9 %collective-permute-done.1 = bf16[64,1024]{1,0:T(8,128)(2,1)S(1)} collective-permute-done((bf16[64,1024]{1,0:T(8,128)(2,1)S(1)}, bf16[64,1024]{1,0:T(8,128)(2,1)S(1)}, u32[]{:S(2)}, u32[]{:S(2)}) %collective-permute-start.1) | collective-permute-done | bytes 131104 | tf_op jit(solution)/shard_map/ppermute | solution.py:25
  11.6 2.3 %collective-permute-start.2 = (bf16[64,1024]{1,0:T(8,128)(2,1)S(1)}, bf16[64,1024]{1,0:T(8,128)(2,1)S(1)}, u32[]{:S(2)}, u32[]{:S(2)}) collective-permute-start(bf16[64,1024]{1,0:T(8,128)(2,1)S(1)} %collective-permute-done.1), channel_id=1, source_target_pairs={{0,4},{2,10},{4,0},{6,14},{8,12},{10,2},{12,8},{14,6},{16,20},{18,... | collective-permute-start | bytes 393224 | tf_op jit(solution)/shard_map/ppermute | solution.py:25
  13.9 0.0 collective-permute-done
  13.9 0.1 fusion.4
  14.0 2.8 %collective-permute-done.2 = bf16[64,1024]{1,0:T(8,128)(2,1)S(1)} collective-permute-done((bf16[64,1024]{1,0:T(8,128)(2,1)S(1)}, bf16[64,1024]{1,0:T(8,128)(2,1)S(1)}, u32[]{:S(2)}, u32[]{:S(2)}) %collective-permute-start.2) | collective-permute-done | bytes 131104 | tf_op jit(solution)/shard_map/ppermute | solution.py:25
  16.9 2.6 %collective-permute-start.3 = (bf16[512,512]{1,0:T(8,128)(2,1)S(1)}, bf16[512,512]{1,0:T(8,128)(2,1)S(1)}, u32[]{:S(2)}, u32[]{:S(2)}) collective-permute-start(bf16[512,512]{1,0:T(8,128)(2,1)S(1)} %pad_maximum_fusion.2), channel_id=1, source_target_pairs={{0,8},{2,6},{4,12},{6,2},{8,0},{10,14},{12,4},{14,10},{16,24},{18,... | collective-permute-start | bytes 1572872 | tf_op jit(solution)/shard_map/ppermute | solution.py:25
  19.6 0.1 collective-permute-start.5
  19.7 7.0 %collective-permute-done.3 = bf16[512,512]{1,0:T(8,128)(2,1)S(1)} collective-permute-done((bf16[512,512]{1,0:T(8,128)(2,1)S(1)}, bf16[512,512]{1,0:T(8,128)(2,1)S(1)}, u32[]{:S(2)}, u32[]{:S(2)}) %collective-permute-start.3) | collective-permute-done | bytes 524320 | tf_op jit(solution)/shard_map/ppermute | solution.py:25
  26.7 0.0 copy-start
  26.7 0.0 copy-start.1
  26.7 0.0 copy-start.2
  26.8 0.1 collective-permute-start.4
  26.8 5.5 %collective-permute-done.5 = bf16[512,512]{1,0:T(8,128)(2,1)S(1)} collective-permute-done((bf16[512,512]{1,0:T(8,128)(2,1)S(1)}, bf16[512,512]{1,0:T(8,128)(2,1)S(1)}, u32[]{:S(2)}, u32[]{:S(2)}) %collective-permute-start.5) | collective-permute-done | bytes 524320 | tf_op jit(solution)/shard_map/ppermute | solution.py:25
  32.4 0.1 collective-permute-start.6
  32.5 0.1 pad_add_fusion.place_ref
  32.5 0.0 collective-permute-done.4.refs_1_
  32.5 0.0 copy-done
  32.5 0.0 copy-done.1
  32.6 0.0 copy-done.2
  32.6 7.9 %shard_map.55 = (bf16[64,2048]{1,0:T(8,128)(2,1)S(1)}, bf16[64,2048]{1,0:T(8,128)(2,1)S(1)}) custom-call(s32[2]{0:T(128)S(1)} %pad_add_fusion.place_ref, s32[2]{0:T(128)S(1)} %copy-done.2, s32[2,16]{1,0:T(2,128)S(1)} %copy-done.1, bf16[128,4096]{1,0:T(8,128)(2,1)S(1)} %copy-done, bf16[1024,512]{1,0:T(8,128)(2,1)S(1)} %constant_dynamic-update-slice_fusion.refs_0_, ...), custom_call_target="tpu_custom_call" | custom-call | flops 4294967296 | bytes 2097152 | tf_op jit(solution)/shard_map/pallas_call | solution.py:174
  40.4 1.6 %collective-permute-start.7 = (bf16[64,2048]{1,0:T(8,128)(2,1)S(1)}, bf16[64,2048]{1,0:T(8,128)(2,1)S(1)}, u32[]{:S(2)}, u32[]{:S(2)}) collective-permute-start(bf16[64,2048]{1,0:T(8,128)(2,1)S(1)} %get-tuple-element.11), channel_id=1, source_target_pairs={{0,1},{1,0},{2,3},{3,2},{4,5},{5,4},{6,7},{7,6},{8,9},{9,8},{10,11... | collective-permute-start | bytes 786440 | tf_op jit(solution)/shard_map/ppermute | solution.py:255
  42.0 0.0 collective-permute-done.6.refs_1_
  42.0 7.9 %shard_map.56 = (bf16[64,2048]{1,0:T(8,128)(2,1)S(1)}, bf16[64,2048]{1,0:T(8,128)(2,1)S(1)}) custom-call(s32[2]{0:T(128)S(1)} %pad_add_fusion.place_ref, s32[2]{0:T(128)S(1)} %copy-done.2, s32[2,16]{1,0:T(2,128)S(1)} %copy-done.1, bf16[128,4096]{1,0:T(8,128)(2,1)S(1)} %copy-done, bf16[1024,512]{1,0:T(8,128)(2,1)S(1)} %constant_dynamic-update-slice_fusion.5.refs_0_, ...), custom_call_target="tpu_custom_call" | custom-call | flops 4294967296 | bytes 2097152 | tf_op jit(solution)/shard_map/pallas_call | solution.py:174
  49.9 0.6 collective-permute-start.8
  50.5 0.1 pad_maximum_fusion
  50.6 0.0 collective-permute-done.7
  50.6 0.0 copy-start.3
  50.6 7.7 %collective-permute-done.8 = bf16[64,2048]{1,0:T(8,128)(2,1)S(1)} collective-permute-done((bf16[64,2048]{1,0:T(8,128)(2,1)S(1)}, bf16[64,2048]{1,0:T(8,128)(2,1)S(1)}, u32[]{:S(2)}, u32[]{:S(2)}) %collective-permute-start.8) | collective-permute-done | bytes 262176 | tf_op jit(solution)/shard_map/ppermute | solution.py:255
  58.4 0.0 copy-done.3
  58.4 0.7 %constant_dynamic-update-slice_fusion.10 = bf16[64,8192]{1,0:T(8,128)(2,1)} fusion(bf16[64,8192]{1,0:T(8,128)(2,1)} %copy-done.3, bf16[64,2048]{1,0:T(8,128)(2,1)S(1)} %collective-permute-done.8, s32[]{:T(128)S(6)} %select_n.22), kind=kLoop, calls=%fused_computation.22 | loop fusion | bytes 524292 | tf_op jit(solution)/shard_map/dynamic_update_slice | solution.py:260
  (7 shorter events, 0.2 us)
Async XLA Ops:
  0.0 7.6 %copy-start.4 = (bf16[128,1024]{1,0:T(8,128)(2,1)S(1)}, bf16[128,1024]{1,0:T(8,128)(2,1)}, u32[]{:S(2)}) copy-start(bf16[128,1024]{1,0:T(8,128)(2,1)} %param.6) | copy-start | bytes 786436
  2.0 11.9 %collective-permute-start = (bf16[192,1024]{1,0:T(8,128)(2,1)S(1)}, bf16[192,1024]{1,0:T(8,128)(2,1)S(1)}, u32[]{:S(2)}, u32[]{:S(2)}) collective-permute-start(bf16[192,1024]{1,0:T(8,128)(2,1)S(1)} %pad_maximum_fusion.1), channel_id=1, source_target_pairs={{0,4},{2,10},{4,0},{6,14},{8,12},{10,2},{12,8},{14,6},{16,20},{18,... | collective-permute-start | bytes 1179656 | tf_op jit(solution)/shard_map/ppermute | solution.py:25
  5.0 6.6 %collective-permute-start.1 = (bf16[64,1024]{1,0:T(8,128)(2,1)S(1)}, bf16[64,1024]{1,0:T(8,128)(2,1)S(1)}, u32[]{:S(2)}, u32[]{:S(2)}) collective-permute-start(bf16[64,1024]{1,0:T(8,128)(2,1)S(1)} %get-tuple-element.23), channel_id=1, source_target_pairs={{0,16},{2,18},{4,20},{6,22},{8,24},{10,26},{12,28},{14,30},{16,0},... | collective-permute-start | bytes 393224 | tf_op jit(solution)/shard_map/ppermute | solution.py:25
  11.6 5.2 %collective-permute-start.2 = (bf16[64,1024]{1,0:T(8,128)(2,1)S(1)}, bf16[64,1024]{1,0:T(8,128)(2,1)S(1)}, u32[]{:S(2)}, u32[]{:S(2)}) collective-permute-start(bf16[64,1024]{1,0:T(8,128)(2,1)S(1)} %collective-permute-done.1), channel_id=1, source_target_pairs={{0,4},{2,10},{4,0},{6,14},{8,12},{10,2},{12,8},{14,6},{16,20},{18,... | collective-permute-start | bytes 393224 | tf_op jit(solution)/shard_map/ppermute | solution.py:25
  16.9 9.8 %collective-permute-start.3 = (bf16[512,512]{1,0:T(8,128)(2,1)S(1)}, bf16[512,512]{1,0:T(8,128)(2,1)S(1)}, u32[]{:S(2)}, u32[]{:S(2)}) collective-permute-start(bf16[512,512]{1,0:T(8,128)(2,1)S(1)} %pad_maximum_fusion.2), channel_id=1, source_target_pairs={{0,8},{2,6},{4,12},{6,2},{8,0},{10,14},{12,4},{14,10},{16,24},{18,... | collective-permute-start | bytes 1572872 | tf_op jit(solution)/shard_map/ppermute | solution.py:25
  19.6 12.7 %collective-permute-start.5 = (bf16[512,512]{1,0:T(8,128)(2,1)S(1)}, bf16[512,512]{1,0:T(8,128)(2,1)S(1)}, u32[]{:S(2)}, u32[]{:S(2)}) collective-permute-start(bf16[512,512]{1,0:T(8,128)(2,1)S(1)} %pad_maximum_fusion.3), channel_id=1, source_target_pairs={{0,8},{2,6},{4,12},{6,2},{8,0},{10,14},{12,4},{14,10},{16,24},{18,... | collective-permute-start | bytes 1572872 | tf_op jit(solution)/shard_map/ppermute | solution.py:25
  26.7 5.8 %copy-start = (bf16[128,4096]{1,0:T(8,128)(2,1)S(1)}, bf16[128,4096]{1,0:T(8,128)(2,1)}, u32[]{:S(2)}) copy-start(bf16[128,4096]{1,0:T(8,128)(2,1)} %q_ref.3) | copy-start | bytes 3145732
  26.7 5.8 %copy-start.1 = (s32[2,16]{1,0:T(2,128)S(1)}, s32[2,16]{1,0:T(2,128)}, u32[]{:S(2)}) copy-start(s32[2,16]{1,0:T(2,128)} %owner_ref.3) | copy-start | bytes 388
  26.7 5.8 %copy-start.2 = (s32[2]{0:T(128)S(1)}, s32[2]{0:T(128)}, u32[]{:S(2)}) copy-start(s32[2]{0:T(128)} %limit_ref.3) | copy-start | bytes 28
  26.8 5.8 %collective-permute-start.4 = (bf16[1024,512]{1,0:T(8,128)(2,1)S(1)}, bf16[1024,512]{1,0:T(8,128)(2,1)}, u32[]{:S(2)}, u32[]{:S(2)}) collective-permute-start(bf16[1024,512]{1,0:T(8,128)(2,1)S(1)} %constant_dynamic-update-slice_fusion.refs_0_), channel_id=1, source_target_pairs={{0,2},{2,0},{4,6},{6,4},{8,10},{10,8},{12,14},{14,12},{16,18},{18,... | collective-permute-start | bytes 3145736 | tf_op jit(solution)/shard_map/ppermute | solution.py:25
  32.4 9.7 %collective-permute-start.6 = (bf16[1024,512]{1,0:T(8,128)(2,1)S(1)}, bf16[1024,512]{1,0:T(8,128)(2,1)}, u32[]{:S(2)}, u32[]{:S(2)}) collective-permute-start(bf16[1024,512]{1,0:T(8,128)(2,1)S(1)} %constant_dynamic-update-slice_fusion.5.refs_0_), channel_id=1, source_target_pairs={{0,2},{2,0},{4,6},{6,4},{8,10},{10,8},{12,14},{14,12},{16,18},{18,... | collective-permute-start | bytes 3145736 | tf_op jit(solution)/shard_map/ppermute | solution.py:25
  40.4 10.2 %collective-permute-start.7 = (bf16[64,2048]{1,0:T(8,128)(2,1)S(1)}, bf16[64,2048]{1,0:T(8,128)(2,1)S(1)}, u32[]{:S(2)}, u32[]{:S(2)}) collective-permute-start(bf16[64,2048]{1,0:T(8,128)(2,1)S(1)} %get-tuple-element.11), channel_id=1, source_target_pairs={{0,1},{1,0},{2,3},{3,2},{4,5},{5,4},{6,7},{7,6},{8,9},{9,8},{10,11... | collective-permute-start | bytes 786440 | tf_op jit(solution)/shard_map/ppermute | solution.py:255
  49.9 8.5 %collective-permute-start.8 = (bf16[64,2048]{1,0:T(8,128)(2,1)S(1)}, bf16[64,2048]{1,0:T(8,128)(2,1)S(1)}, u32[]{:S(2)}, u32[]{:S(2)}) collective-permute-start(bf16[64,2048]{1,0:T(8,128)(2,1)S(1)} %get-tuple-element.12), channel_id=1, source_target_pairs={{0,1},{1,0},{2,3},{3,2},{4,5},{5,4},{6,7},{7,6},{8,9},{9,8},{10,11... | collective-permute-start | bytes 786440 | tf_op jit(solution)/shard_map/ppermute | solution.py:255
  50.6 7.8 %copy-start.3 = (bf16[64,8192]{1,0:T(8,128)(2,1)}, bf16[64,8192]{1,0:T(8,128)(2,1)S(1)}, u32[]{:S(2)}) copy-start(bf16[64,8192]{1,0:T(8,128)(2,1)S(1)} %constant_dynamic-update-slice_fusion.11) | copy-start | bytes 3145732

commit v4 on v3

--- a/solution.py
+++ b/solution.py
@@ -27,6 +27,10 @@
     )
 
 
+def after(first, value):
+    return lax.optimization_barrier((first, value))[1]
+
+
 def shifted(layout, slots):
     return [(slot + slots, kind, rows) for slot, kind, rows in layout]
 
@@ -38,9 +42,14 @@
     return order
 
 
-def attend_kernel(spec, block_heads, groups, place_ref, limit_ref, owner_ref, q_ref, *refs):
-    tokens, page, group_size, head_size, orders, layout = spec
-    halves, outs, refs = refs[:2], refs[2:4], refs[4:]
+def attend_kernel(spec, layout, part, block_heads, groups, place_ref, limit_ref, owner_ref, q_ref, *refs):
+    tokens, page, group_size, head_size, orders = spec
+    first_phase = layout[0][1] == SPAN_ROWS
+    halves, refs = refs[:2], refs[2:]
+    if first_phase:
+        (state_sum, state_top), refs = refs[:2], refs[2:]
+    else:
+        (state_sum, state_top), outs, refs = refs[:2], refs[2:4], refs[4:]
     page_seen, keys, values, scores_a, scores_b, top_a, top_b = refs
     half_keys = halves[0].shape[0]
     chunk = min(KEY_CHUNK, 2 * half_keys)
@@ -53,7 +62,8 @@
         page_seen[owner_ref[request, index]] = jnp.clip(limit_ref[request] - index * page, 0, page)
         return carry
 
-    lax.fori_loop(0, owner_ref.shape[1], note_page, 0)
+    if not first_phase:
+        lax.fori_loop(0, owner_ref.shape[1], note_page, 0)
 
     offsets = [hypercube_order(order) for order in orders]
     for half in range(2):
@@ -78,8 +88,9 @@
     for group in range(groups):
         for half, ref in enumerate(halves):
             at = pl.ds(half * half_keys, half_keys)
-            keys[group, at, :HD] = ref[:, pl.ds(2 * group * HD, HD)]
-            values[group, at, :HD] = ref[:, pl.ds((2 * group + 1) * HD, HD)]
+            column = (part * groups + group) * 2 * HD
+            keys[group, at, :HD] = ref[:, pl.ds(column, HD)]
+            values[group, at, :HD] = ref[:, pl.ds(column + HD, HD)]
 
     block = block_heads * tokens
     blocks_a_group = PER_GROUP // block_heads
@@ -89,36 +100,47 @@
         lax.broadcasted_iota(jnp.int32, (block, tokens), 0) % tokens
     )
 
-    def columns(index):
+    def columns(index, first):
         return [
-            pl.ds(pl.multiple_of((index * block_heads + head) * HD, HD), HD)
+            pl.ds(pl.multiple_of(first + (index * block_heads + head) * HD, HD), HD)
             for head in range(block_heads)
         ]
 
+    def block_rows(index):
+        return pl.ds(pl.multiple_of(index * block, block), block)
+
     def score_steps(index, scores, top):
         group = index // blocks_a_group
-        query = jnp.concatenate([q_ref[:, column] for column in columns(index)], axis=0)
+        first = part * groups * PER_GROUP * HD
+        query = jnp.concatenate([q_ref[:, column] for column in columns(index, first)], axis=0)
         query = jnp.concatenate([query, ones], axis=1)
-        best = jnp.full((block, HD), MASKED, jnp.float32)
+        if first_phase:
+            best = jnp.full((block, HD), MASKED, jnp.float32)
+        else:
+            best = state_top[block_rows(index), :]
         for at in range(chunks):
-            part = lax.dot_general(
+            made = lax.dot_general(
                 query,
                 keys[group, pl.ds(at * chunk, chunk), :],
                 (((1,), (1,)), ((), ())),
                 preferred_element_type=jnp.float32,
             )
-            if at == 0:
-                own = jnp.where(causal, part[:, :tokens], MASKED)
-                part = jnp.concatenate([own, part[:, tokens:]], axis=1)
-            scores[:, pl.ds(at * chunk, chunk)] = part
+            if at == 0 and first_phase:
+                own = jnp.where(causal, made[:, :tokens], MASKED)
+                made = jnp.concatenate([own, made[:, tokens:]], axis=1)
+            scores[:, pl.ds(at * chunk, chunk)] = made
             for lane_at in range(0, chunk, HD):
-                best = jnp.maximum(best, part[:, lane_at : lane_at + HD])
+                best = jnp.maximum(best, made[:, lane_at : lane_at + HD])
             yield
         top[...] = jnp.broadcast_to(jnp.max(best, axis=1, keepdims=True), (block, HD))
 
     def value_steps(index, scores, top):
         group = index // blocks_a_group
-        summed = jnp.zeros((block, 2 * HD), jnp.float32)
+        if first_phase:
+            summed = jnp.zeros((block, 2 * HD), jnp.float32)
+        else:
+            fade = jnp.exp2((state_top[block_rows(index), :] - top[...]) * EXP2_SCALE)
+            summed = state_sum[block_rows(index), :] * jnp.concatenate([fade, fade], axis=1)
         for at in range(chunks):
             weights = []
             for lane_at in range(at * chunk, (at + 1) * chunk, HD):
@@ -130,9 +152,13 @@
                 preferred_element_type=jnp.float32,
             )
             yield
+        if first_phase:
+            state_sum[block_rows(index), :] = summed
+            state_top[block_rows(index), :] = top[...]
+            return
         result = (summed[:, :HD] / summed[:, HD:]).astype(jnp.bfloat16)
         kept = tokens // head_size
-        for head, column in enumerate(columns(index)):
+        for head, column in enumerate(columns(index, 0)):
             one = result[head * tokens : (head + 1) * tokens]
             if head_size == 2:
                 low, high = one[:kept], one[kept:]
@@ -160,27 +186,34 @@
     lax.fori_loop(0, blocks // 2, two_blocks, 0)
 
 
-def attend(place, limits, owners, queries, part, mine, theirs, spec):
+def attend(place, limits, owners, queries, part, parts, mine, theirs, layout, spec, state):
     tokens, _, _, head_size = spec[:4]
-    total_keys, columns = 2 * mine.shape[0], mine.shape[1] // 2 * PER_GROUP
+    total_keys = 2 * mine.shape[0]
+    columns = queries.shape[1] // parts
     groups = columns // (PER_GROUP * HD)
     block_heads = 4
     while block_heads > 1 and block_heads * tokens * total_keys * 4 > SCORE_BYTES:
         block_heads //= 2
     block = block_heads * tokens
+    rows = PER_GROUP * groups * tokens
     whole = pl.BlockSpec(memory_space=pltpu.VMEM)
     scalars = pl.BlockSpec(memory_space=pltpu.SMEM)
     kept = tokens // head_size
-    return pl.pallas_call(
-        functools.partial(attend_kernel, spec, block_heads, groups),
-        grid=(1,),
-        out_shape=[
+    if state is None:
+        state = ()
+        out_shape = [
+            jax.ShapeDtypeStruct((rows, 2 * HD), jnp.float32),
+            jax.ShapeDtypeStruct((rows, HD), jnp.float32),
+        ]
+    else:
+        out_shape = [
             jax.ShapeDtypeStruct((kept, columns), jnp.bfloat16),
             jax.ShapeDtypeStruct((tokens - kept, columns), jnp.bfloat16),
-        ],
-        in_specs=[scalars] * 3
-        + [pl.BlockSpec((tokens, columns), lambda step: (0, part))]
-        + [whole] * 2,
+        ]
+    return pl.pallas_call(
+        functools.partial(attend_kernel, spec, tuple(layout), part, block_heads, groups),
+        out_shape=out_shape,
+        in_specs=[scalars] * 3 + [whole] * (3 + len(state)),
         out_specs=[whole] * 2,
         scratch_shapes=[
             pltpu.SMEM((owners.shape[1],), jnp.int32),
@@ -191,13 +224,13 @@
             pltpu.VMEM((block, HD), jnp.float32),
             pltpu.VMEM((block, HD), jnp.float32),
         ],
-        compiler_params=pltpu.CompilerParams(vmem_limit_bytes=48 * 1024 * 1024),
+        compiler_params=pltpu.CompilerParams(vmem_limit_bytes=40 * 1024 * 1024),
         cost_estimate=pl.CostEstimate(
             flops=8 * tokens * columns * total_keys,
             bytes_accessed=4 * tokens * columns + 2 * total_keys * columns // PER_GROUP,
             transcendentals=0,
         ),
-    )(place, limits, owners, queries, mine, theirs)
+    )(place, limits, owners, queries, mine, theirs, *state)
 
 
 def body(span_query, span_kv, prefix_cache, prefix_len, block_owner):
@@ -209,51 +242,58 @@
     request = me // group_size
     tokens = span_kv.shape[0]
     page = prefix_cache.shape[1]
-    columns = span_kv.shape[1]
-    groups = columns // (2 * HD)
+    groups = span_kv.shape[1] // (2 * HD)
     parts = 2 if groups % 2 == 0 else 1
-    part_columns = columns // parts
     bits = [1 << at for at in range(1, group_size.bit_length() - 1)]
     orders = (bits, bits[::-1])
 
+    def send(rows, stage):
+        return hop(rows, tuple(order[stage] for order in orders))
+
+    def grown(layout, stage):
+        return layout + shifted(layout, 1 << stage)
+
+    stages = len(bits)
     other_page = lax.dynamic_index_in_dim(prefix_cache, 1 - request, 0, keepdims=False)
+    crossed = hop(other_page, (group_size, group_size))
     own_page = lax.dynamic_index_in_dim(prefix_cache, request, 0, keepdims=False)
-    early = [jnp.concatenate([span_kv, own_page], axis=0)]
-    early_rows = [[(0, SPAN_ROWS, tokens), (0, OWN_PAGE, page)]]
-    late = [hop(other_page, (group_size, group_size))]
-    late_rows = [[(0, CROSSED_PAGE, page)]]
-    slots = 1
-    first = (orders[0][0], orders[1][0])
-    early.append(hop(early[0], first))
-    late.append(hop(late[0], first))
-    early_rows.append(shifted(early_rows[0], slots))
-    late_rows.append(shifted(late_rows[0], slots))
-    slots *= 2
-    layout = sum(early_rows + late_rows, [])
-
-    held = []
-    for part in range(parts):
-        cut = slice(part * part_columns, (part + 1) * part_columns)
-        held.append(jnp.concatenate([piece[:, cut] for piece in early + late], axis=0))
-    for pair in list(zip(*orders))[1:]:
-        held = [jnp.concatenate([rows, hop(rows, pair)], axis=0) for rows in held]
-        layout = layout + shifted(layout, slots)
-        slots *= 2
-    swapped = [hop(rows, (1, 1)) for rows in held]
+    span, span_layout = span_kv, [(0, SPAN_ROWS, tokens)]
+    for stage in range(stages):
+        received = send(span, stage)
+        if stage == 0:
+            crossed = after(received, crossed)
+            pages = jnp.concatenate([own_page, crossed], axis=0)
+            pages = jnp.concatenate([pages, send(pages, 0)], axis=0)
+        elif stage == 1:
+            received = after(pages, received)
+        span, span_layout = jnp.concatenate([span, received], axis=0), grown(span_layout, stage)
+    span_swapped = hop(span, (1, 1))
 
     place = jnp.stack([me, my_head])
-    spec = (tokens, page, group_size, head_size, orders, tuple(layout))
+    spec = (tokens, page, group_size, head_size, orders)
+    common = (place, prefix_len, block_owner, span_query)
+    states = [
+        attend(*common, part, parts, span, span_swapped, span_layout, spec, None)
+        for part in range(parts)
+    ]
+
+    page_layout = [(0, OWN_PAGE, page), (0, CROSSED_PAGE, page)]
+    page_layout = grown(page_layout, 0)
+    for stage in range(1, stages):
+        received = send(pages, stage)
+        if stage == stages - 1:
+            received = after(states[0], received)
+        pages, page_layout = jnp.concatenate([pages, received], axis=0), grown(page_layout, stage)
+    pages_swapped = hop(pages, (1, 1))
     results = [
-        attend(place, prefix_len, block_owner, span_query, part, held[part], swapped[part], spec)
+        attend(*common, part, parts, pages, pages_swapped, page_layout, spec, states[part])
         for part in range(parts)
     ]
     if head_size != 2:
         joined = jnp.concatenate([jnp.concatenate(pair, axis=0) for pair in results], axis=1)
         return lax.all_to_all(joined, "head", split_axis=0, concat_axis=1, tiled=True)
     kept = [pair[0] for pair in results]
-    received = [
-        lax.ppermute(pair[1], "head", [(0, 1), (1, 0)]) for pair in results
-    ]
+    received = [lax.ppermute(pair[1], "head", [(0, 1), (1, 0)]) for pair in results]
     joined = jnp.concatenate(kept + kept, axis=1)
     start = (1 - my_head) * span_query.shape[1]
     for one in received:

time: 59.8 us -> 59.2 us (0.990)
  waiting for transfers between devices: 27.1 us -> 18.1 us
  local copies, waits for them, and re-layouts: 1.96 us -> 5.37 us
  Pallas kernels: 15.7 us -> 18.9 us
  other arithmetic: 1.28 us -> 3.2 us
    ppermute x7, waiting for transfers between devices: 19.3 us -> 10.3 us  [hop(): lax.ppermute(value, 'seq', [(source, source ^ bit_of_core[source % 2]) fo...]
    unnamed x10 -> x28, local copies, waits for them, and re-layouts: 0.02 us -> 3.61 us
    pallas_call x2 -> x4, Pallas kernels: 15.7 us -> 18.9 us  [attend(): pl.pallas_call(functools.partial(attend_kernel, spec, tuple(layout), part...]
    concatenate x3 -> x4, other arithmetic: 1.05 us -> 3.02 us  [the longest x1 1.11 us: body(): jnp.concatenate([pages, received], axis=0)]
  transfers between devices with their start and end apart: 9 -> 9, of which waited for: 5 -> 8; matrix products, arithmetic and copies ran while one was open for 1% -> 5% of each run, Pallas kernels for 27% -> 23%
where the time goes in v4:
time: 59.2 us; the launch traced here: 58.9 us
  Pallas kernels  18.9 us (32%)
  waiting for transfers between devices  18.1 us (31%)
  starting transfers between devices  13.1 us (22%)
  local copies, waits for them, and re-layouts  5.37 us (9%)
  other arithmetic  3.2 us (5%)
    pallas_call x4, Pallas kernels, attend(): pl.pallas_call(functools.partial(attend_kernel, spec, tuple(layout), part...  18.9 us
    ppermute x7, starting transfers between devices, hop(): lax.ppermute(value, 'seq', [(source, source ^ bit_of_core[source % 2]) fo...  10.9 us
    ppermute x7, waiting for transfers between devices, hop(): lax.ppermute(value, 'seq', [(source, source ^ bit_of_core[source % 2]) fo...  10.3 us
    ppermute x2, waiting for transfers between devices, body(): lax.ppermute(pair[1], 'head', [(0, 1), (1, 0)])  7.76 us
    unnamed x28, local copies, waits for them, and re-layouts  3.61 us
    ppermute x2, starting transfers between devices, body(): lax.ppermute(pair[1], 'head', [(0, 1), (1, 0)])  2.16 us
  transfers between devices with their start and end apart: 9, of which 8 were waited for; matrix products, arithmetic and copies ran while one was open for 5% of the time, Pallas kernels for 23%

profile of v4, /device:TPU:0, one launch (start us, length us, event | category | flops | bytes accessed | tf_op | source)
XLA Modules:
  0.0 58.9 jit_solution(15973152887746149757)
XLA Ops:
  0.0 2.9 %collective-permute-start = (bf16[128,1024]{1,0:T(8,128)(2,1)}, bf16[128,1024]{1,0:T(8,128)(2,1)S(1)}, u32[]{:S(2)}, u32[]{:S(2)}) collective-permute-start(bf16[128,1024]{1,0:T(8,128)(2,1)} %param.6), channel_id=1, source_target_pairs={{0,4},{2,10},{4,0},{6,14},{8,12},{10,2},{12,8},{14,6},{16,20},{18,... | collective-permute-start | bytes 786440 | tf_op jit(solution)/shard_map/ppermute | solution.py:25
  2.9 1.0 %dynamic-slice_bitcast_fusion.1 = (bf16[64,1024]{1,0:T(8,128)(2,1)S(1)}, bf16[64,1024]{1,0:T(8,128)(2,1)S(1)}) fusion(bf16[2,64,1024]{2,1,0:T(8,128)(2,1)} %param.7, s32[]{:T(128)S(6)} %select_n.19, s32[]{:T(128)S(6)} %select_n.20), kind=kLoop, calls=%fused_computation.6 | loop fusion | bytes 524296 | tf_op jit(solution)/shard_map/jit(dynamic_index_in_dim)/squeeze | solution.py:259
  3.9 2.7 %collective-permute-start.1 = (bf16[64,1024]{1,0:T(8,128)(2,1)S(1)}, bf16[64,1024]{1,0:T(8,128)(2,1)S(1)}, u32[]{:S(2)}, u32[]{:S(2)}) collective-permute-start(bf16[64,1024]{1,0:T(8,128)(2,1)S(1)} %get-tuple-element.28), channel_id=1, source_target_pairs={{0,16},{2,18},{4,20},{6,22},{8,24},{10,26},{12,28},{14,30},{16,0},... | collective-permute-start | bytes 393224 | tf_op jit(solution)/shard_map/ppermute | solution.py:25
  6.6 1.0 %collective-permute-done = bf16[128,1024]{1,0:T(8,128)(2,1)S(1)} collective-permute-done((bf16[128,1024]{1,0:T(8,128)(2,1)}, bf16[128,1024]{1,0:T(8,128)(2,1)S(1)}, u32[]{:S(2)}, u32[]{:S(2)}) %collective-permute-start) | collective-permute-done | bytes 262176 | tf_op jit(solution)/shard_map/ppermute | solution.py:25
  7.6 1.0 %pad_maximum_fusion.3 = bf16[256,1024]{1,0:T(8,128)(2,1)S(1)} fusion(bf16[128,1024]{1,0:T(8,128)(2,1)S(1)} %collective-permute-done, bf16[128,1024]{1,0:T(8,128)(2,1)} %param.6), kind=kLoop, calls=%fused_computation.3 | loop fusion | flops 1048576 | bytes 1048576 | tf_op jit(solution)/shard_map/concatenate | solution.py:269
  8.6 0.0 copy-start
  8.6 0.0 copy-start.3
  8.6 0.0 copy-start.4
  8.6 2.1 %collective-permute-start.3 = (bf16[256,1024]{1,0:T(8,128)(2,1)S(1)}, bf16[256,1024]{1,0:T(8,128)(2,1)S(1)}, u32[]{:S(2)}, u32[]{:S(2)}) collective-permute-start(bf16[256,1024]{1,0:T(8,128)(2,1)S(1)} %pad_maximum_fusion.3), channel_id=1, source_target_pairs={{0,8},{2,6},{4,12},{6,2},{8,0},{10,14},{12,4},{14,10},{16,24},{18,... | collective-permute-start | bytes 1572872 | tf_op jit(solution)/shard_map/ppermute | solution.py:25
  10.7 2.1 %collective-permute-done.1 = bf16[64,1024]{1,0:T(8,128)(2,1)S(1)} collective-permute-done((bf16[64,1024]{1,0:T(8,128)(2,1)S(1)}, bf16[64,1024]{1,0:T(8,128)(2,1)S(1)}, u32[]{:S(2)}, u32[]{:S(2)}) %collective-permute-start.1) | collective-permute-done | bytes 131104 | tf_op jit(solution)/shard_map/ppermute | solution.py:25
  12.8 1.5 %collective-permute-start.2 = (bf16[128,1024]{1,0:T(8,128)(2,1)S(1)}, bf16[128,1024]{1,0:T(8,128)(2,1)S(1)}, u32[]{:S(2)}, u32[]{:S(2)}) collective-permute-start(bf16[128,1024]{1,0:T(8,128)(2,1)S(1)} %pad_maximum_fusion.4), channel_id=1, source_target_pairs={{0,4},{2,10},{4,0},{6,14},{8,12},{10,2},{12,8},{14,6},{16,20},{18,... | collective-permute-start | bytes 786440 | tf_op jit(solution)/shard_map/ppermute | solution.py:25
  14.3 0.0 copy-done.10
  14.4 4.9 %collective-permute-done.2 = bf16[128,1024]{1,0:T(8,128)(2,1)S(1)} collective-permute-done((bf16[128,1024]{1,0:T(8,128)(2,1)S(1)}, bf16[128,1024]{1,0:T(8,128)(2,1)S(1)}, u32[]{:S(2)}, u32[]{:S(2)}) %collective-permute-start.2) | collective-permute-done | bytes 262176 | tf_op jit(solution)/shard_map/ppermute | solution.py:25
  19.3 0.9 %pad_maximum_fusion.2 = bf16[256,1024]{1,0:T(8,128)(2,1)} fusion(bf16[128,1024]{1,0:T(8,128)(2,1)S(1)} %collective-permute-done.2, bf16[64,1024]{1,0:T(8,128)(2,1)S(1)} %collective-permute-done.1, bf16[64,1024]{1,0:T(8,128)(2,1)S(1)} %get-tuple-element.27), kind=kLoop, calls=%fused_computation.2 | loop fusion | flops 1572864 | bytes 1048576 | tf_op jit(solution)/shard_map/concatenate | solution.py:266
  20.2 1.0 %collective-permute-done.3 = bf16[256,1024]{1,0:T(8,128)(2,1)S(1)} collective-permute-done((bf16[256,1024]{1,0:T(8,128)(2,1)S(1)}, bf16[256,1024]{1,0:T(8,128)(2,1)S(1)}, u32[]{:S(2)}, u32[]{:S(2)}) %collective-permute-start.3) | collective-permute-done | bytes 524320 | tf_op jit(solution)/shard_map/ppermute | solution.py:25
  21.2 0.0 copy-done.11
  21.2 0.1 collective-permute-start.4
  21.3 1.6 %collective-permute-start.5 = (bf16[256,1024]{1,0:T(8,128)(2,1)}, bf16[256,1024]{1,0:T(8,128)(2,1)}, u32[]{:S(2)}, u32[]{:S(2)}) collective-permute-start(bf16[256,1024]{1,0:T(8,128)(2,1)} %pad_maximum_fusion.2), channel_id=1, source_target_pairs={{0,8},{2,6},{4,12},{6,2},{8,0},{10,14},{12,4},{14,10},{16,24},{18,... | collective-permute-start | bytes 1572872 | tf_op jit(solution)/shard_map/ppermute | solution.py:25
  22.9 0.1 pad_add_fusion.place_ref
  23.0 1.0 %collective-permute-done.4.refs_1_ = bf16[512,1024]{1,0:T(8,128)(2,1)S(1)} collective-permute-done((bf16[512,1024]{1,0:T(8,128)(2,1)S(1)}, bf16[512,1024]{1,0:T(8,128)(2,1)S(1)}, u32[]{:S(2)}, u32[]{:S(2)}) %collective-permute-start.4) | collective-permute-done | bytes 1048608 | tf_op jit(solution)/shard_map/ppermute | solution.py:25
  23.9 0.0 copy-done
  23.9 0.0 copy-done.3
  23.9 0.0 copy-done.4
  24.0 0.0 copy-start.1
  24.0 4.2 %shard_map.55 = (f32[2048,256]{1,0:T(8,128)S(1)}, f32[2048,128]{1,0:T(8,128)S(1)}) custom-call(s32[2]{0:T(128)S(1)} %pad_add_fusion.place_ref, s32[2]{0:T(128)S(1)} %copy-done.4, s32[2,16]{1,0:T(2,128)S(1)} %copy-done.3, bf16[128,4096]{1,0:T(8,128)(2,1)S(1)} %copy-done, bf16[512,1024]{1,0:T(8,128)(2,1)S(1)} %constant_dynamic-update-slice_fusion.refs_0_, ...), custom_call_target="tpu_custom_call" | custom-call | flops 2147483648 | bytes 1572864 | tf_op jit(solution)/shard_map/pallas_call | solution.py:213
  28.2 0.0 copy-done.1
  28.2 0.0 copy-start.5
  28.2 1.3 %copy-done.5 = f32[2048,256]{1,0:T(8,128)} copy-done((f32[2048,256]{1,0:T(8,128)}, f32[2048,256]{1,0:T(8,128)S(1)}, u32[]{:S(2)}) %copy-start.5) | copy-done | bytes 2097176
  29.5 1.0 %copy-done.7 = f32[2048,128]{1,0:T(8,128)} copy-done((f32[2048,128]{1,0:T(8,128)}, f32[2048,128]{1,0:T(8,128)S(1)}, u32[]{:S(2)}) %copy-start.7) | copy-done | bytes 1048600
  30.5 0.4 collective-permute-done.5
  30.9 0.0 copy-done.12
  30.9 1.1 %pad_maximum_fusion.refs_0_ = bf16[512,1024]{1,0:T(8,128)(2,1)S(1)} fusion(bf16[256,1024]{1,0:T(8,128)(2,1)} %collective-permute-done.5, bf16[128,1024]{1,0:T(8,128)(2,1)S(1)} %copy-done.12, bf16[64,1024]{1,0:T(8,128)(2,1)S(1)} %collective-permute-done.1, bf16[64,1024]{1,0:T(8,128)(2,1)S(1)} %get-tuple-element.27), kind=kLoop, calls=%fused_computation | loop fusion | flops 4194304 | bytes 2097152 | tf_op jit(solution)/shard_map/concatenate | solution.py:286
  32.0 0.1 collective-permute-start.6
  32.1 0.0 copy-start.2
  32.1 1.2 %copy-done.2 = bf16[512,1024]{1,0:T(8,128)(2,1)S(1)} copy-done((bf16[512,1024]{1,0:T(8,128)(2,1)S(1)}, bf16[512,1024]{1,0:T(8,128)(2,1)}, u32[]{:S(2)}) %copy-start.2) | copy-done | bytes 1048600
  33.3 4.3 %shard_map.57 = (f32[2048,256]{1,0:T(8,128)S(1)}, f32[2048,128]{1,0:T(8,128)S(1)}) custom-call(s32[2]{0:T(128)S(1)} %pad_add_fusion.place_ref, s32[2]{0:T(128)S(1)} %copy-done.4, s32[2,16]{1,0:T(2,128)S(1)} %copy-done.3, bf16[128,4096]{1,0:T(8,128)(2,1)S(1)} %copy-done, bf16[512,1024]{1,0:T(8,128)(2,1)S(1)} %constant_dynamic-update-slice_fusion.refs_0_, ...), custom_call_target="tpu_custom_call" | custom-call | flops 2147483648 | bytes 1572864 | tf_op jit(solution)/shard_map/pallas_call | solution.py:213
  37.6 0.0 collective-permute-done.6.refs_1_
  37.6 0.0 copy-done.6
  37.6 0.0 copy-done.8
  37.6 5.3 %shard_map.56 = (bf16[64,2048]{1,0:T(8,128)(2,1)S(1)}, bf16[64,2048]{1,0:T(8,128)(2,1)S(1)}) custom-call(s32[2]{0:T(128)S(1)} %pad_add_fusion.place_ref, s32[2]{0:T(128)S(1)} %copy-done.4, s32[2,16]{1,0:T(2,128)S(1)} %copy-done.3, bf16[128,4096]{1,0:T(8,128)(2,1)S(1)} %copy-done, bf16[512,1024]{1,0:T(8,128)(2,1)S(1)} %pad_maximum_fusion.refs_0_, ...), custom_call_target="tpu_custom_call" | custom-call | flops 2147483648 | bytes 1572864 | tf_op jit(solution)/shard_map/pallas_call | solution.py:213
  42.8 1.6 %collective-permute-start.7 = (bf16[64,2048]{1,0:T(8,128)(2,1)S(1)}, bf16[64,2048]{1,0:T(8,128)(2,1)S(1)}, u32[]{:S(2)}, u32[]{:S(2)}) collective-permute-start(bf16[64,2048]{1,0:T(8,128)(2,1)S(1)} %get-tuple-element.25), channel_id=1, source_target_pairs={{0,1},{1,0},{2,3},{3,2},{4,5},{5,4},{6,7},{7,6},{8,9},{9,8},{10,11... | collective-permute-start | bytes 786440 | tf_op jit(solution)/shard_map/ppermute | solution.py:296
  44.4 5.2 %shard_map.58 = (bf16[64,2048]{1,0:T(8,128)(2,1)S(1)}, bf16[64,2048]{1,0:T(8,128)(2,1)S(1)}) custom-call(s32[2]{0:T(128)S(1)} %pad_add_fusion.place_ref, s32[2]{0:T(128)S(1)} %copy-done.4, s32[2,16]{1,0:T(2,128)S(1)} %copy-done.3, bf16[128,4096]{1,0:T(8,128)(2,1)S(1)} %copy-done, bf16[512,1024]{1,0:T(8,128)(2,1)S(1)} %pad_maximum_fusion.refs_0_, ...), custom_call_target="tpu_custom_call" | custom-call | flops 2147483648 | bytes 1572864 | tf_op jit(solution)/shard_map/pallas_call | solution.py:213
  49.7 0.6 collective-permute-start.8
  50.2 0.1 pad_maximum_fusion.1
  50.3 1.2 %collective-permute-done.7 = bf16[64,2048]{1,0:T(8,128)(2,1)S(1)} collective-permute-done((bf16[64,2048]{1,0:T(8,128)(2,1)S(1)}, bf16[64,2048]{1,0:T(8,128)(2,1)S(1)}, u32[]{:S(2)}, u32[]{:S(2)}) %collective-permute-start.7) | collective-permute-done | bytes 262176 | tf_op jit(solution)/shard_map/ppermute | solution.py:296
  51.6 0.0 copy-start.9
  51.6 6.5 %collective-permute-done.8 = bf16[64,2048]{1,0:T(8,128)(2,1)S(1)} collective-permute-done((bf16[64,2048]{1,0:T(8,128)(2,1)S(1)}, bf16[64,2048]{1,0:T(8,128)(2,1)S(1)}, u32[]{:S(2)}, u32[]{:S(2)}) %collective-permute-start.8) | collective-permute-done | bytes 262176 | tf_op jit(solution)/shard_map/ppermute | solution.py:296
  58.1 0.7 %constant_dynamic-update-slice_fusion.3 = bf16[64,8192]{1,0:T(8,128)(2,1)} fusion(bf16[64,8192]{1,0:T(8,128)(2,1)} %copy-done.9, bf16[64,2048]{1,0:T(8,128)(2,1)S(1)} %collective-permute-done.8, s32[]{:T(128)S(6)} %select_n.22), kind=kLoop, calls=%fused_computation.10 | loop fusion | bytes 524292 | tf_op jit(solution)/shard_map/dynamic_update_slice | solution.py:300
  (12 shorter events, 0.1 us)
Async XLA Ops:
  0.0 14.3 %copy-start.10 = (bf16[128,1024]{1,0:T(8,128)(2,1)S(1)}, bf16[128,1024]{1,0:T(8,128)(2,1)}, u32[]{:S(2)}) copy-start(bf16[128,1024]{1,0:T(8,128)(2,1)} %param.6) | copy-start | bytes 786436
  0.0 7.6 %collective-permute-start = (bf16[128,1024]{1,0:T(8,128)(2,1)}, bf16[128,1024]{1,0:T(8,128)(2,1)S(1)}, u32[]{:S(2)}, u32[]{:S(2)}) collective-permute-start(bf16[128,1024]{1,0:T(8,128)(2,1)} %param.6), channel_id=1, source_target_pairs={{0,4},{2,10},{4,0},{6,14},{8,12},{10,2},{12,8},{14,6},{16,20},{18,... | collective-permute-start | bytes 786440 | tf_op jit(solution)/shard_map/ppermute | solution.py:25
  3.9 8.9 %collective-permute-start.1 = (bf16[64,1024]{1,0:T(8,128)(2,1)S(1)}, bf16[64,1024]{1,0:T(8,128)(2,1)S(1)}, u32[]{:S(2)}, u32[]{:S(2)}) collective-permute-start(bf16[64,1024]{1,0:T(8,128)(2,1)S(1)} %get-tuple-element.28), channel_id=1, source_target_pairs={{0,16},{2,18},{4,20},{6,22},{8,24},{10,26},{12,28},{14,30},{16,0},... | collective-permute-start | bytes 393224 | tf_op jit(solution)/shard_map/ppermute | solution.py:25
  8.6 15.4 %copy-start = (bf16[128,4096]{1,0:T(8,128)(2,1)S(1)}, bf16[128,4096]{1,0:T(8,128)(2,1)}, u32[]{:S(2)}) copy-start(bf16[128,4096]{1,0:T(8,128)(2,1)} %q_ref.7) | copy-start | bytes 3145732
  8.6 15.4 %copy-start.3 = (s32[2,16]{1,0:T(2,128)S(1)}, s32[2,16]{1,0:T(2,128)}, u32[]{:S(2)}) copy-start(s32[2,16]{1,0:T(2,128)} %owner_ref.7) | copy-start | bytes 388
  8.6 15.4 %copy-start.4 = (s32[2]{0:T(128)S(1)}, s32[2]{0:T(128)}, u32[]{:S(2)}) copy-start(s32[2]{0:T(128)} %limit_ref.7) | copy-start | bytes 28
  8.6 12.6 %collective-permute-start.3 = (bf16[256,1024]{1,0:T(8,128)(2,1)S(1)}, bf16[256,1024]{1,0:T(8,128)(2,1)S(1)}, u32[]{:S(2)}, u32[]{:S(2)}) collective-permute-start(bf16[256,1024]{1,0:T(8,128)(2,1)S(1)} %pad_maximum_fusion.3), channel_id=1, source_target_pairs={{0,8},{2,6},{4,12},{6,2},{8,0},{10,14},{12,4},{14,10},{16,24},{18,... | collective-permute-start | bytes 1572872 | tf_op jit(solution)/shard_map/ppermute | solution.py:25
  12.8 6.4 %collective-permute-start.2 = (bf16[128,1024]{1,0:T(8,128)(2,1)S(1)}, bf16[128,1024]{1,0:T(8,128)(2,1)S(1)}, u32[]{:S(2)}, u32[]{:S(2)}) collective-permute-start(bf16[128,1024]{1,0:T(8,128)(2,1)S(1)} %pad_maximum_fusion.4), channel_id=1, source_target_pairs={{0,4},{2,10},{4,0},{6,14},{8,12},{10,2},{12,8},{14,6},{16,20},{18,... | collective-permute-start | bytes 786440 | tf_op jit(solution)/shard_map/ppermute | solution.py:25
  19.3 1.9 %copy-start.11 = (bf16[128,1024]{1,0:T(8,128)(2,1)}, bf16[128,1024]{1,0:T(8,128)(2,1)S(1)}, u32[]{:S(2)}) copy-start(bf16[128,1024]{1,0:T(8,128)(2,1)S(1)} %collective-permute-done.2) | copy-start | bytes 786436
  21.2 2.7 %collective-permute-start.4 = (bf16[512,1024]{1,0:T(8,128)(2,1)S(1)}, bf16[512,1024]{1,0:T(8,128)(2,1)S(1)}, u32[]{:S(2)}, u32[]{:S(2)}) collective-permute-start(bf16[512,1024]{1,0:T(8,128)(2,1)S(1)} %constant_dynamic-update-slice_fusion.refs_0_), channel_id=1, source_target_pairs={{0,2},{2,0},{4,6},{6,4},{8,10},{10,8},{12,14},{14,12},{16,18},{18,... | collective-permute-start | bytes 3145736 | tf_op jit(solution)/shard_map/ppermute | solution.py:25
  21.3 9.6 %collective-permute-start.5 = (bf16[256,1024]{1,0:T(8,128)(2,1)}, bf16[256,1024]{1,0:T(8,128)(2,1)}, u32[]{:S(2)}, u32[]{:S(2)}) collective-permute-start(bf16[256,1024]{1,0:T(8,128)(2,1)} %pad_maximum_fusion.2), channel_id=1, source_target_pairs={{0,8},{2,6},{4,12},{6,2},{8,0},{10,14},{12,4},{14,10},{16,24},{18,... | collective-permute-start | bytes 1572872 | tf_op jit(solution)/shard_map/ppermute | solution.py:25
  23.0 7.9 %copy-start.12 = (bf16[128,1024]{1,0:T(8,128)(2,1)S(1)}, bf16[128,1024]{1,0:T(8,128)(2,1)}, u32[]{:S(2)}) copy-start(bf16[128,1024]{1,0:T(8,128)(2,1)} %copy-done.11) | copy-start | bytes 786436
  24.0 4.2 %copy-start.1 = (bf16[512,1024]{1,0:T(8,128)(2,1)}, bf16[512,1024]{1,0:T(8,128)(2,1)S(1)}, u32[]{:S(2)}) copy-start(bf16[512,1024]{1,0:T(8,128)(2,1)S(1)} %collective-permute-done.4.refs_1_) | copy-start | bytes 3145732
  28.2 1.3 %copy-start.5 = (f32[2048,256]{1,0:T(8,128)}, f32[2048,256]{1,0:T(8,128)S(1)}, u32[]{:S(2)}) copy-start(f32[2048,256]{1,0:T(8,128)S(1)} %get-tuple-element.18.refs_2_) | copy-start | bytes 6291460
  29.5 1.0 %copy-start.7 = (f32[2048,128]{1,0:T(8,128)}, f32[2048,128]{1,0:T(8,128)S(1)}, u32[]{:S(2)}) copy-start(f32[2048,128]{1,0:T(8,128)S(1)} %get-tuple-element.19.refs_3_) | copy-start | bytes 3145732
  32.0 5.6 %collective-permute-start.6 = (bf16[512,1024]{1,0:T(8,128)(2,1)S(1)}, bf16[512,1024]{1,0:T(8,128)(2,1)}, u32[]{:S(2)}, u32[]{:S(2)}) collective-permute-start(bf16[512,1024]{1,0:T(8,128)(2,1)S(1)} %pad_maximum_fusion.refs_0_), channel_id=1, source_target_pairs={{0,2},{2,0},{4,6},{6,4},{8,10},{10,8},{12,14},{14,12},{16,18},{18,... | collective-permute-start | bytes 3145736 | tf_op jit(solution)/shard_map/ppermute | solution.py:25
  32.1 1.2 %copy-start.2 = (bf16[512,1024]{1,0:T(8,128)(2,1)S(1)}, bf16[512,1024]{1,0:T(8,128)(2,1)}, u32[]{:S(2)}) copy-start(bf16[512,1024]{1,0:T(8,128)(2,1)} %copy-done.1) | copy-start | bytes 3145732
  33.3 4.3 %copy-start.6 = (f32[2048,256]{1,0:T(8,128)S(1)}, f32[2048,256]{1,0:T(8,128)}, u32[]{:S(2)}) copy-start(f32[2048,256]{1,0:T(8,128)} %copy-done.5) | copy-start | bytes 6291460
  33.3 4.3 %copy-start.8 = (f32[2048,128]{1,0:T(8,128)S(1)}, f32[2048,128]{1,0:T(8,128)}, u32[]{:S(2)}) copy-start(f32[2048,128]{1,0:T(8,128)} %copy-done.7) | copy-start | bytes 3145732
  42.8 8.8 %collective-permute-start.7 = (bf16[64,2048]{1,0:T(8,128)(2,1)S(1)}, bf16[64,2048]{1,0:T(8,128)(2,1)S(1)}, u32[]{:S(2)}, u32[]{:S(2)}) collective-permute-start(bf16[64,2048]{1,0:T(8,128)(2,1)S(1)} %get-tuple-element.25), channel_id=1, source_target_pairs={{0,1},{1,0},{2,3},{3,2},{4,5},{5,4},{6,7},{7,6},{8,9},{9,8},{10,11... | collective-permute-start | bytes 786440 | tf_op jit(solution)/shard_map/ppermute | solution.py:296
  49.7 8.5 %collective-permute-start.8 = (bf16[64,2048]{1,0:T(8,128)(2,1)S(1)}, bf16[64,2048]{1,0:T(8,128)(2,1)S(1)}, u32[]{:S(2)}, u32[]{:S(2)}) collective-permute-start(bf16[64,2048]{1,0:T(8,128)(2,1)S(1)} %get-tuple-element.26), channel_id=1, source_target_pairs={{0,1},{1,0},{2,3},{3,2},{4,5},{5,4},{6,7},{7,6},{8,9},{9,8},{10,11... | collective-permute-start | bytes 786440 | tf_op jit(solution)/shard_map/ppermute | solution.py:296
  51.6 6.5 %copy-start.9 = (bf16[64,8192]{1,0:T(8,128)(2,1)}, bf16[64,8192]{1,0:T(8,128)(2,1)S(1)}, u32[]{:S(2)}) copy-start(bf16[64,8192]{1,0:T(8,128)(2,1)S(1)} %constant_dynamic-update-slice_fusion.4) | copy-start | bytes 3145732

commit v5 on v4

--- a/solution.py
+++ b/solution.py
@@ -50,7 +50,8 @@
         (state_sum, state_top), refs = refs[:2], refs[2:]
     else:
         (state_sum, state_top), outs, refs = refs[:2], refs[2:4], refs[4:]
-    page_seen, keys, values, scores_a, scores_b, top_a, top_b = refs
+    page_seen, keys, values = refs[:3]
+    scores, weights, tops = refs[3:5], refs[5:7], refs[7:10]
     half_keys = halves[0].shape[0]
     chunk = min(KEY_CHUNK, 2 * half_keys)
     chunks = 2 * half_keys // chunk
@@ -102,12 +103,9 @@
 
     def columns(index, first):
         return [
-            pl.ds(pl.multiple_of(first + (index * block_heads + head) * HD, HD), HD)
+            pl.ds(first + (index * block_heads + head) * HD, HD)
             for head in range(block_heads)
         ]
-
-    def block_rows(index):
-        return pl.ds(pl.multiple_of(index * block, block), block)
 
     def score_steps(index, scores, top):
         group = index // blocks_a_group
@@ -117,7 +115,7 @@
         if first_phase:
             best = jnp.full((block, HD), MASKED, jnp.float32)
         else:
-            best = state_top[block_rows(index), :]
+            best = state_top[pl.ds(index * block, block), :]
         for at in range(chunks):
             made = lax.dot_general(
                 query,
@@ -134,29 +132,26 @@
             yield
         top[...] = jnp.broadcast_to(jnp.max(best, axis=1, keepdims=True), (block, HD))
 
-    def value_steps(index, scores, top):
+    def weight_steps(index, scores, top, weights):
+        for at in range(chunks):
+            for lane_at in range(at * chunk, (at + 1) * chunk, HD):
+                shifted_score = scores[:, pl.ds(lane_at, HD)] - top[...]
+                weights[:, pl.ds(lane_at, HD)] = jnp.exp2(shifted_score * EXP2_SCALE).astype(
+                    jnp.bfloat16
+                )
+            yield
+
+    def finish(index, top, weights):
         group = index // blocks_a_group
+        summed = jnp.dot(weights[...], values[group], preferred_element_type=jnp.float32)
+        rows = pl.ds(index * block, block)
         if first_phase:
-            summed = jnp.zeros((block, 2 * HD), jnp.float32)
-        else:
-            fade = jnp.exp2((state_top[block_rows(index), :] - top[...]) * EXP2_SCALE)
-            summed = state_sum[block_rows(index), :] * jnp.concatenate([fade, fade], axis=1)
-        for at in range(chunks):
-            weights = []
-            for lane_at in range(at * chunk, (at + 1) * chunk, HD):
-                shifted = scores[:, pl.ds(lane_at, HD)] - top[...]
-                weights.append(jnp.exp2(shifted * EXP2_SCALE).astype(jnp.bfloat16))
-            summed = summed + jnp.dot(
-                jnp.concatenate(weights, axis=1),
-                values[group, pl.ds(at * chunk, chunk), :],
-                preferred_element_type=jnp.float32,
-            )
-            yield
-        if first_phase:
-            state_sum[block_rows(index), :] = summed
-            state_top[block_rows(index), :] = top[...]
+            state_sum[rows, :] = summed
+            state_top[rows, :] = top[...]
             return
-        result = (summed[:, :HD] / summed[:, HD:]).astype(jnp.bfloat16)
+        fade = jnp.exp2((state_top[rows, :] - top[...]) * EXP2_SCALE)
+        total = state_sum[rows, HD:] * fade + summed[:, HD:]
+        result = ((state_sum[rows, :HD] * fade + summed[:, :HD]) / total).astype(jnp.bfloat16)
         kept = tokens // head_size
         for head, column in enumerate(columns(index, 0)):
             one = result[head * tokens : (head + 1) * tokens]
@@ -175,15 +170,17 @@
                 if next(step, live) is live:
                     live.remove(step)
 
-    run(score_steps(0, scores_a, top_a))
-
-    def two_blocks(index, carry):
-        run(score_steps(2 * index + 1, scores_b, top_b), value_steps(2 * index, scores_a, top_a))
-        ahead = jnp.minimum(2 * index + 2, blocks - 1)
-        run(score_steps(ahead, scores_a, top_a), value_steps(2 * index + 1, scores_b, top_b))
-        return carry
-
-    lax.fori_loop(0, blocks // 2, two_blocks, 0)
+    for index in range(blocks + 2):
+        if index >= 2:
+            at = (index - 2) % 2
+            finish(index - 2, tops[(index - 2) % 3], weights[at])
+        steps = []
+        if index < blocks:
+            steps.append(score_steps(index, scores[index % 2], tops[index % 3]))
+        if 1 <= index <= blocks:
+            at = (index - 1) % 2
+            steps.append(weight_steps(index - 1, scores[at], tops[(index - 1) % 3], weights[at]))
+        run(*steps)
 
 
 def attend(place, limits, owners, queries, part, parts, mine, theirs, layout, spec, state):
@@ -196,6 +193,9 @@
         block_heads //= 2
     block = block_heads * tokens
     rows = PER_GROUP * groups * tokens
+    operands = queries.size * 2 + mine.size * 4 + rows * HD * 12
+    scratch = groups * total_keys * HD * 8 + block * total_keys * 12 + block * HD * 12
+    limit = operands + scratch + (6 << 20)
     whole = pl.BlockSpec(memory_space=pltpu.VMEM)
     scalars = pl.BlockSpec(memory_space=pltpu.SMEM)
     kept = tokens // head_size
@@ -219,12 +219,11 @@
             pltpu.SMEM((owners.shape[1],), jnp.int32),
             pltpu.VMEM((groups, total_keys, 2 * HD), jnp.bfloat16),
             pltpu.VMEM((groups, total_keys, 2 * HD), jnp.bfloat16),
-            pltpu.VMEM((block, total_keys), jnp.float32),
-            pltpu.VMEM((block, total_keys), jnp.float32),
-            pltpu.VMEM((block, HD), jnp.float32),
-            pltpu.VMEM((block, HD), jnp.float32),
-        ],
-        compiler_params=pltpu.CompilerParams(vmem_limit_bytes=40 * 1024 * 1024),
+        ]
+        + [pltpu.VMEM((block, total_keys), jnp.float32)] * 2
+        + [pltpu.VMEM((block, total_keys), jnp.bfloat16)] * 2
+        + [pltpu.VMEM((block, HD), jnp.float32)] * 3,
+        compiler_params=pltpu.CompilerParams(vmem_limit_bytes=limit),
         cost_estimate=pl.CostEstimate(
             flops=8 * tokens * columns * total_keys,
             bytes_accessed=4 * tokens * columns + 2 * total_keys * columns // PER_GROUP,

time: 59.2 us -> 58.9 us (level)
  no operation moved by 1% of the time
where the time goes in v5:
time: 58.9 us; the launch traced here: 58.6 us
  Pallas kernels  18.5 us (31%)
  waiting for transfers between devices  18.2 us (31%)
  starting transfers between devices  13.1 us (22%)
  local copies, waits for them, and re-layouts  5.37 us (9%)
  other arithmetic  3.2 us (5%)
    pallas_call x4, Pallas kernels, attend(): pl.pallas_call(functools.partial(attend_kernel, spec, tuple(layout), part...  18.5 us
    ppermute x7, starting transfers between devices, hop(): lax.ppermute(value, 'seq', [(source, source ^ bit_of_core[source % 2]) fo...  10.9 us
    ppermute x7, waiting for transfers between devices, hop(): lax.ppermute(value, 'seq', [(source, source ^ bit_of_core[source % 2]) fo...  10.5 us
    ppermute x2, waiting for transfers between devices, body(): lax.ppermute(pair[1], 'head', [(0, 1), (1, 0)])  7.76 us
    unnamed x28, local copies, waits for them, and re-layouts  3.61 us
    ppermute x2, starting transfers between devices, body(): lax.ppermute(pair[1], 'head', [(0, 1), (1, 0)])  2.16 us
  transfers between devices with their start and end apart: 9, of which 8 were waited for; matrix products, arithmetic and copies ran while one was open for 5% of the time, Pallas kernels for 23%

profile of v5, /device:TPU:0, one launch (start us, length us, event | category | flops | bytes accessed | tf_op | source)
XLA Modules:
  0.0 58.6 jit_solution(12708023214375334990)
XLA Ops:
  0.0 2.9 %collective-permute-start = (bf16[128,1024]{1,0:T(8,128)(2,1)}, bf16[128,1024]{1,0:T(8,128)(2,1)S(1)}, u32[]{:S(2)}, u32[]{:S(2)}) collective-permute-start(bf16[128,1024]{1,0:T(8,128)(2,1)} %param.6), channel_id=1, source_target_pairs={{0,4},{2,10},{4,0},{6,14},{8,12},{10,2},{12,8},{14,6},{16,20},{18,... | collective-permute-start | bytes 786440 | tf_op jit(solution)/shard_map/ppermute | solution.py:25
  2.9 1.0 %dynamic-slice_bitcast_fusion.1 = (bf16[64,1024]{1,0:T(8,128)(2,1)S(1)}, bf16[64,1024]{1,0:T(8,128)(2,1)S(1)}) fusion(bf16[2,64,1024]{2,1,0:T(8,128)(2,1)} %param.7, s32[]{:T(128)S(6)} %select_n.19, s32[]{:T(128)S(6)} %select_n.20), kind=kLoop, calls=%fused_computation.6 | loop fusion | bytes 524296 | tf_op jit(solution)/shard_map/jit(dynamic_index_in_dim)/squeeze | solution.py:258
  3.9 2.7 %collective-permute-start.1 = (bf16[64,1024]{1,0:T(8,128)(2,1)S(1)}, bf16[64,1024]{1,0:T(8,128)(2,1)S(1)}, u32[]{:S(2)}, u32[]{:S(2)}) collective-permute-start(bf16[64,1024]{1,0:T(8,128)(2,1)S(1)} %get-tuple-element.28), channel_id=1, source_target_pairs={{0,16},{2,18},{4,20},{6,22},{8,24},{10,26},{12,28},{14,30},{16,0},... | collective-permute-start | bytes 393224 | tf_op jit(solution)/shard_map/ppermute | solution.py:25
  6.6 1.0 %collective-permute-done = bf16[128,1024]{1,0:T(8,128)(2,1)S(1)} collective-permute-done((bf16[128,1024]{1,0:T(8,128)(2,1)}, bf16[128,1024]{1,0:T(8,128)(2,1)S(1)}, u32[]{:S(2)}, u32[]{:S(2)}) %collective-permute-start) | collective-permute-done | bytes 262176 | tf_op jit(solution)/shard_map/ppermute | solution.py:25
  7.6 1.0 %pad_maximum_fusion.3 = bf16[256,1024]{1,0:T(8,128)(2,1)S(1)} fusion(bf16[128,1024]{1,0:T(8,128)(2,1)S(1)} %collective-permute-done, bf16[128,1024]{1,0:T(8,128)(2,1)} %param.6), kind=kLoop, calls=%fused_computation.3 | loop fusion | flops 1048576 | bytes 1048576 | tf_op jit(solution)/shard_map/concatenate | solution.py:268
  8.6 0.0 copy-start
  8.6 0.0 copy-start.3
  8.6 0.0 copy-start.4
  8.6 2.1 %collective-permute-start.3 = (bf16[256,1024]{1,0:T(8,128)(2,1)S(1)}, bf16[256,1024]{1,0:T(8,128)(2,1)S(1)}, u32[]{:S(2)}, u32[]{:S(2)}) collective-permute-start(bf16[256,1024]{1,0:T(8,128)(2,1)S(1)} %pad_maximum_fusion.3), channel_id=1, source_target_pairs={{0,8},{2,6},{4,12},{6,2},{8,0},{10,14},{12,4},{14,10},{16,24},{18,... | collective-permute-start | bytes 1572872 | tf_op jit(solution)/shard_map/ppermute | solution.py:25
  10.7 2.1 %collective-permute-done.1 = bf16[64,1024]{1,0:T(8,128)(2,1)S(1)} collective-permute-done((bf16[64,1024]{1,0:T(8,128)(2,1)S(1)}, bf16[64,1024]{1,0:T(8,128)(2,1)S(1)}, u32[]{:S(2)}, u32[]{:S(2)}) %collective-permute-start.1) | collective-permute-done | bytes 131104 | tf_op jit(solution)/shard_map/ppermute | solution.py:25
  12.8 1.5 %collective-permute-start.2 = (bf16[128,1024]{1,0:T(8,128)(2,1)S(1)}, bf16[128,1024]{1,0:T(8,128)(2,1)S(1)}, u32[]{:S(2)}, u32[]{:S(2)}) collective-permute-start(bf16[128,1024]{1,0:T(8,128)(2,1)S(1)} %pad_maximum_fusion.4), channel_id=1, source_target_pairs={{0,4},{2,10},{4,0},{6,14},{8,12},{10,2},{12,8},{14,6},{16,20},{18,... | collective-permute-start | bytes 786440 | tf_op jit(solution)/shard_map/ppermute | solution.py:25
  14.3 0.0 copy-done.10
  14.4 4.9 %collective-permute-done.2 = bf16[128,1024]{1,0:T(8,128)(2,1)S(1)} collective-permute-done((bf16[128,1024]{1,0:T(8,128)(2,1)S(1)}, bf16[128,1024]{1,0:T(8,128)(2,1)S(1)}, u32[]{:S(2)}, u32[]{:S(2)}) %collective-permute-start.2) | collective-permute-done | bytes 262176 | tf_op jit(solution)/shard_map/ppermute | solution.py:25
  19.3 0.9 %pad_maximum_fusion.2 = bf16[256,1024]{1,0:T(8,128)(2,1)} fusion(bf16[128,1024]{1,0:T(8,128)(2,1)S(1)} %collective-permute-done.2, bf16[64,1024]{1,0:T(8,128)(2,1)S(1)} %collective-permute-done.1, bf16[64,1024]{1,0:T(8,128)(2,1)S(1)} %get-tuple-element.27), kind=kLoop, calls=%fused_computation.2 | loop fusion | flops 1572864 | bytes 1048576 | tf_op jit(solution)/shard_map/concatenate | solution.py:265
  20.2 1.0 %collective-permute-done.3 = bf16[256,1024]{1,0:T(8,128)(2,1)S(1)} collective-permute-done((bf16[256,1024]{1,0:T(8,128)(2,1)S(1)}, bf16[256,1024]{1,0:T(8,128)(2,1)S(1)}, u32[]{:S(2)}, u32[]{:S(2)}) %collective-permute-start.3) | collective-permute-done | bytes 524320 | tf_op jit(solution)/shard_map/ppermute | solution.py:25
  21.2 0.0 copy-done.11
  21.2 0.1 collective-permute-start.4
  21.3 1.6 %collective-permute-start.5 = (bf16[256,1024]{1,0:T(8,128)(2,1)}, bf16[256,1024]{1,0:T(8,128)(2,1)}, u32[]{:S(2)}, u32[]{:S(2)}) collective-permute-start(bf16[256,1024]{1,0:T(8,128)(2,1)} %pad_maximum_fusion.2), channel_id=1, source_target_pairs={{0,8},{2,6},{4,12},{6,2},{8,0},{10,14},{12,4},{14,10},{16,24},{18,... | collective-permute-start | bytes 1572872 | tf_op jit(solution)/shard_map/ppermute | solution.py:25
  22.9 0.1 pad_add_fusion.place_ref
  23.0 1.0 %collective-permute-done.4.refs_1_ = bf16[512,1024]{1,0:T(8,128)(2,1)S(1)} collective-permute-done((bf16[512,1024]{1,0:T(8,128)(2,1)S(1)}, bf16[512,1024]{1,0:T(8,128)(2,1)S(1)}, u32[]{:S(2)}, u32[]{:S(2)}) %collective-permute-start.4) | collective-permute-done | bytes 1048608 | tf_op jit(solution)/shard_map/ppermute | solution.py:25
  23.9 0.0 copy-done
  23.9 0.0 copy-done.3
  23.9 0.0 copy-done.4
  24.0 0.0 copy-start.1
  24.0 4.1 %shard_map.55 = (f32[2048,256]{1,0:T(8,128)S(1)}, f32[2048,128]{1,0:T(8,128)S(1)}) custom-call(s32[2]{0:T(128)S(1)} %pad_add_fusion.place_ref, s32[2]{0:T(128)S(1)} %copy-done.4, s32[2,16]{1,0:T(2,128)S(1)} %copy-done.3, bf16[128,4096]{1,0:T(8,128)(2,1)S(1)} %copy-done, bf16[512,1024]{1,0:T(8,128)(2,1)S(1)} %constant_dynamic-update-slice_fusion.refs_0_, ...), custom_call_target="tpu_custom_call" | custom-call | flops 2147483648 | bytes 1572864 | tf_op jit(solution)/shard_map/pallas_call | solution.py:213
  28.0 0.0 copy-done.1
  28.0 0.0 copy-start.5
  28.1 1.3 %copy-done.5 = f32[2048,256]{1,0:T(8,128)} copy-done((f32[2048,256]{1,0:T(8,128)}, f32[2048,256]{1,0:T(8,128)S(1)}, u32[]{:S(2)}) %copy-start.5) | copy-done | bytes 2097176
  29.4 1.0 %copy-done.7 = f32[2048,128]{1,0:T(8,128)} copy-done((f32[2048,128]{1,0:T(8,128)}, f32[2048,128]{1,0:T(8,128)S(1)}, u32[]{:S(2)}) %copy-start.7) | copy-done | bytes 1048600
  30.4 0.5 collective-permute-done.5
  30.9 0.0 copy-done.12
  30.9 1.1 %pad_maximum_fusion.refs_0_ = bf16[512,1024]{1,0:T(8,128)(2,1)S(1)} fusion(bf16[256,1024]{1,0:T(8,128)(2,1)} %collective-permute-done.5, bf16[128,1024]{1,0:T(8,128)(2,1)S(1)} %copy-done.12, bf16[64,1024]{1,0:T(8,128)(2,1)S(1)} %collective-permute-done.1, bf16[64,1024]{1,0:T(8,128)(2,1)S(1)} %get-tuple-element.27), kind=kLoop, calls=%fused_computation | loop fusion | flops 4194304 | bytes 2097152 | tf_op jit(solution)/shard_map/concatenate | solution.py:285
  32.0 0.1 collective-permute-start.6
  32.1 0.0 copy-start.2
  32.1 1.2 %copy-done.2 = bf16[512,1024]{1,0:T(8,128)(2,1)S(1)} copy-done((bf16[512,1024]{1,0:T(8,128)(2,1)S(1)}, bf16[512,1024]{1,0:T(8,128)(2,1)}, u32[]{:S(2)}) %copy-start.2) | copy-done | bytes 1048600
  33.3 4.1 %shard_map.57 = (f32[2048,256]{1,0:T(8,128)S(1)}, f32[2048,128]{1,0:T(8,128)S(1)}) custom-call(s32[2]{0:T(128)S(1)} %pad_add_fusion.place_ref, s32[2]{0:T(128)S(1)} %copy-done.4, s32[2,16]{1,0:T(2,128)S(1)} %copy-done.3, bf16[128,4096]{1,0:T(8,128)(2,1)S(1)} %copy-done, bf16[512,1024]{1,0:T(8,128)(2,1)S(1)} %constant_dynamic-update-slice_fusion.refs_0_, ...), custom_call_target="tpu_custom_call" | custom-call | flops 2147483648 | bytes 1572864 | tf_op jit(solution)/shard_map/pallas_call | solution.py:213
  37.4 0.0 collective-permute-done.6.refs_1_
  37.4 0.0 copy-done.6
  37.5 5.3 %shard_map.56 = (bf16[64,2048]{1,0:T(8,128)(2,1)S(1)}, bf16[64,2048]{1,0:T(8,128)(2,1)S(1)}) custom-call(s32[2]{0:T(128)S(1)} %pad_add_fusion.place_ref, s32[2]{0:T(128)S(1)} %copy-done.4, s32[2,16]{1,0:T(2,128)S(1)} %copy-done.3, bf16[128,4096]{1,0:T(8,128)(2,1)S(1)} %copy-done, bf16[512,1024]{1,0:T(8,128)(2,1)S(1)} %pad_maximum_fusion.refs_0_, ...), custom_call_target="tpu_custom_call" | custom-call | flops 2147483648 | bytes 1572864 | tf_op jit(solution)/shard_map/pallas_call | solution.py:213
  42.7 1.6 %collective-permute-start.7 = (bf16[64,2048]{1,0:T(8,128)(2,1)S(1)}, bf16[64,2048]{1,0:T(8,128)(2,1)S(1)}, u32[]{:S(2)}, u32[]{:S(2)}) collective-permute-start(bf16[64,2048]{1,0:T(8,128)(2,1)S(1)} %get-tuple-element.25), channel_id=1, source_target_pairs={{0,1},{1,0},{2,3},{3,2},{4,5},{5,4},{6,7},{7,6},{8,9},{9,8},{10,11... | collective-permute-start | bytes 786440 | tf_op jit(solution)/shard_map/ppermute | solution.py:295
  44.3 5.1 %shard_map.58 = (bf16[64,2048]{1,0:T(8,128)(2,1)S(1)}, bf16[64,2048]{1,0:T(8,128)(2,1)S(1)}) custom-call(s32[2]{0:T(128)S(1)} %pad_add_fusion.place_ref, s32[2]{0:T(128)S(1)} %copy-done.4, s32[2,16]{1,0:T(2,128)S(1)} %copy-done.3, bf16[128,4096]{1,0:T(8,128)(2,1)S(1)} %copy-done, bf16[512,1024]{1,0:T(8,128)(2,1)S(1)} %pad_maximum_fusion.refs_0_, ...), custom_call_target="tpu_custom_call" | custom-call | flops 2147483648 | bytes 1572864 | tf_op jit(solution)/shard_map/pallas_call | solution.py:213
  49.4 0.6 collective-permute-start.8
  50.0 0.1 pad_maximum_fusion.1
  50.1 1.4 %collective-permute-done.7 = bf16[64,2048]{1,0:T(8,128)(2,1)S(1)} collective-permute-done((bf16[64,2048]{1,0:T(8,128)(2,1)S(1)}, bf16[64,2048]{1,0:T(8,128)(2,1)S(1)}, u32[]{:S(2)}, u32[]{:S(2)}) %collective-permute-start.7) | collective-permute-done | bytes 262176 | tf_op jit(solution)/shard_map/ppermute | solution.py:295
  51.5 0.0 copy-start.9
  51.5 6.4 %collective-permute-done.8 = bf16[64,2048]{1,0:T(8,128)(2,1)S(1)} collective-permute-done((bf16[64,2048]{1,0:T(8,128)(2,1)S(1)}, bf16[64,2048]{1,0:T(8,128)(2,1)S(1)}, u32[]{:S(2)}, u32[]{:S(2)}) %collective-permute-start.8) | collective-permute-done | bytes 262176 | tf_op jit(solution)/shard_map/ppermute | solution.py:295
  57.9 0.0 copy-done.9
  57.9 0.7 %constant_dynamic-update-slice_fusion.3 = bf16[64,8192]{1,0:T(8,128)(2,1)} fusion(bf16[64,8192]{1,0:T(8,128)(2,1)} %copy-done.9, bf16[64,2048]{1,0:T(8,128)(2,1)S(1)} %collective-permute-done.8, s32[]{:T(128)S(6)} %select_n.22), kind=kLoop, calls=%fused_computation.10 | loop fusion | bytes 524292 | tf_op jit(solution)/shard_map/dynamic_update_slice | solution.py:299
  (12 shorter events, 0.1 us)
Async XLA Ops:
  0.0 14.3 %copy-start.10 = (bf16[128,1024]{1,0:T(8,128)(2,1)S(1)}, bf16[128,1024]{1,0:T(8,128)(2,1)}, u32[]{:S(2)}) copy-start(bf16[128,1024]{1,0:T(8,128)(2,1)} %param.6) | copy-start | bytes 786436
  0.0 7.6 %collective-permute-start = (bf16[128,1024]{1,0:T(8,128)(2,1)}, bf16[128,1024]{1,0:T(8,128)(2,1)S(1)}, u32[]{:S(2)}, u32[]{:S(2)}) collective-permute-start(bf16[128,1024]{1,0:T(8,128)(2,1)} %param.6), channel_id=1, source_target_pairs={{0,4},{2,10},{4,0},{6,14},{8,12},{10,2},{12,8},{14,6},{16,20},{18,... | collective-permute-start | bytes 786440 | tf_op jit(solution)/shard_map/ppermute | solution.py:25
  3.9 8.9 %collective-permute-start.1 = (bf16[64,1024]{1,0:T(8,128)(2,1)S(1)}, bf16[64,1024]{1,0:T(8,128)(2,1)S(1)}, u32[]{:S(2)}, u32[]{:S(2)}) collective-permute-start(bf16[64,1024]{1,0:T(8,128)(2,1)S(1)} %get-tuple-element.28), channel_id=1, source_target_pairs={{0,16},{2,18},{4,20},{6,22},{8,24},{10,26},{12,28},{14,30},{16,0},... | collective-permute-start | bytes 393224 | tf_op jit(solution)/shard_map/ppermute | solution.py:25
  8.6 15.4 %copy-start = (bf16[128,4096]{1,0:T(8,128)(2,1)S(1)}, bf16[128,4096]{1,0:T(8,128)(2,1)}, u32[]{:S(2)}) copy-start(bf16[128,4096]{1,0:T(8,128)(2,1)} %q_ref.7) | copy-start | bytes 3145732
  8.6 15.4 %copy-start.3 = (s32[2,16]{1,0:T(2,128)S(1)}, s32[2,16]{1,0:T(2,128)}, u32[]{:S(2)}) copy-start(s32[2,16]{1,0:T(2,128)} %owner_ref.7) | copy-start | bytes 388
  8.6 15.4 %copy-start.4 = (s32[2]{0:T(128)S(1)}, s32[2]{0:T(128)}, u32[]{:S(2)}) copy-start(s32[2]{0:T(128)} %limit_ref.7) | copy-start | bytes 28
  8.6 12.6 %collective-permute-start.3 = (bf16[256,1024]{1,0:T(8,128)(2,1)S(1)}, bf16[256,1024]{1,0:T(8,128)(2,1)S(1)}, u32[]{:S(2)}, u32[]{:S(2)}) collective-permute-start(bf16[256,1024]{1,0:T(8,128)(2,1)S(1)} %pad_maximum_fusion.3), channel_id=1, source_target_pairs={{0,8},{2,6},{4,12},{6,2},{8,0},{10,14},{12,4},{14,10},{16,24},{18,... | collective-permute-start | bytes 1572872 | tf_op jit(solution)/shard_map/ppermute | solution.py:25
  12.8 6.4 %collective-permute-start.2 = (bf16[128,1024]{1,0:T(8,128)(2,1)S(1)}, bf16[128,1024]{1,0:T(8,128)(2,1)S(1)}, u32[]{:S(2)}, u32[]{:S(2)}) collective-permute-start(bf16[128,1024]{1,0:T(8,128)(2,1)S(1)} %pad_maximum_fusion.4), channel_id=1, source_target_pairs={{0,4},{2,10},{4,0},{6,14},{8,12},{10,2},{12,8},{14,6},{16,20},{18,... | collective-permute-start | bytes 786440 | tf_op jit(solution)/shard_map/ppermute | solution.py:25
  19.3 1.9 %copy-start.11 = (bf16[128,1024]{1,0:T(8,128)(2,1)}, bf16[128,1024]{1,0:T(8,128)(2,1)S(1)}, u32[]{:S(2)}) copy-start(bf16[128,1024]{1,0:T(8,128)(2,1)S(1)} %collective-permute-done.2) | copy-start | bytes 786436
  21.2 2.7 %collective-permute-start.4 = (bf16[512,1024]{1,0:T(8,128)(2,1)S(1)}, bf16[512,1024]{1,0:T(8,128)(2,1)S(1)}, u32[]{:S(2)}, u32[]{:S(2)}) collective-permute-start(bf16[512,1024]{1,0:T(8,128)(2,1)S(1)} %constant_dynamic-update-slice_fusion.refs_0_), channel_id=1, source_target_pairs={{0,2},{2,0},{4,6},{6,4},{8,10},{10,8},{12,14},{14,12},{16,18},{18,... | collective-permute-start | bytes 3145736 | tf_op jit(solution)/shard_map/ppermute | solution.py:25
  21.3 9.6 %collective-permute-start.5 = (bf16[256,1024]{1,0:T(8,128)(2,1)}, bf16[256,1024]{1,0:T(8,128)(2,1)}, u32[]{:S(2)}, u32[]{:S(2)}) collective-permute-start(bf16[256,1024]{1,0:T(8,128)(2,1)} %pad_maximum_fusion.2), channel_id=1, source_target_pairs={{0,8},{2,6},{4,12},{6,2},{8,0},{10,14},{12,4},{14,10},{16,24},{18,... | collective-permute-start | bytes 1572872 | tf_op jit(solution)/shard_map/ppermute | solution.py:25
  23.0 7.9 %copy-start.12 = (bf16[128,1024]{1,0:T(8,128)(2,1)S(1)}, bf16[128,1024]{1,0:T(8,128)(2,1)}, u32[]{:S(2)}) copy-start(bf16[128,1024]{1,0:T(8,128)(2,1)} %copy-done.11) | copy-start | bytes 786436
  24.0 4.1 %copy-start.1 = (bf16[512,1024]{1,0:T(8,128)(2,1)}, bf16[512,1024]{1,0:T(8,128)(2,1)S(1)}, u32[]{:S(2)}) copy-start(bf16[512,1024]{1,0:T(8,128)(2,1)S(1)} %collective-permute-done.4.refs_1_) | copy-start | bytes 3145732
  28.0 1.3 %copy-start.5 = (f32[2048,256]{1,0:T(8,128)}, f32[2048,256]{1,0:T(8,128)S(1)}, u32[]{:S(2)}) copy-start(f32[2048,256]{1,0:T(8,128)S(1)} %get-tuple-element.18.refs_2_) | copy-start | bytes 6291460
  29.4 1.0 %copy-start.7 = (f32[2048,128]{1,0:T(8,128)}, f32[2048,128]{1,0:T(8,128)S(1)}, u32[]{:S(2)}) copy-start(f32[2048,128]{1,0:T(8,128)S(1)} %get-tuple-element.19.refs_3_) | copy-start | bytes 3145732
  32.0 5.5 %collective-permute-start.6 = (bf16[512,1024]{1,0:T(8,128)(2,1)S(1)}, bf16[512,1024]{1,0:T(8,128)(2,1)}, u32[]{:S(2)}, u32[]{:S(2)}) collective-permute-start(bf16[512,1024]{1,0:T(8,128)(2,1)S(1)} %pad_maximum_fusion.refs_0_), channel_id=1, source_target_pairs={{0,2},{2,0},{4,6},{6,4},{8,10},{10,8},{12,14},{14,12},{16,18},{18,... | collective-permute-start | bytes 3145736 | tf_op jit(solution)/shard_map/ppermute | solution.py:25
  32.1 1.2 %copy-start.2 = (bf16[512,1024]{1,0:T(8,128)(2,1)S(1)}, bf16[512,1024]{1,0:T(8,128)(2,1)}, u32[]{:S(2)}) copy-start(bf16[512,1024]{1,0:T(8,128)(2,1)} %copy-done.1) | copy-start | bytes 3145732
  33.3 4.1 %copy-start.6 = (f32[2048,256]{1,0:T(8,128)S(1)}, f32[2048,256]{1,0:T(8,128)}, u32[]{:S(2)}) copy-start(f32[2048,256]{1,0:T(8,128)} %copy-done.5) | copy-start | bytes 6291460
  33.3 4.2 %copy-start.8 = (f32[2048,128]{1,0:T(8,128)S(1)}, f32[2048,128]{1,0:T(8,128)}, u32[]{:S(2)}) copy-start(f32[2048,128]{1,0:T(8,128)} %copy-done.7) | copy-start | bytes 3145732
  42.7 8.8 %collective-permute-start.7 = (bf16[64,2048]{1,0:T(8,128)(2,1)S(1)}, bf16[64,2048]{1,0:T(8,128)(2,1)S(1)}, u32[]{:S(2)}, u32[]{:S(2)}) collective-permute-start(bf16[64,2048]{1,0:T(8,128)(2,1)S(1)} %get-tuple-element.25), channel_id=1, source_target_pairs={{0,1},{1,0},{2,3},{3,2},{4,5},{5,4},{6,7},{7,6},{8,9},{9,8},{10,11... | collective-permute-start | bytes 786440 | tf_op jit(solution)/shard_map/ppermute | solution.py:295
  49.4 8.5 %collective-permute-start.8 = (bf16[64,2048]{1,0:T(8,128)(2,1)S(1)}, bf16[64,2048]{1,0:T(8,128)(2,1)S(1)}, u32[]{:S(2)}, u32[]{:S(2)}) collective-permute-start(bf16[64,2048]{1,0:T(8,128)(2,1)S(1)} %get-tuple-element.26), channel_id=1, source_target_pairs={{0,1},{1,0},{2,3},{3,2},{4,5},{5,4},{6,7},{7,6},{8,9},{9,8},{10,11... | collective-permute-start | bytes 786440 | tf_op jit(solution)/shard_map/ppermute | solution.py:295
  51.5 6.4 %copy-start.9 = (bf16[64,8192]{1,0:T(8,128)(2,1)}, bf16[64,8192]{1,0:T(8,128)(2,1)S(1)}, u32[]{:S(2)}) copy-start(bf16[64,8192]{1,0:T(8,128)(2,1)S(1)} %constant_dynamic-update-slice_fusion.4) | copy-start | bytes 3145732

commit v6 on v5

--- a/solution.py
+++ b/solution.py
@@ -16,7 +16,7 @@
 EXP2_SCALE = HD ** (-0.5) * math.log2(math.e)
 MASKED = -1e30
 SCORE_BYTES = 8 * 1024 * 1024
-KEY_CHUNK = 256
+KEY_CHUNK = 512
 SPAN_ROWS, OWN_PAGE, CROSSED_PAGE = range(3)
 
 
@@ -42,7 +42,7 @@
     return order
 
 
-def attend_kernel(spec, layout, part, block_heads, groups, place_ref, limit_ref, owner_ref, q_ref, *refs):
+def attend_kernel(spec, layout, part, block_heads, groups, limit_ref, owner_ref, q_ref, *refs):
     tokens, page, group_size, head_size, orders = spec
     first_phase = layout[0][1] == SPAN_ROWS
     halves, refs = refs[:2], refs[2:]
@@ -55,8 +55,8 @@
     half_keys = halves[0].shape[0]
     chunk = min(KEY_CHUNK, 2 * half_keys)
     chunks = 2 * half_keys // chunk
-    me = place_ref[0]
-    my_head = place_ref[1]
+    me = lax.axis_index("seq")
+    my_head = lax.axis_index("head")
     request = me // group_size
 
     def note_page(index, carry):
@@ -183,7 +183,7 @@
         run(*steps)
 
 
-def attend(place, limits, owners, queries, part, parts, mine, theirs, layout, spec, state):
+def attend(limits, owners, queries, part, parts, mine, theirs, layout, spec, state):
     tokens, _, _, head_size = spec[:4]
     total_keys = 2 * mine.shape[0]
     columns = queries.shape[1] // parts
@@ -213,7 +213,7 @@
     return pl.pallas_call(
         functools.partial(attend_kernel, spec, tuple(layout), part, block_heads, groups),
         out_shape=out_shape,
-        in_specs=[scalars] * 3 + [whole] * (3 + len(state)),
+        in_specs=[scalars] * 2 + [whole] * (3 + len(state)),
         out_specs=[whole] * 2,
         scratch_shapes=[
             pltpu.SMEM((owners.shape[1],), jnp.int32),
@@ -229,16 +229,67 @@
             bytes_accessed=4 * tokens * columns + 2 * total_keys * columns // PER_GROUP,
             transcendentals=0,
         ),
-    )(place, limits, owners, queries, mine, theirs, *state)
+    )(limits, owners, queries, mine, theirs, *state)
+
+
+def pick_kernel(group_size, cache_ref, span_ref, other_ref, own_ref, copied_ref):
+    request = lax.axis_index("seq") // group_size
+    other_ref[...] = cache_ref[1 - request]
+    own_ref[...] = cache_ref[request]
+    copied_ref[...] = span_ref[...]
+
+
+def pick(cache, span, group_size):
+    whole = pl.BlockSpec(memory_space=pltpu.VMEM)
+    return pl.pallas_call(
+        functools.partial(pick_kernel, group_size),
+        out_shape=[
+            jax.ShapeDtypeStruct(cache.shape[1:], cache.dtype),
+            jax.ShapeDtypeStruct(cache.shape[1:], cache.dtype),
+            jax.ShapeDtypeStruct(span.shape, span.dtype),
+        ],
+        in_specs=[whole] * 2,
+        out_specs=[whole] * 3,
+        compiler_params=pltpu.CompilerParams(vmem_limit_bytes=8 << 20),
+    )(cache, span)
+
+
+def join_kernel(pieces, *refs):
+    parts, (out_ref, done) = refs[:pieces], refs[pieces:]
+    columns = [ref.shape[1] for ref in parts[: pieces // 2]]
+    side = out_ref.shape[1] // 2
+    my_head = lax.axis_index("head")
+    copies = []
+    for at, ref in enumerate(parts):
+        owner = my_head if at < pieces // 2 else 1 - my_head
+        first = pl.multiple_of(owner * side + sum(columns[: at % (pieces // 2)]), HD)
+        copies.append(
+            pltpu.make_async_copy(ref, out_ref.at[:, pl.ds(first, ref.shape[1])], done.at[at])
+        )
+    for copy in copies:
+        copy.start()
+    for copy in copies:
+        copy.wait()
+
+
+def put_together(kept, received):
+    pieces = len(kept) + len(received)
+    rows = kept[0].shape[0]
+    columns = sum(one.shape[1] for one in kept + received)
+    return pl.pallas_call(
+        functools.partial(join_kernel, pieces),
+        out_shape=jax.ShapeDtypeStruct((rows, columns), kept[0].dtype),
+        in_specs=[pl.BlockSpec(memory_space=pltpu.VMEM)] * pieces,
+        out_specs=pl.BlockSpec(memory_space=pl.ANY),
+        scratch_shapes=[pltpu.SemaphoreType.DMA((pieces,))],
+        compiler_params=pltpu.CompilerParams(vmem_limit_bytes=8 << 20),
+    )(*kept, *received)
 
 
 def body(span_query, span_kv, prefix_cache, prefix_len, block_owner):
     seq_size = lax.axis_size("seq")
     head_size = lax.axis_size("head")
     group_size = seq_size // REQS
-    me = lax.axis_index("seq").astype(jnp.int32)
-    my_head = lax.axis_index("head").astype(jnp.int32)
-    request = me // group_size
     tokens = span_kv.shape[0]
     page = prefix_cache.shape[1]
     groups = span_kv.shape[1] // (2 * HD)
@@ -253,12 +304,11 @@
         return layout + shifted(layout, 1 << stage)
 
     stages = len(bits)
-    other_page = lax.dynamic_index_in_dim(prefix_cache, 1 - request, 0, keepdims=False)
+    other_page, own_page, span = pick(prefix_cache, span_kv, group_size)
     crossed = hop(other_page, (group_size, group_size))
-    own_page = lax.dynamic_index_in_dim(prefix_cache, request, 0, keepdims=False)
-    span, span_layout = span_kv, [(0, SPAN_ROWS, tokens)]
+    span_layout = [(0, SPAN_ROWS, tokens)]
     for stage in range(stages):
-        received = send(span, stage)
+        received = send(span if stage else span_kv, stage)
         if stage == 0:
             crossed = after(received, crossed)
             pages = jnp.concatenate([own_page, crossed], axis=0)
@@ -268,9 +318,8 @@
         span, span_layout = jnp.concatenate([span, received], axis=0), grown(span_layout, stage)
     span_swapped = hop(span, (1, 1))
 
-    place = jnp.stack([me, my_head])
     spec = (tokens, page, group_size, head_size, orders)
-    common = (place, prefix_len, block_owner, span_query)
+    common = (prefix_len, block_owner, span_query)
     states = [
         attend(*common, part, parts, span, span_swapped, span_layout, spec, None)
         for part in range(parts)
@@ -293,12 +342,7 @@
         return lax.all_to_all(joined, "head", split_axis=0, concat_axis=1, tiled=True)
     kept = [pair[0] for pair in results]
     received = [lax.ppermute(pair[1], "head", [(0, 1), (1, 0)]) for pair in results]
-    joined = jnp.concatenate(kept + kept, axis=1)
-    start = (1 - my_head) * span_query.shape[1]
-    for one in received:
-        joined = lax.dynamic_update_slice(joined, one, (0, start))
-        start = start + one.shape[1]
-    return joined
+    return put_together(kept, received)
 
 
 def solution(mesh):

time: 58.9 us -> 60 us (1.019)
  waiting for transfers between devices: 18.2 us -> 29.3 us
  starting transfers between devices: 13.1 us -> 9.59 us
  local copies, waits for them, and re-layouts: 5.37 us -> 2.12 us
  other arithmetic: 3.2 us -> 0.05 us
    ppermute x7, waiting for transfers between devices: 10.5 us -> 21.4 us  [hop(): lax.ppermute(value, 'seq', [(source, source ^ bit_of_core[source % 2]) fo...]
    ppermute x7, starting transfers between devices: 10.9 us -> 7.43 us  [hop(): lax.ppermute(value, 'seq', [(source, source ^ bit_of_core[source % 2]) fo...]
    concatenate x3 -> x0, other arithmetic: 2.12 us -> none  [the longest x1 1.11 us: body(): jnp.concatenate([pages, received], axis=0)]
    unnamed x28 -> x14, local copies, waits for them, and re-layouts: 3.61 us -> 1.99 us
    pallas_call x4, Pallas kernels: 18.5 us -> 17.4 us  [attend(): pl.pallas_call(functools.partial(attend_kernel, spec, tuple(layout), part...]
    pallas_call x0 -> x2, Pallas kernels: none -> 1.03 us  [the longest x1 0.99 us: put_together(): pl.pallas_call(functools.partial(join_kernel, pieces), out_shape=jax.Shap...]
    squeeze x1 -> x0, local copies, waits for them, and re-layouts: 0.98 us -> none  [body(): lax.dynamic_index_in_dim(prefix_cache, request, 0, keepdims=False)]
    concatenate x1, other arithmetic: 0.98 us -> 0.03 us  [body(): jnp.concatenate([span, received], axis=0)]
  transfers between devices with their start and end apart: 9 -> 9, of which waited for: 8 -> 7; matrix products, arithmetic and copies ran while one was open for 5% -> 0% of each run, Pallas kernels for 23% -> 21%
where the time goes in v6:
time: 60 us; the launch traced here: 59.8 us
  waiting for transfers between devices  29.3 us (49%)
  Pallas kernels  18.4 us (31%)
  starting transfers between devices  9.59 us (16%)
  local copies, waits for them, and re-layouts  2.12 us (4%)
    ppermute x7, waiting for transfers between devices, hop(): lax.ppermute(value, 'seq', [(source, source ^ bit_of_core[source % 2]) fo...  21.4 us
    pallas_call x4, Pallas kernels, attend(): pl.pallas_call(functools.partial(attend_kernel, spec, tuple(layout), part...  17.4 us
    ppermute x2, waiting for transfers between devices, body(): lax.ppermute(pair[1], 'head', [(0, 1), (1, 0)])  7.92 us
    ppermute x7, starting transfers between devices, hop(): lax.ppermute(value, 'seq', [(source, source ^ bit_of_core[source % 2]) fo...  7.43 us
    ppermute x2, starting transfers between devices, body(): lax.ppermute(pair[1], 'head', [(0, 1), (1, 0)])  2.15 us
    unnamed x14, local copies, waits for them, and re-layouts  1.99 us
  transfers between devices with their start and end apart: 9, of which 7 were waited for; matrix products, arithmetic and copies ran while one was open for 0% of the time, Pallas kernels for 21%

profile of v6, /device:TPU:0, one launch (start us, length us, event | category | flops | bytes accessed | tf_op | source)
XLA Modules:
  0.0 59.8 jit_solution(8643445782767522534)
XLA Ops:
  0.0 2.9 %collective-permute-start = (bf16[128,1024]{1,0:T(8,128)(2,1)}, bf16[128,1024]{1,0:T(8,128)(2,1)S(1)}, u32[]{:S(2)}, u32[]{:S(2)}) collective-permute-start(bf16[128,1024]{1,0:T(8,128)(2,1)} %span_ref.1), channel_id=1, source_target_pairs={{0,4},{2,10},{4,0},{6,14},{8,12},{10,2},{12,8},{14,6},{16,20},{18,... | collective-permute-start | bytes 786440 | tf_op jit(solution)/shard_map/ppermute | solution.py:25
  2.9 0.0 copy-start
  2.9 0.9 %copy-done = bf16[2,64,1024]{2,1,0:T(8,128)(2,1)S(1)} copy-done((bf16[2,64,1024]{2,1,0:T(8,128)(2,1)S(1)}, bf16[2,64,1024]{2,1,0:T(8,128)(2,1)}, u32[]{:S(2)}) %copy-start) | copy-done | bytes 262168
  3.9 0.0 copy-start.1
  3.9 0.9 %copy-done.1 = bf16[128,1024]{1,0:T(8,128)(2,1)S(1)} copy-done((bf16[128,1024]{1,0:T(8,128)(2,1)S(1)}, bf16[128,1024]{1,0:T(8,128)(2,1)}, u32[]{:S(2)}) %copy-start.1) | copy-done | bytes 262168
  4.9 2.7 %collective-permute-start.1 = (bf16[64,1024]{1,0:T(8,128)(2,1)S(1)}, bf16[64,1024]{1,0:T(8,128)(2,1)S(1)}, u32[]{:S(2)}, u32[]{:S(2)}) collective-permute-start(bf16[64,1024]{1,0:T(8,128)(2,1)S(1)} %get-tuple-element.20), channel_id=1, source_target_pairs={{0,16},{2,18},{4,20},{6,22},{8,24},{10,26},{12,28},{14,30},{16,0},... | collective-permute-start | bytes 393224 | tf_op jit(solution)/shard_map/ppermute | solution.py:25
  7.6 6.1 %collective-permute-done.1 = bf16[64,1024]{1,0:T(8,128)(2,1)S(1)} collective-permute-done((bf16[64,1024]{1,0:T(8,128)(2,1)S(1)}, bf16[64,1024]{1,0:T(8,128)(2,1)S(1)}, u32[]{:S(2)}, u32[]{:S(2)}) %collective-permute-start.1) | collective-permute-done | bytes 131104 | tf_op jit(solution)/shard_map/ppermute | solution.py:25
  13.7 0.0 collective-permute-done
  13.7 0.0 copy-start.2
  13.7 0.0 copy-start.3
  13.8 0.0 copy-start.4
  13.8 0.1 collective-permute-start.3
  13.9 1.6 %collective-permute-start.2 = (bf16[128,1024]{1,0:T(8,128)(2,1)S(1)}, bf16[128,1024]{1,0:T(8,128)(2,1)S(1)}, u32[]{:S(2)}, u32[]{:S(2)}) collective-permute-start(bf16[128,1024]{1,0:T(8,128)(2,1)S(1)} %pad_maximum_fusion.1), channel_id=1, source_target_pairs={{0,4},{2,10},{4,0},{6,14},{8,12},{10,2},{12,8},{14,6},{16,20},{18,... | collective-permute-start | bytes 786440 | tf_op jit(solution)/shard_map/ppermute | solution.py:25
  15.5 7.6 %collective-permute-done.2 = bf16[128,1024]{1,0:T(8,128)(2,1)S(1)} collective-permute-done((bf16[128,1024]{1,0:T(8,128)(2,1)S(1)}, bf16[128,1024]{1,0:T(8,128)(2,1)S(1)}, u32[]{:S(2)}, u32[]{:S(2)}) %collective-permute-start.2) | collective-permute-done | bytes 262176 | tf_op jit(solution)/shard_map/ppermute | solution.py:25
  23.2 0.1 constant_dynamic-update-slice_fusion
  23.2 2.6 %collective-permute-done.3 = bf16[256,1024]{1,0:T(8,128)(2,1)S(1)} collective-permute-done((bf16[256,1024]{1,0:T(8,128)(2,1)S(1)}, bf16[256,1024]{1,0:T(8,128)(2,1)S(1)}, u32[]{:S(2)}, u32[]{:S(2)}) %collective-permute-start.3) | collective-permute-done | bytes 524320 | tf_op jit(solution)/shard_map/ppermute | solution.py:25
  25.9 0.1 collective-permute-start.4
  25.9 0.1 collective-permute-start.5
  26.0 2.6 %collective-permute-done.4.refs_1_ = bf16[512,1024]{1,0:T(8,128)(2,1)S(1)} collective-permute-done((bf16[512,1024]{1,0:T(8,128)(2,1)S(1)}, bf16[512,1024]{1,0:T(8,128)(2,1)S(1)}, u32[]{:S(2)}, u32[]{:S(2)}) %collective-permute-start.4) | collective-permute-done | bytes 1048608 | tf_op jit(solution)/shard_map/ppermute | solution.py:25
  28.6 0.0 copy-done.2
  28.6 0.0 copy-done.3
  28.6 0.0 copy-done.4
  28.6 4.1 %shard_map.56 = (f32[2048,256]{1,0:T(8,128)S(1)}, f32[2048,128]{1,0:T(8,128)S(1)}) custom-call(s32[2]{0:T(128)S(1)} %copy-done.4, s32[2,16]{1,0:T(2,128)S(1)} %copy-done.3, bf16[128,4096]{1,0:T(8,128)(2,1)S(1)} %copy-done.2, bf16[512,1024]{1,0:T(8,128)(2,1)S(1)} %constant_dynamic-update-slice_fusion.3.refs_0_, ...), custom_call_target="tpu_custom_call" | custom-call | flops 2147483648 | bytes 1572864 | tf_op jit(solution)/shard_map/pallas_call | solution.py:213
  32.7 2.4 %collective-permute-done.5 = bf16[256,1024]{1,0:T(8,128)(2,1)S(1)} collective-permute-done((bf16[256,1024]{1,0:T(8,128)(2,1)S(1)}, bf16[256,1024]{1,0:T(8,128)(2,1)S(1)}, u32[]{:S(2)}, u32[]{:S(2)}) %collective-permute-start.5) | collective-permute-done | bytes 524320 | tf_op jit(solution)/shard_map/ppermute | solution.py:25
  35.2 0.1 collective-permute-start.6
  35.3 4.1 %shard_map.58 = (f32[2048,256]{1,0:T(8,128)S(1)}, f32[2048,128]{1,0:T(8,128)S(1)}) custom-call(s32[2]{0:T(128)S(1)} %copy-done.4, s32[2,16]{1,0:T(2,128)S(1)} %copy-done.3, bf16[128,4096]{1,0:T(8,128)(2,1)S(1)} %copy-done.2, bf16[512,1024]{1,0:T(8,128)(2,1)S(1)} %constant_dynamic-update-slice_fusion.3.refs_0_, ...), custom_call_target="tpu_custom_call" | custom-call | flops 2147483648 | bytes 1572864 | tf_op jit(solution)/shard_map/pallas_call | solution.py:213
  39.5 0.0 collective-permute-done.6.refs_1_
  39.5 4.6 %shard_map.57 = (bf16[64,2048]{1,0:T(8,128)(2,1)S(1)}, bf16[64,2048]{1,0:T(8,128)(2,1)S(1)}) custom-call(s32[2]{0:T(128)S(1)} %copy-done.4, s32[2,16]{1,0:T(2,128)S(1)} %copy-done.3, bf16[128,4096]{1,0:T(8,128)(2,1)S(1)} %copy-done.2, bf16[512,1024]{1,0:T(8,128)(2,1)S(1)} %constant_dynamic-update-slice_fusion.6.refs_0_, ...), custom_call_target="tpu_custom_call" | custom-call | flops 2147483648 | bytes 1572864 | tf_op jit(solution)/shard_map/pallas_call | solution.py:213
  44.1 1.6 %collective-permute-start.7 = (bf16[64,2048]{1,0:T(8,128)(2,1)S(1)}, bf16[64,2048]{1,0:T(8,128)(2,1)S(1)}, u32[]{:S(2)}, u32[]{:S(2)}) collective-permute-start(bf16[64,2048]{1,0:T(8,128)(2,1)S(1)} %get-tuple-element.31), channel_id=1, source_target_pairs={{0,1},{1,0},{2,3},{3,2},{4,5},{5,4},{6,7},{7,6},{8,9},{9,8},{10,11... | collective-permute-start | bytes 786440 | tf_op jit(solution)/shard_map/ppermute | solution.py:344
  45.7 4.5 %shard_map.59 = (bf16[64,2048]{1,0:T(8,128)(2,1)S(1)}, bf16[64,2048]{1,0:T(8,128)(2,1)S(1)}) custom-call(s32[2]{0:T(128)S(1)} %copy-done.4, s32[2,16]{1,0:T(2,128)S(1)} %copy-done.3, bf16[128,4096]{1,0:T(8,128)(2,1)S(1)} %copy-done.2, bf16[512,1024]{1,0:T(8,128)(2,1)S(1)} %constant_dynamic-update-slice_fusion.6.refs_0_, ...), custom_call_target="tpu_custom_call" | custom-call | flops 2147483648 | bytes 1572864 | tf_op jit(solution)/shard_map/pallas_call | solution.py:213
  50.2 0.6 collective-permute-start.8
  50.7 2.2 %collective-permute-done.7.refs_2_ = bf16[64,2048]{1,0:T(8,128)(2,1)S(1)} collective-permute-done((bf16[64,2048]{1,0:T(8,128)(2,1)S(1)}, bf16[64,2048]{1,0:T(8,128)(2,1)S(1)}, u32[]{:S(2)}, u32[]{:S(2)}) %collective-permute-start.7) | collective-permute-done | bytes 262176 | tf_op jit(solution)/shard_map/ppermute | solution.py:344
  52.9 5.8 %collective-permute-done.8.refs_3_ = bf16[64,2048]{1,0:T(8,128)(2,1)S(1)} collective-permute-done((bf16[64,2048]{1,0:T(8,128)(2,1)S(1)}, bf16[64,2048]{1,0:T(8,128)(2,1)S(1)}, u32[]{:S(2)}, u32[]{:S(2)}) %collective-permute-start.8) | collective-permute-done | bytes 262176 | tf_op jit(solution)/shard_map/ppermute | solution.py:344
  58.7 1.0 %shard_map.60 = bf16[64,8192]{1,0:T(8,128)(2,1)} custom-call(bf16[64,2048]{1,0:T(8,128)(2,1)S(1)} %get-tuple-element.27.refs_0_, bf16[64,2048]{1,0:T(8,128)(2,1)S(1)} %get-tuple-element.30.refs_1_, bf16[64,2048]{1,0:T(8,128)(2,1)S(1)} %collective-permute-done.7.refs_2_, bf16[64,2048]{1,0:T(8,128)(2,1)S(1)} %collective-permute-done.8.refs_3_), custom_call_target="tpu_custom_call" | custom-call | tf_op jit(solution)/shard_map/pallas_call | solution.py:279
  (9 shorter events, 0.2 us)
Async XLA Ops:
  0.0 13.7 %collective-permute-start = (bf16[128,1024]{1,0:T(8,128)(2,1)}, bf16[128,1024]{1,0:T(8,128)(2,1)S(1)}, u32[]{:S(2)}, u32[]{:S(2)}) collective-permute-start(bf16[128,1024]{1,0:T(8,128)(2,1)} %span_ref.1), channel_id=1, source_target_pairs={{0,4},{2,10},{4,0},{6,14},{8,12},{10,2},{12,8},{14,6},{16,20},{18,... | collective-permute-start | bytes 786440 | tf_op jit(solution)/shard_map/ppermute | solution.py:25
  2.9 0.9 %copy-start = (bf16[2,64,1024]{2,1,0:T(8,128)(2,1)S(1)}, bf16[2,64,1024]{2,1,0:T(8,128)(2,1)}, u32[]{:S(2)}) copy-start(bf16[2,64,1024]{2,1,0:T(8,128)(2,1)} %cache_ref.1) | copy-start | bytes 786436
  3.9 0.9 %copy-start.1 = (bf16[128,1024]{1,0:T(8,128)(2,1)S(1)}, bf16[128,1024]{1,0:T(8,128)(2,1)}, u32[]{:S(2)}) copy-start(bf16[128,1024]{1,0:T(8,128)(2,1)} %span_ref.1) | copy-start | bytes 786436
  4.9 8.8 %collective-permute-start.1 = (bf16[64,1024]{1,0:T(8,128)(2,1)S(1)}, bf16[64,1024]{1,0:T(8,128)(2,1)S(1)}, u32[]{:S(2)}, u32[]{:S(2)}) collective-permute-start(bf16[64,1024]{1,0:T(8,128)(2,1)S(1)} %get-tuple-element.20), channel_id=1, source_target_pairs={{0,16},{2,18},{4,20},{6,22},{8,24},{10,26},{12,28},{14,30},{16,0},... | collective-permute-start | bytes 393224 | tf_op jit(solution)/shard_map/ppermute | solution.py:25
  13.7 14.9 %copy-start.2 = (bf16[128,4096]{1,0:T(8,128)(2,1)S(1)}, bf16[128,4096]{1,0:T(8,128)(2,1)}, u32[]{:S(2)}) copy-start(bf16[128,4096]{1,0:T(8,128)(2,1)} %q_ref.7) | copy-start | bytes 3145732
  13.7 14.8 %copy-start.3 = (s32[2,16]{1,0:T(2,128)S(1)}, s32[2,16]{1,0:T(2,128)}, u32[]{:S(2)}) copy-start(s32[2,16]{1,0:T(2,128)} %owner_ref.7) | copy-start | bytes 388
  13.8 14.8 %copy-start.4 = (s32[2]{0:T(128)S(1)}, s32[2]{0:T(128)}, u32[]{:S(2)}) copy-start(s32[2]{0:T(128)} %limit_ref.7) | copy-start | bytes 28
  13.8 12.1 %collective-permute-start.3 = (bf16[256,1024]{1,0:T(8,128)(2,1)S(1)}, bf16[256,1024]{1,0:T(8,128)(2,1)S(1)}, u32[]{:S(2)}, u32[]{:S(2)}) collective-permute-start(bf16[256,1024]{1,0:T(8,128)(2,1)S(1)} %pad_maximum_fusion), channel_id=1, source_target_pairs={{0,8},{2,6},{4,12},{6,2},{8,0},{10,14},{12,4},{14,10},{16,24},{18,... | collective-permute-start | bytes 1572872 | tf_op jit(solution)/shard_map/ppermute | solution.py:25
  13.9 9.3 %collective-permute-start.2 = (bf16[128,1024]{1,0:T(8,128)(2,1)S(1)}, bf16[128,1024]{1,0:T(8,128)(2,1)S(1)}, u32[]{:S(2)}, u32[]{:S(2)}) collective-permute-start(bf16[128,1024]{1,0:T(8,128)(2,1)S(1)} %pad_maximum_fusion.1), channel_id=1, source_target_pairs={{0,4},{2,10},{4,0},{6,14},{8,12},{10,2},{12,8},{14,6},{16,20},{18,... | collective-permute-start | bytes 786440 | tf_op jit(solution)/shard_map/ppermute | solution.py:25
  25.9 2.7 %collective-permute-start.4 = (bf16[512,1024]{1,0:T(8,128)(2,1)S(1)}, bf16[512,1024]{1,0:T(8,128)(2,1)S(1)}, u32[]{:S(2)}, u32[]{:S(2)}) collective-permute-start(bf16[512,1024]{1,0:T(8,128)(2,1)S(1)} %constant_dynamic-update-slice_fusion.3.refs_0_), channel_id=1, source_target_pairs={{0,2},{2,0},{4,6},{6,4},{8,10},{10,8},{12,14},{14,12},{16,18},{18,... | collective-permute-start | bytes 3145736 | tf_op jit(solution)/shard_map/ppermute | solution.py:25
  25.9 9.2 %collective-permute-start.5 = (bf16[256,1024]{1,0:T(8,128)(2,1)S(1)}, bf16[256,1024]{1,0:T(8,128)(2,1)S(1)}, u32[]{:S(2)}, u32[]{:S(2)}) collective-permute-start(bf16[256,1024]{1,0:T(8,128)(2,1)S(1)} %get-tuple-element.33), channel_id=1, source_target_pairs={{0,8},{2,6},{4,12},{6,2},{8,0},{10,14},{12,4},{14,10},{16,24},{18,... | collective-permute-start | bytes 1572872 | tf_op jit(solution)/shard_map/ppermute | solution.py:25
  35.2 4.2 %collective-permute-start.6 = (bf16[512,1024]{1,0:T(8,128)(2,1)S(1)}, bf16[512,1024]{1,0:T(8,128)(2,1)S(1)}, u32[]{:S(2)}, u32[]{:S(2)}) collective-permute-start(bf16[512,1024]{1,0:T(8,128)(2,1)S(1)} %constant_dynamic-update-slice_fusion.6.refs_0_), channel_id=1, source_target_pairs={{0,2},{2,0},{4,6},{6,4},{8,10},{10,8},{12,14},{14,12},{16,18},{18,... | collective-permute-start | bytes 3145736 | tf_op jit(solution)/shard_map/ppermute | solution.py:25
  44.1 8.8 %collective-permute-start.7 = (bf16[64,2048]{1,0:T(8,128)(2,1)S(1)}, bf16[64,2048]{1,0:T(8,128)(2,1)S(1)}, u32[]{:S(2)}, u32[]{:S(2)}) collective-permute-start(bf16[64,2048]{1,0:T(8,128)(2,1)S(1)} %get-tuple-element.31), channel_id=1, source_target_pairs={{0,1},{1,0},{2,3},{3,2},{4,5},{5,4},{6,7},{7,6},{8,9},{9,8},{10,11... | collective-permute-start | bytes 786440 | tf_op jit(solution)/shard_map/ppermute | solution.py:344
  50.2 8.5 %collective-permute-start.8 = (bf16[64,2048]{1,0:T(8,128)(2,1)S(1)}, bf16[64,2048]{1,0:T(8,128)(2,1)S(1)}, u32[]{:S(2)}, u32[]{:S(2)}) collective-permute-start(bf16[64,2048]{1,0:T(8,128)(2,1)S(1)} %get-tuple-element.32), channel_id=1, source_target_pairs={{0,1},{1,0},{2,3},{3,2},{4,5},{5,4},{6,7},{7,6},{8,9},{9,8},{10,11... | collective-permute-start | bytes 786440 | tf_op jit(solution)/shard_map/ppermute | solution.py:344

commit v7 on v6

--- a/solution.py
+++ b/solution.py
@@ -17,6 +17,7 @@
 MASKED = -1e30
 SCORE_BYTES = 8 * 1024 * 1024
 KEY_CHUNK = 512
+BIAS_ROWS = 16
 SPAN_ROWS, OWN_PAGE, CROSSED_PAGE = range(3)
 
 
@@ -67,9 +68,12 @@
         lax.fori_loop(0, owner_ref.shape[1], note_page, 0)
 
     offsets = [hypercube_order(order) for order in orders]
+    row = lax.broadcasted_iota(jnp.int32, (BIAS_ROWS, half_keys), 0)
+    key = lax.broadcasted_iota(jnp.int32, (BIAS_ROWS, half_keys), 1)
     for half in range(2):
         holder = me ^ half
-        start = half * half_keys
+        start = 0
+        seen = row > 0
         for slot, kind, rows in layout:
             source = holder ^ jnp.where(holder % 2 == 0, offsets[0][slot], offsets[1][slot])
             if kind == SPAN_ROWS:
@@ -78,20 +82,18 @@
                 count = page_seen[source]
             else:
                 count = page_seen[source ^ group_size]
-            row = lax.broadcasted_iota(jnp.int32, (rows, HD), 0)
-            lane = lax.broadcasted_iota(jnp.int32, (rows, HD), 1)
-            bias = jnp.where((row < count) | (lane > 0), jnp.float32(0.0), jnp.float32(MASKED))
-            for group in range(groups):
-                keys[group, pl.ds(start, rows), HD:] = bias.astype(jnp.bfloat16)
+            seen = seen | ((key >= start) & (key < start + count))
             start += rows
+        bias = jnp.where(seen, jnp.float32(0.0), jnp.float32(MASKED)).astype(jnp.bfloat16)
+        at = pl.ds(half * half_keys, half_keys)
+        for group in range(groups):
+            column = (part * groups + group) * 2 * HD
+            keys[group, :HD, at] = halves[half][:, pl.ds(column, HD)].T
+            keys[group, pl.ds(HD, BIAS_ROWS), at] = bias
+            values[group, at, :HD] = halves[half][:, pl.ds(column + HD, HD)]
+    rest = HD - BIAS_ROWS
+    keys[:, HD + BIAS_ROWS :, :] = jnp.zeros((groups, rest, 2 * half_keys), jnp.bfloat16)
     values[:, :, HD:] = jnp.ones((groups, 2 * half_keys, HD), jnp.bfloat16)
-
-    for group in range(groups):
-        for half, ref in enumerate(halves):
-            at = pl.ds(half * half_keys, half_keys)
-            column = (part * groups + group) * 2 * HD
-            keys[group, at, :HD] = ref[:, pl.ds(column, HD)]
-            values[group, at, :HD] = ref[:, pl.ds(column + HD, HD)]
 
     block = block_heads * tokens
     blocks_a_group = PER_GROUP // block_heads
@@ -117,18 +119,16 @@
         else:
             best = state_top[pl.ds(index * block, block), :]
         for at in range(chunks):
-            made = lax.dot_general(
-                query,
-                keys[group, pl.ds(at * chunk, chunk), :],
-                (((1,), (1,)), ((), ())),
-                preferred_element_type=jnp.float32,
+            made = jnp.dot(
+                query, keys[group, :, pl.ds(at * chunk, chunk)], preferred_element_type=jnp.float32
             )
             if at == 0 and first_phase:
                 own = jnp.where(causal, made[:, :tokens], MASKED)
                 made = jnp.concatenate([own, made[:, tokens:]], axis=1)
             scores[:, pl.ds(at * chunk, chunk)] = made
-            for lane_at in range(0, chunk, HD):
-                best = jnp.maximum(best, made[:, lane_at : lane_at + HD])
+            for lane_at in range(0, chunk, 2 * HD):
+                left, right = made[:, lane_at : lane_at + HD], made[:, lane_at + HD : lane_at + 2 * HD]
+                best = jnp.maximum(best, jnp.maximum(left, right))
             yield
         top[...] = jnp.broadcast_to(jnp.max(best, axis=1, keepdims=True), (block, HD))
 
@@ -217,7 +217,7 @@
         out_specs=[whole] * 2,
         scratch_shapes=[
             pltpu.SMEM((owners.shape[1],), jnp.int32),
-            pltpu.VMEM((groups, total_keys, 2 * HD), jnp.bfloat16),
+            pltpu.VMEM((groups, 2 * HD, total_keys), jnp.bfloat16),
             pltpu.VMEM((groups, total_keys, 2 * HD), jnp.bfloat16),
         ]
         + [pltpu.VMEM((block, total_keys), jnp.float32)] * 2
@@ -232,15 +232,20 @@
     )(limits, owners, queries, mine, theirs, *state)
 
 
-def pick_kernel(group_size, cache_ref, span_ref, other_ref, own_ref, copied_ref):
+def pick_kernel(group_size, cache_ref, span_ref, other_ref, own_ref, copied_ref, done):
     request = lax.axis_index("seq") // group_size
-    other_ref[...] = cache_ref[1 - request]
-    own_ref[...] = cache_ref[request]
-    copied_ref[...] = span_ref[...]
+    copies = [
+        pltpu.make_async_copy(cache_ref.at[1 - request], other_ref, done.at[0]),
+        pltpu.make_async_copy(cache_ref.at[request], own_ref, done.at[1]),
+        pltpu.make_async_copy(span_ref, copied_ref, done.at[2]),
+    ]
+    for copy in copies:
+        copy.start()
+    for copy in copies:
+        copy.wait()
 
 
 def pick(cache, span, group_size):
-    whole = pl.BlockSpec(memory_space=pltpu.VMEM)
     return pl.pallas_call(
         functools.partial(pick_kernel, group_size),
         out_shape=[
@@ -248,8 +253,9 @@
             jax.ShapeDtypeStruct(cache.shape[1:], cache.dtype),
             jax.ShapeDtypeStruct(span.shape, span.dtype),
         ],
-        in_specs=[whole] * 2,
-        out_specs=[whole] * 3,
+        in_specs=[pl.BlockSpec(memory_space=pl.ANY)] * 2,
+        out_specs=[pl.BlockSpec(memory_space=pltpu.VMEM)] * 3,
+        scratch_shapes=[pltpu.SemaphoreType.DMA((3,))],
         compiler_params=pltpu.CompilerParams(vmem_limit_bytes=8 << 20),
     )(cache, span)
 
@@ -309,13 +315,13 @@
     span_layout = [(0, SPAN_ROWS, tokens)]
     for stage in range(stages):
         received = send(span if stage else span_kv, stage)
+        if stage == 1:
+            received = after(pages, received)
+        span, span_layout = jnp.concatenate([span, received], axis=0), grown(span_layout, stage)
         if stage == 0:
-            crossed = after(received, crossed)
+            crossed = after(span, crossed)
             pages = jnp.concatenate([own_page, crossed], axis=0)
             pages = jnp.concatenate([pages, send(pages, 0)], axis=0)
-        elif stage == 1:
-            received = after(pages, received)
-        span, span_layout = jnp.concatenate([span, received], axis=0), grown(span_layout, stage)
     span_swapped = hop(span, (1, 1))
 
     spec = (tokens, page, group_size, head_size, orders)

time: 60 us -> 56.3 us (0.938)
  waiting for transfers between devices: 29.3 us -> 23.4 us
  starting transfers between devices: 9.59 us -> 11.3 us
    ppermute x7, waiting for transfers between devices: 21.4 us -> 15.5 us  [hop(): lax.ppermute(value, 'seq', [(source, source ^ bit_of_core[source % 2]) fo...]
    ppermute x7, starting transfers between devices: 7.43 us -> 9.11 us  [hop(): lax.ppermute(value, 'seq', [(source, source ^ bit_of_core[source % 2]) fo...]
  transfers between devices with their start and end apart: 9 -> 9, of which waited for: 7 -> 7; matrix products, arithmetic and copies ran while one was open for 0% -> 0% of each run, Pallas kernels for 21% -> 24%
where the time goes in v7:
time: 56.3 us; the launch traced here: 56.1 us
  waiting for transfers between devices  23.4 us (42%)
  Pallas kernels  18.9 us (34%)
  starting transfers between devices  11.3 us (20%)
  local copies, waits for them, and re-layouts  2.19 us (4%)
    pallas_call x4, Pallas kernels, attend(): pl.pallas_call(functools.partial(attend_kernel, spec, tuple(layout), part...  17.6 us
    ppermute x7, waiting for transfers between devices, hop(): lax.ppermute(value, 'seq', [(source, source ^ bit_of_core[source % 2]) fo...  15.5 us
    ppermute x7, starting transfers between devices, hop(): lax.ppermute(value, 'seq', [(source, source ^ bit_of_core[source % 2]) fo...  9.11 us
    ppermute x2, waiting for transfers between devices, body(): lax.ppermute(pair[1], 'head', [(0, 1), (1, 0)])  7.94 us
    ppermute x2, starting transfers between devices, body(): lax.ppermute(pair[1], 'head', [(0, 1), (1, 0)])  2.16 us
    unnamed x14, local copies, waits for them, and re-layouts  2.07 us
  transfers between devices with their start and end apart: 9, of which 7 were waited for; matrix products, arithmetic and copies ran while one was open for 0% of the time, Pallas kernels for 24%

profile of v7, /device:TPU:0, one launch (start us, length us, event | category | flops | bytes accessed | tf_op | source)
XLA Modules:
  0.0 56.1 jit_solution(210453214756657755)
XLA Ops:
  0.0 2.9 %collective-permute-start = (bf16[128,1024]{1,0:T(8,128)(2,1)}, bf16[128,1024]{1,0:T(8,128)(2,1)S(1)}, u32[]{:S(2)}, u32[]{:S(2)}) collective-permute-start(bf16[128,1024]{1,0:T(8,128)(2,1)} %span_ref.1), channel_id=1, source_target_pairs={{0,4},{2,10},{4,0},{6,14},{8,12},{10,2},{12,8},{14,6},{16,20},{18,... | collective-permute-start | bytes 786440 | tf_op jit(solution)/shard_map/ppermute | solution.py:26
  2.9 0.0 copy-start
  2.9 0.9 %copy-done = bf16[2,64,1024]{2,1,0:T(8,128)(2,1)S(1)} copy-done((bf16[2,64,1024]{2,1,0:T(8,128)(2,1)S(1)}, bf16[2,64,1024]{2,1,0:T(8,128)(2,1)}, u32[]{:S(2)}) %copy-start) | copy-done | bytes 262168
  3.9 0.0 copy-start.1
  3.9 0.9 %copy-done.1 = bf16[128,1024]{1,0:T(8,128)(2,1)S(1)} copy-done((bf16[128,1024]{1,0:T(8,128)(2,1)S(1)}, bf16[128,1024]{1,0:T(8,128)(2,1)}, u32[]{:S(2)}) %copy-start.1) | copy-done | bytes 262168
  4.8 0.4 shard_map.55
  5.2 2.7 %collective-permute-start.1 = (bf16[64,1024]{1,0:T(8,128)(2,1)S(1)}, bf16[64,1024]{1,0:T(8,128)(2,1)S(1)}, u32[]{:S(2)}, u32[]{:S(2)}) collective-permute-start(bf16[64,1024]{1,0:T(8,128)(2,1)S(1)} %get-tuple-element.21), channel_id=1, source_target_pairs={{0,16},{2,18},{4,20},{6,22},{8,24},{10,26},{12,28},{14,30},{16,0},... | collective-permute-start | bytes 393224 | tf_op jit(solution)/shard_map/ppermute | solution.py:26
  7.9 0.1 constant_dynamic-update-slice_fusion.7
  7.9 0.0 copy-start.2
  7.9 0.0 copy-start.3
  7.9 0.0 copy-start.4
  8.0 0.0 collective-permute-done
  8.0 0.1 constant_dynamic-update-slice_fusion.6
  8.0 1.7 %collective-permute-start.3 = (bf16[256,1024]{1,0:T(8,128)(2,1)S(1)}, bf16[256,1024]{1,0:T(8,128)(2,1)S(1)}, u32[]{:S(2)}, u32[]{:S(2)}) collective-permute-start(bf16[256,1024]{1,0:T(8,128)(2,1)S(1)} %get-tuple-element.36), channel_id=1, source_target_pairs={{0,8},{2,6},{4,12},{6,2},{8,0},{10,14},{12,4},{14,10},{16,24},{18,... | collective-permute-start | bytes 1572872 | tf_op jit(solution)/shard_map/ppermute | solution.py:26
  9.7 4.4 %collective-permute-done.1 = bf16[64,1024]{1,0:T(8,128)(2,1)S(1)} collective-permute-done((bf16[64,1024]{1,0:T(8,128)(2,1)S(1)}, bf16[64,1024]{1,0:T(8,128)(2,1)S(1)}, u32[]{:S(2)}, u32[]{:S(2)}) %collective-permute-start.1) | collective-permute-done | bytes 131104 | tf_op jit(solution)/shard_map/ppermute | solution.py:26
  14.1 1.6 %collective-permute-start.2 = (bf16[128,1024]{1,0:T(8,128)(2,1)S(1)}, bf16[128,1024]{1,0:T(8,128)(2,1)S(1)}, u32[]{:S(2)}, u32[]{:S(2)}) collective-permute-start(bf16[128,1024]{1,0:T(8,128)(2,1)S(1)} %pad_maximum_fusion), channel_id=1, source_target_pairs={{0,4},{2,10},{4,0},{6,14},{8,12},{10,2},{12,8},{14,6},{16,20},{18,... | collective-permute-start | bytes 786440 | tf_op jit(solution)/shard_map/ppermute | solution.py:26
  15.8 4.8 %collective-permute-done.2 = bf16[128,1024]{1,0:T(8,128)(2,1)S(1)} collective-permute-done((bf16[128,1024]{1,0:T(8,128)(2,1)S(1)}, bf16[128,1024]{1,0:T(8,128)(2,1)S(1)}, u32[]{:S(2)}, u32[]{:S(2)}) %collective-permute-start.2) | collective-permute-done | bytes 262176 | tf_op jit(solution)/shard_map/ppermute | solution.py:26
  20.6 0.1 constant_dynamic-update-slice_fusion.2
  20.6 1.3 %collective-permute-done.3 = bf16[256,1024]{1,0:T(8,128)(2,1)S(1)} collective-permute-done((bf16[256,1024]{1,0:T(8,128)(2,1)S(1)}, bf16[256,1024]{1,0:T(8,128)(2,1)S(1)}, u32[]{:S(2)}, u32[]{:S(2)}) %collective-permute-start.3) | collective-permute-done | bytes 524320 | tf_op jit(solution)/shard_map/ppermute | solution.py:26
  22.0 0.2 collective-permute-start.4
  22.2 0.0 collective-permute-start.5
  22.2 2.5 %collective-permute-done.4.refs_1_ = bf16[512,1024]{1,0:T(8,128)(2,1)S(1)} collective-permute-done((bf16[512,1024]{1,0:T(8,128)(2,1)S(1)}, bf16[512,1024]{1,0:T(8,128)(2,1)S(1)}, u32[]{:S(2)}, u32[]{:S(2)}) %collective-permute-start.4) | collective-permute-done | bytes 1048608 | tf_op jit(solution)/shard_map/ppermute | solution.py:26
  24.7 0.0 copy-done.2
  24.7 0.0 copy-done.3
  24.7 0.0 copy-done.4
  24.7 4.2 %shard_map.56 = (f32[2048,256]{1,0:T(8,128)S(1)}, f32[2048,128]{1,0:T(8,128)S(1)}) custom-call(s32[2]{0:T(128)S(1)} %copy-done.4, s32[2,16]{1,0:T(2,128)S(1)} %copy-done.3, bf16[128,4096]{1,0:T(8,128)(2,1)S(1)} %copy-done.2, bf16[512,1024]{1,0:T(8,128)(2,1)S(1)} %constant_dynamic-update-slice_fusion.5.refs_0_, ...), custom_call_target="tpu_custom_call" | custom-call | flops 2147483648 | bytes 1572864 | tf_op jit(solution)/shard_map/pallas_call | solution.py:213
  28.9 2.4 %collective-permute-done.5 = bf16[256,1024]{1,0:T(8,128)(2,1)S(1)} collective-permute-done((bf16[256,1024]{1,0:T(8,128)(2,1)S(1)}, bf16[256,1024]{1,0:T(8,128)(2,1)S(1)}, u32[]{:S(2)}, u32[]{:S(2)}) %collective-permute-start.5) | collective-permute-done | bytes 524320 | tf_op jit(solution)/shard_map/ppermute | solution.py:26
  31.4 0.1 collective-permute-start.6
  31.5 4.2 %shard_map.58 = (f32[2048,256]{1,0:T(8,128)S(1)}, f32[2048,128]{1,0:T(8,128)S(1)}) custom-call(s32[2]{0:T(128)S(1)} %copy-done.4, s32[2,16]{1,0:T(2,128)S(1)} %copy-done.3, bf16[128,4096]{1,0:T(8,128)(2,1)S(1)} %copy-done.2, bf16[512,1024]{1,0:T(8,128)(2,1)S(1)} %constant_dynamic-update-slice_fusion.5.refs_0_, ...), custom_call_target="tpu_custom_call" | custom-call | flops 2147483648 | bytes 1572864 | tf_op jit(solution)/shard_map/pallas_call | solution.py:213
  35.7 0.0 collective-permute-done.6.refs_1_
  35.7 4.5 %shard_map.57 = (bf16[64,2048]{1,0:T(8,128)(2,1)S(1)}, bf16[64,2048]{1,0:T(8,128)(2,1)S(1)}) custom-call(s32[2]{0:T(128)S(1)} %copy-done.4, s32[2,16]{1,0:T(2,128)S(1)} %copy-done.3, bf16[128,4096]{1,0:T(8,128)(2,1)S(1)} %copy-done.2, bf16[512,1024]{1,0:T(8,128)(2,1)S(1)} %constant_dynamic-update-slice_fusion.8.refs_0_, ...), custom_call_target="tpu_custom_call" | custom-call | flops 2147483648 | bytes 1572864 | tf_op jit(solution)/shard_map/pallas_call | solution.py:213
  40.2 1.6 %collective-permute-start.7 = (bf16[64,2048]{1,0:T(8,128)(2,1)S(1)}, bf16[64,2048]{1,0:T(8,128)(2,1)S(1)}, u32[]{:S(2)}, u32[]{:S(2)}) collective-permute-start(bf16[64,2048]{1,0:T(8,128)(2,1)S(1)} %get-tuple-element.31), channel_id=1, source_target_pairs={{0,1},{1,0},{2,3},{3,2},{4,5},{5,4},{6,7},{7,6},{8,9},{9,8},{10,11... | collective-permute-start | bytes 786440 | tf_op jit(solution)/shard_map/ppermute | solution.py:350
  41.8 4.7 %shard_map.59 = (bf16[64,2048]{1,0:T(8,128)(2,1)S(1)}, bf16[64,2048]{1,0:T(8,128)(2,1)S(1)}) custom-call(s32[2]{0:T(128)S(1)} %copy-done.4, s32[2,16]{1,0:T(2,128)S(1)} %copy-done.3, bf16[128,4096]{1,0:T(8,128)(2,1)S(1)} %copy-done.2, bf16[512,1024]{1,0:T(8,128)(2,1)S(1)} %constant_dynamic-update-slice_fusion.8.refs_0_, ...), custom_call_target="tpu_custom_call" | custom-call | flops 2147483648 | bytes 1572864 | tf_op jit(solution)/shard_map/pallas_call | solution.py:213
  46.5 0.5 collective-permute-start.8
  47.0 1.9 %collective-permute-done.7.refs_2_ = bf16[64,2048]{1,0:T(8,128)(2,1)S(1)} collective-permute-done((bf16[64,2048]{1,0:T(8,128)(2,1)S(1)}, bf16[64,2048]{1,0:T(8,128)(2,1)S(1)}, u32[]{:S(2)}, u32[]{:S(2)}) %collective-permute-start.7) | collective-permute-done | bytes 262176 | tf_op jit(solution)/shard_map/ppermute | solution.py:350
  48.9 6.0 %collective-permute-done.8.refs_3_ = bf16[64,2048]{1,0:T(8,128)(2,1)S(1)} collective-permute-done((bf16[64,2048]{1,0:T(8,128)(2,1)S(1)}, bf16[64,2048]{1,0:T(8,128)(2,1)S(1)}, u32[]{:S(2)}, u32[]{:S(2)}) %collective-permute-start.8) | collective-permute-done | bytes 262176 | tf_op jit(solution)/shard_map/ppermute | solution.py:350
  55.0 1.0 %shard_map.60 = bf16[64,8192]{1,0:T(8,128)(2,1)} custom-call(bf16[64,2048]{1,0:T(8,128)(2,1)S(1)} %get-tuple-element.27.refs_0_, bf16[64,2048]{1,0:T(8,128)(2,1)S(1)} %get-tuple-element.30.refs_1_, bf16[64,2048]{1,0:T(8,128)(2,1)S(1)} %collective-permute-done.7.refs_2_, bf16[64,2048]{1,0:T(8,128)(2,1)S(1)} %collective-permute-done.8.refs_3_), custom_call_target="tpu_custom_call" | custom-call | tf_op jit(solution)/shard_map/pallas_call | solution.py:285
  (5 shorter events, 0.1 us)
Async XLA Ops:
  0.0 8.0 %collective-permute-start = (bf16[128,1024]{1,0:T(8,128)(2,1)}, bf16[128,1024]{1,0:T(8,128)(2,1)S(1)}, u32[]{:S(2)}, u32[]{:S(2)}) collective-permute-start(bf16[128,1024]{1,0:T(8,128)(2,1)} %span_ref.1), channel_id=1, source_target_pairs={{0,4},{2,10},{4,0},{6,14},{8,12},{10,2},{12,8},{14,6},{16,20},{18,... | collective-permute-start | bytes 786440 | tf_op jit(solution)/shard_map/ppermute | solution.py:26
  2.9 0.9 %copy-start = (bf16[2,64,1024]{2,1,0:T(8,128)(2,1)S(1)}, bf16[2,64,1024]{2,1,0:T(8,128)(2,1)}, u32[]{:S(2)}) copy-start(bf16[2,64,1024]{2,1,0:T(8,128)(2,1)} %cache_ref.1) | copy-start | bytes 786436
  3.9 0.9 %copy-start.1 = (bf16[128,1024]{1,0:T(8,128)(2,1)S(1)}, bf16[128,1024]{1,0:T(8,128)(2,1)}, u32[]{:S(2)}) copy-start(bf16[128,1024]{1,0:T(8,128)(2,1)} %span_ref.1) | copy-start | bytes 786436
  5.2 8.9 %collective-permute-start.1 = (bf16[64,1024]{1,0:T(8,128)(2,1)S(1)}, bf16[64,1024]{1,0:T(8,128)(2,1)S(1)}, u32[]{:S(2)}, u32[]{:S(2)}) collective-permute-start(bf16[64,1024]{1,0:T(8,128)(2,1)S(1)} %get-tuple-element.21), channel_id=1, source_target_pairs={{0,16},{2,18},{4,20},{6,22},{8,24},{10,26},{12,28},{14,30},{16,0},... | collective-permute-start | bytes 393224 | tf_op jit(solution)/shard_map/ppermute | solution.py:26
  7.9 16.8 %copy-start.2 = (bf16[128,4096]{1,0:T(8,128)(2,1)S(1)}, bf16[128,4096]{1,0:T(8,128)(2,1)}, u32[]{:S(2)}) copy-start(bf16[128,4096]{1,0:T(8,128)(2,1)} %q_ref.7) | copy-start | bytes 3145732
  7.9 16.8 %copy-start.3 = (s32[2,16]{1,0:T(2,128)S(1)}, s32[2,16]{1,0:T(2,128)}, u32[]{:S(2)}) copy-start(s32[2,16]{1,0:T(2,128)} %owner_ref.7) | copy-start | bytes 388
  7.9 16.8 %copy-start.4 = (s32[2]{0:T(128)S(1)}, s32[2]{0:T(128)}, u32[]{:S(2)}) copy-start(s32[2]{0:T(128)} %limit_ref.7) | copy-start | bytes 28
  8.0 13.9 %collective-permute-start.3 = (bf16[256,1024]{1,0:T(8,128)(2,1)S(1)}, bf16[256,1024]{1,0:T(8,128)(2,1)S(1)}, u32[]{:S(2)}, u32[]{:S(2)}) collective-permute-start(bf16[256,1024]{1,0:T(8,128)(2,1)S(1)} %get-tuple-element.36), channel_id=1, source_target_pairs={{0,8},{2,6},{4,12},{6,2},{8,0},{10,14},{12,4},{14,10},{16,24},{18,... | collective-permute-start | bytes 1572872 | tf_op jit(solution)/shard_map/ppermute | solution.py:26
  14.1 6.4 %collective-permute-start.2 = (bf16[128,1024]{1,0:T(8,128)(2,1)S(1)}, bf16[128,1024]{1,0:T(8,128)(2,1)S(1)}, u32[]{:S(2)}, u32[]{:S(2)}) collective-permute-start(bf16[128,1024]{1,0:T(8,128)(2,1)S(1)} %pad_maximum_fusion), channel_id=1, source_target_pairs={{0,4},{2,10},{4,0},{6,14},{8,12},{10,2},{12,8},{14,6},{16,20},{18,... | collective-permute-start | bytes 786440 | tf_op jit(solution)/shard_map/ppermute | solution.py:26
  22.0 2.7 %collective-permute-start.4 = (bf16[512,1024]{1,0:T(8,128)(2,1)S(1)}, bf16[512,1024]{1,0:T(8,128)(2,1)S(1)}, u32[]{:S(2)}, u32[]{:S(2)}) collective-permute-start(bf16[512,1024]{1,0:T(8,128)(2,1)S(1)} %constant_dynamic-update-slice_fusion.5.refs_0_), channel_id=1, source_target_pairs={{0,2},{2,0},{4,6},{6,4},{8,10},{10,8},{12,14},{14,12},{16,18},{18,... | collective-permute-start | bytes 3145736 | tf_op jit(solution)/shard_map/ppermute | solution.py:26
  22.2 9.2 %collective-permute-start.5 = (bf16[256,1024]{1,0:T(8,128)(2,1)S(1)}, bf16[256,1024]{1,0:T(8,128)(2,1)S(1)}, u32[]{:S(2)}, u32[]{:S(2)}) collective-permute-start(bf16[256,1024]{1,0:T(8,128)(2,1)S(1)} %get-tuple-element.33), channel_id=1, source_target_pairs={{0,8},{2,6},{4,12},{6,2},{8,0},{10,14},{12,4},{14,10},{16,24},{18,... | collective-permute-start | bytes 1572872 | tf_op jit(solution)/shard_map/ppermute | solution.py:26
  31.4 4.3 %collective-permute-start.6 = (bf16[512,1024]{1,0:T(8,128)(2,1)S(1)}, bf16[512,1024]{1,0:T(8,128)(2,1)S(1)}, u32[]{:S(2)}, u32[]{:S(2)}) collective-permute-start(bf16[512,1024]{1,0:T(8,128)(2,1)S(1)} %constant_dynamic-update-slice_fusion.8.refs_0_), channel_id=1, source_target_pairs={{0,2},{2,0},{4,6},{6,4},{8,10},{10,8},{12,14},{14,12},{16,18},{18,... | collective-permute-start | bytes 3145736 | tf_op jit(solution)/shard_map/ppermute | solution.py:26
  40.2 8.8 %collective-permute-start.7 = (bf16[64,2048]{1,0:T(8,128)(2,1)S(1)}, bf16[64,2048]{1,0:T(8,128)(2,1)S(1)}, u32[]{:S(2)}, u32[]{:S(2)}) collective-permute-start(bf16[64,2048]{1,0:T(8,128)(2,1)S(1)} %get-tuple-element.31), channel_id=1, source_target_pairs={{0,1},{1,0},{2,3},{3,2},{4,5},{5,4},{6,7},{7,6},{8,9},{9,8},{10,11... | collective-permute-start | bytes 786440 | tf_op jit(solution)/shard_map/ppermute | solution.py:350
  46.5 8.5 %collective-permute-start.8 = (bf16[64,2048]{1,0:T(8,128)(2,1)S(1)}, bf16[64,2048]{1,0:T(8,128)(2,1)S(1)}, u32[]{:S(2)}, u32[]{:S(2)}) collective-permute-start(bf16[64,2048]{1,0:T(8,128)(2,1)S(1)} %get-tuple-element.32), channel_id=1, source_target_pairs={{0,1},{1,0},{2,3},{3,2},{4,5},{5,4},{6,7},{7,6},{8,9},{9,8},{10,11... | collective-permute-start | bytes 786440 | tf_op jit(solution)/shard_map/ppermute | solution.py:350

commit v8 on v7

v8 whole, which is shorter than its diff:
```python
import functools
import math

import jax
import jax.numpy as jnp
from jax import lax
from jax.experimental import pallas as pl
from jax.experimental.pallas import tpu as pltpu
from jax.sharding import PartitionSpec as P

QH = 64
KVH = 8
HD = 128
REQS = 2
PER_GROUP = QH // KVH
EXP2_SCALE = HD ** (-0.5) * math.log2(math.e)
MASKED = -1e30
KEY_CHUNK = 512
EXTRA_ROWS = 16
SHIFT_STEP = 32.0
LOWEST_TOTAL = 1e-20
SPAN_ROWS, OWN_PAGE, CROSSED_PAGE = range(3)


def hop(value, bit_of_core):
    count = lax.axis_size("seq")
    return lax.ppermute(
        value, "seq", [(source, source ^ bit_of_core[source % 2]) for source in range(count)]
    )


def after(first, value):
    return lax.optimization_barrier((first, value))[1]


def shifted(layout, slots):
    return [(slot + slots, kind, rows) for slot, kind, rows in layout]


def hypercube_order(bits):
    order = [0]
    for bit in bits:
        order = order + [offset ^ bit for offset in order]
    return order


def attend_kernel(spec, layouts, part, block_heads, groups, limit_ref, owner_ref, q_ref, *refs):
    tokens, page, group_size, head_size, orders = spec
    first_phase = len(layouts) == 1
    key_sets, refs = [(refs[2 * at : 2 * at + 2], layout) for at, layout in enumerate(layouts)], refs[
        2 * len(layouts) :
    ]
    (state_sum, state_shift), refs = refs[:2], refs[2:]
    if first_phase:
        page_seen, keys, values = refs[:3]
        weights = refs[3:5]
    else:
        outs = refs[:2]
        page_seen, keys, values = refs[2:5]
        weights, shifts, slow_sum, slow_top = refs[5:7], refs[7:9], refs[9], refs[10]
    half_keys = key_sets[0][0][0].shape[0]
    total_keys = 2 * half_keys
    chunk = min(KEY_CHUNK, total_keys)
    me = lax.axis_index("seq")
    my_head = lax.axis_index("head")
    request = me // group_size
    offsets = [hypercube_order(order) for order in orders]

    def note_page(index, carry):
        page_seen[owner_ref[request, index]] = jnp.clip(limit_ref[request] - index * page, 0, page)
        return carry

    if not first_phase:
        lax.fori_loop(0, owner_ref.shape[1], note_page, 0)

    def fill(halves, layout):
        row = lax.broadcasted_iota(jnp.int32, (EXTRA_ROWS, half_keys), 0)
        key = lax.broadcasted_iota(jnp.int32, (EXTRA_ROWS, half_keys), 1)
        for half in range(2):
            holder = me ^ half
            start = 0
            seen = key < 0
            for slot, kind, rows in layout:
                source = holder ^ jnp.where(holder % 2 == 0, offsets[0][slot], offsets[1][slot])
                if kind == SPAN_ROWS:
                    count = jnp.where(source <= me, tokens, 0)
                elif kind == OWN_PAGE:
                    count = page_seen[source]
                else:
                    count = page_seen[source ^ group_size]
                seen = seen | ((key >= start) & (key < start + count))
                start += rows
            mask = jnp.where(seen, jnp.float32(0.0), jnp.float32(MASKED))
            extra = jnp.where(row == 0, mask, jnp.where(row == 1, jnp.float32(1.0), jnp.float32(0.0)))
            at = pl.ds(half * half_keys, half_keys)
            for group in range(groups):
                column = (part * groups + group) * 2 * HD
                keys[group, :HD, at] = halves[half][:, pl.ds(column, HD)].T
                keys[group, pl.ds(HD, EXTRA_ROWS), at] = extra.astype(jnp.bfloat16)
                values[group, at, :HD] = halves[half][:, pl.ds(column + HD, HD)]
        rest = HD - EXTRA_ROWS
        keys[:, HD + EXTRA_ROWS :, :] = jnp.zeros((groups, rest, total_keys), jnp.bfloat16)
        values[:, :, HD:] = jnp.ones((groups, total_keys, HD), jnp.bfloat16)

    block = block_heads * tokens
    blocks_a_group = PER_GROUP // block_heads
    blocks = groups * blocks_a_group
    lane = lax.broadcasted_iota(jnp.int32, (block, HD), 1)
    causal = lax.broadcasted_iota(jnp.int32, (block, tokens), 1) <= (
        lax.broadcasted_iota(jnp.int32, (block, tokens), 0) % tokens
    )

    def query_rows(index):
        first = (part * blocks + index) * block_heads * HD
        columns = [
            pl.ds(pl.multiple_of(first + head * HD, HD), HD) for head in range(block_heads)
        ]
        return jnp.concatenate([q_ref[:, column] for column in columns], axis=0)

    def scores_of(query, group, start, is_span):
        made = jnp.dot(
            query, keys[group, :, pl.ds(start, chunk)], preferred_element_type=jnp.float32
        )
        if start == 0 and is_span:
            own = jnp.where(causal, made[:, :tokens], MASKED)
            made = jnp.concatenate([own, made[:, tokens:]], axis=1)
        return made

    def give(index, result):
        kept = tokens // head_size
        for head in range(block_heads):
            column = pl.ds((index * block_heads + head) * HD, HD)
            one = result[head * tokens : (head + 1) * tokens]
            if head_size == 2:
                low, high = one[:kept], one[kept:]
                outs[0][:, column] = jnp.where(my_head == 0, low, high)
                outs[1][:, column] = jnp.where(my_head == 0, high, low)
            else:
                outs[0][:, column] = one[:kept]
                outs[1][:, column] = one[kept:]

    fill(*key_sets[-1])
    longest = []
    for group in range(groups):
        key = keys[group, :HD, :].astype(jnp.float32)
        longest.append(jnp.max(jnp.sum(key * key, axis=0, keepdims=True), axis=1, keepdims=True))

    def weigh(index):
        group = index // blocks_a_group
        query = query_rows(index)
        wide = query.astype(jnp.float32)
        bound = jnp.sqrt(jnp.sum(wide * wide, axis=1, keepdims=True) * longest[group])
        shift = jnp.ceil(bound * (1.0 / SHIFT_STEP)) * SHIFT_STEP
        extra = jnp.where(lane == 0, 1.0, jnp.where(lane == 1, -shift, 0.0))
        query = jnp.concatenate([query, extra.astype(jnp.bfloat16)], axis=1)
        shift = jnp.broadcast_to(shift, (block, HD))
        if first_phase:
            state_shift[pl.ds(index * block, block), :] = shift
        else:
            shifts[index % 2][...] = shift
        for start in range(0, total_keys, chunk):
            made = scores_of(query, group, start, first_phase)
            weights[index % 2][:, pl.ds(start, chunk)] = jnp.exp2(made * EXP2_SCALE).astype(
                jnp.bfloat16
            )

    def finish(index, lowest):
        group = index // blocks_a_group
        summed = jnp.dot(
            weights[index % 2][...], values[group], preferred_element_type=jnp.float32
        )
        rows = pl.ds(index * block, block)
        if first_phase:
            state_sum[rows, :] = summed
            return lowest
        before, shift = state_shift[rows, :], shifts[index % 2][...]
        both = jnp.maximum(before, shift)
        fade_before = jnp.exp2((before - both) * EXP2_SCALE)
        fade = jnp.exp2((shift - both) * EXP2_SCALE)
        total = state_sum[rows, HD:] * fade_before + summed[:, HD:] * fade
        result = (state_sum[rows, :HD] * fade_before + summed[:, :HD] * fade) / total
        give(index, result.astype(jnp.bfloat16))
        return jnp.minimum(lowest, total)

    lowest = jnp.ones((block, HD), jnp.float32)
    for index in range(blocks + 1):
        if index >= 1:
            lowest = finish(index - 1, lowest)
        if index < blocks:
            weigh(index)
    if first_phase:
        return

    @pl.when(jnp.min(lowest) < LOWEST_TOTAL)
    def exact():
        for number, (halves, layout) in enumerate(key_sets):
            fill(halves, layout)

            def one_block(index, carry):
                group = index // blocks_a_group
                extra = (lane == 0).astype(jnp.float32).astype(jnp.bfloat16)
                query = jnp.concatenate([query_rows(index), extra], axis=1)
                rows = pl.ds(pl.multiple_of(index * block, block), block)
                if number == 0:
                    top = jnp.full((block, HD), MASKED, jnp.float32)
                    summed = jnp.zeros((block, 2 * HD), jnp.float32)
                else:
                    top = slow_top[rows, :]
                    summed = slow_sum[rows, :]
                best = top
                for start in range(0, total_keys, chunk):
                    made = scores_of(query, group, start, number == 0)
                    for at in range(0, chunk, HD):
                        best = jnp.maximum(best, made[:, at : at + HD])
                best = jnp.broadcast_to(jnp.max(best, axis=1, keepdims=True), (block, HD))
                fade = jnp.exp2((top - best) * EXP2_SCALE)
                summed = summed * jnp.concatenate([fade, fade], axis=1)
                for start in range(0, total_keys, chunk):
                    made = scores_of(query, group, start, number == 0)
                    parts = [
                        jnp.exp2((made[:, at : at + HD] - best) * EXP2_SCALE)
                        for at in range(0, chunk, HD)
                    ]
                    summed = summed + jnp.dot(
                        jnp.concatenate(parts, axis=1).astype(jnp.bfloat16),
                        values[group, pl.ds(start, chunk), :],
                        preferred_element_type=jnp.float32,
                    )
                slow_top[rows, :] = best
                slow_sum[rows, :] = summed
                return carry

            lax.fori_loop(0, blocks, one_block, 0)
        for index in range(blocks):
            rows = pl.ds(index * block, block)
            give(index, (slow_sum[rows, :HD] / slow_sum[rows, HD:]).astype(jnp.bfloat16))


def attend(limits, owners, queries, part, parts, key_sets, spec, state):
    tokens, _, _, head_size = spec[:4]
    half_keys = key_sets[0][0].shape[0]
    total_keys = 2 * half_keys
    columns = queries.shape[1] // parts
    groups = columns // (PER_GROUP * HD)
    block_heads = 4
    block = block_heads * tokens
    rows = PER_GROUP * groups * tokens
    pieces = [piece for mine, theirs, _ in key_sets for piece in (mine, theirs)]
    layouts = tuple(tuple(layout) for _, _, layout in key_sets)
    operands = queries.size * 2 + sum(piece.size for piece in pieces) * 2 + rows * HD * 12
    scratch = groups * total_keys * HD * 8 + block * total_keys * 4 + rows * HD * 12
    whole = pl.BlockSpec(memory_space=pltpu.VMEM)
    scalars = pl.BlockSpec(memory_space=pltpu.SMEM)
    kept = tokens // head_size
    scratch_shapes = [
        pltpu.SMEM((owners.shape[1],), jnp.int32),
        pltpu.VMEM((groups, 2 * HD, total_keys), jnp.bfloat16),
        pltpu.VMEM((groups, total_keys, 2 * HD), jnp.bfloat16),
    ] + [pltpu.VMEM((block, total_keys), jnp.bfloat16)] * 2
    if state is None:
        state = ()
        out_shape = [
            jax.ShapeDtypeStruct((rows, 2 * HD), jnp.float32),
            jax.ShapeDtypeStruct((rows, HD), jnp.float32),
        ]
    else:
        out_shape = [
            jax.ShapeDtypeStruct((kept, columns), jnp.bfloat16),
            jax.ShapeDtypeStruct((tokens - kept, columns), jnp.bfloat16),
        ]
        scratch_shapes += [pltpu.VMEM((block, HD), jnp.float32)] * 2
        scratch_shapes += [
            pltpu.VMEM((rows, 2 * HD), jnp.float32),
            pltpu.VMEM((rows, HD), jnp.float32),
        ]
    return pl.pallas_call(
        functools.partial(attend_kernel, spec, layouts, part, block_heads, groups),
        out_shape=out_shape,
        in_specs=[scalars] * 2 + [whole] * (1 + len(pieces) + len(state)),
        out_specs=[whole] * 2,
        scratch_shapes=scratch_shapes,
        compiler_params=pltpu.CompilerParams(vmem_limit_bytes=operands + scratch + (6 << 20)),
        cost_estimate=pl.CostEstimate(
            flops=8 * tokens * columns * total_keys,
            bytes_accessed=4 * tokens * columns + 2 * total_keys * columns // PER_GROUP,
            transcendentals=0,
        ),
    )(limits, owners, queries, *pieces, *state)


def pick_kernel(group_size, cache_ref, span_ref, other_ref, own_ref, copied_ref, done):
    request = lax.axis_index("seq") // group_size
    copies = [
        pltpu.make_async_copy(cache_ref.at[1 - request], other_ref, done.at[0]),
        pltpu.make_async_copy(cache_ref.at[request], own_ref, done.at[1]),
        pltpu.make_async_copy(span_ref, copied_ref, done.at[2]),
    ]
    for copy in copies:
        copy.start()
    for copy in copies:
        copy.wait()


def pick(cache, span, group_size):
    return pl.pallas_call(
        functools.partial(pick_kernel, group_size),
        out_shape=[
            jax.ShapeDtypeStruct(cache.shape[1:], cache.dtype),
            jax.ShapeDtypeStruct(cache.shape[1:], cache.dtype),
            jax.ShapeDtypeStruct(span.shape, span.dtype),
        ],
        in_specs=[pl.BlockSpec(memory_space=pltpu.HBM)] * 2,
        out_specs=[pl.BlockSpec(memory_space=pltpu.VMEM)] * 3,
        scratch_shapes=[pltpu.SemaphoreType.DMA((3,))],
        compiler_params=pltpu.CompilerParams(vmem_limit_bytes=8 << 20),
    )(cache, span)


def join_kernel(pieces, *refs):
    parts, (out_ref, done) = refs[:pieces], refs[pieces:]
    columns = [ref.shape[1] for ref in parts[: pieces // 2]]
    side = out_ref.shape[1] // 2
    my_head = lax.axis_index("head")
    copies = []
    for at, ref in enumerate(parts):
        owner = my_head if at < pieces // 2 else 1 - my_head
        first = pl.multiple_of(owner * side + sum(columns[: at % (pieces // 2)]), HD)
        copies.append(
            pltpu.make_async_copy(ref, out_ref.at[:, pl.ds(first, ref.shape[1])], done.at[at])
        )
    for copy in copies:
        copy.start()
    for copy in copies:
        copy.wait()


def put_together(kept, received):
    pieces = len(kept) + len(received)
    rows = kept[0].shape[0]
    columns = sum(one.shape[1] for one in kept + received)
    return pl.pallas_call(
        functools.partial(join_kernel, pieces),
        out_shape=jax.ShapeDtypeStruct((rows, columns), kept[0].dtype),
        in_specs=[pl.BlockSpec(memory_space=pltpu.VMEM)] * pieces,
        out_specs=pl.BlockSpec(memory_space=pl.ANY),
        scratch_shapes=[pltpu.SemaphoreType.DMA((pieces,))],
        compiler_params=pltpu.CompilerParams(vmem_limit_bytes=8 << 20),
    )(*kept, *received)


def body(span_query, span_kv, prefix_cache, prefix_len, block_owner):
    seq_size = lax.axis_size("seq")
    head_size = lax.axis_size("head")
    group_size = seq_size // REQS
    tokens = span_kv.shape[0]
    page = prefix_cache.shape[1]
    groups = span_kv.shape[1] // (2 * HD)
    parts = 2 if groups % 2 == 0 else 1
    bits = [1 << at for at in range(1, group_size.bit_length() - 1)]
    orders = (bits, bits[::-1])

    def send(rows, stage):
        return hop(rows, tuple(order[stage] for order in orders))

    def grown(layout, stage):
        return layout + shifted(layout, 1 << stage)

    stages = len(bits)
    other_page, own_page, span = pick(prefix_cache, span_kv, group_size)
    crossed = hop(other_page, (group_size, group_size))
    span_layout = [(0, SPAN_ROWS, tokens)]
    for stage in range(stages):
        received = send(span if stage else span_kv, stage)
        if stage == 1:
            received = after(pages, received)
        span, span_layout = jnp.concatenate([span, received], axis=0), grown(span_layout, stage)
        if stage == 0:
            crossed = after(span, crossed)
            pages = jnp.concatenate([own_page, crossed], axis=0)
            pages = jnp.concatenate([pages, send(pages, 0)], axis=0)
    span_swapped = hop(span, (1, 1))

    spec = (tokens, page, group_size, head_size, orders)
    common = (prefix_len, block_owner, span_query)
    span_set = (span, span_swapped, span_layout)
    states = [attend(*common, part, parts, [span_set], spec, None) for part in range(parts)]

    page_layout = [(0, OWN_PAGE, page), (0, CROSSED_PAGE, page)]
    page_layout = grown(page_layout, 0)
    for stage in range(1, stages):
        received = send(pages, stage)
        if stage == stages - 1:
            received = after(states[0], received)
        pages, page_layout = jnp.concatenate([pages, received], axis=0), grown(page_layout, stage)
    pages_swapped = hop(pages, (1, 1))
    page_set = (pages, pages_swapped, page_layout)
    results = [
        attend(*common, part, parts, [span_set, page_set], spec, states[part])
        for part in range(parts)
    ]
    if head_size != 2:
        joined = jnp.concatenate([jnp.concatenate(pair, axis=0) for pair in results], axis=1)
        return lax.all_to_all(joined, "head", split_axis=0, concat_axis=1, tiled=True)
    kept = [pair[0] for pair in results]
    received = [lax.ppermute(pair[1], "head", [(0, 1), (1, 0)]) for pair in results]
    return put_together(kept, received)


def solution(mesh):
    placed = (P("seq", "head"), P("seq", "head"), P("seq", None, "head"), P(), P())
    return jax.shard_map(
        body, mesh=mesh, in_specs=placed, out_specs=P(("seq", "head"), None), check_vma=False
    )
```

time: 56.3 us -> 54.8 us (0.973)
  Pallas kernels: 18.9 us -> 16.4 us
  waiting for transfers between devices: 23.4 us -> 24.5 us
    pallas_call x4, Pallas kernels: 17.6 us -> 15.1 us  [attend(): pl.pallas_call(functools.partial(attend_kernel, spec, layouts, part, bloc...]
    ppermute x7, waiting for transfers between devices: 15.5 us -> 16.2 us  [hop(): lax.ppermute(value, 'seq', [(source, source ^ bit_of_core[source % 2]) fo...]
  transfers between devices with their start and end apart: 9 -> 9, of which waited for: 7 -> 7; matrix products, arithmetic and copies ran while one was open for 0% -> 0% of each run, Pallas kernels for 24% -> 21%
where the time goes in v8:
time: 54.8 us; the launch traced here: 54.6 us
  waiting for transfers between devices  24.5 us (45%)
  Pallas kernels  16.4 us (30%)
  starting transfers between devices  11.3 us (21%)
  local copies, waits for them, and re-layouts  2.19 us (4%)
    ppermute x7, waiting for transfers between devices, hop(): lax.ppermute(value, 'seq', [(source, source ^ bit_of_core[source % 2]) fo...  16.2 us
    pallas_call x4, Pallas kernels, attend(): pl.pallas_call(functools.partial(attend_kernel, spec, layouts, part, bloc...  15.1 us
    ppermute x7, starting transfers between devices, hop(): lax.ppermute(value, 'seq', [(source, source ^ bit_of_core[source % 2]) fo...  9.11 us
    ppermute x2, waiting for transfers between devices, body(): lax.ppermute(pair[1], 'head', [(0, 1), (1, 0)])  8.22 us
    ppermute x2, starting transfers between devices, body(): lax.ppermute(pair[1], 'head', [(0, 1), (1, 0)])  2.16 us
    unnamed x14, local copies, waits for them, and re-layouts  2.06 us
  transfers between devices with their start and end apart: 9, of which 7 were waited for; matrix products, arithmetic and copies ran while one was open for 0% of the time, Pallas kernels for 21%

profile of v8, /device:TPU:0, one launch (start us, length us, event | category | flops | bytes accessed | tf_op | source)
XLA Modules:
  0.0 54.6 jit_solution(10205904129624372448)
XLA Ops:
  0.0 2.9 %collective-permute-start = (bf16[128,1024]{1,0:T(8,128)(2,1)}, bf16[128,1024]{1,0:T(8,128)(2,1)S(1)}, u32[]{:S(2)}, u32[]{:S(2)}) collective-permute-start(bf16[128,1024]{1,0:T(8,128)(2,1)} %span_ref.1), channel_id=1, source_target_pairs={{0,4},{2,10},{4,0},{6,14},{8,12},{10,2},{12,8},{14,6},{16,20},{18,... | collective-permute-start | bytes 786440 | tf_op jit(solution)/shard_map/ppermute | solution.py:27
  2.9 0.0 copy-start.1
  2.9 0.9 %copy-done.1 = bf16[2,64,1024]{2,1,0:T(8,128)(2,1)S(1)} copy-done((bf16[2,64,1024]{2,1,0:T(8,128)(2,1)S(1)}, bf16[2,64,1024]{2,1,0:T(8,128)(2,1)}, u32[]{:S(2)}) %copy-start.1) | copy-done | bytes 262168
  3.9 0.0 copy-start.2
  3.9 0.9 %copy-done.2 = bf16[128,1024]{1,0:T(8,128)(2,1)S(1)} copy-done((bf16[128,1024]{1,0:T(8,128)(2,1)S(1)}, bf16[128,1024]{1,0:T(8,128)(2,1)}, u32[]{:S(2)}) %copy-start.2) | copy-done | bytes 262168
  4.8 0.4 shard_map.55
  5.2 2.7 %collective-permute-start.1 = (bf16[64,1024]{1,0:T(8,128)(2,1)S(1)}, bf16[64,1024]{1,0:T(8,128)(2,1)S(1)}, u32[]{:S(2)}, u32[]{:S(2)}) collective-permute-start(bf16[64,1024]{1,0:T(8,128)(2,1)S(1)} %get-tuple-element.21), channel_id=1, source_target_pairs={{0,16},{2,18},{4,20},{6,22},{8,24},{10,26},{12,28},{14,30},{16,0},... | collective-permute-start | bytes 393224 | tf_op jit(solution)/shard_map/ppermute | solution.py:27
  7.9 0.1 constant_dynamic-update-slice_fusion.1
  7.9 0.0 copy-start
  7.9 0.0 copy-start.3
  7.9 0.0 copy-start.4
  8.0 0.0 collective-permute-done
  8.0 0.1 constant_dynamic-update-slice_fusion
  8.0 1.7 %collective-permute-start.3 = (bf16[256,1024]{1,0:T(8,128)(2,1)S(1)}, bf16[256,1024]{1,0:T(8,128)(2,1)S(1)}, u32[]{:S(2)}, u32[]{:S(2)}) collective-permute-start(bf16[256,1024]{1,0:T(8,128)(2,1)S(1)} %get-tuple-element.35), channel_id=1, source_target_pairs={{0,8},{2,6},{4,12},{6,2},{8,0},{10,14},{12,4},{14,10},{16,24},{18,... | collective-permute-start | bytes 1572872 | tf_op jit(solution)/shard_map/ppermute | solution.py:27
  9.7 4.4 %collective-permute-done.1 = bf16[64,1024]{1,0:T(8,128)(2,1)S(1)} collective-permute-done((bf16[64,1024]{1,0:T(8,128)(2,1)S(1)}, bf16[64,1024]{1,0:T(8,128)(2,1)S(1)}, u32[]{:S(2)}, u32[]{:S(2)}) %collective-permute-start.1) | collective-permute-done | bytes 131104 | tf_op jit(solution)/shard_map/ppermute | solution.py:27
  14.1 1.6 %collective-permute-start.2 = (bf16[128,1024]{1,0:T(8,128)(2,1)S(1)}, bf16[128,1024]{1,0:T(8,128)(2,1)S(1)}, u32[]{:S(2)}, u32[]{:S(2)}) collective-permute-start(bf16[128,1024]{1,0:T(8,128)(2,1)S(1)} %pad_maximum_fusion), channel_id=1, source_target_pairs={{0,4},{2,10},{4,0},{6,14},{8,12},{10,2},{12,8},{14,6},{16,20},{18,... | collective-permute-start | bytes 786440 | tf_op jit(solution)/shard_map/ppermute | solution.py:27
  15.8 4.8 %collective-permute-done.2 = bf16[128,1024]{1,0:T(8,128)(2,1)S(1)} collective-permute-done((bf16[128,1024]{1,0:T(8,128)(2,1)S(1)}, bf16[128,1024]{1,0:T(8,128)(2,1)S(1)}, u32[]{:S(2)}, u32[]{:S(2)}) %collective-permute-start.2) | collective-permute-done | bytes 262176 | tf_op jit(solution)/shard_map/ppermute | solution.py:27
  20.6 0.1 constant_dynamic-update-slice_fusion.9
  20.6 1.3 %collective-permute-done.3 = bf16[256,1024]{1,0:T(8,128)(2,1)S(1)} collective-permute-done((bf16[256,1024]{1,0:T(8,128)(2,1)S(1)}, bf16[256,1024]{1,0:T(8,128)(2,1)S(1)}, u32[]{:S(2)}, u32[]{:S(2)}) %collective-permute-start.3) | collective-permute-done | bytes 524320 | tf_op jit(solution)/shard_map/ppermute | solution.py:27
  22.0 0.2 collective-permute-start.4
  22.2 0.0 collective-permute-start.5
  22.2 2.5 %collective-permute-done.4.refs_1_ = bf16[512,1024]{1,0:T(8,128)(2,1)S(1)} collective-permute-done((bf16[512,1024]{1,0:T(8,128)(2,1)S(1)}, bf16[512,1024]{1,0:T(8,128)(2,1)S(1)}, u32[]{:S(2)}, u32[]{:S(2)}) %collective-permute-start.4) | collective-permute-done | bytes 1048608 | tf_op jit(solution)/shard_map/ppermute | solution.py:27
  24.7 0.0 copy-done
  24.7 0.0 copy-done.3
  24.7 0.0 copy-done.4
  24.7 3.4 %shard_map.56 = (f32[2048,256]{1,0:T(8,128)S(1)}, f32[2048,128]{1,0:T(8,128)S(1)}) custom-call(s32[2]{0:T(128)S(1)} %copy-done.4, s32[2,16]{1,0:T(2,128)S(1)} %copy-done.3, bf16[128,4096]{1,0:T(8,128)(2,1)S(1)} %copy-done, bf16[512,1024]{1,0:T(8,128)(2,1)S(1)} %constant_dynamic-update-slice_fusion.5.refs_0_, bf16[512,1024]{1,0:T(8,128)(2,1)S(1)} %collective-permute-done.4.refs_1_), custom_call_target="tpu_custom_call" | custom-call | flops 2147483648 | bytes 1572864 | tf_op jit(solution)/shard_map/pallas_call | solution.py:276
  28.2 3.2 %collective-permute-done.5 = bf16[256,1024]{1,0:T(8,128)(2,1)S(1)} collective-permute-done((bf16[256,1024]{1,0:T(8,128)(2,1)S(1)}, bf16[256,1024]{1,0:T(8,128)(2,1)S(1)}, u32[]{:S(2)}, u32[]{:S(2)}) %collective-permute-start.5) | collective-permute-done | bytes 524320 | tf_op jit(solution)/shard_map/ppermute | solution.py:27
  31.4 0.1 collective-permute-start.6
  31.5 3.4 %shard_map.58 = (f32[2048,256]{1,0:T(8,128)S(1)}, f32[2048,128]{1,0:T(8,128)S(1)}) custom-call(s32[2]{0:T(128)S(1)} %copy-done.4, s32[2,16]{1,0:T(2,128)S(1)} %copy-done.3, bf16[128,4096]{1,0:T(8,128)(2,1)S(1)} %copy-done, bf16[512,1024]{1,0:T(8,128)(2,1)S(1)} %constant_dynamic-update-slice_fusion.5.refs_0_, bf16[512,1024]{1,0:T(8,128)(2,1)S(1)} %collective-permute-done.4.refs_1_), custom_call_target="tpu_custom_call" | custom-call | flops 2147483648 | bytes 1572864 | tf_op jit(solution)/shard_map/pallas_call | solution.py:276
  34.9 0.0 collective-permute-done.6.refs_3_
  34.9 4.2 %shard_map.57 = (bf16[64,2048]{1,0:T(8,128)(2,1)S(1)}, bf16[64,2048]{1,0:T(8,128)(2,1)S(1)}) custom-call(s32[2]{0:T(128)S(1)} %copy-done.4, s32[2,16]{1,0:T(2,128)S(1)} %copy-done.3, bf16[128,4096]{1,0:T(8,128)(2,1)S(1)} %copy-done, bf16[512,1024]{1,0:T(8,128)(2,1)S(1)} %constant_dynamic-update-slice_fusion.5.refs_0_, ...), custom_call_target="tpu_custom_call" | custom-call | flops 2147483648 | bytes 1572864 | tf_op jit(solution)/shard_map/pallas_call | solution.py:276
  39.1 1.6 %collective-permute-start.7 = (bf16[64,2048]{1,0:T(8,128)(2,1)S(1)}, bf16[64,2048]{1,0:T(8,128)(2,1)S(1)}, u32[]{:S(2)}, u32[]{:S(2)}) collective-permute-start(bf16[64,2048]{1,0:T(8,128)(2,1)S(1)} %get-tuple-element.31), channel_id=1, source_target_pairs={{0,1},{1,0},{2,3},{3,2},{4,5},{5,4},{6,7},{7,6},{8,9},{9,8},{10,11... | collective-permute-start | bytes 786440 | tf_op jit(solution)/shard_map/ppermute | solution.py:405
  40.7 4.0 %shard_map.59 = (bf16[64,2048]{1,0:T(8,128)(2,1)S(1)}, bf16[64,2048]{1,0:T(8,128)(2,1)S(1)}) custom-call(s32[2]{0:T(128)S(1)} %copy-done.4, s32[2,16]{1,0:T(2,128)S(1)} %copy-done.3, bf16[128,4096]{1,0:T(8,128)(2,1)S(1)} %copy-done, bf16[512,1024]{1,0:T(8,128)(2,1)S(1)} %constant_dynamic-update-slice_fusion.5.refs_0_, ...), custom_call_target="tpu_custom_call" | custom-call | flops 2147483648 | bytes 1572864 | tf_op jit(solution)/shard_map/pallas_call | solution.py:276
  44.7 0.5 collective-permute-start.8
  45.3 2.8 %collective-permute-done.7.refs_2_ = bf16[64,2048]{1,0:T(8,128)(2,1)S(1)} collective-permute-done((bf16[64,2048]{1,0:T(8,128)(2,1)S(1)}, bf16[64,2048]{1,0:T(8,128)(2,1)S(1)}, u32[]{:S(2)}, u32[]{:S(2)}) %collective-permute-start.7) | collective-permute-done | bytes 262176 | tf_op jit(solution)/shard_map/ppermute | solution.py:405
  48.1 5.4 %collective-permute-done.8.refs_3_ = bf16[64,2048]{1,0:T(8,128)(2,1)S(1)} collective-permute-done((bf16[64,2048]{1,0:T(8,128)(2,1)S(1)}, bf16[64,2048]{1,0:T(8,128)(2,1)S(1)}, u32[]{:S(2)}, u32[]{:S(2)}) %collective-permute-start.8) | collective-permute-done | bytes 262176 | tf_op jit(solution)/shard_map/ppermute | solution.py:405
  53.5 1.0 %shard_map.60 = bf16[64,8192]{1,0:T(8,128)(2,1)} custom-call(bf16[64,2048]{1,0:T(8,128)(2,1)S(1)} %get-tuple-element.27.refs_0_, bf16[64,2048]{1,0:T(8,128)(2,1)S(1)} %get-tuple-element.30.refs_1_, bf16[64,2048]{1,0:T(8,128)(2,1)S(1)} %collective-permute-done.7.refs_2_, bf16[64,2048]{1,0:T(8,128)(2,1)S(1)} %collective-permute-done.8.refs_3_), custom_call_target="tpu_custom_call" | custom-call | tf_op jit(solution)/shard_map/pallas_call | solution.py:341
  (5 shorter events, 0.1 us)
Async XLA Ops:
  0.0 8.0 %collective-permute-start = (bf16[128,1024]{1,0:T(8,128)(2,1)}, bf16[128,1024]{1,0:T(8,128)(2,1)S(1)}, u32[]{:S(2)}, u32[]{:S(2)}) collective-permute-start(bf16[128,1024]{1,0:T(8,128)(2,1)} %span_ref.1), channel_id=1, source_target_pairs={{0,4},{2,10},{4,0},{6,14},{8,12},{10,2},{12,8},{14,6},{16,20},{18,... | collective-permute-start | bytes 786440 | tf_op jit(solution)/shard_map/ppermute | solution.py:27
  2.9 0.9 %copy-start.1 = (bf16[2,64,1024]{2,1,0:T(8,128)(2,1)S(1)}, bf16[2,64,1024]{2,1,0:T(8,128)(2,1)}, u32[]{:S(2)}) copy-start(bf16[2,64,1024]{2,1,0:T(8,128)(2,1)} %cache_ref.1) | copy-start | bytes 786436
  3.9 0.9 %copy-start.2 = (bf16[128,1024]{1,0:T(8,128)(2,1)S(1)}, bf16[128,1024]{1,0:T(8,128)(2,1)}, u32[]{:S(2)}) copy-start(bf16[128,1024]{1,0:T(8,128)(2,1)} %span_ref.1) | copy-start | bytes 786436
  5.2 8.9 %collective-permute-start.1 = (bf16[64,1024]{1,0:T(8,128)(2,1)S(1)}, bf16[64,1024]{1,0:T(8,128)(2,1)S(1)}, u32[]{:S(2)}, u32[]{:S(2)}) collective-permute-start(bf16[64,1024]{1,0:T(8,128)(2,1)S(1)} %get-tuple-element.21), channel_id=1, source_target_pairs={{0,16},{2,18},{4,20},{6,22},{8,24},{10,26},{12,28},{14,30},{16,0},... | collective-permute-start | bytes 393224 | tf_op jit(solution)/shard_map/ppermute | solution.py:27
  7.9 16.8 %copy-start = (bf16[128,4096]{1,0:T(8,128)(2,1)S(1)}, bf16[128,4096]{1,0:T(8,128)(2,1)}, u32[]{:S(2)}) copy-start(bf16[128,4096]{1,0:T(8,128)(2,1)} %q_ref.7) | copy-start | bytes 3145732
  7.9 16.8 %copy-start.3 = (s32[2,16]{1,0:T(2,128)S(1)}, s32[2,16]{1,0:T(2,128)}, u32[]{:S(2)}) copy-start(s32[2,16]{1,0:T(2,128)} %owner_ref.7) | copy-start | bytes 388
  7.9 16.8 %copy-start.4 = (s32[2]{0:T(128)S(1)}, s32[2]{0:T(128)}, u32[]{:S(2)}) copy-start(s32[2]{0:T(128)} %limit_ref.7) | copy-start | bytes 28
  8.0 13.9 %collective-permute-start.3 = (bf16[256,1024]{1,0:T(8,128)(2,1)S(1)}, bf16[256,1024]{1,0:T(8,128)(2,1)S(1)}, u32[]{:S(2)}, u32[]{:S(2)}) collective-permute-start(bf16[256,1024]{1,0:T(8,128)(2,1)S(1)} %get-tuple-element.35), channel_id=1, source_target_pairs={{0,8},{2,6},{4,12},{6,2},{8,0},{10,14},{12,4},{14,10},{16,24},{18,... | collective-permute-start | bytes 1572872 | tf_op jit(solution)/shard_map/ppermute | solution.py:27
  14.1 6.4 %collective-permute-start.2 = (bf16[128,1024]{1,0:T(8,128)(2,1)S(1)}, bf16[128,1024]{1,0:T(8,128)(2,1)S(1)}, u32[]{:S(2)}, u32[]{:S(2)}) collective-permute-start(bf16[128,1024]{1,0:T(8,128)(2,1)S(1)} %pad_maximum_fusion), channel_id=1, source_target_pairs={{0,4},{2,10},{4,0},{6,14},{8,12},{10,2},{12,8},{14,6},{16,20},{18,... | collective-permute-start | bytes 786440 | tf_op jit(solution)/shard_map/ppermute | solution.py:27
  22.0 2.7 %collective-permute-start.4 = (bf16[512,1024]{1,0:T(8,128)(2,1)S(1)}, bf16[512,1024]{1,0:T(8,128)(2,1)S(1)}, u32[]{:S(2)}, u32[]{:S(2)}) collective-permute-start(bf16[512,1024]{1,0:T(8,128)(2,1)S(1)} %constant_dynamic-update-slice_fusion.5.refs_0_), channel_id=1, source_target_pairs={{0,2},{2,0},{4,6},{6,4},{8,10},{10,8},{12,14},{14,12},{16,18},{18,... | collective-permute-start | bytes 3145736 | tf_op jit(solution)/shard_map/ppermute | solution.py:27
  22.2 9.2 %collective-permute-start.5 = (bf16[256,1024]{1,0:T(8,128)(2,1)S(1)}, bf16[256,1024]{1,0:T(8,128)(2,1)S(1)}, u32[]{:S(2)}, u32[]{:S(2)}) collective-permute-start(bf16[256,1024]{1,0:T(8,128)(2,1)S(1)} %get-tuple-element.34), channel_id=1, source_target_pairs={{0,8},{2,6},{4,12},{6,2},{8,0},{10,14},{12,4},{14,10},{16,24},{18,... | collective-permute-start | bytes 1572872 | tf_op jit(solution)/shard_map/ppermute | solution.py:27
  31.4 3.5 %collective-permute-start.6 = (bf16[512,1024]{1,0:T(8,128)(2,1)S(1)}, bf16[512,1024]{1,0:T(8,128)(2,1)S(1)}, u32[]{:S(2)}, u32[]{:S(2)}) collective-permute-start(bf16[512,1024]{1,0:T(8,128)(2,1)S(1)} %constant_dynamic-update-slice_fusion.8.refs_2_), channel_id=1, source_target_pairs={{0,2},{2,0},{4,6},{6,4},{8,10},{10,8},{12,14},{14,12},{16,18},{18,... | collective-permute-start | bytes 3145736 | tf_op jit(solution)/shard_map/ppermute | solution.py:27
  39.1 9.0 %collective-permute-start.7 = (bf16[64,2048]{1,0:T(8,128)(2,1)S(1)}, bf16[64,2048]{1,0:T(8,128)(2,1)S(1)}, u32[]{:S(2)}, u32[]{:S(2)}) collective-permute-start(bf16[64,2048]{1,0:T(8,128)(2,1)S(1)} %get-tuple-element.31), channel_id=1, source_target_pairs={{0,1},{1,0},{2,3},{3,2},{4,5},{5,4},{6,7},{7,6},{8,9},{9,8},{10,11... | collective-permute-start | bytes 786440 | tf_op jit(solution)/shard_map/ppermute | solution.py:405
  44.7 8.8 %collective-permute-start.8 = (bf16[64,2048]{1,0:T(8,128)(2,1)S(1)}, bf16[64,2048]{1,0:T(8,128)(2,1)S(1)}, u32[]{:S(2)}, u32[]{:S(2)}) collective-permute-start(bf16[64,2048]{1,0:T(8,128)(2,1)S(1)} %get-tuple-element.32), channel_id=1, source_target_pairs={{0,1},{1,0},{2,3},{3,2},{4,5},{5,4},{6,7},{7,6},{8,9},{9,8},{10,11... | collective-permute-start | bytes 786440 | tf_op jit(solution)/shard_map/ppermute | solution.py:405

commit v9 on v8

--- a/solution.py
+++ b/solution.py
@@ -73,34 +73,36 @@
     if not first_phase:
         lax.fori_loop(0, owner_ref.shape[1], note_page, 0)
 
-    def fill(halves, layout):
+    def extra_rows(layout, half):
         row = lax.broadcasted_iota(jnp.int32, (EXTRA_ROWS, half_keys), 0)
         key = lax.broadcasted_iota(jnp.int32, (EXTRA_ROWS, half_keys), 1)
+        holder = me ^ half
+        start = 0
+        seen = key < 0
+        for slot, kind, rows in layout:
+            source = holder ^ jnp.where(holder % 2 == 0, offsets[0][slot], offsets[1][slot])
+            if kind == SPAN_ROWS:
+                count = jnp.where(source <= me, tokens, 0)
+            elif kind == OWN_PAGE:
+                count = page_seen[source]
+            else:
+                count = page_seen[source ^ group_size]
+            seen = seen | ((key >= start) & (key < start + count))
+            start += rows
+        mask = jnp.where(seen, jnp.float32(0.0), jnp.float32(MASKED))
+        extra = jnp.where(row == 0, mask, jnp.where(row == 1, jnp.float32(1.0), jnp.float32(0.0)))
+        return extra.astype(jnp.bfloat16)
+
+    def fill(group, halves, extras):
         for half in range(2):
-            holder = me ^ half
-            start = 0
-            seen = key < 0
-            for slot, kind, rows in layout:
-                source = holder ^ jnp.where(holder % 2 == 0, offsets[0][slot], offsets[1][slot])
-                if kind == SPAN_ROWS:
-                    count = jnp.where(source <= me, tokens, 0)
-                elif kind == OWN_PAGE:
-                    count = page_seen[source]
-                else:
-                    count = page_seen[source ^ group_size]
-                seen = seen | ((key >= start) & (key < start + count))
-                start += rows
-            mask = jnp.where(seen, jnp.float32(0.0), jnp.float32(MASKED))
-            extra = jnp.where(row == 0, mask, jnp.where(row == 1, jnp.float32(1.0), jnp.float32(0.0)))
+            column = (part * groups + group) * 2 * HD
             at = pl.ds(half * half_keys, half_keys)
-            for group in range(groups):
-                column = (part * groups + group) * 2 * HD
-                keys[group, :HD, at] = halves[half][:, pl.ds(column, HD)].T
-                keys[group, pl.ds(HD, EXTRA_ROWS), at] = extra.astype(jnp.bfloat16)
-                values[group, at, :HD] = halves[half][:, pl.ds(column + HD, HD)]
+            keys[group, :HD, at] = halves[half][:, pl.ds(column, HD)].T
+            keys[group, pl.ds(HD, EXTRA_ROWS), at] = extras[half]
+            values[group, at, :HD] = halves[half][:, pl.ds(column + HD, HD)]
         rest = HD - EXTRA_ROWS
-        keys[:, HD + EXTRA_ROWS :, :] = jnp.zeros((groups, rest, total_keys), jnp.bfloat16)
-        values[:, :, HD:] = jnp.ones((groups, total_keys, HD), jnp.bfloat16)
+        keys[group, HD + EXTRA_ROWS :, :] = jnp.zeros((rest, total_keys), jnp.bfloat16)
+        values[group, :, HD:] = jnp.ones((total_keys, HD), jnp.bfloat16)
 
     block = block_heads * tokens
     blocks_a_group = PER_GROUP // block_heads
@@ -139,11 +141,15 @@
                 outs[0][:, column] = one[:kept]
                 outs[1][:, column] = one[kept:]
 
-    fill(*key_sets[-1])
-    longest = []
-    for group in range(groups):
+    halves, layout = key_sets[-1]
+    extras = [extra_rows(layout, half) for half in range(2)]
+    longest = [None] * groups
+
+    def begin(group):
+        fill(group, halves, extras)
         key = keys[group, :HD, :].astype(jnp.float32)
-        longest.append(jnp.max(jnp.sum(key * key, axis=0, keepdims=True), axis=1, keepdims=True))
+        squares = jnp.sum(key * key, axis=0, keepdims=True)
+        longest[group] = jnp.max(squares, axis=1, keepdims=True)
 
     def weigh(index):
         group = index // blocks_a_group
@@ -173,28 +179,34 @@
         if first_phase:
             state_sum[rows, :] = summed
             return lowest
-        before, shift = state_shift[rows, :], shifts[index % 2][...]
+        old = pl.ds((part * blocks + index) * block, block)
+        before, shift = state_shift[old, :], shifts[index % 2][...]
         both = jnp.maximum(before, shift)
         fade_before = jnp.exp2((before - both) * EXP2_SCALE)
         fade = jnp.exp2((shift - both) * EXP2_SCALE)
-        total = state_sum[rows, HD:] * fade_before + summed[:, HD:] * fade
-        result = (state_sum[rows, :HD] * fade_before + summed[:, :HD] * fade) / total
+        total = state_sum[old, HD:] * fade_before + summed[:, HD:] * fade
+        result = (state_sum[old, :HD] * fade_before + summed[:, :HD] * fade) / total
         give(index, result.astype(jnp.bfloat16))
         return jnp.minimum(lowest, total)
 
+    begin(0)
     lowest = jnp.ones((block, HD), jnp.float32)
     for index in range(blocks + 1):
         if index >= 1:
             lowest = finish(index - 1, lowest)
         if index < blocks:
             weigh(index)
+            if (index + 1) % blocks_a_group == 0 and index + 1 < blocks:
+                begin((index + 1) // blocks_a_group)
     if first_phase:
         return
 
     @pl.when(jnp.min(lowest) < LOWEST_TOTAL)
     def exact():
         for number, (halves, layout) in enumerate(key_sets):
-            fill(halves, layout)
+            extras = [extra_rows(layout, half) for half in range(2)]
+            for group in range(groups):
+                fill(group, halves, extras)
 
             def one_block(index, carry):
                 group = index // blocks_a_group
@@ -288,32 +300,21 @@
     )(limits, owners, queries, *pieces, *state)
 
 
-def pick_kernel(group_size, cache_ref, span_ref, other_ref, own_ref, copied_ref, done):
+def pick_kernel(group_size, cache_ref, other_ref, own_ref):
     request = lax.axis_index("seq") // group_size
-    copies = [
-        pltpu.make_async_copy(cache_ref.at[1 - request], other_ref, done.at[0]),
-        pltpu.make_async_copy(cache_ref.at[request], own_ref, done.at[1]),
-        pltpu.make_async_copy(span_ref, copied_ref, done.at[2]),
-    ]
-    for copy in copies:
-        copy.start()
-    for copy in copies:
-        copy.wait()
-
-
-def pick(cache, span, group_size):
+    other_ref[...] = cache_ref[1 - request]
+    own_ref[...] = cache_ref[request]
+
+
+def pick(cache, group_size):
+    whole = pl.BlockSpec(memory_space=pltpu.VMEM)
     return pl.pallas_call(
         functools.partial(pick_kernel, group_size),
-        out_shape=[
-            jax.ShapeDtypeStruct(cache.shape[1:], cache.dtype),
-            jax.ShapeDtypeStruct(cache.shape[1:], cache.dtype),
-            jax.ShapeDtypeStruct(span.shape, span.dtype),
-        ],
-        in_specs=[pl.BlockSpec(memory_space=pltpu.HBM)] * 2,
-        out_specs=[pl.BlockSpec(memory_space=pltpu.VMEM)] * 3,
-        scratch_shapes=[pltpu.SemaphoreType.DMA((3,))],
+        out_shape=[jax.ShapeDtypeStruct(cache.shape[1:], cache.dtype)] * 2,
+        in_specs=[whole],
+        out_specs=[whole] * 2,
         compiler_params=pltpu.CompilerParams(vmem_limit_bytes=8 << 20),
-    )(cache, span)
+    )(cache)
 
 
 def join_kernel(pieces, *refs):
@@ -359,48 +360,53 @@
     bits = [1 << at for at in range(1, group_size.bit_length() - 1)]
     orders = (bits, bits[::-1])
 
+    stages = len(bits)
+
     def send(rows, stage):
         return hop(rows, tuple(order[stage] for order in orders))
 
-    def grown(layout, stage):
-        return layout + shifted(layout, 1 << stage)
-
-    stages = len(bits)
-    other_page, own_page, span = pick(prefix_cache, span_kv, group_size)
+    def whole_layout(layout):
+        for stage in range(stages):
+            layout = layout + shifted(layout, 1 << stage)
+        return layout
+
+    span_layout = whole_layout([(0, SPAN_ROWS, tokens)])
+    page_layout = whole_layout([(0, OWN_PAGE, page), (0, CROSSED_PAGE, page)])
+
+    other_page, own_page = pick(prefix_cache, group_size)
     crossed = hop(other_page, (group_size, group_size))
-    span_layout = [(0, SPAN_ROWS, tokens)]
-    for stage in range(stages):
-        received = send(span if stage else span_kv, stage)
-        if stage == 1:
-            received = after(pages, received)
-        span, span_layout = jnp.concatenate([span, received], axis=0), grown(span_layout, stage)
-        if stage == 0:
-            crossed = after(span, crossed)
-            pages = jnp.concatenate([own_page, crossed], axis=0)
-            pages = jnp.concatenate([pages, send(pages, 0)], axis=0)
+
+    span_early = send(span_kv, stages - 1)
+    span_forward = send(span_kv, 0)
+    for stage in range(1, stages - 1):
+        seen = jnp.concatenate([span_kv, span_forward], axis=0)
+        span_forward = jnp.concatenate([span_forward, send(seen, stage)], axis=0)
+    span = jnp.concatenate([span_kv, span_forward], axis=0)
+    span_late = send(span_forward, stages - 1)
+    crossed = after(span, crossed)
+    pages = jnp.concatenate([own_page, crossed], axis=0)
+    pages = jnp.concatenate([pages, send(pages, 0)], axis=0)
+    span_late = after(pages, span_late)
+    span = jnp.concatenate([span, span_early, span_late], axis=0)
     span_swapped = hop(span, (1, 1))
 
     spec = (tokens, page, group_size, head_size, orders)
     common = (prefix_len, block_owner, span_query)
     span_set = (span, span_swapped, span_layout)
-    states = [attend(*common, part, parts, [span_set], spec, None) for part in range(parts)]
-
-    page_layout = [(0, OWN_PAGE, page), (0, CROSSED_PAGE, page)]
-    page_layout = grown(page_layout, 0)
+    state = attend(*common, 0, 1, [span_set], spec, None)
+
     for stage in range(1, stages):
         received = send(pages, stage)
         if stage == stages - 1:
-            received = after(states[0], received)
-        pages, page_layout = jnp.concatenate([pages, received], axis=0), grown(page_layout, stage)
-    pages_swapped = hop(pages, (1, 1))
-    page_set = (pages, pages_swapped, page_layout)
+            received = after(state, received)
+        pages = jnp.concatenate([pages, received], axis=0)
+    page_set = (pages, hop(pages, (1, 1)), page_layout)
     results = [
-        attend(*common, part, parts, [span_set, page_set], spec, states[part])
-        for part in range(parts)
+        attend(*common, part, parts, [span_set, page_set], spec, state) for part in range(parts)
     ]
     if head_size != 2:
-        joined = jnp.concatenate([jnp.concatenate(pair, axis=0) for pair in results], axis=1)
-        return lax.all_to_all(joined, "head", split_axis=0, concat_axis=1, tiled=True)
+        rows = jnp.concatenate([jnp.concatenate(pair, axis=0) for pair in results], axis=1)
+        return lax.all_to_all(rows, "head", split_axis=0, concat_axis=1, tiled=True)
     kept = [pair[0] for pair in results]
     received = [lax.ppermute(pair[1], "head", [(0, 1), (1, 0)]) for pair in results]
     return put_together(kept, received)

time: 54.8 us -> 52.5 us (0.958)
  waiting for transfers between devices: 24.5 us -> 22.5 us
  Pallas kernels: 16.4 us -> 15.1 us
  starting transfers between devices: 11.3 us -> 12.4 us
    ppermute x7 -> x8, waiting for transfers between devices: 16.2 us -> 14.6 us  [hop(): lax.ppermute(value, 'seq', [(source, source ^ bit_of_core[source % 2]) fo...]
    ppermute x7 -> x8, starting transfers between devices: 9.11 us -> 10.3 us  [hop(): lax.ppermute(value, 'seq', [(source, source ^ bit_of_core[source % 2]) fo...]
    pallas_call x4 -> x3, Pallas kernels: 15.1 us -> 14.1 us  [attend(): pl.pallas_call(functools.partial(attend_kernel, spec, layouts, part, bloc...]
    unnamed x14 -> x11, local copies, waits for them, and re-layouts: 2.06 us -> 2.05 us
  transfers between devices with their start and end apart: 9 -> 10, of which waited for: 7 -> 10; matrix products, arithmetic and copies ran while one was open for 0% -> 2% of each run, Pallas kernels for 21% -> 19%
where the time goes in v9:
time: 52.5 us; the launch traced here: 52.4 us
  waiting for transfers between devices  22.5 us (43%)
  Pallas kernels  15.1 us (29%)
  starting transfers between devices  12.4 us (24%)
  local copies, waits for them, and re-layouts  2.07 us (4%)
    ppermute x8, waiting for transfers between devices, hop(): lax.ppermute(value, 'seq', [(source, source ^ bit_of_core[source % 2]) fo...  14.6 us
    pallas_call x3, Pallas kernels, attend(): pl.pallas_call(functools.partial(attend_kernel, spec, layouts, part, bloc...  14.1 us
    ppermute x8, starting transfers between devices, hop(): lax.ppermute(value, 'seq', [(source, source ^ bit_of_core[source % 2]) fo...  10.3 us
    ppermute x2, waiting for transfers between devices, body(): lax.ppermute(pair[1], 'head', [(0, 1), (1, 0)])  7.87 us
    ppermute x2, starting transfers between devices, body(): lax.ppermute(pair[1], 'head', [(0, 1), (1, 0)])  2.16 us
    unnamed x11, local copies, waits for them, and re-layouts  2.05 us
  transfers between devices with their start and end apart: 10, of which 10 were waited for; matrix products, arithmetic and copies ran while one was open for 2% of the time, Pallas kernels for 19%

profile of v9, /device:TPU:0, one launch (start us, length us, event | category | flops | bytes accessed | tf_op | source)
XLA Modules:
  0.0 52.4 jit_solution(657800931957678115)
XLA Ops:
  0.0 0.0 copy-start
  0.0 0.0 copy-start.1
  0.0 1.0 %copy-done.1 = bf16[2,64,1024]{2,1,0:T(8,128)(2,1)S(1)} copy-done((bf16[2,64,1024]{2,1,0:T(8,128)(2,1)S(1)}, bf16[2,64,1024]{2,1,0:T(8,128)(2,1)}, u32[]{:S(2)}) %copy-start.1) | copy-done | bytes 262168
  1.0 0.0 copy-start.2
  1.0 0.0 copy-start.3
  1.1 4.1 %collective-permute-start.2 = (bf16[64,1024]{1,0:T(8,128)(2,1)S(1)}, bf16[64,1024]{1,0:T(8,128)(2,1)S(1)}, u32[]{:S(2)}, u32[]{:S(2)}) collective-permute-start(bf16[64,1024]{1,0:T(8,128)(2,1)S(1)} %get-tuple-element.16), channel_id=1, source_target_pairs={{0,16},{2,18},{4,20},{6,22},{8,24},{10,26},{12,28},{14,30},{16,0},... | collective-permute-start | bytes 393224 | tf_op jit(solution)/shard_map/ppermute | solution.py:27
  5.2 1.5 %collective-permute-start = (bf16[128,1024]{1,0:T(8,128)(2,1)}, bf16[128,1024]{1,0:T(8,128)(2,1)S(1)}, u32[]{:S(2)}, u32[]{:S(2)}) collective-permute-start(bf16[128,1024]{1,0:T(8,128)(2,1)} %param.6), channel_id=1, source_target_pairs={{0,4},{2,10},{4,0},{6,14},{8,12},{10,2},{12,8},{14,6},{16,20},{18,... | collective-permute-start | bytes 786440 | tf_op jit(solution)/shard_map/ppermute | solution.py:27
  6.7 1.6 %collective-permute-start.1 = (bf16[128,1024]{1,0:T(8,128)(2,1)}, bf16[128,1024]{1,0:T(8,128)(2,1)S(1)}, u32[]{:S(2)}, u32[]{:S(2)}) collective-permute-start(bf16[128,1024]{1,0:T(8,128)(2,1)} %param.6), channel_id=1, source_target_pairs={{0,8},{2,6},{4,12},{6,2},{8,0},{10,14},{12,4},{14,10},{16,24},{18,... | collective-permute-start | bytes 786440 | tf_op jit(solution)/shard_map/ppermute | solution.py:27
  8.2 3.3 %collective-permute-done.2 = bf16[64,1024]{1,0:T(8,128)(2,1)S(1)} collective-permute-done((bf16[64,1024]{1,0:T(8,128)(2,1)S(1)}, bf16[64,1024]{1,0:T(8,128)(2,1)S(1)}, u32[]{:S(2)}, u32[]{:S(2)}) %collective-permute-start.2) | collective-permute-done | bytes 131104 | tf_op jit(solution)/shard_map/ppermute | solution.py:27
  11.6 1.6 %collective-permute-start.3 = (bf16[128,1024]{1,0:T(8,128)(2,1)S(1)}, bf16[128,1024]{1,0:T(8,128)(2,1)S(1)}, u32[]{:S(2)}, u32[]{:S(2)}) collective-permute-start(bf16[128,1024]{1,0:T(8,128)(2,1)S(1)} %pad_maximum_fusion.2), channel_id=1, source_target_pairs={{0,4},{2,10},{4,0},{6,14},{8,12},{10,2},{12,8},{14,6},{16,20},{18,... | collective-permute-start | bytes 786440 | tf_op jit(solution)/shard_map/ppermute | solution.py:27
  13.2 1.0 %constant_dynamic-update-slice_fusion.3 = bf16[512,1024]{1,0:T(8,128)(2,1)S(1)} fusion(bf16[128,1024]{1,0:T(8,128)(2,1)} %param.6), kind=kLoop, calls=%fused_computation.6 | loop fusion | bytes 524288
  14.2 0.3 collective-permute-done
  14.4 0.4 collective-permute-start.4
  14.9 1.4 %collective-permute-done.1 = bf16[128,1024]{1,0:T(8,128)(2,1)S(1)} collective-permute-done((bf16[128,1024]{1,0:T(8,128)(2,1)}, bf16[128,1024]{1,0:T(8,128)(2,1)S(1)}, u32[]{:S(2)}, u32[]{:S(2)}) %collective-permute-start.1) | collective-permute-done | bytes 262176 | tf_op jit(solution)/shard_map/ppermute | solution.py:27
  16.3 4.1 %collective-permute-done.3 = bf16[128,1024]{1,0:T(8,128)(2,1)S(1)} collective-permute-done((bf16[128,1024]{1,0:T(8,128)(2,1)S(1)}, bf16[128,1024]{1,0:T(8,128)(2,1)S(1)}, u32[]{:S(2)}, u32[]{:S(2)}) %collective-permute-start.3) | collective-permute-done | bytes 262176 | tf_op jit(solution)/shard_map/ppermute | solution.py:27
  20.5 0.3 collective-permute-done.4
  20.8 0.2 collective-permute-start.5
  21.0 0.8 %collective-permute-start.6 = (bf16[256,1024]{1,0:T(8,128)(2,1)S(1)}, bf16[256,1024]{1,0:T(8,128)(2,1)S(1)}, u32[]{:S(2)}, u32[]{:S(2)}) collective-permute-start(bf16[256,1024]{1,0:T(8,128)(2,1)S(1)} %pad_maximum_fusion.1), channel_id=1, source_target_pairs={{0,8},{2,6},{4,12},{6,2},{8,0},{10,14},{12,4},{14,10},{16,24},{18,... | collective-permute-start | bytes 1572872 | tf_op jit(solution)/shard_map/ppermute | solution.py:27
  21.8 1.8 %collective-permute-done.5.refs_1_ = bf16[512,1024]{1,0:T(8,128)(2,1)S(1)} collective-permute-done((bf16[512,1024]{1,0:T(8,128)(2,1)S(1)}, bf16[512,1024]{1,0:T(8,128)(2,1)S(1)}, u32[]{:S(2)}, u32[]{:S(2)}) %collective-permute-start.5) | collective-permute-done | bytes 1048608 | tf_op jit(solution)/shard_map/ppermute | solution.py:27
  23.6 0.0 copy-done
  23.6 0.0 copy-done.2
  23.6 0.0 copy-done.3
  23.6 5.9 %shard_map.56 = (f32[4096,256]{1,0:T(8,128)S(1)}, f32[4096,128]{1,0:T(8,128)S(1)}) custom-call(s32[2]{0:T(128)S(1)} %copy-done.3, s32[2,16]{1,0:T(2,128)S(1)} %copy-done.2, bf16[128,4096]{1,0:T(8,128)(2,1)S(1)} %copy-done, bf16[512,1024]{1,0:T(8,128)(2,1)S(1)} %constant_dynamic-update-slice_fusion.refs_0_, bf16[512,1024]{1,0:T(8,128)(2,1)S(1)} %collective-permute-done.5.refs_1_), custom_call_target="tpu_custom_call" | custom-call | flops 4294967296 | bytes 3145728 | tf_op jit(solution)/shard_map/pallas_call | solution.py:288
  29.5 0.7 %collective-permute-done.6 = bf16[256,1024]{1,0:T(8,128)(2,1)S(1)} collective-permute-done((bf16[256,1024]{1,0:T(8,128)(2,1)S(1)}, bf16[256,1024]{1,0:T(8,128)(2,1)S(1)}, u32[]{:S(2)}, u32[]{:S(2)}) %collective-permute-start.6) | collective-permute-done | bytes 524320 | tf_op jit(solution)/shard_map/ppermute | solution.py:27
  30.2 0.1 pad_maximum_fusion.refs_2_
  30.3 0.1 collective-permute-start.7
  30.4 2.6 %collective-permute-done.7.refs_3_ = bf16[512,1024]{1,0:T(8,128)(2,1)S(1)} collective-permute-done((bf16[512,1024]{1,0:T(8,128)(2,1)S(1)}, bf16[512,1024]{1,0:T(8,128)(2,1)S(1)}, u32[]{:S(2)}, u32[]{:S(2)}) %collective-permute-start.7) | collective-permute-done | bytes 1048608 | tf_op jit(solution)/shard_map/ppermute | solution.py:27
  33.0 4.2 %shard_map.58 = (bf16[64,2048]{1,0:T(8,128)(2,1)S(1)}, bf16[64,2048]{1,0:T(8,128)(2,1)S(1)}) custom-call(s32[2]{0:T(128)S(1)} %copy-done.3, s32[2,16]{1,0:T(2,128)S(1)} %copy-done.2, bf16[128,4096]{1,0:T(8,128)(2,1)S(1)} %copy-done, bf16[512,1024]{1,0:T(8,128)(2,1)S(1)} %constant_dynamic-update-slice_fusion.refs_0_, ...), custom_call_target="tpu_custom_call" | custom-call | flops 2147483648 | bytes 1572864 | tf_op jit(solution)/shard_map/pallas_call | solution.py:288
  37.2 1.6 %collective-permute-start.9 = (bf16[64,2048]{1,0:T(8,128)(2,1)S(1)}, bf16[64,2048]{1,0:T(8,128)(2,1)S(1)}, u32[]{:S(2)}, u32[]{:S(2)}) collective-permute-start(bf16[64,2048]{1,0:T(8,128)(2,1)S(1)} %get-tuple-element.24), channel_id=1, source_target_pairs={{0,1},{1,0},{2,3},{3,2},{4,5},{5,4},{6,7},{7,6},{8,9},{9,8},{10,11... | collective-permute-start | bytes 786440 | tf_op jit(solution)/shard_map/ppermute | solution.py:411
  38.8 4.0 %shard_map.57 = (bf16[64,2048]{1,0:T(8,128)(2,1)S(1)}, bf16[64,2048]{1,0:T(8,128)(2,1)S(1)}) custom-call(s32[2]{0:T(128)S(1)} %copy-done.3, s32[2,16]{1,0:T(2,128)S(1)} %copy-done.2, bf16[128,4096]{1,0:T(8,128)(2,1)S(1)} %copy-done, bf16[512,1024]{1,0:T(8,128)(2,1)S(1)} %constant_dynamic-update-slice_fusion.refs_0_, ...), custom_call_target="tpu_custom_call" | custom-call | flops 2147483648 | bytes 1572864 | tf_op jit(solution)/shard_map/pallas_call | solution.py:288
  42.8 0.6 %collective-permute-start.8 = (bf16[64,2048]{1,0:T(8,128)(2,1)S(1)}, bf16[64,2048]{1,0:T(8,128)(2,1)S(1)}, u32[]{:S(2)}, u32[]{:S(2)}) collective-permute-start(bf16[64,2048]{1,0:T(8,128)(2,1)S(1)} %get-tuple-element.23), channel_id=1, source_target_pairs={{0,1},{1,0},{2,3},{3,2},{4,5},{5,4},{6,7},{7,6},{8,9},{9,8},{10,11... | collective-permute-start | bytes 786440 | tf_op jit(solution)/shard_map/ppermute | solution.py:411
  43.4 2.5 %collective-permute-done.9.refs_3_ = bf16[64,2048]{1,0:T(8,128)(2,1)S(1)} collective-permute-done((bf16[64,2048]{1,0:T(8,128)(2,1)S(1)}, bf16[64,2048]{1,0:T(8,128)(2,1)S(1)}, u32[]{:S(2)}, u32[]{:S(2)}) %collective-permute-start.9) | collective-permute-done | bytes 262176 | tf_op jit(solution)/shard_map/ppermute | solution.py:411
  45.9 5.4 %collective-permute-done.8.refs_2_ = bf16[64,2048]{1,0:T(8,128)(2,1)S(1)} collective-permute-done((bf16[64,2048]{1,0:T(8,128)(2,1)S(1)}, bf16[64,2048]{1,0:T(8,128)(2,1)S(1)}, u32[]{:S(2)}, u32[]{:S(2)}) %collective-permute-start.8) | collective-permute-done | bytes 262176 | tf_op jit(solution)/shard_map/ppermute | solution.py:411
  51.2 1.0 %shard_map.59 = bf16[64,8192]{1,0:T(8,128)(2,1)} custom-call(bf16[64,2048]{1,0:T(8,128)(2,1)S(1)} %get-tuple-element.21.refs_0_, bf16[64,2048]{1,0:T(8,128)(2,1)S(1)} %get-tuple-element.22.refs_1_, bf16[64,2048]{1,0:T(8,128)(2,1)S(1)} %collective-permute-done.8.refs_2_, bf16[64,2048]{1,0:T(8,128)(2,1)S(1)} %collective-permute-done.9.refs_3_), custom_call_target="tpu_custom_call" | custom-call | tf_op jit(solution)/shard_map/pallas_call | solution.py:342
  (6 shorter events, 0.1 us)
Async XLA Ops:
  0.0 23.6 %copy-start = (bf16[128,4096]{1,0:T(8,128)(2,1)S(1)}, bf16[128,4096]{1,0:T(8,128)(2,1)}, u32[]{:S(2)}) copy-start(bf16[128,4096]{1,0:T(8,128)(2,1)} %q_ref.5) | copy-start | bytes 3145732
  0.0 1.0 %copy-start.1 = (bf16[2,64,1024]{2,1,0:T(8,128)(2,1)S(1)}, bf16[2,64,1024]{2,1,0:T(8,128)(2,1)}, u32[]{:S(2)}) copy-start(bf16[2,64,1024]{2,1,0:T(8,128)(2,1)} %cache_ref.1) | copy-start | bytes 786436
  1.0 22.5 %copy-start.2 = (s32[2,16]{1,0:T(2,128)S(1)}, s32[2,16]{1,0:T(2,128)}, u32[]{:S(2)}) copy-start(s32[2,16]{1,0:T(2,128)} %owner_ref.5) | copy-start | bytes 388
  1.0 22.5 %copy-start.3 = (s32[2]{0:T(128)S(1)}, s32[2]{0:T(128)}, u32[]{:S(2)}) copy-start(s32[2]{0:T(128)} %limit_ref.5) | copy-start | bytes 28
  1.1 10.5 %collective-permute-start.2 = (bf16[64,1024]{1,0:T(8,128)(2,1)S(1)}, bf16[64,1024]{1,0:T(8,128)(2,1)S(1)}, u32[]{:S(2)}, u32[]{:S(2)}) collective-permute-start(bf16[64,1024]{1,0:T(8,128)(2,1)S(1)} %get-tuple-element.16), channel_id=1, source_target_pairs={{0,16},{2,18},{4,20},{6,22},{8,24},{10,26},{12,28},{14,30},{16,0},... | collective-permute-start | bytes 393224 | tf_op jit(solution)/shard_map/ppermute | solution.py:27
  5.2 9.3 %collective-permute-start = (bf16[128,1024]{1,0:T(8,128)(2,1)}, bf16[128,1024]{1,0:T(8,128)(2,1)S(1)}, u32[]{:S(2)}, u32[]{:S(2)}) collective-permute-start(bf16[128,1024]{1,0:T(8,128)(2,1)} %param.6), channel_id=1, source_target_pairs={{0,4},{2,10},{4,0},{6,14},{8,12},{10,2},{12,8},{14,6},{16,20},{18,... | collective-permute-start | bytes 786440 | tf_op jit(solution)/shard_map/ppermute | solution.py:27
  6.7 9.7 %collective-permute-start.1 = (bf16[128,1024]{1,0:T(8,128)(2,1)}, bf16[128,1024]{1,0:T(8,128)(2,1)S(1)}, u32[]{:S(2)}, u32[]{:S(2)}) collective-permute-start(bf16[128,1024]{1,0:T(8,128)(2,1)} %param.6), channel_id=1, source_target_pairs={{0,8},{2,6},{4,12},{6,2},{8,0},{10,14},{12,4},{14,10},{16,24},{18,... | collective-permute-start | bytes 786440 | tf_op jit(solution)/shard_map/ppermute | solution.py:27
  11.6 8.8 %collective-permute-start.3 = (bf16[128,1024]{1,0:T(8,128)(2,1)S(1)}, bf16[128,1024]{1,0:T(8,128)(2,1)S(1)}, u32[]{:S(2)}, u32[]{:S(2)}) collective-permute-start(bf16[128,1024]{1,0:T(8,128)(2,1)S(1)} %pad_maximum_fusion.2), channel_id=1, source_target_pairs={{0,4},{2,10},{4,0},{6,14},{8,12},{10,2},{12,8},{14,6},{16,20},{18,... | collective-permute-start | bytes 786440 | tf_op jit(solution)/shard_map/ppermute | solution.py:27
  14.4 6.4 %collective-permute-start.4 = (bf16[128,1024]{1,0:T(8,128)(2,1)S(1)}, bf16[128,1024]{1,0:T(8,128)(2,1)S(1)}, u32[]{:S(2)}, u32[]{:S(2)}) collective-permute-start(bf16[128,1024]{1,0:T(8,128)(2,1)S(1)} %collective-permute-done), channel_id=1, source_target_pairs={{0,8},{2,6},{4,12},{6,2},{8,0},{10,14},{12,4},{14,10},{16,24},{18,... | collective-permute-start | bytes 786440 | tf_op jit(solution)/shard_map/ppermute | solution.py:27
  20.8 2.7 %collective-permute-start.5 = (bf16[512,1024]{1,0:T(8,128)(2,1)S(1)}, bf16[512,1024]{1,0:T(8,128)(2,1)S(1)}, u32[]{:S(2)}, u32[]{:S(2)}) collective-permute-start(bf16[512,1024]{1,0:T(8,128)(2,1)S(1)} %constant_dynamic-update-slice_fusion.refs_0_), channel_id=1, source_target_pairs={{0,2},{2,0},{4,6},{6,4},{8,10},{10,8},{12,14},{14,12},{16,18},{18,... | collective-permute-start | bytes 3145736 | tf_op jit(solution)/shard_map/ppermute | solution.py:27
  21.0 9.2 %collective-permute-start.6 = (bf16[256,1024]{1,0:T(8,128)(2,1)S(1)}, bf16[256,1024]{1,0:T(8,128)(2,1)S(1)}, u32[]{:S(2)}, u32[]{:S(2)}) collective-permute-start(bf16[256,1024]{1,0:T(8,128)(2,1)S(1)} %pad_maximum_fusion.1), channel_id=1, source_target_pairs={{0,8},{2,6},{4,12},{6,2},{8,0},{10,14},{12,4},{14,10},{16,24},{18,... | collective-permute-start | bytes 1572872 | tf_op jit(solution)/shard_map/ppermute | solution.py:27
  30.3 2.7 %collective-permute-start.7 = (bf16[512,1024]{1,0:T(8,128)(2,1)S(1)}, bf16[512,1024]{1,0:T(8,128)(2,1)S(1)}, u32[]{:S(2)}, u32[]{:S(2)}) collective-permute-start(bf16[512,1024]{1,0:T(8,128)(2,1)S(1)} %pad_maximum_fusion.refs_2_), channel_id=1, source_target_pairs={{0,2},{2,0},{4,6},{6,4},{8,10},{10,8},{12,14},{14,12},{16,18},{18,... | collective-permute-start | bytes 3145736 | tf_op jit(solution)/shard_map/ppermute | solution.py:27
  37.2 8.7 %collective-permute-start.9 = (bf16[64,2048]{1,0:T(8,128)(2,1)S(1)}, bf16[64,2048]{1,0:T(8,128)(2,1)S(1)}, u32[]{:S(2)}, u32[]{:S(2)}) collective-permute-start(bf16[64,2048]{1,0:T(8,128)(2,1)S(1)} %get-tuple-element.24), channel_id=1, source_target_pairs={{0,1},{1,0},{2,3},{3,2},{4,5},{5,4},{6,7},{7,6},{8,9},{9,8},{10,11... | collective-permute-start | bytes 786440 | tf_op jit(solution)/shard_map/ppermute | solution.py:411
  42.8 8.4 %collective-permute-start.8 = (bf16[64,2048]{1,0:T(8,128)(2,1)S(1)}, bf16[64,2048]{1,0:T(8,128)(2,1)S(1)}, u32[]{:S(2)}, u32[]{:S(2)}) collective-permute-start(bf16[64,2048]{1,0:T(8,128)(2,1)S(1)} %get-tuple-element.23), channel_id=1, source_target_pairs={{0,1},{1,0},{2,3},{3,2},{4,5},{5,4},{6,7},{7,6},{8,9},{9,8},{10,11... | collective-permute-start | bytes 786440 | tf_op jit(solution)/shard_map/ppermute | solution.py:411

commit v10 on v9

--- a/solution.py
+++ b/solution.py
@@ -19,6 +19,7 @@
 EXTRA_ROWS = 16
 SHIFT_STEP = 32.0
 LOWEST_TOTAL = 1e-20
+HIGHEST_TOTAL = 1e30
 SPAN_ROWS, OWN_PAGE, CROSSED_PAGE = range(3)
 
 
@@ -50,14 +51,14 @@
     key_sets, refs = [(refs[2 * at : 2 * at + 2], layout) for at, layout in enumerate(layouts)], refs[
         2 * len(layouts) :
     ]
-    (state_sum, state_shift), refs = refs[:2], refs[2:]
+    (state_sum, state_extra), refs = refs[:2], refs[2:]
     if first_phase:
         page_seen, keys, values = refs[:3]
         weights = refs[3:5]
     else:
         outs = refs[:2]
         page_seen, keys, values = refs[2:5]
-        weights, shifts, slow_sum, slow_top = refs[5:7], refs[7:9], refs[9], refs[10]
+        weights, slow_sum, slow_top = refs[5:7], refs[7], refs[8]
     half_keys = key_sets[0][0][0].shape[0]
     total_keys = 2 * half_keys
     chunk = min(KEY_CHUNK, total_keys)
@@ -95,7 +96,7 @@
 
     def fill(group, halves, extras):
         for half in range(2):
-            column = (part * groups + group) * 2 * HD
+            column = (part * groups + group) * 2 * HD % halves[half].shape[1]
             at = pl.ds(half * half_keys, half_keys)
             keys[group, :HD, at] = halves[half][:, pl.ds(column, HD)].T
             keys[group, pl.ds(HD, EXTRA_ROWS), at] = extras[half]
@@ -147,30 +148,31 @@
 
     def begin(group):
         fill(group, halves, extras)
-        key = keys[group, :HD, :].astype(jnp.float32)
-        squares = jnp.sum(key * key, axis=0, keepdims=True)
-        longest[group] = jnp.max(squares, axis=1, keepdims=True)
+        if first_phase:
+            key = keys[group, :HD, :].astype(jnp.float32)
+            squares = jnp.sum(key * key, axis=0, keepdims=True)
+            longest[group] = jnp.max(squares, axis=1, keepdims=True)
 
     def weigh(index):
         group = index // blocks_a_group
         query = query_rows(index)
-        wide = query.astype(jnp.float32)
-        bound = jnp.sqrt(jnp.sum(wide * wide, axis=1, keepdims=True) * longest[group])
-        shift = jnp.ceil(bound * (1.0 / SHIFT_STEP)) * SHIFT_STEP
-        extra = jnp.where(lane == 0, 1.0, jnp.where(lane == 1, -shift, 0.0))
-        query = jnp.concatenate([query, extra.astype(jnp.bfloat16)], axis=1)
-        shift = jnp.broadcast_to(shift, (block, HD))
         if first_phase:
-            state_shift[pl.ds(index * block, block), :] = shift
+            wide = query.astype(jnp.float32)
+            bound = jnp.sqrt(jnp.sum(wide * wide, axis=1, keepdims=True) * longest[group])
+            shift = jnp.ceil(bound * (1.0 / SHIFT_STEP)) * SHIFT_STEP
+            extra = jnp.where(lane == 0, 1.0, jnp.where(lane == 1, -shift, 0.0))
+            extra = extra.astype(jnp.bfloat16)
+            state_extra[pl.ds(index * block, block), :] = extra
         else:
-            shifts[index % 2][...] = shift
+            extra = state_extra[pl.ds((part * blocks + index) * block, block), :]
+        query = jnp.concatenate([query, extra], axis=1)
         for start in range(0, total_keys, chunk):
             made = scores_of(query, group, start, first_phase)
             weights[index % 2][:, pl.ds(start, chunk)] = jnp.exp2(made * EXP2_SCALE).astype(
                 jnp.bfloat16
             )
 
-    def finish(index, lowest):
+    def finish(index, extremes):
         group = index // blocks_a_group
         summed = jnp.dot(
             weights[index % 2][...], values[group], preferred_element_type=jnp.float32
@@ -178,22 +180,18 @@
         rows = pl.ds(index * block, block)
         if first_phase:
             state_sum[rows, :] = summed
-            return lowest
+            return extremes
         old = pl.ds((part * blocks + index) * block, block)
-        before, shift = state_shift[old, :], shifts[index % 2][...]
-        both = jnp.maximum(before, shift)
-        fade_before = jnp.exp2((before - both) * EXP2_SCALE)
-        fade = jnp.exp2((shift - both) * EXP2_SCALE)
-        total = state_sum[old, HD:] * fade_before + summed[:, HD:] * fade
-        result = (state_sum[old, :HD] * fade_before + summed[:, :HD] * fade) / total
-        give(index, result.astype(jnp.bfloat16))
-        return jnp.minimum(lowest, total)
+        summed = summed + state_sum[old, :]
+        total = summed[:, HD:]
+        give(index, (summed[:, :HD] / total).astype(jnp.bfloat16))
+        return jnp.minimum(extremes[0], total), jnp.maximum(extremes[1], total)
 
     begin(0)
-    lowest = jnp.ones((block, HD), jnp.float32)
+    extremes = (jnp.ones((block, HD), jnp.float32),) * 2
     for index in range(blocks + 1):
         if index >= 1:
-            lowest = finish(index - 1, lowest)
+            extremes = finish(index - 1, extremes)
         if index < blocks:
             weigh(index)
             if (index + 1) % blocks_a_group == 0 and index + 1 < blocks:
@@ -201,7 +199,7 @@
     if first_phase:
         return
 
-    @pl.when(jnp.min(lowest) < LOWEST_TOTAL)
+    @pl.when((jnp.min(extremes[0]) < LOWEST_TOTAL) | (jnp.max(extremes[1]) > HIGHEST_TOTAL))
     def exact():
         for number, (halves, layout) in enumerate(key_sets):
             extras = [extra_rows(layout, half) for half in range(2)]
@@ -273,14 +271,13 @@
         state = ()
         out_shape = [
             jax.ShapeDtypeStruct((rows, 2 * HD), jnp.float32),
-            jax.ShapeDtypeStruct((rows, HD), jnp.float32),
+            jax.ShapeDtypeStruct((rows, HD), jnp.bfloat16),
         ]
     else:
         out_shape = [
             jax.ShapeDtypeStruct((kept, columns), jnp.bfloat16),
             jax.ShapeDtypeStruct((tokens - kept, columns), jnp.bfloat16),
         ]
-        scratch_shapes += [pltpu.VMEM((block, HD), jnp.float32)] * 2
         scratch_shapes += [
             pltpu.VMEM((rows, 2 * HD), jnp.float32),
             pltpu.VMEM((rows, HD), jnp.float32),
@@ -317,15 +314,14 @@
     )(cache)
 
 
-def join_kernel(pieces, *refs):
-    parts, (out_ref, done) = refs[:pieces], refs[pieces:]
-    columns = [ref.shape[1] for ref in parts[: pieces // 2]]
+def join_kernel(spots, count, *refs):
+    parts, (out_ref, done) = refs[len(refs) - 2 - count : -2], refs[-2:]
     side = out_ref.shape[1] // 2
     my_head = lax.axis_index("head")
     copies = []
-    for at, ref in enumerate(parts):
-        owner = my_head if at < pieces // 2 else 1 - my_head
-        first = pl.multiple_of(owner * side + sum(columns[: at % (pieces // 2)]), HD)
+    for at, (ref, (received, start)) in enumerate(zip(parts, spots)):
+        owner = 1 - my_head if received else my_head
+        first = pl.multiple_of(owner * side + start, HD)
         copies.append(
             pltpu.make_async_copy(ref, out_ref.at[:, pl.ds(first, ref.shape[1])], done.at[at])
         )
@@ -335,18 +331,26 @@
         copy.wait()
 
 
+def join(pieces, spots, columns, partial):
+    earlier = [] if partial is None else [partial]
+    return pl.pallas_call(
+        functools.partial(join_kernel, spots, len(pieces)),
+        out_shape=jax.ShapeDtypeStruct((pieces[0].shape[0], columns), pieces[0].dtype),
+        in_specs=[pl.BlockSpec(memory_space=pl.ANY)] * len(earlier)
+        + [pl.BlockSpec(memory_space=pltpu.VMEM)] * len(pieces),
+        out_specs=pl.BlockSpec(memory_space=pl.ANY),
+        scratch_shapes=[pltpu.SemaphoreType.DMA((len(pieces),))],
+        input_output_aliases={0: 0} if earlier else {},
+        compiler_params=pltpu.CompilerParams(vmem_limit_bytes=8 << 20),
+    )(*earlier, *pieces)
+
+
 def put_together(kept, received):
-    pieces = len(kept) + len(received)
-    rows = kept[0].shape[0]
-    columns = sum(one.shape[1] for one in kept + received)
-    return pl.pallas_call(
-        functools.partial(join_kernel, pieces),
-        out_shape=jax.ShapeDtypeStruct((rows, columns), kept[0].dtype),
-        in_specs=[pl.BlockSpec(memory_space=pltpu.VMEM)] * pieces,
-        out_specs=pl.BlockSpec(memory_space=pl.ANY),
-        scratch_shapes=[pltpu.SemaphoreType.DMA((pieces,))],
-        compiler_params=pltpu.CompilerParams(vmem_limit_bytes=8 << 20),
-    )(*kept, *received)
+    columns = kept[0].shape[1]
+    pieces = kept + received
+    spots = [(at >= len(kept), at % len(kept) * columns) for at in range(len(pieces))]
+    out = join(pieces[:-1], spots[:-1], columns * len(pieces), None)
+    return join(pieces[-1:], spots[-1:], columns * len(pieces), out)
 
 
 def body(span_query, span_kv, prefix_cache, prefix_len, block_owner):
@@ -376,13 +380,17 @@
     other_page, own_page = pick(prefix_cache, group_size)
     crossed = hop(other_page, (group_size, group_size))
 
+    span_forward = send(span_kv, 0)
     span_early = send(span_kv, stages - 1)
-    span_forward = send(span_kv, 0)
+    if stages == 2:
+        across = sum(bits)
+        span_late = hop(span_kv, (across, across))
     for stage in range(1, stages - 1):
         seen = jnp.concatenate([span_kv, span_forward], axis=0)
         span_forward = jnp.concatenate([span_forward, send(seen, stage)], axis=0)
+    if stages != 2:
+        span_late = send(span_forward, stages - 1)
     span = jnp.concatenate([span_kv, span_forward], axis=0)
-    span_late = send(span_forward, stages - 1)
     crossed = after(span, crossed)
     pages = jnp.concatenate([own_page, crossed], axis=0)
     pages = jnp.concatenate([pages, send(pages, 0)], axis=0)
@@ -400,10 +408,12 @@
         if stage == stages - 1:
             received = after(state, received)
         pages = jnp.concatenate([pages, received], axis=0)
-    page_set = (pages, hop(pages, (1, 1)), page_layout)
-    results = [
-        attend(*common, part, parts, [span_set, page_set], spec, state) for part in range(parts)
-    ]
+    columns = pages.shape[1] // parts
+    results = []
+    for part in range(parts):
+        theirs = hop(pages[:, part * columns : (part + 1) * columns], (1, 1))
+        page_set = (pages, theirs, page_layout)
+        results.append(attend(*common, part, parts, [span_set, page_set], spec, state))
     if head_size != 2:
         rows = jnp.concatenate([jnp.concatenate(pair, axis=0) for pair in results], axis=1)
         return lax.all_to_all(rows, "head", split_axis=0, concat_axis=1, tiled=True)

time: 52.5 us -> 75.1 us (1.43)
  Pallas kernels: 15.1 us -> 37.3 us
  starting transfers between devices: 12.4 us -> 13.3 us
    pallas_call x3, Pallas kernels: 14.1 us -> 35.7 us  [attend(): pl.pallas_call(functools.partial(attend_kernel, spec, layouts, part, bloc...]
    ppermute x2, waiting for transfers between devices: 7.87 us -> 6.68 us  [body(): lax.ppermute(pair[1], 'head', [(0, 1), (1, 0)])]
    ppermute x8 -> x9, starting transfers between devices: 10.3 us -> 11.1 us  [hop(): lax.ppermute(value, 'seq', [(source, source ^ bit_of_core[source % 2]) fo...]
    ppermute x8 -> x9, waiting for transfers between devices: 14.6 us -> 15.2 us  [hop(): lax.ppermute(value, 'seq', [(source, source ^ bit_of_core[source % 2]) fo...]
    pallas_call x1 -> x2, Pallas kernels: 0.99 us -> 1.61 us  [join(): pl.pallas_call(functools.partial(join_kernel, spots, len(pieces)), out_sh...]
  transfers between devices with their start and end apart: 10 -> 11, of which waited for: 10 -> 8; matrix products, arithmetic and copies ran while one was open for 2% -> 1% of each run, Pallas kernels for 19% -> 49%
where the time goes in v10:
time: 75.1 us; the launch traced here: 74.9 us
  Pallas kernels  37.3 us (50%)
  waiting for transfers between devices  21.9 us (29%)
  starting transfers between devices  13.3 us (18%)
  local copies, waits for them, and re-layouts  2.06 us (3%)
    pallas_call x3, Pallas kernels, attend(): pl.pallas_call(functools.partial(attend_kernel, spec, layouts, part, bloc...  35.7 us
    ppermute x9, waiting for transfers between devices, hop(): lax.ppermute(value, 'seq', [(source, source ^ bit_of_core[source % 2]) fo...  15.2 us
    ppermute x9, starting transfers between devices, hop(): lax.ppermute(value, 'seq', [(source, source ^ bit_of_core[source % 2]) fo...  11.1 us
    ppermute x2, waiting for transfers between devices, body(): lax.ppermute(pair[1], 'head', [(0, 1), (1, 0)])  6.68 us
    ppermute x2, starting transfers between devices, body(): lax.ppermute(pair[1], 'head', [(0, 1), (1, 0)])  2.16 us
    unnamed x11, local copies, waits for them, and re-layouts  1.96 us
    pallas_call x2, Pallas kernels, join(): pl.pallas_call(functools.partial(join_kernel, spots, len(pieces)), out_sh...  1.61 us
  transfers between devices with their start and end apart: 11, of which 8 were waited for; matrix products, arithmetic and copies ran while one was open for 1% of the time, Pallas kernels for 49%

profile of v10, /device:TPU:0, one launch (start us, length us, event | category | flops | bytes accessed | tf_op | source)
XLA Modules:
  0.0 74.9 jit_solution(168466895647218536)
XLA Ops:
  0.0 0.0 copy-start.1
  0.0 0.9 %copy-done.1 = bf16[2,64,1024]{2,1,0:T(8,128)(2,1)S(1)} copy-done((bf16[2,64,1024]{2,1,0:T(8,128)(2,1)S(1)}, bf16[2,64,1024]{2,1,0:T(8,128)(2,1)}, u32[]{:S(2)}) %copy-start.1) | copy-done | bytes 262168
  1.0 0.0 copy-start
  1.0 0.0 copy-start.2
  1.0 0.0 copy-start.3
  1.0 4.1 %collective-permute-start.2 = (bf16[64,1024]{1,0:T(8,128)(2,1)S(1)}, bf16[64,1024]{1,0:T(8,128)(2,1)S(1)}, u32[]{:S(2)}, u32[]{:S(2)}) collective-permute-start(bf16[64,1024]{1,0:T(8,128)(2,1)S(1)} %get-tuple-element.16), channel_id=1, source_target_pairs={{0,16},{2,18},{4,20},{6,22},{8,24},{10,26},{12,28},{14,30},{16,0},... | collective-permute-start | bytes 393224 | tf_op jit(solution)/shard_map/ppermute | solution.py:28
  5.1 1.5 %collective-permute-start = (bf16[128,1024]{1,0:T(8,128)(2,1)}, bf16[128,1024]{1,0:T(8,128)(2,1)S(1)}, u32[]{:S(2)}, u32[]{:S(2)}) collective-permute-start(bf16[128,1024]{1,0:T(8,128)(2,1)} %param.6), channel_id=1, source_target_pairs={{0,4},{2,10},{4,0},{6,14},{8,12},{10,2},{12,8},{14,6},{16,20},{18,... | collective-permute-start | bytes 786440 | tf_op jit(solution)/shard_map/ppermute | solution.py:28
  6.6 1.6 %collective-permute-start.1 = (bf16[128,1024]{1,0:T(8,128)(2,1)}, bf16[128,1024]{1,0:T(8,128)(2,1)S(1)}, u32[]{:S(2)}, u32[]{:S(2)}) collective-permute-start(bf16[128,1024]{1,0:T(8,128)(2,1)} %param.6), channel_id=1, source_target_pairs={{0,8},{2,6},{4,12},{6,2},{8,0},{10,14},{12,4},{14,10},{16,24},{18,... | collective-permute-start | bytes 786440 | tf_op jit(solution)/shard_map/ppermute | solution.py:28
  8.1 0.4 collective-permute-start.4
  8.6 2.9 %collective-permute-done.2 = bf16[64,1024]{1,0:T(8,128)(2,1)S(1)} collective-permute-done((bf16[64,1024]{1,0:T(8,128)(2,1)S(1)}, bf16[64,1024]{1,0:T(8,128)(2,1)S(1)}, u32[]{:S(2)}, u32[]{:S(2)}) %collective-permute-start.2) | collective-permute-done | bytes 131104 | tf_op jit(solution)/shard_map/ppermute | solution.py:28
  11.5 1.6 %collective-permute-start.3 = (bf16[128,1024]{1,0:T(8,128)(2,1)S(1)}, bf16[128,1024]{1,0:T(8,128)(2,1)S(1)}, u32[]{:S(2)}, u32[]{:S(2)}) collective-permute-start(bf16[128,1024]{1,0:T(8,128)(2,1)S(1)} %pad_maximum_fusion.2), channel_id=1, source_target_pairs={{0,4},{2,10},{4,0},{6,14},{8,12},{10,2},{12,8},{14,6},{16,20},{18,... | collective-permute-start | bytes 786440 | tf_op jit(solution)/shard_map/ppermute | solution.py:28
  13.1 1.0 %constant_dynamic-update-slice_fusion.3 = bf16[512,1024]{1,0:T(8,128)(2,1)S(1)} fusion(bf16[128,1024]{1,0:T(8,128)(2,1)} %param.6), kind=kLoop, calls=%fused_computation.6 | loop fusion | bytes 524288
  14.1 1.1 %collective-permute-done = bf16[128,1024]{1,0:T(8,128)(2,1)S(1)} collective-permute-done((bf16[128,1024]{1,0:T(8,128)(2,1)}, bf16[128,1024]{1,0:T(8,128)(2,1)S(1)}, u32[]{:S(2)}, u32[]{:S(2)}) %collective-permute-start) | collective-permute-done | bytes 262176 | tf_op jit(solution)/shard_map/ppermute | solution.py:28
  15.2 1.7 %collective-permute-done.1 = bf16[128,1024]{1,0:T(8,128)(2,1)S(1)} collective-permute-done((bf16[128,1024]{1,0:T(8,128)(2,1)}, bf16[128,1024]{1,0:T(8,128)(2,1)S(1)}, u32[]{:S(2)}, u32[]{:S(2)}) %collective-permute-start.1) | collective-permute-done | bytes 262176 | tf_op jit(solution)/shard_map/ppermute | solution.py:28
  16.9 6.1 %collective-permute-done.3 = bf16[128,1024]{1,0:T(8,128)(2,1)S(1)} collective-permute-done((bf16[128,1024]{1,0:T(8,128)(2,1)S(1)}, bf16[128,1024]{1,0:T(8,128)(2,1)S(1)}, u32[]{:S(2)}, u32[]{:S(2)}) %collective-permute-start.3) | collective-permute-done | bytes 262176 | tf_op jit(solution)/shard_map/ppermute | solution.py:28
  23.0 0.0 collective-permute-done.4
  23.1 0.2 collective-permute-start.5
  23.3 1.2 %collective-permute-start.6 = (bf16[256,1024]{1,0:T(8,128)(2,1)S(1)}, bf16[256,1024]{1,0:T(8,128)(2,1)S(1)}, u32[]{:S(2)}, u32[]{:S(2)}) collective-permute-start(bf16[256,1024]{1,0:T(8,128)(2,1)S(1)} %pad_maximum_fusion.1), channel_id=1, source_target_pairs={{0,8},{2,6},{4,12},{6,2},{8,0},{10,14},{12,4},{14,10},{16,24},{18,... | collective-permute-start | bytes 1572872 | tf_op jit(solution)/shard_map/ppermute | solution.py:28
  24.4 1.4 %collective-permute-done.5.refs_1_ = bf16[512,1024]{1,0:T(8,128)(2,1)S(1)} collective-permute-done((bf16[512,1024]{1,0:T(8,128)(2,1)S(1)}, bf16[512,1024]{1,0:T(8,128)(2,1)S(1)}, u32[]{:S(2)}, u32[]{:S(2)}) %collective-permute-start.5) | collective-permute-done | bytes 1048608 | tf_op jit(solution)/shard_map/ppermute | solution.py:28
  25.8 0.0 copy-done
  25.8 0.0 copy-done.2
  25.8 0.0 copy-done.3
  25.8 6.0 %shard_map.56 = (f32[4096,256]{1,0:T(8,128)S(1)}, bf16[4096,128]{1,0:T(8,128)(2,1)S(1)}) custom-call(s32[2]{0:T(128)S(1)} %copy-done.3, s32[2,16]{1,0:T(2,128)S(1)} %copy-done.2, bf16[128,4096]{1,0:T(8,128)(2,1)S(1)} %copy-done, bf16[512,1024]{1,0:T(8,128)(2,1)S(1)} %constant_dynamic-update-slice_fusion.refs_0_, ...), custom_call_target="tpu_custom_call" | custom-call | flops 4294967296 | bytes 3145728 | tf_op jit(solution)/shard_map/pallas_call | solution.py:285
  31.8 0.7 collective-permute-done.6
  32.4 0.1 pad_maximum_fusion.refs_2_
  32.5 0.1 fusion
  32.6 0.1 collective-permute-start.7
  32.7 0.5 collective-permute-start.8
  33.2 1.4 %collective-permute-done.7.refs_3_ = bf16[512,512]{1,0:T(8,128)(2,1)S(1)} collective-permute-done((bf16[512,512]{1,0:T(8,128)(2,1)S(1)}, bf16[512,512]{1,0:T(8,128)(2,1)S(1)}, u32[]{:S(2)}, u32[]{:S(2)}) %collective-permute-start.7) | collective-permute-done | bytes 524320 | tf_op jit(solution)/shard_map/ppermute | solution.py:28
  34.6 15.0 %shard_map.57 = (bf16[64,2048]{1,0:T(8,128)(2,1)S(1)}, bf16[64,2048]{1,0:T(8,128)(2,1)S(1)}) custom-call(s32[2]{0:T(128)S(1)} %copy-done.3, s32[2,16]{1,0:T(2,128)S(1)} %copy-done.2, bf16[128,4096]{1,0:T(8,128)(2,1)S(1)} %copy-done, bf16[512,1024]{1,0:T(8,128)(2,1)S(1)} %constant_dynamic-update-slice_fusion.refs_0_, ...), custom_call_target="tpu_custom_call" | custom-call | flops 2147483648 | bytes 1572864 | tf_op jit(solution)/shard_map/pallas_call | solution.py:285
  49.5 1.6 %collective-permute-start.9 = (bf16[64,2048]{1,0:T(8,128)(2,1)S(1)}, bf16[64,2048]{1,0:T(8,128)(2,1)S(1)}, u32[]{:S(2)}, u32[]{:S(2)}) collective-permute-start(bf16[64,2048]{1,0:T(8,128)(2,1)S(1)} %get-tuple-element.23), channel_id=1, source_target_pairs={{0,1},{1,0},{2,3},{3,2},{4,5},{5,4},{6,7},{7,6},{8,9},{9,8},{10,11... | collective-permute-start | bytes 786440 | tf_op jit(solution)/shard_map/ppermute | solution.py:421
  51.1 0.0 collective-permute-done.8.refs_3_
  51.2 14.8 %shard_map.58 = (bf16[64,2048]{1,0:T(8,128)(2,1)S(1)}, bf16[64,2048]{1,0:T(8,128)(2,1)S(1)}) custom-call(s32[2]{0:T(128)S(1)} %copy-done.3, s32[2,16]{1,0:T(2,128)S(1)} %copy-done.2, bf16[128,4096]{1,0:T(8,128)(2,1)S(1)} %copy-done, bf16[512,1024]{1,0:T(8,128)(2,1)S(1)} %constant_dynamic-update-slice_fusion.refs_0_, ...), custom_call_target="tpu_custom_call" | custom-call | flops 2147483648 | bytes 1572864 | tf_op jit(solution)/shard_map/pallas_call | solution.py:285
  65.9 0.5 collective-permute-start.10
  66.5 0.0 collective-permute-done.9.refs_2_
  66.5 0.9 %shard_map.59.refs_0_ = bf16[64,8192]{1,0:T(8,128)(2,1)} custom-call(bf16[64,2048]{1,0:T(8,128)(2,1)S(1)} %get-tuple-element.21.refs_0_, bf16[64,2048]{1,0:T(8,128)(2,1)S(1)} %get-tuple-element.22.refs_1_, bf16[64,2048]{1,0:T(8,128)(2,1)S(1)} %collective-permute-done.9.refs_2_), custom_call_target="tpu_custom_call" | custom-call | tf_op jit(solution)/shard_map/pallas_call | solution.py:336
  67.4 6.7 %collective-permute-done.10.refs_1_ = bf16[64,2048]{1,0:T(8,128)(2,1)S(1)} collective-permute-done((bf16[64,2048]{1,0:T(8,128)(2,1)S(1)}, bf16[64,2048]{1,0:T(8,128)(2,1)S(1)}, u32[]{:S(2)}, u32[]{:S(2)}) %collective-permute-start.10) | collective-permute-done | bytes 262176 | tf_op jit(solution)/shard_map/ppermute | solution.py:421
  74.1 0.7 shard_map.60
  (6 shorter events, 0.1 us)
Async XLA Ops:
  0.0 0.9 %copy-start.1 = (bf16[2,64,1024]{2,1,0:T(8,128)(2,1)S(1)}, bf16[2,64,1024]{2,1,0:T(8,128)(2,1)}, u32[]{:S(2)}) copy-start(bf16[2,64,1024]{2,1,0:T(8,128)(2,1)} %cache_ref.1) | copy-start | bytes 786436
  1.0 24.9 %copy-start = (bf16[128,4096]{1,0:T(8,128)(2,1)S(1)}, bf16[128,4096]{1,0:T(8,128)(2,1)}, u32[]{:S(2)}) copy-start(bf16[128,4096]{1,0:T(8,128)(2,1)} %q_ref.5) | copy-start | bytes 3145732
  1.0 24.9 %copy-start.2 = (s32[2,16]{1,0:T(2,128)S(1)}, s32[2,16]{1,0:T(2,128)}, u32[]{:S(2)}) copy-start(s32[2,16]{1,0:T(2,128)} %owner_ref.5) | copy-start | bytes 388
  1.0 24.9 %copy-start.3 = (s32[2]{0:T(128)S(1)}, s32[2]{0:T(128)}, u32[]{:S(2)}) copy-start(s32[2]{0:T(128)} %limit_ref.5) | copy-start | bytes 28
  1.0 10.5 %collective-permute-start.2 = (bf16[64,1024]{1,0:T(8,128)(2,1)S(1)}, bf16[64,1024]{1,0:T(8,128)(2,1)S(1)}, u32[]{:S(2)}, u32[]{:S(2)}) collective-permute-start(bf16[64,1024]{1,0:T(8,128)(2,1)S(1)} %get-tuple-element.16), channel_id=1, source_target_pairs={{0,16},{2,18},{4,20},{6,22},{8,24},{10,26},{12,28},{14,30},{16,0},... | collective-permute-start | bytes 393224 | tf_op jit(solution)/shard_map/ppermute | solution.py:28
  5.1 10.1 %collective-permute-start = (bf16[128,1024]{1,0:T(8,128)(2,1)}, bf16[128,1024]{1,0:T(8,128)(2,1)S(1)}, u32[]{:S(2)}, u32[]{:S(2)}) collective-permute-start(bf16[128,1024]{1,0:T(8,128)(2,1)} %param.6), channel_id=1, source_target_pairs={{0,4},{2,10},{4,0},{6,14},{8,12},{10,2},{12,8},{14,6},{16,20},{18,... | collective-permute-start | bytes 786440 | tf_op jit(solution)/shard_map/ppermute | solution.py:28
  6.6 10.3 %collective-permute-start.1 = (bf16[128,1024]{1,0:T(8,128)(2,1)}, bf16[128,1024]{1,0:T(8,128)(2,1)S(1)}, u32[]{:S(2)}, u32[]{:S(2)}) collective-permute-start(bf16[128,1024]{1,0:T(8,128)(2,1)} %param.6), channel_id=1, source_target_pairs={{0,8},{2,6},{4,12},{6,2},{8,0},{10,14},{12,4},{14,10},{16,24},{18,... | collective-permute-start | bytes 786440 | tf_op jit(solution)/shard_map/ppermute | solution.py:28
  8.1 14.9 %collective-permute-start.4 = (bf16[128,1024]{1,0:T(8,128)(2,1)}, bf16[128,1024]{1,0:T(8,128)(2,1)S(1)}, u32[]{:S(2)}, u32[]{:S(2)}) collective-permute-start(bf16[128,1024]{1,0:T(8,128)(2,1)} %param.6), channel_id=1, source_target_pairs={{0,12},{2,14},{4,8},{6,10},{8,4},{10,6},{12,0},{14,2},{16,28},{18,... | collective-permute-start | bytes 786440 | tf_op jit(solution)/shard_map/ppermute | solution.py:28
  11.5 11.5 %collective-permute-start.3 = (bf16[128,1024]{1,0:T(8,128)(2,1)S(1)}, bf16[128,1024]{1,0:T(8,128)(2,1)S(1)}, u32[]{:S(2)}, u32[]{:S(2)}) collective-permute-start(bf16[128,1024]{1,0:T(8,128)(2,1)S(1)} %pad_maximum_fusion.2), channel_id=1, source_target_pairs={{0,4},{2,10},{4,0},{6,14},{8,12},{10,2},{12,8},{14,6},{16,20},{18,... | collective-permute-start | bytes 786440 | tf_op jit(solution)/shard_map/ppermute | solution.py:28
  23.1 2.7 %collective-permute-start.5 = (bf16[512,1024]{1,0:T(8,128)(2,1)S(1)}, bf16[512,1024]{1,0:T(8,128)(2,1)S(1)}, u32[]{:S(2)}, u32[]{:S(2)}) collective-permute-start(bf16[512,1024]{1,0:T(8,128)(2,1)S(1)} %constant_dynamic-update-slice_fusion.refs_0_), channel_id=1, source_target_pairs={{0,2},{2,0},{4,6},{6,4},{8,10},{10,8},{12,14},{14,12},{16,18},{18,... | collective-permute-start | bytes 3145736 | tf_op jit(solution)/shard_map/ppermute | solution.py:28
  23.3 9.2 %collective-permute-start.6 = (bf16[256,1024]{1,0:T(8,128)(2,1)S(1)}, bf16[256,1024]{1,0:T(8,128)(2,1)S(1)}, u32[]{:S(2)}, u32[]{:S(2)}) collective-permute-start(bf16[256,1024]{1,0:T(8,128)(2,1)S(1)} %pad_maximum_fusion.1), channel_id=1, source_target_pairs={{0,8},{2,6},{4,12},{6,2},{8,0},{10,14},{12,4},{14,10},{16,24},{18,... | collective-permute-start | bytes 1572872 | tf_op jit(solution)/shard_map/ppermute | solution.py:28
  32.6 2.0 %collective-permute-start.7 = (bf16[512,512]{1,0:T(8,128)(2,1)S(1)}, bf16[512,512]{1,0:T(8,128)(2,1)S(1)}, u32[]{:S(2)}, u32[]{:S(2)}) collective-permute-start(bf16[512,512]{1,0:T(8,128)(2,1)S(1)} %get-tuple-element.26), channel_id=1, source_target_pairs={{0,2},{2,0},{4,6},{6,4},{8,10},{10,8},{12,14},{14,12},{16,18},{18,... | collective-permute-start | bytes 1572872 | tf_op jit(solution)/shard_map/ppermute | solution.py:28
  32.7 18.5 %collective-permute-start.8 = (bf16[512,512]{1,0:T(8,128)(2,1)S(1)}, bf16[512,512]{1,0:T(8,128)(2,1)S(1)}, u32[]{:S(2)}, u32[]{:S(2)}) collective-permute-start(bf16[512,512]{1,0:T(8,128)(2,1)S(1)} %get-tuple-element.25), channel_id=1, source_target_pairs={{0,2},{2,0},{4,6},{6,4},{8,10},{10,8},{12,14},{14,12},{16,18},{18,... | collective-permute-start | bytes 1572872 | tf_op jit(solution)/shard_map/ppermute | solution.py:28
  49.5 17.0 %collective-permute-start.9 = (bf16[64,2048]{1,0:T(8,128)(2,1)S(1)}, bf16[64,2048]{1,0:T(8,128)(2,1)S(1)}, u32[]{:S(2)}, u32[]{:S(2)}) collective-permute-start(bf16[64,2048]{1,0:T(8,128)(2,1)S(1)} %get-tuple-element.23), channel_id=1, source_target_pairs={{0,1},{1,0},{2,3},{3,2},{4,5},{5,4},{6,7},{7,6},{8,9},{9,8},{10,11... | collective-permute-start | bytes 786440 | tf_op jit(solution)/shard_map/ppermute | solution.py:421
  65.9 8.1 %collective-permute-start.10 = (bf16[64,2048]{1,0:T(8,128)(2,1)S(1)}, bf16[64,2048]{1,0:T(8,128)(2,1)S(1)}, u32[]{:S(2)}, u32[]{:S(2)}) collective-permute-start(bf16[64,2048]{1,0:T(8,128)(2,1)S(1)} %get-tuple-element.24), channel_id=1, source_target_pairs={{0,1},{1,0},{2,3},{3,2},{4,5},{5,4},{6,7},{7,6},{8,9},{9,8},{10,11... | collective-permute-start | bytes 786440 | tf_op jit(solution)/shard_map/ppermute | solution.py:421

commit v11 on v10

--- a/solution.py
+++ b/solution.py
@@ -30,8 +30,8 @@
     )
 
 
-def after(first, value):
-    return lax.optimization_barrier((first, value))[1]
+def together(*values):
+    return lax.optimization_barrier(values)
 
 
 def shifted(layout, slots):
@@ -48,9 +48,13 @@
 def attend_kernel(spec, layouts, part, block_heads, groups, limit_ref, owner_ref, q_ref, *refs):
     tokens, page, group_size, head_size, orders = spec
     first_phase = len(layouts) == 1
-    key_sets, refs = [(refs[2 * at : 2 * at + 2], layout) for at, layout in enumerate(layouts)], refs[
-        2 * len(layouts) :
-    ]
+    key_sets = []
+    for layout, counts in layouts:
+        halves = []
+        for count in counts:
+            halves.append(refs[:count])
+            refs = refs[count:]
+        key_sets.append((halves, layout))
     (state_sum, state_extra), refs = refs[:2], refs[2:]
     if first_phase:
         page_seen, keys, values = refs[:3]
@@ -59,7 +63,7 @@
         outs = refs[:2]
         page_seen, keys, values = refs[2:5]
         weights, slow_sum, slow_top = refs[5:7], refs[7], refs[8]
-    half_keys = key_sets[0][0][0].shape[0]
+    half_keys = sum(ref.shape[0] for ref in key_sets[0][0][0])
     total_keys = 2 * half_keys
     chunk = min(KEY_CHUNK, total_keys)
     me = lax.axis_index("seq")
@@ -96,11 +100,14 @@
 
     def fill(group, halves, extras):
         for half in range(2):
-            column = (part * groups + group) * 2 * HD % halves[half].shape[1]
-            at = pl.ds(half * half_keys, half_keys)
-            keys[group, :HD, at] = halves[half][:, pl.ds(column, HD)].T
-            keys[group, pl.ds(HD, EXTRA_ROWS), at] = extras[half]
-            values[group, at, :HD] = halves[half][:, pl.ds(column + HD, HD)]
+            start = half * half_keys
+            keys[group, pl.ds(HD, EXTRA_ROWS), pl.ds(start, half_keys)] = extras[half]
+            for ref in halves[half]:
+                column = (part * groups + group) * 2 * HD % ref.shape[1]
+                at = pl.ds(start, ref.shape[0])
+                keys[group, :HD, at] = ref[:, pl.ds(column, HD)].T
+                values[group, at, :HD] = ref[:, pl.ds(column + HD, HD)]
+                start += ref.shape[0]
         rest = HD - EXTRA_ROWS
         keys[group, HD + EXTRA_ROWS :, :] = jnp.zeros((rest, total_keys), jnp.bfloat16)
         values[group, :, HD:] = jnp.ones((total_keys, HD), jnp.bfloat16)
@@ -248,15 +255,17 @@
 
 def attend(limits, owners, queries, part, parts, key_sets, spec, state):
     tokens, _, _, head_size = spec[:4]
-    half_keys = key_sets[0][0].shape[0]
+    half_keys = sum(piece.shape[0] for piece in key_sets[0][0])
     total_keys = 2 * half_keys
     columns = queries.shape[1] // parts
     groups = columns // (PER_GROUP * HD)
     block_heads = 4
     block = block_heads * tokens
     rows = PER_GROUP * groups * tokens
-    pieces = [piece for mine, theirs, _ in key_sets for piece in (mine, theirs)]
-    layouts = tuple(tuple(layout) for _, _, layout in key_sets)
+    pieces = [piece for mine, theirs, _ in key_sets for piece in mine + theirs]
+    layouts = tuple(
+        (tuple(layout), (len(mine), len(theirs))) for mine, theirs, layout in key_sets
+    )
     operands = queries.size * 2 + sum(piece.size for piece in pieces) * 2 + rows * HD * 12
     scratch = groups * total_keys * HD * 8 + block * total_keys * 4 + rows * HD * 12
     whole = pl.BlockSpec(memory_space=pltpu.VMEM)
@@ -369,6 +378,9 @@
     def send(rows, stage):
         return hop(rows, tuple(order[stage] for order in orders))
 
+    def swap_cores(pieces):
+        return hop(pieces[0] if len(pieces) == 1 else jnp.concatenate(pieces, axis=0), (1, 1))
+
     def whole_layout(layout):
         for stage in range(stages):
             layout = layout + shifted(layout, 1 << stage)
@@ -380,39 +392,36 @@
     other_page, own_page = pick(prefix_cache, group_size)
     crossed = hop(other_page, (group_size, group_size))
 
+    span_early = send(span_kv, stages - 1)
     span_forward = send(span_kv, 0)
-    span_early = send(span_kv, stages - 1)
-    if stages == 2:
-        across = sum(bits)
-        span_late = hop(span_kv, (across, across))
     for stage in range(1, stages - 1):
         seen = jnp.concatenate([span_kv, span_forward], axis=0)
         span_forward = jnp.concatenate([span_forward, send(seen, stage)], axis=0)
-    if stages != 2:
-        span_late = send(span_forward, stages - 1)
-    span = jnp.concatenate([span_kv, span_forward], axis=0)
-    crossed = after(span, crossed)
-    pages = jnp.concatenate([own_page, crossed], axis=0)
-    pages = jnp.concatenate([pages, send(pages, 0)], axis=0)
-    span_late = after(pages, span_late)
-    span = jnp.concatenate([span, span_early, span_late], axis=0)
-    span_swapped = hop(span, (1, 1))
+    span_late = send(span_forward, stages - 1)
+    span_forward, crossed = together(span_forward, crossed)
+    pages = [jnp.concatenate([own_page, crossed], axis=0)]
+    pages.append(send(pages[0], 0))
+    span_early, span_late = together(span_early, span_late)
+    pages[1], span_late = together(pages[1], span_late)
+    span = [jnp.concatenate([span_kv, span_forward, span_early, span_late], axis=0)]
+    span_swapped = [swap_cores(span)]
 
     spec = (tokens, page, group_size, head_size, orders)
     common = (prefix_len, block_owner, span_query)
     span_set = (span, span_swapped, span_layout)
     state = attend(*common, 0, 1, [span_set], spec, None)
 
-    for stage in range(1, stages):
-        received = send(pages, stage)
-        if stage == stages - 1:
-            received = after(state, received)
-        pages = jnp.concatenate([pages, received], axis=0)
-    columns = pages.shape[1] // parts
+    for stage in range(1, stages - 1):
+        pages.append(send(jnp.concatenate(pages, axis=0), stage))
+    columns = span_kv.shape[1] // parts
+    cuts = [slice(part * columns, (part + 1) * columns) for part in range(parts)]
+    held = [jnp.concatenate([piece[:, cut] for piece in pages], axis=0) for cut in cuts]
+    arrived = [send(rows, stages - 1) for rows in held]
     results = []
     for part in range(parts):
-        theirs = hop(pages[:, part * columns : (part + 1) * columns], (1, 1))
-        page_set = (pages, theirs, page_layout)
+        arrived[part], state = together(arrived[part], state)
+        mine = [held[part], arrived[part]]
+        page_set = (mine, [swap_cores(mine)], page_layout)
         results.append(attend(*common, part, parts, [span_set, page_set], spec, state))
     if head_size != 2:
         rows = jnp.concatenate([jnp.concatenate(pair, axis=0) for pair in results], axis=1)

time: 75.1 us -> 72.5 us (0.965)
  waiting for transfers between devices: 21.9 us -> 19.9 us
    ppermute x9 -> x10, waiting for transfers between devices: 15.2 us -> 13 us  [hop(): lax.ppermute(value, 'seq', [(source, source ^ bit_of_core[source % 2]) fo...]
    ppermute x9 -> x10, starting transfers between devices: 11.1 us -> 11.3 us  [hop(): lax.ppermute(value, 'seq', [(source, source ^ bit_of_core[source % 2]) fo...]
    unnamed x11 -> x12, local copies, waits for them, and re-layouts: 1.96 us -> 1.97 us
  transfers between devices with their start and end apart: 11 -> 12, of which waited for: 8 -> 6; matrix products, arithmetic and copies ran while one was open for 1% -> 2% of each run, Pallas kernels for 49% -> 50%
where the time goes in v11:
time: 72.5 us; the launch traced here: 73 us
  Pallas kernels  37.2 us (51%)
  waiting for transfers between devices  19.9 us (27%)
  starting transfers between devices  13.5 us (19%)
  local copies, waits for them, and re-layouts  2.04 us (3%)
    pallas_call x3, Pallas kernels, attend(): pl.pallas_call(functools.partial(attend_kernel, spec, layouts, part, bloc...  35.6 us
    ppermute x10, waiting for transfers between devices, hop(): lax.ppermute(value, 'seq', [(source, source ^ bit_of_core[source % 2]) fo...  13 us
    ppermute x10, starting transfers between devices, hop(): lax.ppermute(value, 'seq', [(source, source ^ bit_of_core[source % 2]) fo...  11.3 us
    ppermute x2, waiting for transfers between devices, body(): lax.ppermute(pair[1], 'head', [(0, 1), (1, 0)])  6.9 us
    ppermute x2, starting transfers between devices, body(): lax.ppermute(pair[1], 'head', [(0, 1), (1, 0)])  2.16 us
    unnamed x12, local copies, waits for them, and re-layouts  1.97 us
    pallas_call x2, Pallas kernels, join(): pl.pallas_call(functools.partial(join_kernel, spots, len(pieces)), out_sh...  1.61 us
  transfers between devices with their start and end apart: 12, of which 6 were waited for; matrix products, arithmetic and copies ran while one was open for 2% of the time, Pallas kernels for 50%

profile of v11, /device:TPU:0, one launch (start us, length us, event | category | flops | bytes accessed | tf_op | source)
XLA Modules:
  0.0 73.0 jit_solution(12945467814611026578)
XLA Ops:
  0.0 0.0 copy-start
  0.0 2.9 %collective-permute-start = (bf16[128,1024]{1,0:T(8,128)(2,1)}, bf16[128,1024]{1,0:T(8,128)(2,1)S(1)}, u32[]{:S(2)}, u32[]{:S(2)}) collective-permute-start(bf16[128,1024]{1,0:T(8,128)(2,1)} %param.6), channel_id=1, source_target_pairs={{0,4},{2,10},{4,0},{6,14},{8,12},{10,2},{12,8},{14,6},{16,20},{18,... | collective-permute-start | bytes 786440 | tf_op jit(solution)/shard_map/ppermute | solution.py:28
  2.9 0.0 copy-start.1
  2.9 0.9 %copy-done.1 = bf16[2,64,1024]{2,1,0:T(8,128)(2,1)S(1)} copy-done((bf16[2,64,1024]{2,1,0:T(8,128)(2,1)S(1)}, bf16[2,64,1024]{2,1,0:T(8,128)(2,1)}, u32[]{:S(2)}) %copy-start.1) | copy-done | bytes 262168
  3.9 0.0 copy-start.2
  3.9 0.0 copy-start.3
  3.9 2.7 %collective-permute-start.1 = (bf16[64,1024]{1,0:T(8,128)(2,1)S(1)}, bf16[64,1024]{1,0:T(8,128)(2,1)S(1)}, u32[]{:S(2)}, u32[]{:S(2)}) collective-permute-start(bf16[64,1024]{1,0:T(8,128)(2,1)S(1)} %get-tuple-element.25), channel_id=1, source_target_pairs={{0,16},{2,18},{4,20},{6,22},{8,24},{10,26},{12,28},{14,30},{16,0},... | collective-permute-start | bytes 393224 | tf_op jit(solution)/shard_map/ppermute | solution.py:28
  6.6 1.6 %collective-permute-start.2 = (bf16[128,1024]{1,0:T(8,128)(2,1)}, bf16[128,1024]{1,0:T(8,128)(2,1)S(1)}, u32[]{:S(2)}, u32[]{:S(2)}) collective-permute-start(bf16[128,1024]{1,0:T(8,128)(2,1)} %param.6), channel_id=1, source_target_pairs={{0,8},{2,6},{4,12},{6,2},{8,0},{10,14},{12,4},{14,10},{16,24},{18,... | collective-permute-start | bytes 786440 | tf_op jit(solution)/shard_map/ppermute | solution.py:28
  8.2 4.7 %collective-permute-done.1 = bf16[64,1024]{1,0:T(8,128)(2,1)S(1)} collective-permute-done((bf16[64,1024]{1,0:T(8,128)(2,1)S(1)}, bf16[64,1024]{1,0:T(8,128)(2,1)S(1)}, u32[]{:S(2)}, u32[]{:S(2)}) %collective-permute-start.1) | collective-permute-done | bytes 131104 | tf_op jit(solution)/shard_map/ppermute | solution.py:28
  12.8 0.0 collective-permute-done
  12.8 0.0 collective-permute-start.3
  12.9 1.6 %collective-permute-start.4 = (bf16[128,1024]{1,0:T(8,128)(2,1)S(1)}, bf16[128,1024]{1,0:T(8,128)(2,1)S(1)}, u32[]{:S(2)}, u32[]{:S(2)}) collective-permute-start(bf16[128,1024]{1,0:T(8,128)(2,1)S(1)} %constant_dynamic-update-slice_fusion), channel_id=1, source_target_pairs={{0,4},{2,10},{4,0},{6,14},{8,12},{10,2},{12,8},{14,6},{16,20},{18,... | collective-permute-start | bytes 786440 | tf_op jit(solution)/shard_map/ppermute | solution.py:28
  14.4 1.0 %constant_dynamic-update-slice_fusion.5 = bf16[512,1024]{1,0:T(8,128)(2,1)S(1)} fusion(bf16[128,1024]{1,0:T(8,128)(2,1)} %param.6), kind=kLoop, calls=%fused_computation.9 | loop fusion | bytes 524288
  15.4 0.0 collective-permute-done.2
  15.4 6.3 %collective-permute-done.3 = bf16[128,1024]{1,0:T(8,128)(2,1)S(1)} collective-permute-done((bf16[128,1024]{1,0:T(8,128)(2,1)S(1)}, bf16[128,1024]{1,0:T(8,128)(2,1)S(1)}, u32[]{:S(2)}, u32[]{:S(2)}) %collective-permute-start.3) | collective-permute-done | bytes 262176 | tf_op jit(solution)/shard_map/ppermute | solution.py:28
  21.7 0.0 collective-permute-done.4
  21.8 0.2 collective-permute-start.5
  22.0 0.1 collective-permute-start.6
  22.2 2.1 %collective-permute-start.8 = (bf16[256,512]{1,0:T(8,128)(2,1)S(1)}, bf16[256,512]{1,0:T(8,128)(2,1)S(1)}, u32[]{:S(2)}, u32[]{:S(2)}) collective-permute-start(bf16[256,512]{1,0:T(8,128)(2,1)S(1)} %pad_maximum_fusion.3.refs_2_), channel_id=1, source_target_pairs={{0,8},{2,6},{4,12},{6,2},{8,0},{10,14},{12,4},{14,10},{16,24},{18,... | collective-permute-start | bytes 786440 | tf_op jit(solution)/shard_map/ppermute | solution.py:28
  24.2 0.3 collective-permute-done.5.refs_1_
  24.5 0.0 copy-done
  24.5 0.0 copy-done.2
  24.5 0.0 copy-done.3
  24.5 6.0 %shard_map.56 = (f32[4096,256]{1,0:T(8,128)S(1)}, bf16[4096,128]{1,0:T(8,128)(2,1)S(1)}) custom-call(s32[2]{0:T(128)S(1)} %copy-done.3, s32[2,16]{1,0:T(2,128)S(1)} %copy-done.2, bf16[128,4096]{1,0:T(8,128)(2,1)S(1)} %copy-done, bf16[512,1024]{1,0:T(8,128)(2,1)S(1)} %constant_dynamic-update-slice_fusion.2.refs_0_, ...), custom_call_target="tpu_custom_call" | custom-call | flops 4294967296 | bytes 3145728 | tf_op jit(solution)/shard_map/pallas_call | solution.py:294
  30.5 0.0 collective-permute-done.6.refs_3_
  30.6 0.2 collective-permute-start.7
  30.8 0.5 collective-permute-done.8.refs_3_
  31.3 0.1 collective-permute-start.9
  31.4 1.1 %collective-permute-done.7.refs_4_ = bf16[512,512]{1,0:T(8,128)(2,1)S(1)} collective-permute-done((bf16[512,512]{1,0:T(8,128)(2,1)S(1)}, bf16[512,512]{1,0:T(8,128)(2,1)S(1)}, u32[]{:S(2)}, u32[]{:S(2)}) %collective-permute-start.7) | collective-permute-done | bytes 524320 | tf_op jit(solution)/shard_map/ppermute | solution.py:28
  32.5 14.9 %shard_map.57 = (bf16[64,2048]{1,0:T(8,128)(2,1)S(1)}, bf16[64,2048]{1,0:T(8,128)(2,1)S(1)}) custom-call(s32[2]{0:T(128)S(1)} %copy-done.3, s32[2,16]{1,0:T(2,128)S(1)} %copy-done.2, bf16[128,4096]{1,0:T(8,128)(2,1)S(1)} %copy-done, bf16[512,1024]{1,0:T(8,128)(2,1)S(1)} %constant_dynamic-update-slice_fusion.2.refs_0_, ...), custom_call_target="tpu_custom_call" | custom-call | flops 2147483648 | bytes 1572864 | tf_op jit(solution)/shard_map/pallas_call | solution.py:294
  47.5 1.8 %collective-permute-start.10 = (bf16[64,2048]{1,0:T(8,128)(2,1)S(1)}, bf16[64,2048]{1,0:T(8,128)(2,1)S(1)}, u32[]{:S(2)}, u32[]{:S(2)}) collective-permute-start(bf16[64,2048]{1,0:T(8,128)(2,1)S(1)} %get-tuple-element.43), channel_id=1, source_target_pairs={{0,1},{1,0},{2,3},{3,2},{4,5},{5,4},{6,7},{7,6},{8,9},{9,8},{10,11... | collective-permute-start | bytes 786440 | tf_op jit(solution)/shard_map/ppermute | solution.py:430
  49.3 0.0 collective-permute-done.9.refs_4_
  49.3 14.7 %shard_map.58 = (bf16[64,2048]{1,0:T(8,128)(2,1)S(1)}, bf16[64,2048]{1,0:T(8,128)(2,1)S(1)}) custom-call(s32[2]{0:T(128)S(1)} %copy-done.3, s32[2,16]{1,0:T(2,128)S(1)} %copy-done.2, bf16[128,4096]{1,0:T(8,128)(2,1)S(1)} %copy-done, bf16[512,1024]{1,0:T(8,128)(2,1)S(1)} %constant_dynamic-update-slice_fusion.2.refs_0_, ...), custom_call_target="tpu_custom_call" | custom-call | flops 2147483648 | bytes 1572864 | tf_op jit(solution)/shard_map/pallas_call | solution.py:294
  64.0 0.3 collective-permute-start.11
  64.4 0.0 collective-permute-done.10.refs_2_
  64.4 0.9 %shard_map.59.refs_0_ = bf16[64,8192]{1,0:T(8,128)(2,1)} custom-call(bf16[64,2048]{1,0:T(8,128)(2,1)S(1)} %get-tuple-element.38.refs_0_, bf16[64,2048]{1,0:T(8,128)(2,1)S(1)} %get-tuple-element.42.refs_1_, bf16[64,2048]{1,0:T(8,128)(2,1)S(1)} %collective-permute-done.10.refs_2_), custom_call_target="tpu_custom_call" | custom-call | tf_op jit(solution)/shard_map/pallas_call | solution.py:345
  65.3 6.9 %collective-permute-done.11.refs_1_ = bf16[64,2048]{1,0:T(8,128)(2,1)S(1)} collective-permute-done((bf16[64,2048]{1,0:T(8,128)(2,1)S(1)}, bf16[64,2048]{1,0:T(8,128)(2,1)S(1)}, u32[]{:S(2)}, u32[]{:S(2)}) %collective-permute-start.11) | collective-permute-done | bytes 262176 | tf_op jit(solution)/shard_map/ppermute | solution.py:430
  72.2 0.7 shard_map.60
  (12 shorter events, 0.2 us)
Async XLA Ops:
  0.0 24.5 %copy-start = (bf16[128,4096]{1,0:T(8,128)(2,1)S(1)}, bf16[128,4096]{1,0:T(8,128)(2,1)}, u32[]{:S(2)}) copy-start(bf16[128,4096]{1,0:T(8,128)(2,1)} %q_ref.5) | copy-start | bytes 3145732
  0.0 12.8 %collective-permute-start = (bf16[128,1024]{1,0:T(8,128)(2,1)}, bf16[128,1024]{1,0:T(8,128)(2,1)S(1)}, u32[]{:S(2)}, u32[]{:S(2)}) collective-permute-start(bf16[128,1024]{1,0:T(8,128)(2,1)} %param.6), channel_id=1, source_target_pairs={{0,4},{2,10},{4,0},{6,14},{8,12},{10,2},{12,8},{14,6},{16,20},{18,... | collective-permute-start | bytes 786440 | tf_op jit(solution)/shard_map/ppermute | solution.py:28
  2.9 0.9 %copy-start.1 = (bf16[2,64,1024]{2,1,0:T(8,128)(2,1)S(1)}, bf16[2,64,1024]{2,1,0:T(8,128)(2,1)}, u32[]{:S(2)}) copy-start(bf16[2,64,1024]{2,1,0:T(8,128)(2,1)} %cache_ref.1) | copy-start | bytes 786436
  3.9 20.6 %copy-start.2 = (s32[2,16]{1,0:T(2,128)S(1)}, s32[2,16]{1,0:T(2,128)}, u32[]{:S(2)}) copy-start(s32[2,16]{1,0:T(2,128)} %owner_ref.5) | copy-start | bytes 388
  3.9 20.6 %copy-start.3 = (s32[2]{0:T(128)S(1)}, s32[2]{0:T(128)}, u32[]{:S(2)}) copy-start(s32[2]{0:T(128)} %limit_ref.5) | copy-start | bytes 28
  3.9 8.9 %collective-permute-start.1 = (bf16[64,1024]{1,0:T(8,128)(2,1)S(1)}, bf16[64,1024]{1,0:T(8,128)(2,1)S(1)}, u32[]{:S(2)}, u32[]{:S(2)}) collective-permute-start(bf16[64,1024]{1,0:T(8,128)(2,1)S(1)} %get-tuple-element.25), channel_id=1, source_target_pairs={{0,16},{2,18},{4,20},{6,22},{8,24},{10,26},{12,28},{14,30},{16,0},... | collective-permute-start | bytes 393224 | tf_op jit(solution)/shard_map/ppermute | solution.py:28
  6.6 8.8 %collective-permute-start.2 = (bf16[128,1024]{1,0:T(8,128)(2,1)}, bf16[128,1024]{1,0:T(8,128)(2,1)S(1)}, u32[]{:S(2)}, u32[]{:S(2)}) collective-permute-start(bf16[128,1024]{1,0:T(8,128)(2,1)} %param.6), channel_id=1, source_target_pairs={{0,8},{2,6},{4,12},{6,2},{8,0},{10,14},{12,4},{14,10},{16,24},{18,... | collective-permute-start | bytes 786440 | tf_op jit(solution)/shard_map/ppermute | solution.py:28
  12.8 8.9 %collective-permute-start.3 = (bf16[128,1024]{1,0:T(8,128)(2,1)S(1)}, bf16[128,1024]{1,0:T(8,128)(2,1)S(1)}, u32[]{:S(2)}, u32[]{:S(2)}) collective-permute-start(bf16[128,1024]{1,0:T(8,128)(2,1)S(1)} %collective-permute-done), channel_id=1, source_target_pairs={{0,8},{2,6},{4,12},{6,2},{8,0},{10,14},{12,4},{14,10},{16,24},{18,... | collective-permute-start | bytes 786440 | tf_op jit(solution)/shard_map/ppermute | solution.py:28
  12.9 8.9 %collective-permute-start.4 = (bf16[128,1024]{1,0:T(8,128)(2,1)S(1)}, bf16[128,1024]{1,0:T(8,128)(2,1)S(1)}, u32[]{:S(2)}, u32[]{:S(2)}) collective-permute-start(bf16[128,1024]{1,0:T(8,128)(2,1)S(1)} %constant_dynamic-update-slice_fusion), channel_id=1, source_target_pairs={{0,4},{2,10},{4,0},{6,14},{8,12},{10,2},{12,8},{14,6},{16,20},{18,... | collective-permute-start | bytes 786440 | tf_op jit(solution)/shard_map/ppermute | solution.py:28
  21.8 2.7 %collective-permute-start.5 = (bf16[512,1024]{1,0:T(8,128)(2,1)S(1)}, bf16[512,1024]{1,0:T(8,128)(2,1)S(1)}, u32[]{:S(2)}, u32[]{:S(2)}) collective-permute-start(bf16[512,1024]{1,0:T(8,128)(2,1)S(1)} %constant_dynamic-update-slice_fusion.2.refs_0_), channel_id=1, source_target_pairs={{0,2},{2,0},{4,6},{6,4},{8,10},{10,8},{12,14},{14,12},{16,18},{18,... | collective-permute-start | bytes 3145736 | tf_op jit(solution)/shard_map/ppermute | solution.py:28
  22.0 8.5 %collective-permute-start.6 = (bf16[256,512]{1,0:T(8,128)(2,1)S(1)}, bf16[256,512]{1,0:T(8,128)(2,1)S(1)}, u32[]{:S(2)}, u32[]{:S(2)}) collective-permute-start(bf16[256,512]{1,0:T(8,128)(2,1)S(1)} %pad_maximum_fusion.2.refs_2_), channel_id=1, source_target_pairs={{0,8},{2,6},{4,12},{6,2},{8,0},{10,14},{12,4},{14,10},{16,24},{18,... | collective-permute-start | bytes 786440 | tf_op jit(solution)/shard_map/ppermute | solution.py:28
  22.2 9.1 %collective-permute-start.8 = (bf16[256,512]{1,0:T(8,128)(2,1)S(1)}, bf16[256,512]{1,0:T(8,128)(2,1)S(1)}, u32[]{:S(2)}, u32[]{:S(2)}) collective-permute-start(bf16[256,512]{1,0:T(8,128)(2,1)S(1)} %pad_maximum_fusion.3.refs_2_), channel_id=1, source_target_pairs={{0,8},{2,6},{4,12},{6,2},{8,0},{10,14},{12,4},{14,10},{16,24},{18,... | collective-permute-start | bytes 786440 | tf_op jit(solution)/shard_map/ppermute | solution.py:28
  30.6 2.0 %collective-permute-start.7 = (bf16[512,512]{1,0:T(8,128)(2,1)S(1)}, bf16[512,512]{1,0:T(8,128)(2,1)S(1)}, u32[]{:S(2)}, u32[]{:S(2)}) collective-permute-start(bf16[512,512]{1,0:T(8,128)(2,1)S(1)} %pad_maximum_fusion), channel_id=1, source_target_pairs={{0,2},{2,0},{4,6},{6,4},{8,10},{10,8},{12,14},{14,12},{16,18},{18,... | collective-permute-start | bytes 1572872 | tf_op jit(solution)/shard_map/ppermute | solution.py:28
  31.3 18.0 %collective-permute-start.9 = (bf16[512,512]{1,0:T(8,128)(2,1)S(1)}, bf16[512,512]{1,0:T(8,128)(2,1)S(1)}, u32[]{:S(2)}, u32[]{:S(2)}) collective-permute-start(bf16[512,512]{1,0:T(8,128)(2,1)S(1)} %pad_maximum_fusion.1), channel_id=1, source_target_pairs={{0,2},{2,0},{4,6},{6,4},{8,10},{10,8},{12,14},{14,12},{16,18},{18,... | collective-permute-start | bytes 1572872 | tf_op jit(solution)/shard_map/ppermute | solution.py:28
  47.5 16.9 %collective-permute-start.10 = (bf16[64,2048]{1,0:T(8,128)(2,1)S(1)}, bf16[64,2048]{1,0:T(8,128)(2,1)S(1)}, u32[]{:S(2)}, u32[]{:S(2)}) collective-permute-start(bf16[64,2048]{1,0:T(8,128)(2,1)S(1)} %get-tuple-element.43), channel_id=1, source_target_pairs={{0,1},{1,0},{2,3},{3,2},{4,5},{5,4},{6,7},{7,6},{8,9},{9,8},{10,11... | collective-permute-start | bytes 786440 | tf_op jit(solution)/shard_map/ppermute | solution.py:430
  64.0 8.1 %collective-permute-start.11 = (bf16[64,2048]{1,0:T(8,128)(2,1)S(1)}, bf16[64,2048]{1,0:T(8,128)(2,1)S(1)}, u32[]{:S(2)}, u32[]{:S(2)}) collective-permute-start(bf16[64,2048]{1,0:T(8,128)(2,1)S(1)} %get-tuple-element.44), channel_id=1, source_target_pairs={{0,1},{1,0},{2,3},{3,2},{4,5},{5,4},{6,7},{7,6},{8,9},{9,8},{10,11... | collective-permute-start | bytes 786440 | tf_op jit(solution)/shard_map/ppermute | solution.py:430

commit v12 on v11

--- a/solution.py
+++ b/solution.py
@@ -15,8 +15,7 @@
 PER_GROUP = QH // KVH
 EXP2_SCALE = HD ** (-0.5) * math.log2(math.e)
 MASKED = -1e30
-KEY_CHUNK = 512
-EXTRA_ROWS = 16
+KEY_CHUNK = 256
 SHIFT_STEP = 32.0
 LOWEST_TOTAL = 1e-20
 HIGHEST_TOTAL = 1e30
@@ -63,9 +62,7 @@
         outs = refs[:2]
         page_seen, keys, values = refs[2:5]
         weights, slow_sum, slow_top = refs[5:7], refs[7], refs[8]
-    half_keys = sum(ref.shape[0] for ref in key_sets[0][0][0])
-    total_keys = 2 * half_keys
-    chunk = min(KEY_CHUNK, total_keys)
+    chunk = KEY_CHUNK
     me = lax.axis_index("seq")
     my_head = lax.axis_index("head")
     request = me // group_size
@@ -78,12 +75,9 @@
     if not first_phase:
         lax.fori_loop(0, owner_ref.shape[1], note_page, 0)
 
-    def extra_rows(layout, half):
-        row = lax.broadcasted_iota(jnp.int32, (EXTRA_ROWS, half_keys), 0)
-        key = lax.broadcasted_iota(jnp.int32, (EXTRA_ROWS, half_keys), 1)
+    def extra_columns(layout, half):
         holder = me ^ half
-        start = 0
-        seen = key < 0
+        pieces = []
         for slot, kind, rows in layout:
             source = holder ^ jnp.where(holder % 2 == 0, offsets[0][slot], offsets[1][slot])
             if kind == SPAN_ROWS:
@@ -92,25 +86,32 @@
                 count = page_seen[source]
             else:
                 count = page_seen[source ^ group_size]
-            seen = seen | ((key >= start) & (key < start + count))
-            start += rows
-        mask = jnp.where(seen, jnp.float32(0.0), jnp.float32(MASKED))
-        extra = jnp.where(row == 0, mask, jnp.where(row == 1, jnp.float32(1.0), jnp.float32(0.0)))
-        return extra.astype(jnp.bfloat16)
+            row = lax.broadcasted_iota(jnp.int32, (rows, HD), 0)
+            column = lax.broadcasted_iota(jnp.int32, (rows, HD), 1)
+            mask = jnp.where(row < count, jnp.float32(0.0), jnp.float32(MASKED))
+            one = jnp.where(column == 1, jnp.float32(1.0), jnp.float32(0.0))
+            pieces.append(jnp.where(column == 0, mask, one).astype(jnp.bfloat16))
+        return pieces
+
+    def key_count(halves):
+        return sum(ref.shape[0] for half in halves for ref in half)
 
     def fill(group, halves, extras):
+        total_keys = key_count(halves)
+        half_keys = total_keys // 2
         for half in range(2):
             start = half * half_keys
-            keys[group, pl.ds(HD, EXTRA_ROWS), pl.ds(start, half_keys)] = extras[half]
+            for piece in extras[half]:
+                keys[group, pl.ds(start, piece.shape[0]), HD:] = piece
+                start += piece.shape[0]
+            start = half * half_keys
             for ref in halves[half]:
                 column = (part * groups + group) * 2 * HD % ref.shape[1]
                 at = pl.ds(start, ref.shape[0])
-                keys[group, :HD, at] = ref[:, pl.ds(column, HD)].T
+                keys[group, at, :HD] = ref[:, pl.ds(column, HD)]
                 values[group, at, :HD] = ref[:, pl.ds(column + HD, HD)]
                 start += ref.shape[0]
-        rest = HD - EXTRA_ROWS
-        keys[group, HD + EXTRA_ROWS :, :] = jnp.zeros((rest, total_keys), jnp.bfloat16)
-        values[group, :, HD:] = jnp.ones((total_keys, HD), jnp.bfloat16)
+        values[group, :total_keys, HD:] = jnp.ones((total_keys, HD), jnp.bfloat16)
 
     block = block_heads * tokens
     blocks_a_group = PER_GROUP // block_heads
@@ -128,8 +129,11 @@
         return jnp.concatenate([q_ref[:, column] for column in columns], axis=0)
 
     def scores_of(query, group, start, is_span):
-        made = jnp.dot(
-            query, keys[group, :, pl.ds(start, chunk)], preferred_element_type=jnp.float32
+        made = lax.dot_general(
+            query,
+            keys[group, pl.ds(start, chunk), :],
+            (((1,), (1,)), ((), ())),
+            preferred_element_type=jnp.float32,
         )
         if start == 0 and is_span:
             own = jnp.where(causal, made[:, :tokens], MASKED)
@@ -150,15 +154,16 @@
                 outs[1][:, column] = one[kept:]
 
     halves, layout = key_sets[-1]
-    extras = [extra_rows(layout, half) for half in range(2)]
+    total_keys = key_count(halves)
+    extras = [extra_columns(layout, half) for half in range(2)]
     longest = [None] * groups
 
     def begin(group):
         fill(group, halves, extras)
         if first_phase:
-            key = keys[group, :HD, :].astype(jnp.float32)
-            squares = jnp.sum(key * key, axis=0, keepdims=True)
-            longest[group] = jnp.max(squares, axis=1, keepdims=True)
+            key = keys[group, :total_keys, :HD].astype(jnp.float32)
+            squares = jnp.sum(key * key, axis=1, keepdims=True)
+            longest[group] = jnp.max(squares, axis=0, keepdims=True)
 
     def weigh(index):
         group = index // blocks_a_group
@@ -182,7 +187,9 @@
     def finish(index, extremes):
         group = index // blocks_a_group
         summed = jnp.dot(
-            weights[index % 2][...], values[group], preferred_element_type=jnp.float32
+            weights[index % 2][:, :total_keys],
+            values[group, :total_keys, :],
+            preferred_element_type=jnp.float32,
         )
         rows = pl.ds(index * block, block)
         if first_phase:
@@ -209,7 +216,7 @@
     @pl.when((jnp.min(extremes[0]) < LOWEST_TOTAL) | (jnp.max(extremes[1]) > HIGHEST_TOTAL))
     def exact():
         for number, (halves, layout) in enumerate(key_sets):
-            extras = [extra_rows(layout, half) for half in range(2)]
+            extras = [extra_columns(layout, half) for half in range(2)]
             for group in range(groups):
                 fill(group, halves, extras)
 
@@ -225,14 +232,14 @@
                     top = slow_top[rows, :]
                     summed = slow_sum[rows, :]
                 best = top
-                for start in range(0, total_keys, chunk):
+                for start in range(0, key_count(halves), chunk):
                     made = scores_of(query, group, start, number == 0)
                     for at in range(0, chunk, HD):
                         best = jnp.maximum(best, made[:, at : at + HD])
                 best = jnp.broadcast_to(jnp.max(best, axis=1, keepdims=True), (block, HD))
                 fade = jnp.exp2((top - best) * EXP2_SCALE)
                 summed = summed * jnp.concatenate([fade, fade], axis=1)
-                for start in range(0, total_keys, chunk):
+                for start in range(0, key_count(halves), chunk):
                     made = scores_of(query, group, start, number == 0)
                     parts = [
                         jnp.exp2((made[:, at : at + HD] - best) * EXP2_SCALE)
@@ -255,8 +262,7 @@
 
 def attend(limits, owners, queries, part, parts, key_sets, spec, state):
     tokens, _, _, head_size = spec[:4]
-    half_keys = sum(piece.shape[0] for piece in key_sets[0][0])
-    total_keys = 2 * half_keys
+    total_keys = 2 * max(sum(piece.shape[0] for piece in mine) for mine, _, _ in key_sets)
     columns = queries.shape[1] // parts
     groups = columns // (PER_GROUP * HD)
     block_heads = 4
@@ -273,7 +279,7 @@
     kept = tokens // head_size
     scratch_shapes = [
         pltpu.SMEM((owners.shape[1],), jnp.int32),
-        pltpu.VMEM((groups, 2 * HD, total_keys), jnp.bfloat16),
+        pltpu.VMEM((groups, total_keys, 2 * HD), jnp.bfloat16),
         pltpu.VMEM((groups, total_keys, 2 * HD), jnp.bfloat16),
     ] + [pltpu.VMEM((block, total_keys), jnp.bfloat16)] * 2
     if state is None:
@@ -323,6 +329,21 @@
     )(cache)
 
 
+def hold_kernel(from_ref, to_ref):
+    to_ref[...] = from_ref[...]
+
+
+def hold(value):
+    whole = pl.BlockSpec(memory_space=pltpu.VMEM)
+    return pl.pallas_call(
+        hold_kernel,
+        out_shape=jax.ShapeDtypeStruct(value.shape, value.dtype),
+        in_specs=[whole],
+        out_specs=whole,
+        compiler_params=pltpu.CompilerParams(vmem_limit_bytes=8 << 20),
+    )(value)
+
+
 def join_kernel(spots, count, *refs):
     parts, (out_ref, done) = refs[len(refs) - 2 - count : -2], refs[-2:]
     side = out_ref.shape[1] // 2
@@ -388,6 +409,8 @@
 
     span_layout = whole_layout([(0, SPAN_ROWS, tokens)])
     page_layout = whole_layout([(0, OWN_PAGE, page), (0, CROSSED_PAGE, page)])
+    near_count = (1 << (stages - 1)) + 1
+    near_layout, far_layout = span_layout[:near_count], span_layout[near_count:] + page_layout
 
     other_page, own_page = pick(prefix_cache, group_size)
     crossed = hop(other_page, (group_size, group_size))
@@ -398,19 +421,17 @@
         seen = jnp.concatenate([span_kv, span_forward], axis=0)
         span_forward = jnp.concatenate([span_forward, send(seen, stage)], axis=0)
     span_late = send(span_forward, stages - 1)
-    span_forward, crossed = together(span_forward, crossed)
+    span_forward, span_own, crossed = together(span_forward, hold(span_kv), crossed)
     pages = [jnp.concatenate([own_page, crossed], axis=0)]
     pages.append(send(pages[0], 0))
-    span_early, span_late = together(span_early, span_late)
-    pages[1], span_late = together(pages[1], span_late)
-    span = [jnp.concatenate([span_kv, span_forward, span_early, span_late], axis=0)]
-    span_swapped = [swap_cores(span)]
 
     spec = (tokens, page, group_size, head_size, orders)
     common = (prefix_len, block_owner, span_query)
-    span_set = (span, span_swapped, span_layout)
-    state = attend(*common, 0, 1, [span_set], spec, None)
-
+    near = [span_own, span_forward, span_early]
+    near_set = (near, [swap_cores(near)], near_layout)
+    state = attend(*common, 0, 1, [near_set], spec, None)
+
+    pages[1], span_late, state = together(pages[1], span_late, state)
     for stage in range(1, stages - 1):
         pages.append(send(jnp.concatenate(pages, axis=0), stage))
     columns = span_kv.shape[1] // parts
@@ -419,10 +440,9 @@
     arrived = [send(rows, stages - 1) for rows in held]
     results = []
     for part in range(parts):
-        arrived[part], state = together(arrived[part], state)
-        mine = [held[part], arrived[part]]
-        page_set = (mine, [swap_cores(mine)], page_layout)
-        results.append(attend(*common, part, parts, [span_set, page_set], spec, state))
+        mine = [span_late[:, cuts[part]], held[part], arrived[part]]
+        far_set = (mine, [swap_cores(mine)], far_layout)
+        results.append(attend(*common, part, parts, [near_set, far_set], spec, state))
     if head_size != 2:
         rows = jnp.concatenate([jnp.concatenate(pair, axis=0) for pair in results], axis=1)
         return lax.all_to_all(rows, "head", split_axis=0, concat_axis=1, tiled=True)

time: 72.5 us -> 73.7 us (1.017); the launches traced: 73 us -> 72.9 us
  waiting for transfers between devices: 19.9 us -> 18.7 us
    ppermute x10, starting transfers between devices: 11.3 us -> 13.7 us  [hop(): lax.ppermute(value, 'seq', [(source, source ^ bit_of_core[source % 2]) fo...]
    ppermute x10, waiting for transfers between devices: 13 us -> 10.9 us  [hop(): lax.ppermute(value, 'seq', [(source, source ^ bit_of_core[source % 2]) fo...]
    ppermute x2, starting transfers between devices: 2.16 us -> 0.14 us  [body(): lax.ppermute(pair[1], 'head', [(0, 1), (1, 0)])]
    ppermute x2, waiting for transfers between devices: 6.9 us -> 7.76 us  [body(): lax.ppermute(pair[1], 'head', [(0, 1), (1, 0)])]
    unnamed x12 -> x11, local copies, waits for them, and re-layouts: 1.97 us -> 1.93 us
  transfers between devices with their start and end apart: 12 -> 12, of which waited for: 6 -> 5; matrix products, arithmetic and copies ran while one was open for 2% -> 0% of each run, Pallas kernels for 50% -> 51%
where the time goes in v12:
time: 73.7 us; the launch traced here: 72.9 us
  Pallas kernels  37.9 us (51%)
  waiting for transfers between devices  18.7 us (25%)
  starting transfers between devices  13.8 us (19%)
  local copies, waits for them, and re-layouts  1.99 us (3%)
    pallas_call x3, Pallas kernels, attend(): pl.pallas_call(functools.partial(attend_kernel, spec, layouts, part, bloc...  36.3 us
    ppermute x10, starting transfers between devices, hop(): lax.ppermute(value, 'seq', [(source, source ^ bit_of_core[source % 2]) fo...  13.7 us
    ppermute x10, waiting for transfers between devices, hop(): lax.ppermute(value, 'seq', [(source, source ^ bit_of_core[source % 2]) fo...  10.9 us
    ppermute x2, waiting for transfers between devices, body(): lax.ppermute(pair[1], 'head', [(0, 1), (1, 0)])  7.76 us
    unnamed x11, local copies, waits for them, and re-layouts  1.93 us
    pallas_call x2, Pallas kernels, join(): pl.pallas_call(functools.partial(join_kernel, spots, len(pieces)), out_sh...  1.62 us
  transfers between devices with their start and end apart: 12, of which 5 were waited for; matrix products, arithmetic and copies ran while one was open for 0% of the time, Pallas kernels for 51%

profile of v12, /device:TPU:0, one launch (start us, length us, event | category | flops | bytes accessed | tf_op | source)
XLA Modules:
  0.0 72.9 jit_solution(14064536866842788202)
XLA Ops:
  0.0 2.9 %collective-permute-start = (bf16[128,1024]{1,0:T(8,128)(2,1)}, bf16[128,1024]{1,0:T(8,128)(2,1)S(1)}, u32[]{:S(2)}, u32[]{:S(2)}) collective-permute-start(bf16[128,1024]{1,0:T(8,128)(2,1)} %from_ref.1), channel_id=1, source_target_pairs={{0,4},{2,10},{4,0},{6,14},{8,12},{10,2},{12,8},{14,6},{16,20},{18,... | collective-permute-start | bytes 786440 | tf_op jit(solution)/shard_map/ppermute | solution.py:27
  2.9 1.6 %collective-permute-start.2 = (bf16[128,1024]{1,0:T(8,128)(2,1)}, bf16[128,1024]{1,0:T(8,128)(2,1)S(1)}, u32[]{:S(2)}, u32[]{:S(2)}) collective-permute-start(bf16[128,1024]{1,0:T(8,128)(2,1)} %from_ref.1), channel_id=1, source_target_pairs={{0,8},{2,6},{4,12},{6,2},{8,0},{10,14},{12,4},{14,10},{16,24},{18,... | collective-permute-start | bytes 786440 | tf_op jit(solution)/shard_map/ppermute | solution.py:27
  4.5 0.0 copy-start
  4.5 0.9 %copy-done = bf16[2,64,1024]{2,1,0:T(8,128)(2,1)S(1)} copy-done((bf16[2,64,1024]{2,1,0:T(8,128)(2,1)S(1)}, bf16[2,64,1024]{2,1,0:T(8,128)(2,1)}, u32[]{:S(2)}) %copy-start) | copy-done | bytes 262168
  5.5 2.7 %collective-permute-start.1 = (bf16[64,1024]{1,0:T(8,128)(2,1)S(1)}, bf16[64,1024]{1,0:T(8,128)(2,1)S(1)}, u32[]{:S(2)}, u32[]{:S(2)}) collective-permute-start(bf16[64,1024]{1,0:T(8,128)(2,1)S(1)} %get-tuple-element.20), channel_id=1, source_target_pairs={{0,16},{2,18},{4,20},{6,22},{8,24},{10,26},{12,28},{14,30},{16,0},... | collective-permute-start | bytes 393224 | tf_op jit(solution)/shard_map/ppermute | solution.py:27
  8.1 0.0 copy-start.1
  8.1 0.9 %copy-done.1 = bf16[128,1024]{1,0:T(8,128)(2,1)S(1)} copy-done((bf16[128,1024]{1,0:T(8,128)(2,1)S(1)}, bf16[128,1024]{1,0:T(8,128)(2,1)}, u32[]{:S(2)}) %copy-start.1) | copy-done | bytes 262168
  9.1 0.0 copy-start.2
  9.1 0.0 copy-start.3
  9.1 0.0 copy-start.4
  9.2 3.4 %collective-permute-done.1 = bf16[64,1024]{1,0:T(8,128)(2,1)S(1)} collective-permute-done((bf16[64,1024]{1,0:T(8,128)(2,1)S(1)}, bf16[64,1024]{1,0:T(8,128)(2,1)S(1)}, u32[]{:S(2)}, u32[]{:S(2)}) %collective-permute-start.1) | collective-permute-done | bytes 131104 | tf_op jit(solution)/shard_map/ppermute | solution.py:27
  12.5 0.0 collective-permute-done.refs_1_
  12.5 0.0 collective-permute-done.2.refs_2_
  12.5 0.1 pad_maximum_fusion
  12.6 0.1 collective-permute-start.3
  12.7 1.5 %collective-permute-start.4 = (bf16[128,1024]{1,0:T(8,128)(2,1)S(1)}, bf16[128,1024]{1,0:T(8,128)(2,1)S(1)}, u32[]{:S(2)}, u32[]{:S(2)}) collective-permute-start(bf16[128,1024]{1,0:T(8,128)(2,1)S(1)} %constant_dynamic-update-slice_fusion), channel_id=1, source_target_pairs={{0,4},{2,10},{4,0},{6,14},{8,12},{10,2},{12,8},{14,6},{16,20},{18,... | collective-permute-start | bytes 786440 | tf_op jit(solution)/shard_map/ppermute | solution.py:27
  14.2 2.6 %collective-permute-start.5 = (bf16[128,1024]{1,0:T(8,128)(2,1)S(1)}, bf16[128,1024]{1,0:T(8,128)(2,1)S(1)}, u32[]{:S(2)}, u32[]{:S(2)}) collective-permute-start(bf16[128,1024]{1,0:T(8,128)(2,1)S(1)} %collective-permute-done.refs_1_), channel_id=1, source_target_pairs={{0,8},{2,6},{4,12},{6,2},{8,0},{10,14},{12,4},{14,10},{16,24},{18,... | collective-permute-start | bytes 786440 | tf_op jit(solution)/shard_map/ppermute | solution.py:27
  16.9 0.0 collective-permute-done.3.refs_3_
  16.9 0.0 copy-done.2
  16.9 0.0 copy-done.3
  16.9 0.0 copy-done.4
  16.9 4.8 %shard_map.57 = (f32[4096,256]{1,0:T(8,128)S(1)}, bf16[4096,128]{1,0:T(8,128)(2,1)S(1)}) custom-call(s32[2]{0:T(128)S(1)} %copy-done.4, s32[2,16]{1,0:T(2,128)S(1)} %copy-done.3, bf16[128,4096]{1,0:T(8,128)(2,1)S(1)} %copy-done.2, bf16[128,1024]{1,0:T(8,128)(2,1)S(1)} %shard_map.55.refs_0_, bf16[128,1024]{1,0:T(8,128)(2,1)S(1)} %collective-permute-done.refs_1_, ...), custom_call_target="tpu_custom_call" | custom-call | flops 3221225472 | bytes 2883584 | tf_op jit(solution)/shard_map/pallas_call | solution.py:300
  21.7 0.0 collective-permute-done.4
  21.7 0.6 collective-permute-done.5
  22.4 1.9 %collective-permute-start.6 = (bf16[256,512]{1,0:T(8,128)(2,1)S(1)}, bf16[256,512]{1,0:T(8,128)(2,1)S(1)}, u32[]{:S(2)}, u32[]{:S(2)}) collective-permute-start(bf16[256,512]{1,0:T(8,128)(2,1)S(1)} %pad_maximum_fusion.3.refs_5_), channel_id=1, source_target_pairs={{0,8},{2,6},{4,12},{6,2},{8,0},{10,14},{12,4},{14,10},{16,24},{18,... | collective-permute-start | bytes 786440 | tf_op jit(solution)/shard_map/ppermute | solution.py:27
  24.3 0.3 collective-permute-start.8
  24.6 4.2 %collective-permute-done.6.refs_6_ = bf16[256,512]{1,0:T(8,128)(2,1)S(1)} collective-permute-done((bf16[256,512]{1,0:T(8,128)(2,1)S(1)}, bf16[256,512]{1,0:T(8,128)(2,1)S(1)}, u32[]{:S(2)}, u32[]{:S(2)}) %collective-permute-start.6) | collective-permute-done | bytes 262176 | tf_op jit(solution)/shard_map/ppermute | solution.py:27
  28.8 0.1 collective-permute-start.7
  28.9 2.7 %collective-permute-done.8.refs_6_ = bf16[256,512]{1,0:T(8,128)(2,1)S(1)} collective-permute-done((bf16[256,512]{1,0:T(8,128)(2,1)S(1)}, bf16[256,512]{1,0:T(8,128)(2,1)S(1)}, u32[]{:S(2)}, u32[]{:S(2)}) %collective-permute-start.8) | collective-permute-done | bytes 262176 | tf_op jit(solution)/shard_map/ppermute | solution.py:27
  31.7 0.1 collective-permute-start.9
  31.7 0.0 collective-permute-done.7.refs_7_
  31.7 15.8 %shard_map.58 = (bf16[64,2048]{1,0:T(8,128)(2,1)S(1)}, bf16[64,2048]{1,0:T(8,128)(2,1)S(1)}) custom-call(s32[2]{0:T(128)S(1)} %copy-done.4, s32[2,16]{1,0:T(2,128)S(1)} %copy-done.3, bf16[128,4096]{1,0:T(8,128)(2,1)S(1)} %copy-done.2, bf16[128,1024]{1,0:T(8,128)(2,1)S(1)} %shard_map.55.refs_0_, bf16[128,1024]{1,0:T(8,128)(2,1)S(1)} %collective-permute-done.refs_1_, ...), custom_call_target="tpu_custom_call" | custom-call | flops 2684354560 | bytes 1703936 | tf_op jit(solution)/shard_map/pallas_call | solution.py:300
  47.6 0.1 collective-permute-start.10
  47.6 0.0 collective-permute-done.9.refs_7_
  47.7 15.6 %shard_map.59 = (bf16[64,2048]{1,0:T(8,128)(2,1)S(1)}, bf16[64,2048]{1,0:T(8,128)(2,1)S(1)}) custom-call(s32[2]{0:T(128)S(1)} %copy-done.4, s32[2,16]{1,0:T(2,128)S(1)} %copy-done.3, bf16[128,4096]{1,0:T(8,128)(2,1)S(1)} %copy-done.2, bf16[128,1024]{1,0:T(8,128)(2,1)S(1)} %shard_map.55.refs_0_, bf16[128,1024]{1,0:T(8,128)(2,1)S(1)} %collective-permute-done.refs_1_, ...), custom_call_target="tpu_custom_call" | custom-call | flops 2684354560 | bytes 1703936 | tf_op jit(solution)/shard_map/pallas_call | solution.py:300
  63.3 0.1 collective-permute-start.11
  63.4 0.0 collective-permute-done.10.refs_2_
  63.4 0.9 %shard_map.60.refs_0_ = bf16[64,8192]{1,0:T(8,128)(2,1)} custom-call(bf16[64,2048]{1,0:T(8,128)(2,1)S(1)} %get-tuple-element.31.refs_0_, bf16[64,2048]{1,0:T(8,128)(2,1)S(1)} %get-tuple-element.32.refs_1_, bf16[64,2048]{1,0:T(8,128)(2,1)S(1)} %collective-permute-done.10.refs_2_), custom_call_target="tpu_custom_call" | custom-call | tf_op jit(solution)/shard_map/pallas_call | solution.py:366
  64.3 7.8 %collective-permute-done.11.refs_1_ = bf16[64,2048]{1,0:T(8,128)(2,1)S(1)} collective-permute-done((bf16[64,2048]{1,0:T(8,128)(2,1)S(1)}, bf16[64,2048]{1,0:T(8,128)(2,1)S(1)}, u32[]{:S(2)}, u32[]{:S(2)}) %collective-permute-start.11) | collective-permute-done | bytes 262176 | tf_op jit(solution)/shard_map/ppermute | solution.py:450
  72.1 0.7 shard_map.61
  (11 shorter events, 0.2 us)
Async XLA Ops:
  0.0 12.5 %collective-permute-start = (bf16[128,1024]{1,0:T(8,128)(2,1)}, bf16[128,1024]{1,0:T(8,128)(2,1)S(1)}, u32[]{:S(2)}, u32[]{:S(2)}) collective-permute-start(bf16[128,1024]{1,0:T(8,128)(2,1)} %from_ref.1), channel_id=1, source_target_pairs={{0,4},{2,10},{4,0},{6,14},{8,12},{10,2},{12,8},{14,6},{16,20},{18,... | collective-permute-start | bytes 786440 | tf_op jit(solution)/shard_map/ppermute | solution.py:27
  2.9 9.6 %collective-permute-start.2 = (bf16[128,1024]{1,0:T(8,128)(2,1)}, bf16[128,1024]{1,0:T(8,128)(2,1)S(1)}, u32[]{:S(2)}, u32[]{:S(2)}) collective-permute-start(bf16[128,1024]{1,0:T(8,128)(2,1)} %from_ref.1), channel_id=1, source_target_pairs={{0,8},{2,6},{4,12},{6,2},{8,0},{10,14},{12,4},{14,10},{16,24},{18,... | collective-permute-start | bytes 786440 | tf_op jit(solution)/shard_map/ppermute | solution.py:27
  4.5 0.9 %copy-start = (bf16[2,64,1024]{2,1,0:T(8,128)(2,1)S(1)}, bf16[2,64,1024]{2,1,0:T(8,128)(2,1)}, u32[]{:S(2)}) copy-start(bf16[2,64,1024]{2,1,0:T(8,128)(2,1)} %cache_ref.1) | copy-start | bytes 786436
  5.5 7.0 %collective-permute-start.1 = (bf16[64,1024]{1,0:T(8,128)(2,1)S(1)}, bf16[64,1024]{1,0:T(8,128)(2,1)S(1)}, u32[]{:S(2)}, u32[]{:S(2)}) collective-permute-start(bf16[64,1024]{1,0:T(8,128)(2,1)S(1)} %get-tuple-element.20), channel_id=1, source_target_pairs={{0,16},{2,18},{4,20},{6,22},{8,24},{10,26},{12,28},{14,30},{16,0},... | collective-permute-start | bytes 393224 | tf_op jit(solution)/shard_map/ppermute | solution.py:27
  8.1 0.9 %copy-start.1 = (bf16[128,1024]{1,0:T(8,128)(2,1)S(1)}, bf16[128,1024]{1,0:T(8,128)(2,1)}, u32[]{:S(2)}) copy-start(bf16[128,1024]{1,0:T(8,128)(2,1)} %from_ref.1) | copy-start | bytes 786436
  9.1 7.8 %copy-start.2 = (bf16[128,4096]{1,0:T(8,128)(2,1)S(1)}, bf16[128,4096]{1,0:T(8,128)(2,1)}, u32[]{:S(2)}) copy-start(bf16[128,4096]{1,0:T(8,128)(2,1)} %q_ref.5) | copy-start | bytes 3145732
  9.1 7.8 %copy-start.3 = (s32[2,16]{1,0:T(2,128)S(1)}, s32[2,16]{1,0:T(2,128)}, u32[]{:S(2)}) copy-start(s32[2,16]{1,0:T(2,128)} %owner_ref.5) | copy-start | bytes 388
  9.1 7.8 %copy-start.4 = (s32[2]{0:T(128)S(1)}, s32[2]{0:T(128)}, u32[]{:S(2)}) copy-start(s32[2]{0:T(128)} %limit_ref.5) | copy-start | bytes 28
  12.6 4.3 %collective-permute-start.3 = (bf16[384,1024]{1,0:T(8,128)(2,1)S(1)}, bf16[384,1024]{1,0:T(8,128)(2,1)S(1)}, u32[]{:S(2)}, u32[]{:S(2)}) collective-permute-start(bf16[384,1024]{1,0:T(8,128)(2,1)S(1)} %pad_maximum_fusion), channel_id=1, source_target_pairs={{0,2},{2,0},{4,6},{6,4},{8,10},{10,8},{12,14},{14,12},{16,18},{18,... | collective-permute-start | bytes 2359304 | tf_op jit(solution)/shard_map/ppermute | solution.py:27
  12.7 9.0 %collective-permute-start.4 = (bf16[128,1024]{1,0:T(8,128)(2,1)S(1)}, bf16[128,1024]{1,0:T(8,128)(2,1)S(1)}, u32[]{:S(2)}, u32[]{:S(2)}) collective-permute-start(bf16[128,1024]{1,0:T(8,128)(2,1)S(1)} %constant_dynamic-update-slice_fusion), channel_id=1, source_target_pairs={{0,4},{2,10},{4,0},{6,14},{8,12},{10,2},{12,8},{14,6},{16,20},{18,... | collective-permute-start | bytes 786440 | tf_op jit(solution)/shard_map/ppermute | solution.py:27
  14.2 8.1 %collective-permute-start.5 = (bf16[128,1024]{1,0:T(8,128)(2,1)S(1)}, bf16[128,1024]{1,0:T(8,128)(2,1)S(1)}, u32[]{:S(2)}, u32[]{:S(2)}) collective-permute-start(bf16[128,1024]{1,0:T(8,128)(2,1)S(1)} %collective-permute-done.refs_1_), channel_id=1, source_target_pairs={{0,8},{2,6},{4,12},{6,2},{8,0},{10,14},{12,4},{14,10},{16,24},{18,... | collective-permute-start | bytes 786440 | tf_op jit(solution)/shard_map/ppermute | solution.py:27
  22.4 6.4 %collective-permute-start.6 = (bf16[256,512]{1,0:T(8,128)(2,1)S(1)}, bf16[256,512]{1,0:T(8,128)(2,1)S(1)}, u32[]{:S(2)}, u32[]{:S(2)}) collective-permute-start(bf16[256,512]{1,0:T(8,128)(2,1)S(1)} %pad_maximum_fusion.3.refs_5_), channel_id=1, source_target_pairs={{0,8},{2,6},{4,12},{6,2},{8,0},{10,14},{12,4},{14,10},{16,24},{18,... | collective-permute-start | bytes 786440 | tf_op jit(solution)/shard_map/ppermute | solution.py:27
  24.3 7.3 %collective-permute-start.8 = (bf16[256,512]{1,0:T(8,128)(2,1)S(1)}, bf16[256,512]{1,0:T(8,128)(2,1)S(1)}, u32[]{:S(2)}, u32[]{:S(2)}) collective-permute-start(bf16[256,512]{1,0:T(8,128)(2,1)S(1)} %pad_maximum_fusion.4.refs_5_), channel_id=1, source_target_pairs={{0,8},{2,6},{4,12},{6,2},{8,0},{10,14},{12,4},{14,10},{16,24},{18,... | collective-permute-start | bytes 786440 | tf_op jit(solution)/shard_map/ppermute | solution.py:27
  28.8 2.9 %collective-permute-start.7 = (bf16[640,512]{1,0:T(8,128)(2,1)S(1)}, bf16[640,512]{1,0:T(8,128)(2,1)S(1)}, u32[]{:S(2)}, u32[]{:S(2)}) collective-permute-start(bf16[640,512]{1,0:T(8,128)(2,1)S(1)} %pad_maximum_fusion.1), channel_id=1, source_target_pairs={{0,2},{2,0},{4,6},{6,4},{8,10},{10,8},{12,14},{14,12},{16,18},{18,... | collective-permute-start | bytes 1966088 | tf_op jit(solution)/shard_map/ppermute | solution.py:27
  31.7 16.0 %collective-permute-start.9 = (bf16[640,512]{1,0:T(8,128)(2,1)S(1)}, bf16[640,512]{1,0:T(8,128)(2,1)S(1)}, u32[]{:S(2)}, u32[]{:S(2)}) collective-permute-start(bf16[640,512]{1,0:T(8,128)(2,1)S(1)} %pad_maximum_fusion.2), channel_id=1, source_target_pairs={{0,2},{2,0},{4,6},{6,4},{8,10},{10,8},{12,14},{14,12},{16,18},{18,... | collective-permute-start | bytes 1966088 | tf_op jit(solution)/shard_map/ppermute | solution.py:27
  47.6 15.8 %collective-permute-start.10 = (bf16[64,2048]{1,0:T(8,128)(2,1)S(1)}, bf16[64,2048]{1,0:T(8,128)(2,1)S(1)}, u32[]{:S(2)}, u32[]{:S(2)}) collective-permute-start(bf16[64,2048]{1,0:T(8,128)(2,1)S(1)} %get-tuple-element.33), channel_id=1, source_target_pairs={{0,1},{1,0},{2,3},{3,2},{4,5},{5,4},{6,7},{7,6},{8,9},{9,8},{10,11... | collective-permute-start | bytes 786440 | tf_op jit(solution)/shard_map/ppermute | solution.py:450
  63.3 8.8 %collective-permute-start.11 = (bf16[64,2048]{1,0:T(8,128)(2,1)S(1)}, bf16[64,2048]{1,0:T(8,128)(2,1)S(1)}, u32[]{:S(2)}, u32[]{:S(2)}) collective-permute-start(bf16[64,2048]{1,0:T(8,128)(2,1)S(1)} %get-tuple-element.34), channel_id=1, source_target_pairs={{0,1},{1,0},{2,3},{3,2},{4,5},{5,4},{6,7},{7,6},{8,9},{9,8},{10,11... | collective-permute-start | bytes 786440 | tf_op jit(solution)/shard_map/ppermute | solution.py:450

commit v13 on v12

--- a/solution.py
+++ b/solution.py
@@ -412,8 +412,11 @@
     near_count = (1 << (stages - 1)) + 1
     near_layout, far_layout = span_layout[:near_count], span_layout[near_count:] + page_layout
 
+    columns = span_kv.shape[1] // parts
+    cuts = [slice(part * columns, (part + 1) * columns) for part in range(parts)]
+
     other_page, own_page = pick(prefix_cache, group_size)
-    crossed = hop(other_page, (group_size, group_size))
+    crossed = [hop(other_page[:, cut], (group_size, group_size)) for cut in cuts]
 
     span_early = send(span_kv, stages - 1)
     span_forward = send(span_kv, 0)
@@ -421,26 +424,36 @@
         seen = jnp.concatenate([span_kv, span_forward], axis=0)
         span_forward = jnp.concatenate([span_forward, send(seen, stage)], axis=0)
     span_late = send(span_forward, stages - 1)
-    span_forward, span_own, crossed = together(span_forward, hold(span_kv), crossed)
-    pages = [jnp.concatenate([own_page, crossed], axis=0)]
-    pages.append(send(pages[0], 0))
+    span_own, crossed[0] = together(hold(span_kv), crossed[0])
+
+    span_forward, span_early, *rest = together(span_forward, span_early, *crossed[1:])
+    crossed = crossed[:1] + rest
+    pages = [
+        [jnp.concatenate([own_page[:, cut], one], axis=0)] for cut, one in zip(cuts, crossed)
+    ]
+    for mine in pages:
+        mine.append(send(mine[0], 0))
+
+    def held(part):
+        for stage in range(1, stages - 1):
+            pages[part].append(send(jnp.concatenate(pages[part], axis=0), stage))
+        return jnp.concatenate(pages[part], axis=0)
 
     spec = (tokens, page, group_size, head_size, orders)
     common = (prefix_len, block_owner, span_query)
+    full = [held(part) for part in range(parts)]
     near = [span_own, span_forward, span_early]
-    near_set = (near, [swap_cores(near)], near_layout)
+    near_swapped, *full = together(swap_cores(near), *full)
+    near_set = (near, [near_swapped], near_layout)
     state = attend(*common, 0, 1, [near_set], spec, None)
 
-    pages[1], span_late, state = together(pages[1], span_late, state)
-    for stage in range(1, stages - 1):
-        pages.append(send(jnp.concatenate(pages, axis=0), stage))
-    columns = span_kv.shape[1] // parts
-    cuts = [slice(part * columns, (part + 1) * columns) for part in range(parts)]
-    held = [jnp.concatenate([piece[:, cut] for piece in pages], axis=0) for cut in cuts]
-    arrived = [send(rows, stages - 1) for rows in held]
+    arrived = [send(rows, stages - 1) for rows in full]
+    span_late, arrived[0], state = together(span_late, arrived[0], state)
     results = []
     for part in range(parts):
-        mine = [span_late[:, cuts[part]], held[part], arrived[part]]
+        if part:
+            arrived[part], state = together(arrived[part], state)
+        mine = [span_late[:, cuts[part]], full[part], arrived[part]]
         far_set = (mine, [swap_cores(mine)], far_layout)
         results.append(attend(*common, part, parts, [near_set, far_set], spec, state))
     if head_size != 2:

time: 73.7 us -> 72.2 us (0.980)
  the two profiles are of different devices: /device:TPU:0 before, /device:TPU:8 now
where the time goes in v13:
time: 72.2 us; the launch traced here: 70.8 us
  Pallas kernels  37.9 us (52%)
  waiting for transfers between devices  19.2 us (27%)
  starting transfers between devices  11.2 us (16%)
  local copies, waits for them, and re-layouts  1.96 us (3%)
    pallas_call x3, Pallas kernels, attend(): pl.pallas_call(functools.partial(attend_kernel, spec, layouts, part, bloc...  36.3 us
    ppermute x12, waiting for transfers between devices, hop(): lax.ppermute(value, 'seq', [(source, source ^ bit_of_core[source % 2]) fo...  11.5 us
    ppermute x12, starting transfers between devices, hop(): lax.ppermute(value, 'seq', [(source, source ^ bit_of_core[source % 2]) fo...  11 us
    ppermute x2, waiting for transfers between devices, body(): lax.ppermute(pair[1], 'head', [(0, 1), (1, 0)])  7.76 us
    unnamed x10, local copies, waits for them, and re-layouts  1.92 us
    pallas_call x2, Pallas kernels, join(): pl.pallas_call(functools.partial(join_kernel, spots, len(pieces)), out_sh...  1.62 us
  transfers between devices with their start and end apart: 14, of which 6 were waited for; matrix products, arithmetic and copies ran while one was open for 0% of the time, Pallas kernels for 53%

profile of v13, /device:TPU:8, one launch (start us, length us, event | category | flops | bytes accessed | tf_op | source)
XLA Modules:
  0.0 70.8 jit_solution(6590520603291170159)
XLA Ops:
  0.0 1.5 %collective-permute-start.1 = (bf16[128,1024]{1,0:T(8,128)(2,1)}, bf16[128,1024]{1,0:T(8,128)(2,1)S(1)}, u32[]{:S(2)}, u32[]{:S(2)}) collective-permute-start(bf16[128,1024]{1,0:T(8,128)(2,1)} %from_ref.1), channel_id=1, source_target_pairs={{0,4},{2,10},{4,0},{6,14},{8,12},{10,2},{12,8},{14,6},{16,20},{18,... | collective-permute-start | bytes 786440 | tf_op jit(solution)/shard_map/ppermute | solution.py:27
  1.5 0.4 collective-permute-start.2
  1.9 0.0 copy-start
  1.9 0.9 %copy-done = bf16[2,64,1024]{2,1,0:T(8,128)(2,1)S(1)} copy-done((bf16[2,64,1024]{2,1,0:T(8,128)(2,1)S(1)}, bf16[2,64,1024]{2,1,0:T(8,128)(2,1)}, u32[]{:S(2)}) %copy-start) | copy-done | bytes 262168
  2.9 2.7 %collective-permute-start = (bf16[64,512]{1,0:T(8,128)(2,1)S(1)}, bf16[64,512]{1,0:T(8,128)(2,1)S(1)}, u32[]{:S(2)}, u32[]{:S(2)}) collective-permute-start(bf16[64,512]{1,0:T(8,128)(2,1)S(1)} %get-tuple-element.56), channel_id=1, source_target_pairs={{0,16},{2,18},{4,20},{6,22},{8,24},{10,26},{12,28},{14,30},{16,0},... | collective-permute-start | bytes 196616 | tf_op jit(solution)/shard_map/ppermute | solution.py:27
  5.6 0.3 collective-permute-start.3
  5.9 0.0 copy-start.1
  5.9 0.9 %copy-done.1 = bf16[128,1024]{1,0:T(8,128)(2,1)S(1)} copy-done((bf16[128,1024]{1,0:T(8,128)(2,1)S(1)}, bf16[128,1024]{1,0:T(8,128)(2,1)}, u32[]{:S(2)}) %copy-start.1) | copy-done | bytes 262168
  6.9 4.6 %collective-permute-done = bf16[64,512]{1,0:T(8,128)(2,1)S(1)} collective-permute-done((bf16[64,512]{1,0:T(8,128)(2,1)S(1)}, bf16[64,512]{1,0:T(8,128)(2,1)S(1)}, u32[]{:S(2)}, u32[]{:S(2)}) %collective-permute-start) | collective-permute-done | bytes 65568 | tf_op jit(solution)/shard_map/ppermute | solution.py:27
  11.5 0.7 collective-permute-done.3
  12.2 0.0 collective-permute-done.1.refs_1_
  12.2 0.0 collective-permute-done.2.refs_2_
  12.2 0.1 pad_maximum_fusion
  12.2 0.0 copy-start.2
  12.3 0.0 copy-start.3
  12.3 0.0 copy-start.4
  12.3 0.1 collective-permute-start.4
  12.4 1.5 %collective-permute-start.5 = (bf16[128,512]{1,0:T(8,128)(2,1)S(1)}, bf16[128,512]{1,0:T(8,128)(2,1)S(1)}, u32[]{:S(2)}, u32[]{:S(2)}) collective-permute-start(bf16[128,512]{1,0:T(8,128)(2,1)S(1)} %pad_maximum_fusion.5), channel_id=1, source_target_pairs={{0,4},{2,10},{4,0},{6,14},{8,12},{10,2},{12,8},{14,6},{16,20},{18,... | collective-permute-start | bytes 393224 | tf_op jit(solution)/shard_map/ppermute | solution.py:27
  13.9 0.7 collective-permute-start.6
  14.6 2.9 %collective-permute-done.5 = bf16[128,512]{1,0:T(8,128)(2,1)S(1)} collective-permute-done((bf16[128,512]{1,0:T(8,128)(2,1)S(1)}, bf16[128,512]{1,0:T(8,128)(2,1)S(1)}, u32[]{:S(2)}, u32[]{:S(2)}) %collective-permute-start.5) | collective-permute-done | bytes 131104 | tf_op jit(solution)/shard_map/ppermute | solution.py:27
  17.5 1.6 %collective-permute-start.7 = (bf16[128,1024]{1,0:T(8,128)(2,1)S(1)}, bf16[128,1024]{1,0:T(8,128)(2,1)S(1)}, u32[]{:S(2)}, u32[]{:S(2)}) collective-permute-start(bf16[128,1024]{1,0:T(8,128)(2,1)S(1)} %collective-permute-done.1.refs_1_), channel_id=1, source_target_pairs={{0,8},{2,6},{4,12},{6,2},{8,0},{10,14},{12,4},{14,10},{16,24},{18,... | collective-permute-start | bytes 786440 | tf_op jit(solution)/shard_map/ppermute | solution.py:27
  19.1 0.0 collective-permute-done.6
  19.1 0.0 collective-permute-done.4.refs_3_
  19.1 1.4 %collective-permute-start.8 = (bf16[256,512]{1,0:T(8,128)(2,1)S(1)}, bf16[256,512]{1,0:T(8,128)(2,1)S(1)}, u32[]{:S(2)}, u32[]{:S(2)}) collective-permute-start(bf16[256,512]{1,0:T(8,128)(2,1)S(1)} %pad_maximum_fusion.3.refs_5_), channel_id=1, source_target_pairs={{0,8},{2,6},{4,12},{6,2},{8,0},{10,14},{12,4},{14,10},{16,24},{18,... | collective-permute-start | bytes 786440 | tf_op jit(solution)/shard_map/ppermute | solution.py:27
  20.5 0.7 %collective-permute-start.10 = (bf16[256,512]{1,0:T(8,128)(2,1)S(1)}, bf16[256,512]{1,0:T(8,128)(2,1)S(1)}, u32[]{:S(2)}, u32[]{:S(2)}) collective-permute-start(bf16[256,512]{1,0:T(8,128)(2,1)S(1)} %pad_maximum_fusion.4.refs_5_), channel_id=1, source_target_pairs={{0,8},{2,6},{4,12},{6,2},{8,0},{10,14},{12,4},{14,10},{16,24},{18,... | collective-permute-start | bytes 786440 | tf_op jit(solution)/shard_map/ppermute | solution.py:27
  21.2 0.0 copy-done.2
  21.2 0.0 copy-done.3
  21.2 0.0 copy-done.4
  21.2 4.8 %shard_map.57 = (f32[4096,256]{1,0:T(8,128)S(1)}, bf16[4096,128]{1,0:T(8,128)(2,1)S(1)}) custom-call(s32[2]{0:T(128)S(1)} %copy-done.4, s32[2,16]{1,0:T(2,128)S(1)} %copy-done.3, bf16[128,4096]{1,0:T(8,128)(2,1)S(1)} %copy-done.2, bf16[128,1024]{1,0:T(8,128)(2,1)S(1)} %shard_map.55.refs_0_, bf16[128,1024]{1,0:T(8,128)(2,1)S(1)} %collective-permute-done.1.refs_1_, ...), custom_call_target="tpu_custom_call" | custom-call | flops 3221225472 | bytes 2883584 | tf_op jit(solution)/shard_map/pallas_call | solution.py:300
  26.0 0.0 collective-permute-done.7
  26.0 0.7 collective-permute-done.8.refs_6_
  26.8 0.1 collective-permute-start.9
  26.9 2.7 %collective-permute-done.10.refs_6_ = bf16[256,512]{1,0:T(8,128)(2,1)S(1)} collective-permute-done((bf16[256,512]{1,0:T(8,128)(2,1)S(1)}, bf16[256,512]{1,0:T(8,128)(2,1)S(1)}, u32[]{:S(2)}, u32[]{:S(2)}) %collective-permute-start.10) | collective-permute-done | bytes 262176 | tf_op jit(solution)/shard_map/ppermute | solution.py:27
  29.6 0.1 collective-permute-start.11
  29.6 0.0 collective-permute-done.9.refs_7_
  29.6 15.8 %shard_map.58 = (bf16[64,2048]{1,0:T(8,128)(2,1)S(1)}, bf16[64,2048]{1,0:T(8,128)(2,1)S(1)}) custom-call(s32[2]{0:T(128)S(1)} %copy-done.4, s32[2,16]{1,0:T(2,128)S(1)} %copy-done.3, bf16[128,4096]{1,0:T(8,128)(2,1)S(1)} %copy-done.2, bf16[128,1024]{1,0:T(8,128)(2,1)S(1)} %shard_map.55.refs_0_, bf16[128,1024]{1,0:T(8,128)(2,1)S(1)} %collective-permute-done.1.refs_1_, ...), custom_call_target="tpu_custom_call" | custom-call | flops 2684354560 | bytes 1703936 | tf_op jit(solution)/shard_map/pallas_call | solution.py:300
  45.5 0.1 collective-permute-start.12
  45.5 0.0 collective-permute-done.11.refs_7_
  45.6 15.6 %shard_map.59 = (bf16[64,2048]{1,0:T(8,128)(2,1)S(1)}, bf16[64,2048]{1,0:T(8,128)(2,1)S(1)}) custom-call(s32[2]{0:T(128)S(1)} %copy-done.4, s32[2,16]{1,0:T(2,128)S(1)} %copy-done.3, bf16[128,4096]{1,0:T(8,128)(2,1)S(1)} %copy-done.2, bf16[128,1024]{1,0:T(8,128)(2,1)S(1)} %shard_map.55.refs_0_, bf16[128,1024]{1,0:T(8,128)(2,1)S(1)} %collective-permute-done.1.refs_1_, ...), custom_call_target="tpu_custom_call" | custom-call | flops 2684354560 | bytes 1703936 | tf_op jit(solution)/shard_map/pallas_call | solution.py:300
  61.2 0.1 collective-permute-start.13
  61.3 0.0 collective-permute-done.12.refs_2_
  61.3 0.9 %shard_map.60.refs_0_ = bf16[64,8192]{1,0:T(8,128)(2,1)} custom-call(bf16[64,2048]{1,0:T(8,128)(2,1)S(1)} %get-tuple-element.43.refs_0_, bf16[64,2048]{1,0:T(8,128)(2,1)S(1)} %get-tuple-element.48.refs_1_, bf16[64,2048]{1,0:T(8,128)(2,1)S(1)} %collective-permute-done.12.refs_2_), custom_call_target="tpu_custom_call" | custom-call | tf_op jit(solution)/shard_map/pallas_call | solution.py:366
  62.2 7.8 %collective-permute-done.13.refs_1_ = bf16[64,2048]{1,0:T(8,128)(2,1)S(1)} collective-permute-done((bf16[64,2048]{1,0:T(8,128)(2,1)S(1)}, bf16[64,2048]{1,0:T(8,128)(2,1)S(1)}, u32[]{:S(2)}, u32[]{:S(2)}) %collective-permute-start.13) | collective-permute-done | bytes 262176 | tf_op jit(solution)/shard_map/ppermute | solution.py:463
  70.0 0.7 %shard_map.61 = bf16[64,8192]{1,0:T(8,128)(2,1)} custom-call(bf16[64,8192]{1,0:T(8,128)(2,1)} %shard_map.60.refs_0_, bf16[64,2048]{1,0:T(8,128)(2,1)S(1)} %collective-permute-done.13.refs_1_), custom_call_target="tpu_custom_call", output_to_operand_aliasing={{}: (0, {})} | custom-call | tf_op jit(solution)/shard_map/pallas_call | solution.py:366
  (11 shorter events, 0.2 us)
Async XLA Ops:
  0.0 12.2 %collective-permute-start.1 = (bf16[128,1024]{1,0:T(8,128)(2,1)}, bf16[128,1024]{1,0:T(8,128)(2,1)S(1)}, u32[]{:S(2)}, u32[]{:S(2)}) collective-permute-start(bf16[128,1024]{1,0:T(8,128)(2,1)} %from_ref.1), channel_id=1, source_target_pairs={{0,4},{2,10},{4,0},{6,14},{8,12},{10,2},{12,8},{14,6},{16,20},{18,... | collective-permute-start | bytes 786440 | tf_op jit(solution)/shard_map/ppermute | solution.py:27
  1.5 10.7 %collective-permute-start.2 = (bf16[128,1024]{1,0:T(8,128)(2,1)}, bf16[128,1024]{1,0:T(8,128)(2,1)S(1)}, u32[]{:S(2)}, u32[]{:S(2)}) collective-permute-start(bf16[128,1024]{1,0:T(8,128)(2,1)} %from_ref.1), channel_id=1, source_target_pairs={{0,8},{2,6},{4,12},{6,2},{8,0},{10,14},{12,4},{14,10},{16,24},{18,... | collective-permute-start | bytes 786440 | tf_op jit(solution)/shard_map/ppermute | solution.py:27
  1.9 0.9 %copy-start = (bf16[2,64,1024]{2,1,0:T(8,128)(2,1)S(1)}, bf16[2,64,1024]{2,1,0:T(8,128)(2,1)}, u32[]{:S(2)}) copy-start(bf16[2,64,1024]{2,1,0:T(8,128)(2,1)} %cache_ref.1) | copy-start | bytes 786436
  2.9 8.5 %collective-permute-start = (bf16[64,512]{1,0:T(8,128)(2,1)S(1)}, bf16[64,512]{1,0:T(8,128)(2,1)S(1)}, u32[]{:S(2)}, u32[]{:S(2)}) collective-permute-start(bf16[64,512]{1,0:T(8,128)(2,1)S(1)} %get-tuple-element.56), channel_id=1, source_target_pairs={{0,16},{2,18},{4,20},{6,22},{8,24},{10,26},{12,28},{14,30},{16,0},... | collective-permute-start | bytes 196616 | tf_op jit(solution)/shard_map/ppermute | solution.py:27
  5.6 6.6 %collective-permute-start.3 = (bf16[64,512]{1,0:T(8,128)(2,1)S(1)}, bf16[64,512]{1,0:T(8,128)(2,1)S(1)}, u32[]{:S(2)}, u32[]{:S(2)}) collective-permute-start(bf16[64,512]{1,0:T(8,128)(2,1)S(1)} %get-tuple-element.55), channel_id=1, source_target_pairs={{0,16},{2,18},{4,20},{6,22},{8,24},{10,26},{12,28},{14,30},{16,0},... | collective-permute-start | bytes 196616 | tf_op jit(solution)/shard_map/ppermute | solution.py:27
  5.9 0.9 %copy-start.1 = (bf16[128,1024]{1,0:T(8,128)(2,1)S(1)}, bf16[128,1024]{1,0:T(8,128)(2,1)}, u32[]{:S(2)}) copy-start(bf16[128,1024]{1,0:T(8,128)(2,1)} %from_ref.1) | copy-start | bytes 786436
  12.2 9.0 %copy-start.2 = (bf16[128,4096]{1,0:T(8,128)(2,1)S(1)}, bf16[128,4096]{1,0:T(8,128)(2,1)}, u32[]{:S(2)}) copy-start(bf16[128,4096]{1,0:T(8,128)(2,1)} %q_ref.5) | copy-start | bytes 3145732
  12.3 8.9 %copy-start.3 = (s32[2,16]{1,0:T(2,128)S(1)}, s32[2,16]{1,0:T(2,128)}, u32[]{:S(2)}) copy-start(s32[2,16]{1,0:T(2,128)} %owner_ref.5) | copy-start | bytes 388
  12.3 8.9 %copy-start.4 = (s32[2]{0:T(128)S(1)}, s32[2]{0:T(128)}, u32[]{:S(2)}) copy-start(s32[2]{0:T(128)} %limit_ref.5) | copy-start | bytes 28
  12.3 6.8 %collective-permute-start.4 = (bf16[384,1024]{1,0:T(8,128)(2,1)S(1)}, bf16[384,1024]{1,0:T(8,128)(2,1)S(1)}, u32[]{:S(2)}, u32[]{:S(2)}) collective-permute-start(bf16[384,1024]{1,0:T(8,128)(2,1)S(1)} %pad_maximum_fusion), channel_id=1, source_target_pairs={{0,2},{2,0},{4,6},{6,4},{8,10},{10,8},{12,14},{14,12},{16,18},{18,... | collective-permute-start | bytes 2359304 | tf_op jit(solution)/shard_map/ppermute | solution.py:27
  12.4 5.0 %collective-permute-start.5 = (bf16[128,512]{1,0:T(8,128)(2,1)S(1)}, bf16[128,512]{1,0:T(8,128)(2,1)S(1)}, u32[]{:S(2)}, u32[]{:S(2)}) collective-permute-start(bf16[128,512]{1,0:T(8,128)(2,1)S(1)} %pad_maximum_fusion.5), channel_id=1, source_target_pairs={{0,4},{2,10},{4,0},{6,14},{8,12},{10,2},{12,8},{14,6},{16,20},{18,... | collective-permute-start | bytes 393224 | tf_op jit(solution)/shard_map/ppermute | solution.py:27
  13.9 5.2 %collective-permute-start.6 = (bf16[128,512]{1,0:T(8,128)(2,1)S(1)}, bf16[128,512]{1,0:T(8,128)(2,1)S(1)}, u32[]{:S(2)}, u32[]{:S(2)}) collective-permute-start(bf16[128,512]{1,0:T(8,128)(2,1)S(1)} %pad_maximum_fusion.6), channel_id=1, source_target_pairs={{0,4},{2,10},{4,0},{6,14},{8,12},{10,2},{12,8},{14,6},{16,20},{18,... | collective-permute-start | bytes 393224 | tf_op jit(solution)/shard_map/ppermute | solution.py:27
  17.5 8.6 %collective-permute-start.7 = (bf16[128,1024]{1,0:T(8,128)(2,1)S(1)}, bf16[128,1024]{1,0:T(8,128)(2,1)S(1)}, u32[]{:S(2)}, u32[]{:S(2)}) collective-permute-start(bf16[128,1024]{1,0:T(8,128)(2,1)S(1)} %collective-permute-done.1.refs_1_), channel_id=1, source_target_pairs={{0,8},{2,6},{4,12},{6,2},{8,0},{10,14},{12,4},{14,10},{16,24},{18,... | collective-permute-start | bytes 786440 | tf_op jit(solution)/shard_map/ppermute | solution.py:27
  19.1 7.6 %collective-permute-start.8 = (bf16[256,512]{1,0:T(8,128)(2,1)S(1)}, bf16[256,512]{1,0:T(8,128)(2,1)S(1)}, u32[]{:S(2)}, u32[]{:S(2)}) collective-permute-start(bf16[256,512]{1,0:T(8,128)(2,1)S(1)} %pad_maximum_fusion.3.refs_5_), channel_id=1, source_target_pairs={{0,8},{2,6},{4,12},{6,2},{8,0},{10,14},{12,4},{14,10},{16,24},{18,... | collective-permute-start | bytes 786440 | tf_op jit(solution)/shard_map/ppermute | solution.py:27
  20.5 9.0 %collective-permute-start.10 = (bf16[256,512]{1,0:T(8,128)(2,1)S(1)}, bf16[256,512]{1,0:T(8,128)(2,1)S(1)}, u32[]{:S(2)}, u32[]{:S(2)}) collective-permute-start(bf16[256,512]{1,0:T(8,128)(2,1)S(1)} %pad_maximum_fusion.4.refs_5_), channel_id=1, source_target_pairs={{0,8},{2,6},{4,12},{6,2},{8,0},{10,14},{12,4},{14,10},{16,24},{18,... | collective-permute-start | bytes 786440 | tf_op jit(solution)/shard_map/ppermute | solution.py:27
  26.8 2.9 %collective-permute-start.9 = (bf16[640,512]{1,0:T(8,128)(2,1)S(1)}, bf16[640,512]{1,0:T(8,128)(2,1)S(1)}, u32[]{:S(2)}, u32[]{:S(2)}) collective-permute-start(bf16[640,512]{1,0:T(8,128)(2,1)S(1)} %pad_maximum_fusion.1), channel_id=1, source_target_pairs={{0,2},{2,0},{4,6},{6,4},{8,10},{10,8},{12,14},{14,12},{16,18},{18,... | collective-permute-start | bytes 1966088 | tf_op jit(solution)/shard_map/ppermute | solution.py:27
  29.6 16.0 %collective-permute-start.11 = (bf16[640,512]{1,0:T(8,128)(2,1)S(1)}, bf16[640,512]{1,0:T(8,128)(2,1)S(1)}, u32[]{:S(2)}, u32[]{:S(2)}) collective-permute-start(bf16[640,512]{1,0:T(8,128)(2,1)S(1)} %pad_maximum_fusion.2), channel_id=1, source_target_pairs={{0,2},{2,0},{4,6},{6,4},{8,10},{10,8},{12,14},{14,12},{16,18},{18,... | collective-permute-start | bytes 1966088 | tf_op jit(solution)/shard_map/ppermute | solution.py:27
  45.5 15.8 %collective-permute-start.12 = (bf16[64,2048]{1,0:T(8,128)(2,1)S(1)}, bf16[64,2048]{1,0:T(8,128)(2,1)S(1)}, u32[]{:S(2)}, u32[]{:S(2)}) collective-permute-start(bf16[64,2048]{1,0:T(8,128)(2,1)S(1)} %get-tuple-element.49), channel_id=1, source_target_pairs={{0,1},{1,0},{2,3},{3,2},{4,5},{5,4},{6,7},{7,6},{8,9},{9,8},{10,11... | collective-permute-start | bytes 786440 | tf_op jit(solution)/shard_map/ppermute | solution.py:463
  61.2 8.8 %collective-permute-start.13 = (bf16[64,2048]{1,0:T(8,128)(2,1)S(1)}, bf16[64,2048]{1,0:T(8,128)(2,1)S(1)}, u32[]{:S(2)}, u32[]{:S(2)}) collective-permute-start(bf16[64,2048]{1,0:T(8,128)(2,1)S(1)} %get-tuple-element.50), channel_id=1, source_target_pairs={{0,1},{1,0},{2,3},{3,2},{4,5},{5,4},{6,7},{7,6},{8,9},{9,8},{10,11... | collective-permute-start | bytes 786440 | tf_op jit(solution)/shard_map/ppermute | solution.py:463

commit v14 on v13

--- a/solution.py
+++ b/solution.py
@@ -183,33 +183,41 @@
             weights[index % 2][:, pl.ds(start, chunk)] = jnp.exp2(made * EXP2_SCALE).astype(
                 jnp.bfloat16
             )
-
-    def finish(index, extremes):
+            yield
+
+    def gather_values(index):
         group = index // blocks_a_group
-        summed = jnp.dot(
-            weights[index % 2][:, :total_keys],
-            values[group, :total_keys, :],
-            preferred_element_type=jnp.float32,
-        )
-        rows = pl.ds(index * block, block)
         if first_phase:
-            state_sum[rows, :] = summed
-            return extremes
-        old = pl.ds((part * blocks + index) * block, block)
-        summed = summed + state_sum[old, :]
+            summed = None
+        else:
+            summed = state_sum[pl.ds((part * blocks + index) * block, block), :]
+        for start in range(0, total_keys, chunk):
+            at = pl.ds(start, chunk)
+            more = jnp.dot(
+                weights[index % 2][:, at], values[group, at, :], preferred_element_type=jnp.float32
+            )
+            summed = more if summed is None else summed + more
+            yield
+        if first_phase:
+            state_sum[pl.ds(index * block, block), :] = summed
+            return
         total = summed[:, HD:]
         give(index, (summed[:, :HD] / total).astype(jnp.bfloat16))
-        return jnp.minimum(extremes[0], total), jnp.maximum(extremes[1], total)
+        extremes[0] = jnp.minimum(extremes[0], total)
+        extremes[1] = jnp.maximum(extremes[1], total)
 
     begin(0)
-    extremes = (jnp.ones((block, HD), jnp.float32),) * 2
+    extremes = [jnp.ones((block, HD), jnp.float32)] * 2
     for index in range(blocks + 1):
+        steps = []
+        if index < blocks:
+            steps.append(weigh(index))
         if index >= 1:
-            extremes = finish(index - 1, extremes)
-        if index < blocks:
-            weigh(index)
-            if (index + 1) % blocks_a_group == 0 and index + 1 < blocks:
-                begin((index + 1) // blocks_a_group)
+            steps.append(gather_values(index - 1))
+        while steps:
+            steps = [step for step in steps if next(step, steps) is not steps]
+        if (index + 1) % blocks_a_group == 0 and index + 1 < blocks:
+            begin((index + 1) // blocks_a_group)
     if first_phase:
         return
 
@@ -303,7 +311,7 @@
         in_specs=[scalars] * 2 + [whole] * (1 + len(pieces) + len(state)),
         out_specs=[whole] * 2,
         scratch_shapes=scratch_shapes,
-        compiler_params=pltpu.CompilerParams(vmem_limit_bytes=operands + scratch + (6 << 20)),
+        compiler_params=pltpu.CompilerParams(vmem_limit_bytes=operands + scratch + block * total_keys * 4 + (6 << 20)),
         cost_estimate=pl.CostEstimate(
             flops=8 * tokens * columns * total_keys,
             bytes_accessed=4 * tokens * columns + 2 * total_keys * columns // PER_GROUP,
@@ -443,16 +451,14 @@
     common = (prefix_len, block_owner, span_query)
     full = [held(part) for part in range(parts)]
     near = [span_own, span_forward, span_early]
-    near_swapped, *full = together(swap_cores(near), *full)
+    near_swapped, span_late, *full = together(swap_cores(near), span_late, *full)
     near_set = (near, [near_swapped], near_layout)
     state = attend(*common, 0, 1, [near_set], spec, None)
 
     arrived = [send(rows, stages - 1) for rows in full]
-    span_late, arrived[0], state = together(span_late, arrived[0], state)
     results = []
     for part in range(parts):
-        if part:
-            arrived[part], state = together(arrived[part], state)
+        arrived[part], state = together(arrived[part], state)
         mine = [span_late[:, cuts[part]], full[part], arrived[part]]
         far_set = (mine, [swap_cores(mine)], far_layout)
         results.append(attend(*common, part, parts, [near_set, far_set], spec, state))

time: 72.2 us -> 74.2 us (1.028)
  the two profiles are of different devices: /device:TPU:8 before, /device:TPU:2 now
where the time goes in v14:
time: 74.2 us; the launch traced here: 73.2 us
  Pallas kernels  38.4 us (52%)
  waiting for transfers between devices  18.6 us (25%)
  starting transfers between devices  13.8 us (19%)
  local copies, waits for them, and re-layouts  1.96 us (3%)
    pallas_call x3, Pallas kernels, attend(): pl.pallas_call(functools.partial(attend_kernel, spec, layouts, part, bloc...  36.7 us
    ppermute x12, waiting for transfers between devices, hop(): lax.ppermute(value, 'seq', [(source, source ^ bit_of_core[source % 2]) fo...  11.7 us
    ppermute x12, starting transfers between devices, hop(): lax.ppermute(value, 'seq', [(source, source ^ bit_of_core[source % 2]) fo...  11.7 us
    ppermute x2, waiting for transfers between devices, body(): lax.ppermute(pair[1], 'head', [(0, 1), (1, 0)])  6.86 us
    ppermute x2, starting transfers between devices, body(): lax.ppermute(pair[1], 'head', [(0, 1), (1, 0)])  2.16 us
    unnamed x10, local copies, waits for them, and re-layouts  1.92 us
    pallas_call x2, Pallas kernels, join(): pl.pallas_call(functools.partial(join_kernel, spots, len(pieces)), out_sh...  1.61 us
  transfers between devices with their start and end apart: 14, of which 8 were waited for; matrix products, arithmetic and copies ran while one was open for 0% of the time, Pallas kernels for 51%

profile of v14, /device:TPU:2, one launch (start us, length us, event | category | flops | bytes accessed | tf_op | source)
XLA Modules:
  0.0 73.2 jit_solution(7174889131563023775)
XLA Ops:
  0.0 0.0 collective-permute-start.1
  0.0 2.1 %collective-permute-start.2 = (bf16[128,1024]{1,0:T(8,128)(2,1)}, bf16[128,1024]{1,0:T(8,128)(2,1)S(1)}, u32[]{:S(2)}, u32[]{:S(2)}) collective-permute-start(bf16[128,1024]{1,0:T(8,128)(2,1)} %from_ref.1), channel_id=1, source_target_pairs={{0,8},{2,6},{4,12},{6,2},{8,0},{10,14},{12,4},{14,10},{16,24},{18,... | collective-permute-start | bytes 786440 | tf_op jit(solution)/shard_map/ppermute | solution.py:27
  2.1 0.0 copy-start
  2.1 0.9 %copy-done = bf16[2,64,1024]{2,1,0:T(8,128)(2,1)S(1)} copy-done((bf16[2,64,1024]{2,1,0:T(8,128)(2,1)S(1)}, bf16[2,64,1024]{2,1,0:T(8,128)(2,1)}, u32[]{:S(2)}) %copy-start) | copy-done | bytes 262168
  3.1 2.7 %collective-permute-start = (bf16[64,512]{1,0:T(8,128)(2,1)S(1)}, bf16[64,512]{1,0:T(8,128)(2,1)S(1)}, u32[]{:S(2)}, u32[]{:S(2)}) collective-permute-start(bf16[64,512]{1,0:T(8,128)(2,1)S(1)} %get-tuple-element.56), channel_id=1, source_target_pairs={{0,16},{2,18},{4,20},{6,22},{8,24},{10,26},{12,28},{14,30},{16,0},... | collective-permute-start | bytes 196616 | tf_op jit(solution)/shard_map/ppermute | solution.py:27
  5.8 0.3 collective-permute-start.3
  6.1 0.0 copy-start.1
  6.1 0.9 %copy-done.1 = bf16[128,1024]{1,0:T(8,128)(2,1)S(1)} copy-done((bf16[128,1024]{1,0:T(8,128)(2,1)S(1)}, bf16[128,1024]{1,0:T(8,128)(2,1)}, u32[]{:S(2)}) %copy-start.1) | copy-done | bytes 262168
  7.1 2.4 %collective-permute-done = bf16[64,512]{1,0:T(8,128)(2,1)S(1)} collective-permute-done((bf16[64,512]{1,0:T(8,128)(2,1)S(1)}, bf16[64,512]{1,0:T(8,128)(2,1)S(1)}, u32[]{:S(2)}, u32[]{:S(2)}) %collective-permute-start) | collective-permute-done | bytes 65568 | tf_op jit(solution)/shard_map/ppermute | solution.py:27
  9.5 2.0 %collective-permute-done.3 = bf16[64,512]{1,0:T(8,128)(2,1)S(1)} collective-permute-done((bf16[64,512]{1,0:T(8,128)(2,1)S(1)}, bf16[64,512]{1,0:T(8,128)(2,1)S(1)}, u32[]{:S(2)}, u32[]{:S(2)}) %collective-permute-start.3) | collective-permute-done | bytes 65568 | tf_op jit(solution)/shard_map/ppermute | solution.py:27
  11.5 0.0 collective-permute-done.1.refs_1_
  11.5 0.0 collective-permute-done.2.refs_2_
  11.5 0.1 pad_maximum_fusion
  11.6 0.0 copy-start.2
  11.6 0.0 copy-start.3
  11.6 0.0 copy-start.4
  11.6 0.1 collective-permute-start.4
  11.7 2.4 %collective-permute-start.6 = (bf16[128,512]{1,0:T(8,128)(2,1)S(1)}, bf16[128,512]{1,0:T(8,128)(2,1)S(1)}, u32[]{:S(2)}, u32[]{:S(2)}) collective-permute-start(bf16[128,512]{1,0:T(8,128)(2,1)S(1)} %pad_maximum_fusion.5), channel_id=1, source_target_pairs={{0,4},{2,10},{4,0},{6,14},{8,12},{10,2},{12,8},{14,6},{16,20},{18,... | collective-permute-start | bytes 393224 | tf_op jit(solution)/shard_map/ppermute | solution.py:27
  14.1 0.5 collective-permute-start.5
  14.6 1.5 %collective-permute-start.7 = (bf16[128,512]{1,0:T(8,128)(2,1)S(1)}, bf16[128,512]{1,0:T(8,128)(2,1)S(1)}, u32[]{:S(2)}, u32[]{:S(2)}) collective-permute-start(bf16[128,512]{1,0:T(8,128)(2,1)S(1)} %pad_maximum_fusion.6), channel_id=1, source_target_pairs={{0,4},{2,10},{4,0},{6,14},{8,12},{10,2},{12,8},{14,6},{16,20},{18,... | collective-permute-start | bytes 393224 | tf_op jit(solution)/shard_map/ppermute | solution.py:27
  16.0 1.9 %collective-permute-done.6 = bf16[128,512]{1,0:T(8,128)(2,1)S(1)} collective-permute-done((bf16[128,512]{1,0:T(8,128)(2,1)S(1)}, bf16[128,512]{1,0:T(8,128)(2,1)S(1)}, u32[]{:S(2)}, u32[]{:S(2)}) %collective-permute-start.6) | collective-permute-done | bytes 131104 | tf_op jit(solution)/shard_map/ppermute | solution.py:27
  18.0 3.1 %collective-permute-done.7 = bf16[128,512]{1,0:T(8,128)(2,1)S(1)} collective-permute-done((bf16[128,512]{1,0:T(8,128)(2,1)S(1)}, bf16[128,512]{1,0:T(8,128)(2,1)S(1)}, u32[]{:S(2)}, u32[]{:S(2)}) %collective-permute-start.7) | collective-permute-done | bytes 131104 | tf_op jit(solution)/shard_map/ppermute | solution.py:27
  21.1 0.3 collective-permute-done.5
  21.4 0.0 collective-permute-done.4.refs_3_
  21.4 1.5 %collective-permute-start.8 = (bf16[256,512]{1,0:T(8,128)(2,1)S(1)}, bf16[256,512]{1,0:T(8,128)(2,1)S(1)}, u32[]{:S(2)}, u32[]{:S(2)}) collective-permute-start(bf16[256,512]{1,0:T(8,128)(2,1)S(1)} %pad_maximum_fusion.3.refs_5_), channel_id=1, source_target_pairs={{0,8},{2,6},{4,12},{6,2},{8,0},{10,14},{12,4},{14,10},{16,24},{18,... | collective-permute-start | bytes 786440 | tf_op jit(solution)/shard_map/ppermute | solution.py:27
  22.9 0.5 collective-permute-start.10
  23.4 0.0 copy-done.2
  23.4 0.0 copy-done.3
  23.4 0.0 copy-done.4
  23.4 5.2 %shard_map.57 = (f32[4096,256]{1,0:T(8,128)S(1)}, bf16[4096,128]{1,0:T(8,128)(2,1)S(1)}) custom-call(s32[2]{0:T(128)S(1)} %copy-done.4, s32[2,16]{1,0:T(2,128)S(1)} %copy-done.3, bf16[128,4096]{1,0:T(8,128)(2,1)S(1)} %copy-done.2, bf16[128,1024]{1,0:T(8,128)(2,1)S(1)} %shard_map.55.refs_0_, bf16[128,1024]{1,0:T(8,128)(2,1)S(1)} %collective-permute-done.1.refs_1_, ...), custom_call_target="tpu_custom_call" | custom-call | flops 3221225472 | bytes 2883584 | tf_op jit(solution)/shard_map/pallas_call | solution.py:308
  28.6 0.0 collective-permute-done.8.refs_6_
  28.7 0.1 collective-permute-start.9
  28.8 1.8 %collective-permute-done.10.refs_6_ = bf16[256,512]{1,0:T(8,128)(2,1)S(1)} collective-permute-done((bf16[256,512]{1,0:T(8,128)(2,1)S(1)}, bf16[256,512]{1,0:T(8,128)(2,1)S(1)}, u32[]{:S(2)}, u32[]{:S(2)}) %collective-permute-start.10) | collective-permute-done | bytes 262176 | tf_op jit(solution)/shard_map/ppermute | solution.py:27
  30.6 0.1 collective-permute-start.11
  30.7 0.2 collective-permute-done.9.refs_7_
  30.9 15.9 %shard_map.58 = (bf16[64,2048]{1,0:T(8,128)(2,1)S(1)}, bf16[64,2048]{1,0:T(8,128)(2,1)S(1)}) custom-call(s32[2]{0:T(128)S(1)} %copy-done.4, s32[2,16]{1,0:T(2,128)S(1)} %copy-done.3, bf16[128,4096]{1,0:T(8,128)(2,1)S(1)} %copy-done.2, bf16[128,1024]{1,0:T(8,128)(2,1)S(1)} %shard_map.55.refs_0_, bf16[128,1024]{1,0:T(8,128)(2,1)S(1)} %collective-permute-done.1.refs_1_, ...), custom_call_target="tpu_custom_call" | custom-call | flops 2684354560 | bytes 1703936 | tf_op jit(solution)/shard_map/pallas_call | solution.py:308
  46.7 1.6 %collective-permute-start.12 = (bf16[64,2048]{1,0:T(8,128)(2,1)S(1)}, bf16[64,2048]{1,0:T(8,128)(2,1)S(1)}, u32[]{:S(2)}, u32[]{:S(2)}) collective-permute-start(bf16[64,2048]{1,0:T(8,128)(2,1)S(1)} %get-tuple-element.49), channel_id=1, source_target_pairs={{0,1},{1,0},{2,3},{3,2},{4,5},{5,4},{6,7},{7,6},{8,9},{9,8},{10,11... | collective-permute-start | bytes 786440 | tf_op jit(solution)/shard_map/ppermute | solution.py:469
  48.3 0.0 collective-permute-done.11.refs_7_
  48.3 15.7 %shard_map.59 = (bf16[64,2048]{1,0:T(8,128)(2,1)S(1)}, bf16[64,2048]{1,0:T(8,128)(2,1)S(1)}) custom-call(s32[2]{0:T(128)S(1)} %copy-done.4, s32[2,16]{1,0:T(2,128)S(1)} %copy-done.3, bf16[128,4096]{1,0:T(8,128)(2,1)S(1)} %copy-done.2, bf16[128,1024]{1,0:T(8,128)(2,1)S(1)} %shard_map.55.refs_0_, bf16[128,1024]{1,0:T(8,128)(2,1)S(1)} %collective-permute-done.1.refs_1_, ...), custom_call_target="tpu_custom_call" | custom-call | flops 2684354560 | bytes 1703936 | tf_op jit(solution)/shard_map/pallas_call | solution.py:308
  64.0 0.6 collective-permute-start.13
  64.6 0.0 collective-permute-done.12.refs_2_
  64.6 0.9 %shard_map.60.refs_0_ = bf16[64,8192]{1,0:T(8,128)(2,1)} custom-call(bf16[64,2048]{1,0:T(8,128)(2,1)S(1)} %get-tuple-element.43.refs_0_, bf16[64,2048]{1,0:T(8,128)(2,1)S(1)} %get-tuple-element.48.refs_1_, bf16[64,2048]{1,0:T(8,128)(2,1)S(1)} %collective-permute-done.12.refs_2_), custom_call_target="tpu_custom_call" | custom-call | tf_op jit(solution)/shard_map/pallas_call | solution.py:374
  65.5 6.9 %collective-permute-done.13.refs_1_ = bf16[64,2048]{1,0:T(8,128)(2,1)S(1)} collective-permute-done((bf16[64,2048]{1,0:T(8,128)(2,1)S(1)}, bf16[64,2048]{1,0:T(8,128)(2,1)S(1)}, u32[]{:S(2)}, u32[]{:S(2)}) %collective-permute-start.13) | collective-permute-done | bytes 262176 | tf_op jit(solution)/shard_map/ppermute | solution.py:469
  72.4 0.7 shard_map.61
  (11 shorter events, 0.2 us)
Async XLA Ops:
  0.0 11.5 %collective-permute-start.1 = (bf16[128,1024]{1,0:T(8,128)(2,1)}, bf16[128,1024]{1,0:T(8,128)(2,1)S(1)}, u32[]{:S(2)}, u32[]{:S(2)}) collective-permute-start(bf16[128,1024]{1,0:T(8,128)(2,1)} %from_ref.1), channel_id=1, source_target_pairs={{0,4},{2,10},{4,0},{6,14},{8,12},{10,2},{12,8},{14,6},{16,20},{18,... | collective-permute-start | bytes 786440 | tf_op jit(solution)/shard_map/ppermute | solution.py:27
  0.0 11.5 %collective-permute-start.2 = (bf16[128,1024]{1,0:T(8,128)(2,1)}, bf16[128,1024]{1,0:T(8,128)(2,1)S(1)}, u32[]{:S(2)}, u32[]{:S(2)}) collective-permute-start(bf16[128,1024]{1,0:T(8,128)(2,1)} %from_ref.1), channel_id=1, source_target_pairs={{0,8},{2,6},{4,12},{6,2},{8,0},{10,14},{12,4},{14,10},{16,24},{18,... | collective-permute-start | bytes 786440 | tf_op jit(solution)/shard_map/ppermute | solution.py:27
  2.1 0.9 %copy-start = (bf16[2,64,1024]{2,1,0:T(8,128)(2,1)S(1)}, bf16[2,64,1024]{2,1,0:T(8,128)(2,1)}, u32[]{:S(2)}) copy-start(bf16[2,64,1024]{2,1,0:T(8,128)(2,1)} %cache_ref.1) | copy-start | bytes 786436
  3.1 6.4 %collective-permute-start = (bf16[64,512]{1,0:T(8,128)(2,1)S(1)}, bf16[64,512]{1,0:T(8,128)(2,1)S(1)}, u32[]{:S(2)}, u32[]{:S(2)}) collective-permute-start(bf16[64,512]{1,0:T(8,128)(2,1)S(1)} %get-tuple-element.56), channel_id=1, source_target_pairs={{0,16},{2,18},{4,20},{6,22},{8,24},{10,26},{12,28},{14,30},{16,0},... | collective-permute-start | bytes 196616 | tf_op jit(solution)/shard_map/ppermute | solution.py:27
  5.8 5.7 %collective-permute-start.3 = (bf16[64,512]{1,0:T(8,128)(2,1)S(1)}, bf16[64,512]{1,0:T(8,128)(2,1)S(1)}, u32[]{:S(2)}, u32[]{:S(2)}) collective-permute-start(bf16[64,512]{1,0:T(8,128)(2,1)S(1)} %get-tuple-element.55), channel_id=1, source_target_pairs={{0,16},{2,18},{4,20},{6,22},{8,24},{10,26},{12,28},{14,30},{16,0},... | collective-permute-start | bytes 196616 | tf_op jit(solution)/shard_map/ppermute | solution.py:27
  6.1 0.9 %copy-start.1 = (bf16[128,1024]{1,0:T(8,128)(2,1)S(1)}, bf16[128,1024]{1,0:T(8,128)(2,1)}, u32[]{:S(2)}) copy-start(bf16[128,1024]{1,0:T(8,128)(2,1)} %from_ref.1) | copy-start | bytes 786436
  11.6 11.9 %copy-start.2 = (bf16[128,4096]{1,0:T(8,128)(2,1)S(1)}, bf16[128,4096]{1,0:T(8,128)(2,1)}, u32[]{:S(2)}) copy-start(bf16[128,4096]{1,0:T(8,128)(2,1)} %q_ref.5) | copy-start | bytes 3145732
  11.6 11.9 %copy-start.3 = (s32[2,16]{1,0:T(2,128)S(1)}, s32[2,16]{1,0:T(2,128)}, u32[]{:S(2)}) copy-start(s32[2,16]{1,0:T(2,128)} %owner_ref.5) | copy-start | bytes 388
  11.6 11.8 %copy-start.4 = (s32[2]{0:T(128)S(1)}, s32[2]{0:T(128)}, u32[]{:S(2)}) copy-start(s32[2]{0:T(128)} %limit_ref.5) | copy-start | bytes 28
  11.6 9.8 %collective-permute-start.4 = (bf16[384,1024]{1,0:T(8,128)(2,1)S(1)}, bf16[384,1024]{1,0:T(8,128)(2,1)S(1)}, u32[]{:S(2)}, u32[]{:S(2)}) collective-permute-start(bf16[384,1024]{1,0:T(8,128)(2,1)S(1)} %pad_maximum_fusion), channel_id=1, source_target_pairs={{0,2},{2,0},{4,6},{6,4},{8,10},{10,8},{12,14},{14,12},{16,18},{18,... | collective-permute-start | bytes 2359304 | tf_op jit(solution)/shard_map/ppermute | solution.py:27
  11.7 6.3 %collective-permute-start.6 = (bf16[128,512]{1,0:T(8,128)(2,1)S(1)}, bf16[128,512]{1,0:T(8,128)(2,1)S(1)}, u32[]{:S(2)}, u32[]{:S(2)}) collective-permute-start(bf16[128,512]{1,0:T(8,128)(2,1)S(1)} %pad_maximum_fusion.5), channel_id=1, source_target_pairs={{0,4},{2,10},{4,0},{6,14},{8,12},{10,2},{12,8},{14,6},{16,20},{18,... | collective-permute-start | bytes 393224 | tf_op jit(solution)/shard_map/ppermute | solution.py:27
  14.1 7.3 %collective-permute-start.5 = (bf16[128,1024]{1,0:T(8,128)(2,1)S(1)}, bf16[128,1024]{1,0:T(8,128)(2,1)S(1)}, u32[]{:S(2)}, u32[]{:S(2)}) collective-permute-start(bf16[128,1024]{1,0:T(8,128)(2,1)S(1)} %collective-permute-done.1.refs_1_), channel_id=1, source_target_pairs={{0,8},{2,6},{4,12},{6,2},{8,0},{10,14},{12,4},{14,10},{16,24},{18,... | collective-permute-start | bytes 786440 | tf_op jit(solution)/shard_map/ppermute | solution.py:27
  14.6 6.5 %collective-permute-start.7 = (bf16[128,512]{1,0:T(8,128)(2,1)S(1)}, bf16[128,512]{1,0:T(8,128)(2,1)S(1)}, u32[]{:S(2)}, u32[]{:S(2)}) collective-permute-start(bf16[128,512]{1,0:T(8,128)(2,1)S(1)} %pad_maximum_fusion.6), channel_id=1, source_target_pairs={{0,4},{2,10},{4,0},{6,14},{8,12},{10,2},{12,8},{14,6},{16,20},{18,... | collective-permute-start | bytes 393224 | tf_op jit(solution)/shard_map/ppermute | solution.py:27
  21.4 7.2 %collective-permute-start.8 = (bf16[256,512]{1,0:T(8,128)(2,1)S(1)}, bf16[256,512]{1,0:T(8,128)(2,1)S(1)}, u32[]{:S(2)}, u32[]{:S(2)}) collective-permute-start(bf16[256,512]{1,0:T(8,128)(2,1)S(1)} %pad_maximum_fusion.3.refs_5_), channel_id=1, source_target_pairs={{0,8},{2,6},{4,12},{6,2},{8,0},{10,14},{12,4},{14,10},{16,24},{18,... | collective-permute-start | bytes 786440 | tf_op jit(solution)/shard_map/ppermute | solution.py:27
  22.9 7.6 %collective-permute-start.10 = (bf16[256,512]{1,0:T(8,128)(2,1)S(1)}, bf16[256,512]{1,0:T(8,128)(2,1)S(1)}, u32[]{:S(2)}, u32[]{:S(2)}) collective-permute-start(bf16[256,512]{1,0:T(8,128)(2,1)S(1)} %pad_maximum_fusion.4.refs_5_), channel_id=1, source_target_pairs={{0,8},{2,6},{4,12},{6,2},{8,0},{10,14},{12,4},{14,10},{16,24},{18,... | collective-permute-start | bytes 786440 | tf_op jit(solution)/shard_map/ppermute | solution.py:27
  28.7 2.2 %collective-permute-start.9 = (bf16[640,512]{1,0:T(8,128)(2,1)S(1)}, bf16[640,512]{1,0:T(8,128)(2,1)S(1)}, u32[]{:S(2)}, u32[]{:S(2)}) collective-permute-start(bf16[640,512]{1,0:T(8,128)(2,1)S(1)} %pad_maximum_fusion.1), channel_id=1, source_target_pairs={{0,2},{2,0},{4,6},{6,4},{8,10},{10,8},{12,14},{14,12},{16,18},{18,... | collective-permute-start | bytes 1966088 | tf_op jit(solution)/shard_map/ppermute | solution.py:27
  30.6 17.7 %collective-permute-start.11 = (bf16[640,512]{1,0:T(8,128)(2,1)S(1)}, bf16[640,512]{1,0:T(8,128)(2,1)S(1)}, u32[]{:S(2)}, u32[]{:S(2)}) collective-permute-start(bf16[640,512]{1,0:T(8,128)(2,1)S(1)} %pad_maximum_fusion.2), channel_id=1, source_target_pairs={{0,2},{2,0},{4,6},{6,4},{8,10},{10,8},{12,14},{14,12},{16,18},{18,... | collective-permute-start | bytes 1966088 | tf_op jit(solution)/shard_map/ppermute | solution.py:27
  46.7 17.9 %collective-permute-start.12 = (bf16[64,2048]{1,0:T(8,128)(2,1)S(1)}, bf16[64,2048]{1,0:T(8,128)(2,1)S(1)}, u32[]{:S(2)}, u32[]{:S(2)}) collective-permute-start(bf16[64,2048]{1,0:T(8,128)(2,1)S(1)} %get-tuple-element.49), channel_id=1, source_target_pairs={{0,1},{1,0},{2,3},{3,2},{4,5},{5,4},{6,7},{7,6},{8,9},{9,8},{10,11... | collective-permute-start | bytes 786440 | tf_op jit(solution)/shard_map/ppermute | solution.py:469
  64.0 8.3 %collective-permute-start.13 = (bf16[64,2048]{1,0:T(8,128)(2,1)S(1)}, bf16[64,2048]{1,0:T(8,128)(2,1)S(1)}, u32[]{:S(2)}, u32[]{:S(2)}) collective-permute-start(bf16[64,2048]{1,0:T(8,128)(2,1)S(1)} %get-tuple-element.50), channel_id=1, source_target_pairs={{0,1},{1,0},{2,3},{3,2},{4,5},{5,4},{6,7},{7,6},{8,9},{9,8},{10,11... | collective-permute-start | bytes 786440 | tf_op jit(solution)/shard_map/ppermute | solution.py:469

commit v15 on v12

--- a/solution.py
+++ b/solution.py
@@ -176,7 +176,7 @@
             extra = extra.astype(jnp.bfloat16)
             state_extra[pl.ds(index * block, block), :] = extra
         else:
-            extra = state_extra[pl.ds((part * blocks + index) * block, block), :]
+            extra = state_extra[pl.ds(index * block, block), :]
         query = jnp.concatenate([query, extra], axis=1)
         for start in range(0, total_keys, chunk):
             made = scores_of(query, group, start, first_phase)
@@ -195,8 +195,7 @@
         if first_phase:
             state_sum[rows, :] = summed
             return extremes
-        old = pl.ds((part * blocks + index) * block, block)
-        summed = summed + state_sum[old, :]
+        summed = summed + state_sum[rows, :]
         total = summed[:, HD:]
         give(index, (summed[:, :HD] / total).astype(jnp.bfloat16))
         return jnp.minimum(extremes[0], total), jnp.maximum(extremes[1], total)
@@ -312,36 +311,46 @@
     )(limits, owners, queries, *pieces, *state)
 
 
-def pick_kernel(group_size, cache_ref, other_ref, own_ref):
+def pick_kernel(group_size, parts, cache_ref, *refs):
     request = lax.axis_index("seq") // group_size
-    other_ref[...] = cache_ref[1 - request]
-    own_ref[...] = cache_ref[request]
-
-
-def pick(cache, group_size):
+    columns = cache_ref.shape[2] // parts
+    for part in range(parts):
+        at = pl.ds(part * columns, columns)
+        refs[part][...] = cache_ref[1 - request, :, at]
+        refs[parts + part][...] = cache_ref[request, :, at]
+
+
+def pick(cache, group_size, parts):
     whole = pl.BlockSpec(memory_space=pltpu.VMEM)
-    return pl.pallas_call(
-        functools.partial(pick_kernel, group_size),
-        out_shape=[jax.ShapeDtypeStruct(cache.shape[1:], cache.dtype)] * 2,
+    one = jax.ShapeDtypeStruct((cache.shape[1], cache.shape[2] // parts), cache.dtype)
+    picked = pl.pallas_call(
+        functools.partial(pick_kernel, group_size, parts),
+        out_shape=[one] * (2 * parts),
         in_specs=[whole],
-        out_specs=[whole] * 2,
+        out_specs=[whole] * (2 * parts),
         compiler_params=pltpu.CompilerParams(vmem_limit_bytes=8 << 20),
     )(cache)
-
-
-def hold_kernel(from_ref, to_ref):
-    to_ref[...] = from_ref[...]
-
-
-def hold(value):
+    return list(picked[:parts]), list(picked[parts:])
+
+
+def split_kernel(from_ref, *to_refs):
+    columns = to_refs[0].shape[1]
+    for part, ref in enumerate(to_refs):
+        ref[...] = from_ref[:, pl.ds(part * columns, columns)]
+
+
+def split(value, parts):
     whole = pl.BlockSpec(memory_space=pltpu.VMEM)
-    return pl.pallas_call(
-        hold_kernel,
-        out_shape=jax.ShapeDtypeStruct(value.shape, value.dtype),
-        in_specs=[whole],
-        out_specs=whole,
-        compiler_params=pltpu.CompilerParams(vmem_limit_bytes=8 << 20),
-    )(value)
+    one = jax.ShapeDtypeStruct((value.shape[0], value.shape[1] // parts), value.dtype)
+    return list(
+        pl.pallas_call(
+            split_kernel,
+            out_shape=[one] * parts,
+            in_specs=[whole],
+            out_specs=[whole] * parts,
+            compiler_params=pltpu.CompilerParams(vmem_limit_bytes=8 << 20),
+        )(value)
+    )
 
 
 def join_kernel(spots, count, *refs):
@@ -412,36 +421,59 @@
     near_count = (1 << (stages - 1)) + 1
     near_layout, far_layout = span_layout[:near_count], span_layout[near_count:] + page_layout
 
-    other_page, own_page = pick(prefix_cache, group_size)
-    crossed = hop(other_page, (group_size, group_size))
-
-    span_early = send(span_kv, stages - 1)
-    span_forward = send(span_kv, 0)
-    for stage in range(1, stages - 1):
-        seen = jnp.concatenate([span_kv, span_forward], axis=0)
-        span_forward = jnp.concatenate([span_forward, send(seen, stage)], axis=0)
-    span_late = send(span_forward, stages - 1)
-    span_forward, span_own, crossed = together(span_forward, hold(span_kv), crossed)
-    pages = [jnp.concatenate([own_page, crossed], axis=0)]
-    pages.append(send(pages[0], 0))
-
     spec = (tokens, page, group_size, head_size, orders)
     common = (prefix_len, block_owner, span_query)
-    near = [span_own, span_forward, span_early]
-    near_set = (near, [swap_cores(near)], near_layout)
-    state = attend(*common, 0, 1, [near_set], spec, None)
-
-    pages[1], span_late, state = together(pages[1], span_late, state)
-    for stage in range(1, stages - 1):
-        pages.append(send(jnp.concatenate(pages, axis=0), stage))
-    columns = span_kv.shape[1] // parts
-    cuts = [slice(part * columns, (part + 1) * columns) for part in range(parts)]
-    held = [jnp.concatenate([piece[:, cut] for piece in pages], axis=0) for cut in cuts]
-    arrived = [send(rows, stages - 1) for rows in held]
+
+    def exchange(rows):
+        early = send(rows, stages - 1)
+        forward = send(rows, 0)
+        for stage in range(1, stages - 1):
+            seen = jnp.concatenate([rows, forward], axis=0)
+            forward = jnp.concatenate([forward, send(seen, stage)], axis=0)
+        return early, forward
+
+    def round_pages(rows, first):
+        pieces = [rows, first]
+        for stage in range(1, stages - 1):
+            pieces.append(send(jnp.concatenate(pieces, axis=0), stage))
+        return jnp.concatenate(pieces, axis=0)
+
+    span = split(span_kv, parts)
+    other_pages, own_pages = pick(prefix_cache, group_size, parts)
+    crossed, early, forward = [], [], []
+    for part in range(parts):
+        if part:
+            forward[-1], span[part] = together(forward[-1], span[part])
+            crossed[-1], other_pages[part] = together(crossed[-1], other_pages[part])
+        crossed.append(hop(other_pages[part], (group_size, group_size)))
+        one_early, one_forward = exchange(span[part])
+        early.append(one_early)
+        forward.append(one_forward)
+    near = [list(pieces) for pieces in zip(span, forward, early)]
+    late = [send(rows, stages - 1) for rows in forward]
+    pages = [jnp.concatenate(pair, axis=0) for pair in zip(own_pages, crossed)]
+    full = [round_pages(pages[0], send(pages[0], 0))] + [None] * (parts - 1)
+    near_swapped = [swap_cores(near[0])]
+    near_swapped[0], full[0], *tied = together(
+        near_swapped[0], full[0], *pages[1:], *forward[1:], *early[1:]
+    )
+    for part in range(1, parts):
+        pages[part], forward[part], early[part] = tied[part - 1 :: parts - 1]
+        late[part] = send(forward[part], stages - 1)
+        near[part] = [span[part], forward[part], early[part]]
+        near_swapped.append(swap_cores(near[part]))
+
     results = []
     for part in range(parts):
-        mine = [span_late[:, cuts[part]], held[part], arrived[part]]
-        far_set = (mine, [swap_cores(mine)], far_layout)
+        near_set = (near[part], [near_swapped[part]], near_layout)
+        state = attend(*common, part, parts, [near_set], spec, None)
+        arrived, state = together(send(full[part], stages - 1), state)
+        if part + 1 < parts:
+            first, state = together(send(pages[part + 1], 0), state)
+            full[part + 1] = round_pages(pages[part + 1], first)
+        mine = [late[part], full[part], arrived]
+        swapped = swap_cores(mine)
+        far_set = (mine, [swapped], far_layout)
         results.append(attend(*common, part, parts, [near_set, far_set], spec, state))
     if head_size != 2:
         rows = jnp.concatenate([jnp.concatenate(pair, axis=0) for pair in results], axis=1)

time: 73.7 us -> 78.1 us (1.060)
  starting transfers between devices: 13.8 us -> 16.2 us
  Pallas kernels: 37.9 us -> 39 us
  waiting for transfers between devices: 18.7 us -> 19.7 us
    ppermute x10 -> x16, starting transfers between devices: 13.7 us -> 16 us  [hop(): lax.ppermute(value, 'seq', [(source, source ^ bit_of_core[source % 2]) fo...]
    pallas_call x3 -> x4, Pallas kernels: 36.3 us -> 37.3 us  [attend(): pl.pallas_call(functools.partial(attend_kernel, spec, layouts, part, bloc...]
    ppermute x10 -> x16, waiting for transfers between devices: 10.9 us -> 11.9 us  [hop(): lax.ppermute(value, 'seq', [(source, source ^ bit_of_core[source % 2]) fo...]
  transfers between devices with their start and end apart: 12 -> 18, of which waited for: 5 -> 7; matrix products, arithmetic and copies ran while one was open for 0% -> 0% of each run, Pallas kernels for 51% -> 49%
where the time goes in v15:
time: 78.1 us; the launch traced here: 77.3 us
  Pallas kernels  39 us (50%)
  waiting for transfers between devices  19.7 us (25%)
  starting transfers between devices  16.2 us (21%)
  local copies, waits for them, and re-layouts  1.93 us (2%)
    pallas_call x4, Pallas kernels, attend(): pl.pallas_call(functools.partial(attend_kernel, spec, layouts, part, bloc...  37.3 us
    ppermute x16, starting transfers between devices, hop(): lax.ppermute(value, 'seq', [(source, source ^ bit_of_core[source % 2]) fo...  16 us
    ppermute x16, waiting for transfers between devices, hop(): lax.ppermute(value, 'seq', [(source, source ^ bit_of_core[source % 2]) fo...  11.9 us
    ppermute x2, waiting for transfers between devices, body(): lax.ppermute(pair[1], 'head', [(0, 1), (1, 0)])  7.76 us
    unnamed x11, local copies, waits for them, and re-layouts  1.92 us
    pallas_call x2, Pallas kernels, join(): pl.pallas_call(functools.partial(join_kernel, spots, len(pieces)), out_sh...  1.62 us
  transfers between devices with their start and end apart: 18, of which 7 were waited for; matrix products, arithmetic and copies ran while one was open for 0% of the time, Pallas kernels for 49%

profile of v15, /device:TPU:0, one launch (start us, length us, event | category | flops | bytes accessed | tf_op | source)
XLA Modules:
  0.0 77.3 jit_solution(17394209511494656730)
XLA Ops:
  0.0 0.0 copy-start
  0.0 0.9 %copy-done = bf16[128,1024]{1,0:T(8,128)(2,1)S(1)} copy-done((bf16[128,1024]{1,0:T(8,128)(2,1)S(1)}, bf16[128,1024]{1,0:T(8,128)(2,1)}, u32[]{:S(2)}) %copy-start) | copy-done | bytes 262168
  1.0 3.0 %collective-permute-start = (bf16[128,512]{1,0:T(8,128)(2,1)S(1)}, bf16[128,512]{1,0:T(8,128)(2,1)S(1)}, u32[]{:S(2)}, u32[]{:S(2)}) collective-permute-start(bf16[128,512]{1,0:T(8,128)(2,1)S(1)} %get-tuple-element.37.refs_0_), channel_id=1, source_target_pairs={{0,4},{2,10},{4,0},{6,14},{8,12},{10,2},{12,8},{14,6},{16,20},{18,... | collective-permute-start | bytes 393224 | tf_op jit(solution)/shard_map/ppermute | solution.py:27
  4.0 1.6 %collective-permute-start.1 = (bf16[128,512]{1,0:T(8,128)(2,1)S(1)}, bf16[128,512]{1,0:T(8,128)(2,1)S(1)}, u32[]{:S(2)}, u32[]{:S(2)}) collective-permute-start(bf16[128,512]{1,0:T(8,128)(2,1)S(1)} %get-tuple-element.37.refs_0_), channel_id=1, source_target_pairs={{0,8},{2,6},{4,12},{6,2},{8,0},{10,14},{12,4},{14,10},{16,24},{18,... | collective-permute-start | bytes 393224 | tf_op jit(solution)/shard_map/ppermute | solution.py:27
  5.6 0.9 %copy-done.1 = bf16[2,64,1024]{2,1,0:T(8,128)(2,1)S(1)} copy-done((bf16[2,64,1024]{2,1,0:T(8,128)(2,1)S(1)}, bf16[2,64,1024]{2,1,0:T(8,128)(2,1)}, u32[]{:S(2)}) %copy-start.1) | copy-done | bytes 262168
  6.5 2.7 %collective-permute-start.3 = (bf16[64,512]{1,0:T(8,128)(2,1)S(1)}, bf16[64,512]{1,0:T(8,128)(2,1)S(1)}, u32[]{:S(2)}, u32[]{:S(2)}) collective-permute-start(bf16[64,512]{1,0:T(8,128)(2,1)S(1)} %get-tuple-element.41), channel_id=1, source_target_pairs={{0,16},{2,18},{4,20},{6,22},{8,24},{10,26},{12,28},{14,30},{16,0},... | collective-permute-start | bytes 196616 | tf_op jit(solution)/shard_map/ppermute | solution.py:27
  9.2 0.0 collective-permute-done.refs_1_
  9.2 0.0 collective-permute-done.1.refs_2_
  9.2 0.1 collective-permute-start.2
  9.3 3.1 %collective-permute-done.3 = bf16[64,512]{1,0:T(8,128)(2,1)S(1)} collective-permute-done((bf16[64,512]{1,0:T(8,128)(2,1)S(1)}, bf16[64,512]{1,0:T(8,128)(2,1)S(1)}, u32[]{:S(2)}, u32[]{:S(2)}) %collective-permute-start.3) | collective-permute-done | bytes 65568 | tf_op jit(solution)/shard_map/ppermute | solution.py:27
  12.5 1.9 %collective-permute-start.5 = (bf16[64,512]{1,0:T(8,128)(2,1)S(1)}, bf16[64,512]{1,0:T(8,128)(2,1)S(1)}, u32[]{:S(2)}, u32[]{:S(2)}) collective-permute-start(bf16[64,512]{1,0:T(8,128)(2,1)S(1)} %get-tuple-element.45), channel_id=1, source_target_pairs={{0,16},{2,18},{4,20},{6,22},{8,24},{10,26},{12,28},{14,30},{16,0},... | collective-permute-start | bytes 196616 | tf_op jit(solution)/shard_map/ppermute | solution.py:27
  14.4 0.6 collective-permute-start.4
  15.0 1.5 %collective-permute-start.6 = (bf16[128,512]{1,0:T(8,128)(2,1)S(1)}, bf16[128,512]{1,0:T(8,128)(2,1)S(1)}, u32[]{:S(2)}, u32[]{:S(2)}) collective-permute-start(bf16[128,512]{1,0:T(8,128)(2,1)S(1)} %get-tuple-element.46.refs_0_), channel_id=1, source_target_pairs={{0,4},{2,10},{4,0},{6,14},{8,12},{10,2},{12,8},{14,6},{16,20},{18,... | collective-permute-start | bytes 393224 | tf_op jit(solution)/shard_map/ppermute | solution.py:27
  16.4 0.5 collective-permute-start.7
  16.9 1.4 %collective-permute-done.5 = bf16[64,512]{1,0:T(8,128)(2,1)S(1)} collective-permute-done((bf16[64,512]{1,0:T(8,128)(2,1)S(1)}, bf16[64,512]{1,0:T(8,128)(2,1)S(1)}, u32[]{:S(2)}, u32[]{:S(2)}) %collective-permute-start.5) | collective-permute-done | bytes 65568 | tf_op jit(solution)/shard_map/ppermute | solution.py:27
  18.3 0.3 collective-permute-start.8
  18.7 2.2 %collective-permute-done.4 = bf16[128,512]{1,0:T(8,128)(2,1)S(1)} collective-permute-done((bf16[128,512]{1,0:T(8,128)(2,1)S(1)}, bf16[128,512]{1,0:T(8,128)(2,1)S(1)}, u32[]{:S(2)}, u32[]{:S(2)}) %collective-permute-start.4) | collective-permute-done | bytes 131104 | tf_op jit(solution)/shard_map/ppermute | solution.py:27
  20.8 2.2 %collective-permute-done.6.refs_1_ = bf16[128,512]{1,0:T(8,128)(2,1)S(1)} collective-permute-done((bf16[128,512]{1,0:T(8,128)(2,1)S(1)}, bf16[128,512]{1,0:T(8,128)(2,1)S(1)}, u32[]{:S(2)}, u32[]{:S(2)}) %collective-permute-start.6) | collective-permute-done | bytes 131104 | tf_op jit(solution)/shard_map/ppermute | solution.py:27
  23.0 0.0 collective-permute-done.7.refs_2_
  23.0 0.0 collective-permute-done.2.refs_3_
  23.0 1.0 %collective-permute-start.9 = (bf16[256,512]{1,0:T(8,128)(2,1)S(1)}, bf16[256,512]{1,0:T(8,128)(2,1)S(1)}, u32[]{:S(2)}, u32[]{:S(2)}) collective-permute-start(bf16[256,512]{1,0:T(8,128)(2,1)S(1)} %pad_maximum_fusion.4.refs_5_), channel_id=1, source_target_pairs={{0,8},{2,6},{4,12},{6,2},{8,0},{10,14},{12,4},{14,10},{16,24},{18,... | collective-permute-start | bytes 786440 | tf_op jit(solution)/shard_map/ppermute | solution.py:27
  24.1 0.5 collective-permute-start.11
  24.6 1.1 %collective-permute-start.13 = (bf16[128,512]{1,0:T(8,128)(2,1)S(1)}, bf16[128,512]{1,0:T(8,128)(2,1)S(1)}, u32[]{:S(2)}, u32[]{:S(2)}) collective-permute-start(bf16[128,512]{1,0:T(8,128)(2,1)S(1)} %collective-permute-done.6.refs_1_), channel_id=1, source_target_pairs={{0,8},{2,6},{4,12},{6,2},{8,0},{10,14},{12,4},{14,10},{16,24},{18,... | collective-permute-start | bytes 393224 | tf_op jit(solution)/shard_map/ppermute | solution.py:27
  25.7 0.1 collective-permute-start.12
  25.8 0.0 copy-done.2
  25.8 0.0 copy-done.3
  25.8 0.0 copy-done.4
  25.8 2.9 %shard_map.57 = (f32[2048,256]{1,0:T(8,128)S(1)}, bf16[2048,128]{1,0:T(8,128)(2,1)S(1)}) custom-call(s32[2]{0:T(128)S(1)} %copy-done.4, s32[2,16]{1,0:T(2,128)S(1)} %copy-done.3, bf16[128,4096]{1,0:T(8,128)(2,1)S(1)} %copy-done.2, bf16[128,512]{1,0:T(8,128)(2,1)S(1)} %get-tuple-element.37.refs_0_, bf16[128,512]{1,0:T(8,128)(2,1)S(1)} %collective-permute-done.refs_1_, ...), custom_call_target="tpu_custom_call" | custom-call | flops 1610612736 | bytes 1441792 | tf_op jit(solution)/shard_map/pallas_call | solution.py:299
  28.7 0.7 collective-permute-done.9.refs_6_
  29.4 0.0 collective-permute-done.11
  29.4 1.1 %collective-permute-start.14 = (bf16[256,512]{1,0:T(8,128)(2,1)S(1)}, bf16[256,512]{1,0:T(8,128)(2,1)S(1)}, u32[]{:S(2)}, u32[]{:S(2)}) collective-permute-start(bf16[256,512]{1,0:T(8,128)(2,1)S(1)} %constant_dynamic-update-slice_fusion.refs_5_), channel_id=1, source_target_pairs={{0,8},{2,6},{4,12},{6,2},{8,0},{10,14},{12,4},{14,10},{16,24},{18,... | collective-permute-start | bytes 786440 | tf_op jit(solution)/shard_map/ppermute | solution.py:27
  30.5 0.0 collective-permute-done.8.refs_4_
  30.6 0.1 collective-permute-start.10
  30.7 0.0 collective-permute-done.12.refs_3_
  30.7 2.9 %shard_map.59 = (f32[2048,256]{1,0:T(8,128)S(1)}, bf16[2048,128]{1,0:T(8,128)(2,1)S(1)}) custom-call(s32[2]{0:T(128)S(1)} %copy-done.4, s32[2,16]{1,0:T(2,128)S(1)} %copy-done.3, bf16[128,4096]{1,0:T(8,128)(2,1)S(1)} %copy-done.2, bf16[128,512]{1,0:T(8,128)(2,1)S(1)} %get-tuple-element.46.refs_0_, bf16[128,512]{1,0:T(8,128)(2,1)S(1)} %collective-permute-done.6.refs_1_, ...), custom_call_target="tpu_custom_call" | custom-call | flops 1610612736 | bytes 1441792 | tf_op jit(solution)/shard_map/pallas_call | solution.py:299
  33.6 2.3 %collective-permute-done.14.refs_6_ = bf16[256,512]{1,0:T(8,128)(2,1)S(1)} collective-permute-done((bf16[256,512]{1,0:T(8,128)(2,1)S(1)}, bf16[256,512]{1,0:T(8,128)(2,1)S(1)}, u32[]{:S(2)}, u32[]{:S(2)}) %collective-permute-start.14) | collective-permute-done | bytes 262176 | tf_op jit(solution)/shard_map/ppermute | solution.py:27
  35.9 0.0 collective-permute-done.13.refs_4_
  35.9 0.1 collective-permute-start.15
  36.0 0.0 collective-permute-done.10.refs_7_
  36.0 15.9 %shard_map.58 = (bf16[64,2048]{1,0:T(8,128)(2,1)S(1)}, bf16[64,2048]{1,0:T(8,128)(2,1)S(1)}) custom-call(s32[2]{0:T(128)S(1)} %copy-done.4, s32[2,16]{1,0:T(2,128)S(1)} %copy-done.3, bf16[128,4096]{1,0:T(8,128)(2,1)S(1)} %copy-done.2, bf16[128,512]{1,0:T(8,128)(2,1)S(1)} %get-tuple-element.37.refs_0_, bf16[128,512]{1,0:T(8,128)(2,1)S(1)} %collective-permute-done.refs_1_, ...), custom_call_target="tpu_custom_call" | custom-call | flops 2684354560 | bytes 1703936 | tf_op jit(solution)/shard_map/pallas_call | solution.py:299
  51.9 0.1 collective-permute-start.16
  52.0 0.0 collective-permute-done.15.refs_7_
  52.0 15.7 %shard_map.60 = (bf16[64,2048]{1,0:T(8,128)(2,1)S(1)}, bf16[64,2048]{1,0:T(8,128)(2,1)S(1)}) custom-call(s32[2]{0:T(128)S(1)} %copy-done.4, s32[2,16]{1,0:T(2,128)S(1)} %copy-done.3, bf16[128,4096]{1,0:T(8,128)(2,1)S(1)} %copy-done.2, bf16[128,512]{1,0:T(8,128)(2,1)S(1)} %get-tuple-element.46.refs_0_, bf16[128,512]{1,0:T(8,128)(2,1)S(1)} %collective-permute-done.6.refs_1_, ...), custom_call_target="tpu_custom_call" | custom-call | flops 2684354560 | bytes 1703936 | tf_op jit(solution)/shard_map/pallas_call | solution.py:299
  67.6 0.1 collective-permute-start.17
  67.7 0.0 collective-permute-done.16.refs_2_
  67.7 0.9 %shard_map.61.refs_0_ = bf16[64,8192]{1,0:T(8,128)(2,1)} custom-call(bf16[64,2048]{1,0:T(8,128)(2,1)S(1)} %get-tuple-element.57.refs_0_, bf16[64,2048]{1,0:T(8,128)(2,1)S(1)} %get-tuple-element.66.refs_1_, bf16[64,2048]{1,0:T(8,128)(2,1)S(1)} %collective-permute-done.16.refs_2_), custom_call_target="tpu_custom_call" | custom-call | tf_op jit(solution)/shard_map/pallas_call | solution.py:375
  68.6 7.8 %collective-permute-done.17.refs_1_ = bf16[64,2048]{1,0:T(8,128)(2,1)S(1)} collective-permute-done((bf16[64,2048]{1,0:T(8,128)(2,1)S(1)}, bf16[64,2048]{1,0:T(8,128)(2,1)S(1)}, u32[]{:S(2)}, u32[]{:S(2)}) %collective-permute-start.17) | collective-permute-done | bytes 262176 | tf_op jit(solution)/shard_map/ppermute | solution.py:482
  76.4 0.7 shard_map.62
  (15 shorter events, 0.2 us)
Async XLA Ops:
  0.0 0.9 %copy-start = (bf16[128,1024]{1,0:T(8,128)(2,1)S(1)}, bf16[128,1024]{1,0:T(8,128)(2,1)}, u32[]{:S(2)}) copy-start(bf16[128,1024]{1,0:T(8,128)(2,1)} %from_ref.1) | copy-start | bytes 786436
  1.0 8.2 %collective-permute-start = (bf16[128,512]{1,0:T(8,128)(2,1)S(1)}, bf16[128,512]{1,0:T(8,128)(2,1)S(1)}, u32[]{:S(2)}, u32[]{:S(2)}) collective-permute-start(bf16[128,512]{1,0:T(8,128)(2,1)S(1)} %get-tuple-element.37.refs_0_), channel_id=1, source_target_pairs={{0,4},{2,10},{4,0},{6,14},{8,12},{10,2},{12,8},{14,6},{16,20},{18,... | collective-permute-start | bytes 393224 | tf_op jit(solution)/shard_map/ppermute | solution.py:27
  4.0 5.2 %collective-permute-start.1 = (bf16[128,512]{1,0:T(8,128)(2,1)S(1)}, bf16[128,512]{1,0:T(8,128)(2,1)S(1)}, u32[]{:S(2)}, u32[]{:S(2)}) collective-permute-start(bf16[128,512]{1,0:T(8,128)(2,1)S(1)} %get-tuple-element.37.refs_0_), channel_id=1, source_target_pairs={{0,8},{2,6},{4,12},{6,2},{8,0},{10,14},{12,4},{14,10},{16,24},{18,... | collective-permute-start | bytes 393224 | tf_op jit(solution)/shard_map/ppermute | solution.py:27
  5.6 0.9 %copy-start.1 = (bf16[2,64,1024]{2,1,0:T(8,128)(2,1)S(1)}, bf16[2,64,1024]{2,1,0:T(8,128)(2,1)}, u32[]{:S(2)}) copy-start(bf16[2,64,1024]{2,1,0:T(8,128)(2,1)} %cache_ref.1) | copy-start | bytes 786436
  6.5 5.9 %collective-permute-start.3 = (bf16[64,512]{1,0:T(8,128)(2,1)S(1)}, bf16[64,512]{1,0:T(8,128)(2,1)S(1)}, u32[]{:S(2)}, u32[]{:S(2)}) collective-permute-start(bf16[64,512]{1,0:T(8,128)(2,1)S(1)} %get-tuple-element.41), channel_id=1, source_target_pairs={{0,16},{2,18},{4,20},{6,22},{8,24},{10,26},{12,28},{14,30},{16,0},... | collective-permute-start | bytes 196616 | tf_op jit(solution)/shard_map/ppermute | solution.py:27
  9.2 16.6 %copy-start.2 = (bf16[128,4096]{1,0:T(8,128)(2,1)S(1)}, bf16[128,4096]{1,0:T(8,128)(2,1)}, u32[]{:S(2)}) copy-start(bf16[128,4096]{1,0:T(8,128)(2,1)} %q_ref.7) | copy-start | bytes 3145732
  9.2 16.6 %copy-start.3 = (s32[2,16]{1,0:T(2,128)S(1)}, s32[2,16]{1,0:T(2,128)}, u32[]{:S(2)}) copy-start(s32[2,16]{1,0:T(2,128)} %owner_ref.7) | copy-start | bytes 388
  9.2 16.6 %copy-start.4 = (s32[2]{0:T(128)S(1)}, s32[2]{0:T(128)}, u32[]{:S(2)}) copy-start(s32[2]{0:T(128)} %limit_ref.7) | copy-start | bytes 28
  9.2 13.8 %collective-permute-start.2 = (bf16[384,512]{1,0:T(8,128)(2,1)S(1)}, bf16[384,512]{1,0:T(8,128)(2,1)S(1)}, u32[]{:S(2)}, u32[]{:S(2)}) collective-permute-start(bf16[384,512]{1,0:T(8,128)(2,1)S(1)} %pad_maximum_fusion.2), channel_id=1, source_target_pairs={{0,2},{2,0},{4,6},{6,4},{8,10},{10,8},{12,14},{14,12},{16,18},{18,... | collective-permute-start | bytes 1179656 | tf_op jit(solution)/shard_map/ppermute | solution.py:27
  12.5 5.9 %collective-permute-start.5 = (bf16[64,512]{1,0:T(8,128)(2,1)S(1)}, bf16[64,512]{1,0:T(8,128)(2,1)S(1)}, u32[]{:S(2)}, u32[]{:S(2)}) collective-permute-start(bf16[64,512]{1,0:T(8,128)(2,1)S(1)} %get-tuple-element.45), channel_id=1, source_target_pairs={{0,16},{2,18},{4,20},{6,22},{8,24},{10,26},{12,28},{14,30},{16,0},... | collective-permute-start | bytes 196616 | tf_op jit(solution)/shard_map/ppermute | solution.py:27
  14.4 6.5 %collective-permute-start.4 = (bf16[128,512]{1,0:T(8,128)(2,1)S(1)}, bf16[128,512]{1,0:T(8,128)(2,1)S(1)}, u32[]{:S(2)}, u32[]{:S(2)}) collective-permute-start(bf16[128,512]{1,0:T(8,128)(2,1)S(1)} %pad_maximum_fusion.5), channel_id=1, source_target_pairs={{0,4},{2,10},{4,0},{6,14},{8,12},{10,2},{12,8},{14,6},{16,20},{18,... | collective-permute-start | bytes 393224 | tf_op jit(solution)/shard_map/ppermute | solution.py:27
  15.0 8.1 %collective-permute-start.6 = (bf16[128,512]{1,0:T(8,128)(2,1)S(1)}, bf16[128,512]{1,0:T(8,128)(2,1)S(1)}, u32[]{:S(2)}, u32[]{:S(2)}) collective-permute-start(bf16[128,512]{1,0:T(8,128)(2,1)S(1)} %get-tuple-element.46.refs_0_), channel_id=1, source_target_pairs={{0,4},{2,10},{4,0},{6,14},{8,12},{10,2},{12,8},{14,6},{16,20},{18,... | collective-permute-start | bytes 393224 | tf_op jit(solution)/shard_map/ppermute | solution.py:27
  16.4 6.6 %collective-permute-start.7 = (bf16[128,512]{1,0:T(8,128)(2,1)S(1)}, bf16[128,512]{1,0:T(8,128)(2,1)S(1)}, u32[]{:S(2)}, u32[]{:S(2)}) collective-permute-start(bf16[128,512]{1,0:T(8,128)(2,1)S(1)} %get-tuple-element.46.refs_0_), channel_id=1, source_target_pairs={{0,8},{2,6},{4,12},{6,2},{8,0},{10,14},{12,4},{14,10},{16,24},{18,... | collective-permute-start | bytes 393224 | tf_op jit(solution)/shard_map/ppermute | solution.py:27
  18.3 12.2 %collective-permute-start.8 = (bf16[128,512]{1,0:T(8,128)(2,1)S(1)}, bf16[128,512]{1,0:T(8,128)(2,1)S(1)}, u32[]{:S(2)}, u32[]{:S(2)}) collective-permute-start(bf16[128,512]{1,0:T(8,128)(2,1)S(1)} %collective-permute-done.refs_1_), channel_id=1, source_target_pairs={{0,8},{2,6},{4,12},{6,2},{8,0},{10,14},{12,4},{14,10},{16,24},{18,... | collective-permute-start | bytes 393224 | tf_op jit(solution)/shard_map/ppermute | solution.py:27
  23.0 6.4 %collective-permute-start.9 = (bf16[256,512]{1,0:T(8,128)(2,1)S(1)}, bf16[256,512]{1,0:T(8,128)(2,1)S(1)}, u32[]{:S(2)}, u32[]{:S(2)}) collective-permute-start(bf16[256,512]{1,0:T(8,128)(2,1)S(1)} %pad_maximum_fusion.4.refs_5_), channel_id=1, source_target_pairs={{0,8},{2,6},{4,12},{6,2},{8,0},{10,14},{12,4},{14,10},{16,24},{18,... | collective-permute-start | bytes 786440 | tf_op jit(solution)/shard_map/ppermute | solution.py:27
  24.1 5.3 %collective-permute-start.11 = (bf16[128,512]{1,0:T(8,128)(2,1)S(1)}, bf16[128,512]{1,0:T(8,128)(2,1)S(1)}, u32[]{:S(2)}, u32[]{:S(2)}) collective-permute-start(bf16[128,512]{1,0:T(8,128)(2,1)S(1)} %pad_maximum_fusion.6), channel_id=1, source_target_pairs={{0,4},{2,10},{4,0},{6,14},{8,12},{10,2},{12,8},{14,6},{16,20},{18,... | collective-permute-start | bytes 393224 | tf_op jit(solution)/shard_map/ppermute | solution.py:27
  24.6 11.3 %collective-permute-start.13 = (bf16[128,512]{1,0:T(8,128)(2,1)S(1)}, bf16[128,512]{1,0:T(8,128)(2,1)S(1)}, u32[]{:S(2)}, u32[]{:S(2)}) collective-permute-start(bf16[128,512]{1,0:T(8,128)(2,1)S(1)} %collective-permute-done.6.refs_1_), channel_id=1, source_target_pairs={{0,8},{2,6},{4,12},{6,2},{8,0},{10,14},{12,4},{14,10},{16,24},{18,... | collective-permute-start | bytes 393224 | tf_op jit(solution)/shard_map/ppermute | solution.py:27
  25.7 4.9 %collective-permute-start.12 = (bf16[384,512]{1,0:T(8,128)(2,1)S(1)}, bf16[384,512]{1,0:T(8,128)(2,1)S(1)}, u32[]{:S(2)}, u32[]{:S(2)}) collective-permute-start(bf16[384,512]{1,0:T(8,128)(2,1)S(1)} %pad_maximum_fusion.3), channel_id=1, source_target_pairs={{0,2},{2,0},{4,6},{6,4},{8,10},{10,8},{12,14},{14,12},{16,18},{18,... | collective-permute-start | bytes 1179656 | tf_op jit(solution)/shard_map/ppermute | solution.py:27
  29.4 6.4 %collective-permute-start.14 = (bf16[256,512]{1,0:T(8,128)(2,1)S(1)}, bf16[256,512]{1,0:T(8,128)(2,1)S(1)}, u32[]{:S(2)}, u32[]{:S(2)}) collective-permute-start(bf16[256,512]{1,0:T(8,128)(2,1)S(1)} %constant_dynamic-update-slice_fusion.refs_5_), channel_id=1, source_target_pairs={{0,8},{2,6},{4,12},{6,2},{8,0},{10,14},{12,4},{14,10},{16,24},{18,... | collective-permute-start | bytes 786440 | tf_op jit(solution)/shard_map/ppermute | solution.py:27
  30.6 5.4 %collective-permute-start.10 = (bf16[640,512]{1,0:T(8,128)(2,1)S(1)}, bf16[640,512]{1,0:T(8,128)(2,1)S(1)}, u32[]{:S(2)}, u32[]{:S(2)}) collective-permute-start(bf16[640,512]{1,0:T(8,128)(2,1)S(1)} %pad_maximum_fusion), channel_id=1, source_target_pairs={{0,2},{2,0},{4,6},{6,4},{8,10},{10,8},{12,14},{14,12},{16,18},{18,... | collective-permute-start | bytes 1966088 | tf_op jit(solution)/shard_map/ppermute | solution.py:27
  35.9 16.0 %collective-permute-start.15 = (bf16[640,512]{1,0:T(8,128)(2,1)S(1)}, bf16[640,512]{1,0:T(8,128)(2,1)S(1)}, u32[]{:S(2)}, u32[]{:S(2)}) collective-permute-start(bf16[640,512]{1,0:T(8,128)(2,1)S(1)} %pad_maximum_fusion.1), channel_id=1, source_target_pairs={{0,2},{2,0},{4,6},{6,4},{8,10},{10,8},{12,14},{14,12},{16,18},{18,... | collective-permute-start | bytes 1966088 | tf_op jit(solution)/shard_map/ppermute | solution.py:27
  51.9 15.8 %collective-permute-start.16 = (bf16[64,2048]{1,0:T(8,128)(2,1)S(1)}, bf16[64,2048]{1,0:T(8,128)(2,1)S(1)}, u32[]{:S(2)}, u32[]{:S(2)}) collective-permute-start(bf16[64,2048]{1,0:T(8,128)(2,1)S(1)} %get-tuple-element.67), channel_id=1, source_target_pairs={{0,1},{1,0},{2,3},{3,2},{4,5},{5,4},{6,7},{7,6},{8,9},{9,8},{10,11... | collective-permute-start | bytes 786440 | tf_op jit(solution)/shard_map/ppermute | solution.py:482
  67.6 8.8 %collective-permute-start.17 = (bf16[64,2048]{1,0:T(8,128)(2,1)S(1)}, bf16[64,2048]{1,0:T(8,128)(2,1)S(1)}, u32[]{:S(2)}, u32[]{:S(2)}) collective-permute-start(bf16[64,2048]{1,0:T(8,128)(2,1)S(1)} %get-tuple-element.68), channel_id=1, source_target_pairs={{0,1},{1,0},{2,3},{3,2},{4,5},{5,4},{6,7},{7,6},{8,9},{9,8},{10,11... | collective-permute-start | bytes 786440 | tf_op jit(solution)/shard_map/ppermute | solution.py:482

commit v16 on v12

v16 whole, which is shorter than its diff:
```python
import functools
import math

import jax
import jax.numpy as jnp
from jax import lax
from jax.experimental import pallas as pl
from jax.experimental.pallas import tpu as pltpu
from jax.sharding import PartitionSpec as P

QH = 64
KVH = 8
HD = 128
REQS = 2
PER_GROUP = QH // KVH
EXP2_SCALE = HD ** (-0.5) * math.log2(math.e)
MASKED = -1e30
KEY_CHUNK = 256
HEADS_A_BLOCK = (2, 4, 2)
SHIFT_STEP = 32.0
LOWEST_TOTAL = 1e-20
HIGHEST_TOTAL = 1e30
SPAN_ROWS, OWN_PAGE, CROSSED_PAGE = range(3)


def hop(value, bit_of_core):
    count = lax.axis_size("seq")
    return lax.ppermute(
        value, "seq", [(source, source ^ bit_of_core[source % 2]) for source in range(count)]
    )


def together(*values):
    return lax.optimization_barrier(values)


def shifted(layout, slots):
    return [(slot + slots, kind, rows) for slot, kind, rows in layout]


def hypercube_order(bits):
    order = [0]
    for bit in bits:
        order = order + [offset ^ bit for offset in order]
    return order


def mask_kernel(spec, layouts, limit_ref, owner_ref, *refs):
    tokens, page, group_size, _, orders = spec
    outs, page_seen = refs[:-1], refs[-1]
    me = lax.axis_index("seq")
    request = me // group_size
    offsets = [hypercube_order(order) for order in orders]

    def note_page(index, carry):
        page_seen[owner_ref[request, index]] = jnp.clip(limit_ref[request] - index * page, 0, page)
        return carry

    lax.fori_loop(0, owner_ref.shape[1], note_page, 0)
    for out, layout in zip(outs, layouts):
        start = 0
        for half in range(2):
            holder = me ^ half
            for slot, kind, rows in layout:
                source = holder ^ jnp.where(holder % 2 == 0, offsets[0][slot], offsets[1][slot])
                if kind == SPAN_ROWS:
                    count = jnp.where(source <= me, tokens, 0)
                elif kind == OWN_PAGE:
                    count = page_seen[source]
                else:
                    count = page_seen[source ^ group_size]
                row = lax.broadcasted_iota(jnp.int32, (rows, HD), 0)
                column = lax.broadcasted_iota(jnp.int32, (rows, HD), 1)
                mask = jnp.where(row < count, jnp.float32(0.0), jnp.float32(MASKED))
                one = jnp.where(column == 1, jnp.float32(1.0), jnp.float32(0.0))
                out[pl.ds(start, rows), :] = jnp.where(column == 0, mask, one).astype(jnp.bfloat16)
                start += rows


def masks(limits, owners, layouts, spec):
    scalars = pl.BlockSpec(memory_space=pltpu.SMEM)
    counts = [2 * sum(rows for _, _, rows in layout) for layout in layouts]
    return list(
        pl.pallas_call(
            functools.partial(mask_kernel, spec, layouts),
            out_shape=[jax.ShapeDtypeStruct((count, HD), jnp.bfloat16) for count in counts],
            in_specs=[scalars] * 2,
            out_specs=[pl.BlockSpec(memory_space=pltpu.VMEM)] * len(counts),
            scratch_shapes=[pltpu.SMEM((owners.shape[1],), jnp.int32)],
            compiler_params=pltpu.CompilerParams(vmem_limit_bytes=16 << 20),
        )(limits, owners)
    )


def attend_kernel(spec, sizes, part, groups, q_ref, *refs):
    tokens, _, _, head_size, _ = spec
    first_phase = len(sizes) == 1
    key_sets = []
    for counts in sizes:
        extra, refs = refs[0], refs[1:]
        halves = []
        for count in counts:
            halves.append(refs[:count])
            refs = refs[count:]
        key_sets.append((halves, extra))
    (state_sum, state_extra), refs = refs[:2], refs[2:]
    if first_phase:
        keys, values, weights = refs[0], refs[1], refs[2:4]
    else:
        outs, keys, values, weights = refs[:2], refs[2], refs[3], refs[4:6]
        slow_sum, slow_top = refs[6], refs[7]
    chunk = KEY_CHUNK
    my_head = lax.axis_index("head")

    def key_count(halves):
        return sum(ref.shape[0] for half in halves for ref in half)

    def fill(group, halves, extra):
        total_keys = key_count(halves)
        column = (part * groups + group) * 2 * HD
        start = 0
        for ref in [ref for half in halves for ref in half]:
            at = pl.ds(start, ref.shape[0])
            first = column % ref.shape[1]
            keys[group, at, :HD] = ref[:, pl.ds(first, HD)]
            values[group, at, :HD] = ref[:, pl.ds(first + HD, HD)]
            start += ref.shape[0]
        keys[group, :total_keys, HD:] = extra[...]
        values[group, :total_keys, HD:] = jnp.ones((total_keys, HD), jnp.bfloat16)

    def lane_of(heads):
        return lax.broadcasted_iota(jnp.int32, (heads * tokens, HD), 1)

    def query_rows(first, heads):
        at = part * groups * PER_GROUP + first
        columns = [pl.ds(pl.multiple_of((at + head) * HD, HD), HD) for head in range(heads)]
        return jnp.concatenate([q_ref[:, column] for column in columns], axis=0)

    def scores_of(query, group, start, is_span):
        made = lax.dot_general(
            query,
            keys[group, pl.ds(start, chunk), :],
            (((1,), (1,)), ((), ())),
            preferred_element_type=jnp.float32,
        )
        if start == 0 and is_span:
            rows = query.shape[0]
            causal = lax.broadcasted_iota(jnp.int32, (rows, tokens), 1) <= (
                lax.broadcasted_iota(jnp.int32, (rows, tokens), 0) % tokens
            )
            own = jnp.where(causal, made[:, :tokens], MASKED)
            made = jnp.concatenate([own, made[:, tokens:]], axis=1)
        return made

    def give(first, heads, result):
        kept = tokens // head_size
        for head in range(heads):
            column = pl.ds((first + head) * HD, HD)
            one = result[head * tokens : (head + 1) * tokens]
            if head_size == 2:
                low, high = one[:kept], one[kept:]
                outs[0][:, column] = jnp.where(my_head == 0, low, high)
                outs[1][:, column] = jnp.where(my_head == 0, high, low)
            else:
                outs[0][:, column] = one[:kept]
                outs[1][:, column] = one[kept:]

    halves, extra_ref = key_sets[-1]
    total_keys = key_count(halves)
    longest = [None] * groups

    def begin(group):
        fill(group, halves, extra_ref)
        if first_phase:
            key = keys[group, :total_keys, :HD].astype(jnp.float32)
            squares = jnp.sum(key * key, axis=1, keepdims=True)
            longest[group] = jnp.max(squares, axis=0, keepdims=True)

    def weigh(index):
        group, first, heads = blocks[index]
        rows = pl.ds(first * tokens, heads * tokens)
        query = query_rows(first, heads)
        if first_phase:
            wide = query.astype(jnp.float32)
            bound = jnp.sqrt(jnp.sum(wide * wide, axis=1, keepdims=True) * longest[group])
            shift = jnp.ceil(bound * (1.0 / SHIFT_STEP)) * SHIFT_STEP
            lane = lane_of(heads)
            extra = jnp.where(lane == 0, 1.0, jnp.where(lane == 1, -shift, 0.0))
            extra = extra.astype(jnp.bfloat16)
            state_extra[rows, :] = extra
        else:
            extra = state_extra[pl.ds((part * groups * PER_GROUP + first) * tokens, heads * tokens), :]
        query = jnp.concatenate([query, extra], axis=1)
        for start in range(0, total_keys, chunk):
            made = scores_of(query, group, start, first_phase)
            weights[index % 2][: heads * tokens, pl.ds(start, chunk)] = jnp.exp2(
                made * EXP2_SCALE
            ).astype(jnp.bfloat16)

    def finish(index, extremes):
        group, first, heads = blocks[index]
        summed = jnp.dot(
            weights[index % 2][: heads * tokens, :total_keys],
            values[group, :total_keys, :],
            preferred_element_type=jnp.float32,
        )
        if first_phase:
            state_sum[pl.ds(first * tokens, heads * tokens), :] = summed
            return extremes
        old = pl.ds((part * groups * PER_GROUP + first) * tokens, heads * tokens)
        summed = summed + state_sum[old, :]
        total = summed[:, HD:]
        give(first, heads, (summed[:, :HD] / total).astype(jnp.bfloat16))
        lowest, highest = extremes
        for head in range(heads):
            one = total[head * tokens : (head + 1) * tokens]
            lowest, highest = jnp.minimum(lowest, one), jnp.maximum(highest, one)
        return lowest, highest

    blocks = []
    for group in range(groups):
        at = group * PER_GROUP
        for heads in HEADS_A_BLOCK:
            blocks.append((group, at, heads))
            at += heads
    begin(0)
    extremes = (jnp.ones((tokens, HD), jnp.float32),) * 2
    for index in range(len(blocks) + 1):
        if index >= 1:
            extremes = finish(index - 1, extremes)
        if index < len(blocks):
            weigh(index)
            if index + 1 < len(blocks) and blocks[index + 1][0] != blocks[index][0]:
                begin(blocks[index + 1][0])
    if first_phase:
        return

    @pl.when((jnp.min(extremes[0]) < LOWEST_TOTAL) | (jnp.max(extremes[1]) > HIGHEST_TOTAL))
    def exact():
        heads = 4
        block = heads * tokens
        count = groups * PER_GROUP // heads
        for number, (halves, extra_ref) in enumerate(key_sets):
            for group in range(groups):
                fill(group, halves, extra_ref)

            def one_block(index, carry):
                group = index * heads // PER_GROUP
                extra = (lane_of(heads) == 0).astype(jnp.float32).astype(jnp.bfloat16)
                query = jnp.concatenate([query_rows(index * heads, heads), extra], axis=1)
                rows = pl.ds(pl.multiple_of(index * block, block), block)
                if number == 0:
                    top = jnp.full((block, HD), MASKED, jnp.float32)
                    summed = jnp.zeros((block, 2 * HD), jnp.float32)
                else:
                    top = slow_top[rows, :]
                    summed = slow_sum[rows, :]
                best = top
                for start in range(0, key_count(halves), chunk):
                    made = scores_of(query, group, start, number == 0)
                    for at in range(0, chunk, HD):
                        best = jnp.maximum(best, made[:, at : at + HD])
                best = jnp.broadcast_to(jnp.max(best, axis=1, keepdims=True), (block, HD))
                fade = jnp.exp2((top - best) * EXP2_SCALE)
                summed = summed * jnp.concatenate([fade, fade], axis=1)
                for start in range(0, key_count(halves), chunk):
                    made = scores_of(query, group, start, number == 0)
                    parts = [
                        jnp.exp2((made[:, at : at + HD] - best) * EXP2_SCALE)
                        for at in range(0, chunk, HD)
                    ]
                    summed = summed + jnp.dot(
                        jnp.concatenate(parts, axis=1).astype(jnp.bfloat16),
                        values[group, pl.ds(start, chunk), :],
                        preferred_element_type=jnp.float32,
                    )
                slow_top[rows, :] = best
                slow_sum[rows, :] = summed
                return carry

            lax.fori_loop(0, count, one_block, 0)
        for index in range(count):
            rows = pl.ds(index * block, block)
            result = (slow_sum[rows, :HD] / slow_sum[rows, HD:]).astype(jnp.bfloat16)
            give(index * heads, heads, result)


def attend(queries, part, parts, key_sets, spec, state):
    tokens, _, _, head_size = spec[:4]
    total_keys = max(extra.shape[0] for _, _, extra in key_sets)
    columns = queries.shape[1] // parts
    groups = columns // (PER_GROUP * HD)
    block = max(HEADS_A_BLOCK) * tokens
    rows = PER_GROUP * groups * tokens
    pieces = [piece for mine, theirs, extra in key_sets for piece in [extra] + mine + theirs]
    sizes = tuple((len(mine), len(theirs)) for mine, theirs, _ in key_sets)
    operands = queries.size * 2 + sum(piece.size for piece in pieces) * 2 + rows * HD * 12
    scratch = groups * total_keys * HD * 8 + block * total_keys * 4 + rows * HD * 12
    whole = pl.BlockSpec(memory_space=pltpu.VMEM)
    kept = tokens // head_size
    scratch_shapes = [pltpu.VMEM((groups, total_keys, 2 * HD), jnp.bfloat16)] * 2
    scratch_shapes += [pltpu.VMEM((block, total_keys), jnp.bfloat16)] * 2
    if state is None:
        state = ()
        out_shape = [
            jax.ShapeDtypeStruct((rows, 2 * HD), jnp.float32),
            jax.ShapeDtypeStruct((rows, HD), jnp.bfloat16),
        ]
    else:
        out_shape = [
            jax.ShapeDtypeStruct((kept, columns), jnp.bfloat16),
            jax.ShapeDtypeStruct((tokens - kept, columns), jnp.bfloat16),
        ]
        scratch_shapes += [
            pltpu.VMEM((rows, 2 * HD), jnp.float32),
            pltpu.VMEM((rows, HD), jnp.float32),
        ]
    return pl.pallas_call(
        functools.partial(attend_kernel, spec, sizes, part, groups),
        out_shape=out_shape,
        in_specs=[whole] * (1 + len(pieces) + len(state)),
        out_specs=[whole] * 2,
        scratch_shapes=scratch_shapes,
        compiler_params=pltpu.CompilerParams(vmem_limit_bytes=operands + scratch + (8 << 20)),
        cost_estimate=pl.CostEstimate(
            flops=8 * tokens * columns * total_keys,
            bytes_accessed=4 * tokens * columns + 2 * total_keys * columns // PER_GROUP,
            transcendentals=0,
        ),
    )(queries, *pieces, *state)


def pick_kernel(group_size, cache_ref, other_ref, own_ref):
    request = lax.axis_index("seq") // group_size
    other_ref[...] = cache_ref[1 - request]
    own_ref[...] = cache_ref[request]


def pick(cache, group_size):
    whole = pl.BlockSpec(memory_space=pltpu.VMEM)
    return pl.pallas_call(
        functools.partial(pick_kernel, group_size),
        out_shape=[jax.ShapeDtypeStruct(cache.shape[1:], cache.dtype)] * 2,
        in_specs=[whole],
        out_specs=[whole] * 2,
        compiler_params=pltpu.CompilerParams(vmem_limit_bytes=8 << 20),
    )(cache)


def join_kernel(spots, count, *refs):
    parts, (out_ref, done) = refs[len(refs) - 2 - count : -2], refs[-2:]
    side = out_ref.shape[1] // 2
    my_head = lax.axis_index("head")
    copies = []
    for at, (ref, (received, start)) in enumerate(zip(parts, spots)):
        owner = 1 - my_head if received else my_head
        first = pl.multiple_of(owner * side + start, HD)
        copies.append(
            pltpu.make_async_copy(ref, out_ref.at[:, pl.ds(first, ref.shape[1])], done.at[at])
        )
    for copy in copies:
        copy.start()
    for copy in copies:
        copy.wait()


def join(pieces, spots, columns, partial):
    earlier = [] if partial is None else [partial]
    return pl.pallas_call(
        functools.partial(join_kernel, spots, len(pieces)),
        out_shape=jax.ShapeDtypeStruct((pieces[0].shape[0], columns), pieces[0].dtype),
        in_specs=[pl.BlockSpec(memory_space=pl.ANY)] * len(earlier)
        + [pl.BlockSpec(memory_space=pltpu.VMEM)] * len(pieces),
        out_specs=pl.BlockSpec(memory_space=pl.ANY),
        scratch_shapes=[pltpu.SemaphoreType.DMA((len(pieces),))],
        input_output_aliases={0: 0} if earlier else {},
        compiler_params=pltpu.CompilerParams(vmem_limit_bytes=8 << 20),
    )(*earlier, *pieces)


def put_together(kept, received):
    columns = kept[0].shape[1]
    pieces = kept + received
    spots = [(at >= len(kept), at % len(kept) * columns) for at in range(len(pieces))]
    out = join(pieces[:-1], spots[:-1], columns * len(pieces), None)
    return join(pieces[-1:], spots[-1:], columns * len(pieces), out)


def body(span_query, span_kv, prefix_cache, prefix_len, block_owner):
    seq_size = lax.axis_size("seq")
    head_size = lax.axis_size("head")
    group_size = seq_size // REQS
    tokens = span_kv.shape[0]
    page = prefix_cache.shape[1]
    groups = span_kv.shape[1] // (2 * HD)
    parts = 2 if groups % 2 == 0 else 1
    bits = [1 << at for at in range(1, group_size.bit_length() - 1)]
    orders = (bits, bits[::-1])

    stages = len(bits)

    def send(rows, stage):
        return hop(rows, tuple(order[stage] for order in orders))

    def swap_cores(pieces):
        return hop(pieces[0] if len(pieces) == 1 else jnp.concatenate(pieces, axis=0), (1, 1))

    def whole_layout(layout):
        for stage in range(stages):
            layout = layout + shifted(layout, 1 << stage)
        return layout

    span_layout = whole_layout([(0, SPAN_ROWS, tokens)])
    page_layout = whole_layout([(0, OWN_PAGE, page), (0, CROSSED_PAGE, page)])

    other_page, own_page = pick(prefix_cache, group_size)
    crossed = hop(other_page, (group_size, group_size))

    span_early = send(span_kv, stages - 1)
    span_forward = send(span_kv, 0)
    for stage in range(1, stages - 1):
        seen = jnp.concatenate([span_kv, span_forward], axis=0)
        span_forward = jnp.concatenate([span_forward, send(seen, stage)], axis=0)
    span_late = send(span_forward, stages - 1)
    spec = (tokens, page, group_size, head_size, orders)
    span_masks, page_masks = masks(prefix_len, block_owner, (span_layout, page_layout), spec)
    span_forward, span_masks, crossed = together(span_forward, span_masks, crossed)
    pages = [jnp.concatenate([own_page, crossed], axis=0)]
    pages.append(send(pages[0], 0))
    span_early, span_late = together(span_early, span_late)
    pages[1], span_late = together(pages[1], span_late)
    span = [jnp.concatenate([span_kv, span_forward, span_early, span_late], axis=0)]
    span_swapped = [swap_cores(span)]

    span_set = (span, span_swapped, span_masks)
    state = attend(span_query, 0, 1, [span_set], spec, None)

    for stage in range(1, stages - 1):
        pages.append(send(jnp.concatenate(pages, axis=0), stage))
    columns = span_kv.shape[1] // parts
    cuts = [slice(part * columns, (part + 1) * columns) for part in range(parts)]
    held = [jnp.concatenate([piece[:, cut] for piece in pages], axis=0) for cut in cuts]
    arrived = [send(rows, stages - 1) for rows in held]
    results = []
    for part in range(parts):
        arrived[part], state = together(arrived[part], state)
        mine = [held[part], arrived[part]]
        page_set = (mine, [swap_cores(mine)], page_masks)
        results.append(attend(span_query, part, parts, [span_set, page_set], spec, state))
    if head_size != 2:
        rows = jnp.concatenate([jnp.concatenate(pair, axis=0) for pair in results], axis=1)
        return lax.all_to_all(rows, "head", split_axis=0, concat_axis=1, tiled=True)
    kept = [pair[0] for pair in results]
    received = [lax.ppermute(pair[1], "head", [(0, 1), (1, 0)]) for pair in results]
    return put_together(kept, received)


def solution(mesh):
    placed = (P("seq", "head"), P("seq", "head"), P("seq", None, "head"), P(), P())
    return jax.shard_map(
        body, mesh=mesh, in_specs=placed, out_specs=P(("seq", "head"), None), check_vma=False
    )
```

time: 73.7 us -> 70.3 us (0.954)
  Pallas kernels: 37.9 us -> 13.4 us
  starting transfers between devices: 13.8 us -> 36.4 us
  waiting for transfers between devices: 18.7 us -> 16.5 us
  local copies, waits for them, and re-layouts: 1.99 us -> 3.37 us
    ppermute x2, starting transfers between devices: 0.14 us -> 25.1 us  [body(): lax.ppermute(pair[1], 'head', [(0, 1), (1, 0)])]
    pallas_call x4, Pallas kernels: 36.3 us -> 11.8 us  [the longest x3 11 us: attend(): pl.pallas_call(functools.partial(attend_kernel, spec, sizes, part, groups...]
    ppermute x10, starting transfers between devices: 13.7 us -> 11.3 us  [hop(): lax.ppermute(value, 'seq', [(source, source ^ bit_of_core[source % 2]) fo...]
    ppermute x2, waiting for transfers between devices: 7.76 us -> 5.7 us  [body(): lax.ppermute(pair[1], 'head', [(0, 1), (1, 0)])]
    unnamed x11 -> x12, local copies, waits for them, and re-layouts: 1.93 us -> 3.3 us
  transfers between devices with their start and end apart: 12 -> 12, of which waited for: 5 -> 6; matrix products, arithmetic and copies ran while one was open for 0% -> 2% of each run, Pallas kernels for 51% -> 18%
where the time goes in v16:
time: 70.3 us; the launch traced here: 70.1 us
  starting transfers between devices  36.4 us (52%)
  waiting for transfers between devices  16.5 us (23%)
  Pallas kernels  13.4 us (19%)
  local copies, waits for them, and re-layouts  3.37 us (5%)
    ppermute x2, starting transfers between devices, body(): lax.ppermute(pair[1], 'head', [(0, 1), (1, 0)])  25.1 us
    ppermute x10, starting transfers between devices, hop(): lax.ppermute(value, 'seq', [(source, source ^ bit_of_core[source % 2]) fo...  11.3 us
    pallas_call x3, Pallas kernels, attend(): pl.pallas_call(functools.partial(attend_kernel, spec, sizes, part, groups...  11 us
    ppermute x10, waiting for transfers between devices, hop(): lax.ppermute(value, 'seq', [(source, source ^ bit_of_core[source % 2]) fo...  10.8 us
    ppermute x2, waiting for transfers between devices, body(): lax.ppermute(pair[1], 'head', [(0, 1), (1, 0)])  5.7 us
    unnamed x12, local copies, waits for them, and re-layouts  3.3 us
    pallas_call x2, Pallas kernels, join(): pl.pallas_call(functools.partial(join_kernel, spots, len(pieces)), out_sh...  1.61 us
  transfers between devices with their start and end apart: 12, of which 6 were waited for; matrix products, arithmetic and copies ran while one was open for 2% of the time, Pallas kernels for 18%

profile of v16, /device:TPU:0, one launch (start us, length us, event | category | flops | bytes accessed | tf_op | source)
XLA Modules:
  0.0 70.1 jit_solution(8026180223662130881)
XLA Ops:
  0.0 0.0 copy-start
  0.0 2.9 %collective-permute-start = (bf16[128,1024]{1,0:T(8,128)(2,1)}, bf16[128,1024]{1,0:T(8,128)(2,1)S(1)}, u32[]{:S(2)}, u32[]{:S(2)}) collective-permute-start(bf16[128,1024]{1,0:T(8,128)(2,1)} %param.6), channel_id=1, source_target_pairs={{0,4},{2,10},{4,0},{6,14},{8,12},{10,2},{12,8},{14,6},{16,20},{18,... | collective-permute-start | bytes 786440 | tf_op jit(solution)/shard_map/ppermute | solution.py:28
  2.9 0.0 copy-start.1
  2.9 0.9 %copy-done.1 = bf16[2,64,1024]{2,1,0:T(8,128)(2,1)S(1)} copy-done((bf16[2,64,1024]{2,1,0:T(8,128)(2,1)S(1)}, bf16[2,64,1024]{2,1,0:T(8,128)(2,1)}, u32[]{:S(2)}) %copy-start.1) | copy-done | bytes 262168
  3.9 2.7 %collective-permute-start.1 = (bf16[64,1024]{1,0:T(8,128)(2,1)S(1)}, bf16[64,1024]{1,0:T(8,128)(2,1)S(1)}, u32[]{:S(2)}, u32[]{:S(2)}) collective-permute-start(bf16[64,1024]{1,0:T(8,128)(2,1)S(1)} %get-tuple-element.29), channel_id=1, source_target_pairs={{0,16},{2,18},{4,20},{6,22},{8,24},{10,26},{12,28},{14,30},{16,0},... | collective-permute-start | bytes 393224 | tf_op jit(solution)/shard_map/ppermute | solution.py:28
  6.6 1.6 %collective-permute-start.2 = (bf16[128,1024]{1,0:T(8,128)(2,1)}, bf16[128,1024]{1,0:T(8,128)(2,1)S(1)}, u32[]{:S(2)}, u32[]{:S(2)}) collective-permute-start(bf16[128,1024]{1,0:T(8,128)(2,1)} %param.6), channel_id=1, source_target_pairs={{0,8},{2,6},{4,12},{6,2},{8,0},{10,14},{12,4},{14,10},{16,24},{18,... | collective-permute-start | bytes 786440 | tf_op jit(solution)/shard_map/ppermute | solution.py:28
  8.1 0.0 copy-start.2
  8.1 0.7 copy-done.2
  8.8 0.0 copy-start.3
  8.8 0.7 copy-done.3
  9.5 0.8 %shard_map.55 = (bf16[1024,128]{1,0:T(8,128)(2,1)S(1)}, bf16[1024,128]{1,0:T(8,128)(2,1)S(1)}) custom-call(s32[2]{0:T(128)S(1)} %copy-done.3, s32[2,16]{1,0:T(2,128)S(1)} %copy-done.2), custom_call_target="tpu_custom_call" | custom-call | tf_op jit(solution)/shard_map/pallas_call | solution.py:84
  10.3 2.5 %collective-permute-done.1 = bf16[64,1024]{1,0:T(8,128)(2,1)S(1)} collective-permute-done((bf16[64,1024]{1,0:T(8,128)(2,1)S(1)}, bf16[64,1024]{1,0:T(8,128)(2,1)S(1)}, u32[]{:S(2)}, u32[]{:S(2)}) %collective-permute-start.1) | collective-permute-done | bytes 131104 | tf_op jit(solution)/shard_map/ppermute | solution.py:28
  12.8 0.0 collective-permute-done
  12.8 0.0 collective-permute-start.3
  12.9 1.6 %collective-permute-start.4 = (bf16[128,1024]{1,0:T(8,128)(2,1)S(1)}, bf16[128,1024]{1,0:T(8,128)(2,1)S(1)}, u32[]{:S(2)}, u32[]{:S(2)}) collective-permute-start(bf16[128,1024]{1,0:T(8,128)(2,1)S(1)} %constant_dynamic-update-slice_fusion), channel_id=1, source_target_pairs={{0,4},{2,10},{4,0},{6,14},{8,12},{10,2},{12,8},{14,6},{16,20},{18,... | collective-permute-start | bytes 786440 | tf_op jit(solution)/shard_map/ppermute | solution.py:28
  14.4 1.0 %constant_dynamic-update-slice_fusion.5 = bf16[512,1024]{1,0:T(8,128)(2,1)S(1)} fusion(bf16[128,1024]{1,0:T(8,128)(2,1)} %param.6), kind=kLoop, calls=%fused_computation.9 | loop fusion | bytes 524288
  15.4 0.0 collective-permute-done.2
  15.4 6.3 %collective-permute-done.3 = bf16[128,1024]{1,0:T(8,128)(2,1)S(1)} collective-permute-done((bf16[128,1024]{1,0:T(8,128)(2,1)S(1)}, bf16[128,1024]{1,0:T(8,128)(2,1)S(1)}, u32[]{:S(2)}, u32[]{:S(2)}) %collective-permute-start.3) | collective-permute-done | bytes 262176 | tf_op jit(solution)/shard_map/ppermute | solution.py:28
  21.7 0.0 collective-permute-done.4
  21.8 0.2 collective-permute-start.5
  22.0 0.1 collective-permute-start.6
  22.2 2.1 %collective-permute-start.8 = (bf16[256,512]{1,0:T(8,128)(2,1)S(1)}, bf16[256,512]{1,0:T(8,128)(2,1)S(1)}, u32[]{:S(2)}, u32[]{:S(2)}) collective-permute-start(bf16[256,512]{1,0:T(8,128)(2,1)S(1)} %pad_maximum_fusion.3.refs_4_), channel_id=1, source_target_pairs={{0,8},{2,6},{4,12},{6,2},{8,0},{10,14},{12,4},{14,10},{16,24},{18,... | collective-permute-start | bytes 786440 | tf_op jit(solution)/shard_map/ppermute | solution.py:28
  24.2 0.3 collective-permute-done.5.refs_2_
  24.5 0.0 copy-done
  24.5 5.6 %shard_map.57 = (f32[4096,256]{1,0:T(8,128)S(1)}, bf16[4096,128]{1,0:T(8,128)(2,1)S(1)}) custom-call(bf16[128,4096]{1,0:T(8,128)(2,1)S(1)} %copy-done, bf16[1024,128]{1,0:T(8,128)(2,1)S(1)} %get-tuple-element.30.refs_0_, bf16[512,1024]{1,0:T(8,128)(2,1)S(1)} %constant_dynamic-update-slice_fusion.2.refs_1_, bf16[512,1024]{1,0:T(8,128)(2,1)S(1)} %collective-permute-done.5.refs_2_), custom_call_target="tpu_custom_call" | custom-call | flops 4294967296 | bytes 3145728 | tf_op jit(solution)/shard_map/pallas_call | solution.py:318
  30.1 0.0 collective-permute-done.6.refs_5_
  30.1 0.2 collective-permute-start.7
  30.3 0.9 %collective-permute-done.8.refs_5_ = bf16[256,512]{1,0:T(8,128)(2,1)S(1)} collective-permute-done((bf16[256,512]{1,0:T(8,128)(2,1)S(1)}, bf16[256,512]{1,0:T(8,128)(2,1)S(1)}, u32[]{:S(2)}, u32[]{:S(2)}) %collective-permute-start.8) | collective-permute-done | bytes 262176 | tf_op jit(solution)/shard_map/ppermute | solution.py:28
  31.3 0.1 collective-permute-start.9
  31.4 0.7 %collective-permute-done.7.refs_6_ = bf16[512,512]{1,0:T(8,128)(2,1)S(1)} collective-permute-done((bf16[512,512]{1,0:T(8,128)(2,1)S(1)}, bf16[512,512]{1,0:T(8,128)(2,1)S(1)}, u32[]{:S(2)}, u32[]{:S(2)}) %collective-permute-start.7) | collective-permute-done | bytes 524320 | tf_op jit(solution)/shard_map/ppermute | solution.py:28
  32.1 2.8 %shard_map.58 = (bf16[64,2048]{1,0:T(8,128)(2,1)S(1)}, bf16[64,2048]{1,0:T(8,128)(2,1)S(1)}) custom-call(bf16[128,4096]{1,0:T(8,128)(2,1)S(1)} %copy-done, bf16[1024,128]{1,0:T(8,128)(2,1)S(1)} %get-tuple-element.30.refs_0_, bf16[512,1024]{1,0:T(8,128)(2,1)S(1)} %constant_dynamic-update-slice_fusion.2.refs_1_, ...), custom_call_target="tpu_custom_call" | custom-call | flops 2147483648 | bytes 1572864 | tf_op jit(solution)/shard_map/pallas_call | solution.py:318
  34.9 13.4 %collective-permute-start.10 = (bf16[64,2048]{1,0:T(8,128)(2,1)S(1)}, bf16[64,2048]{1,0:T(8,128)(2,1)S(1)}, u32[]{:S(2)}, u32[]{:S(2)}) collective-permute-start(bf16[64,2048]{1,0:T(8,128)(2,1)S(1)} %get-tuple-element.49), channel_id=1, source_target_pairs={{0,1},{1,0},{2,3},{3,2},{4,5},{5,4},{6,7},{7,6},{8,9},{9,8},{10,11... | collective-permute-start | bytes 786440 | tf_op jit(solution)/shard_map/ppermute | solution.py:454
  48.3 0.0 collective-permute-done.9.refs_6_
  48.3 2.6 %shard_map.59 = (bf16[64,2048]{1,0:T(8,128)(2,1)S(1)}, bf16[64,2048]{1,0:T(8,128)(2,1)S(1)}) custom-call(bf16[128,4096]{1,0:T(8,128)(2,1)S(1)} %copy-done, bf16[1024,128]{1,0:T(8,128)(2,1)S(1)} %get-tuple-element.30.refs_0_, bf16[512,1024]{1,0:T(8,128)(2,1)S(1)} %constant_dynamic-update-slice_fusion.2.refs_1_, ...), custom_call_target="tpu_custom_call" | custom-call | flops 2147483648 | bytes 1572864 | tf_op jit(solution)/shard_map/pallas_call | solution.py:318
  51.0 11.7 %collective-permute-start.11 = (bf16[64,2048]{1,0:T(8,128)(2,1)S(1)}, bf16[64,2048]{1,0:T(8,128)(2,1)S(1)}, u32[]{:S(2)}, u32[]{:S(2)}) collective-permute-start(bf16[64,2048]{1,0:T(8,128)(2,1)S(1)} %get-tuple-element.50), channel_id=1, source_target_pairs={{0,1},{1,0},{2,3},{3,2},{4,5},{5,4},{6,7},{7,6},{8,9},{9,8},{10,11... | collective-permute-start | bytes 786440 | tf_op jit(solution)/shard_map/ppermute | solution.py:454
  62.6 0.0 collective-permute-done.10.refs_2_
  62.6 0.9 %shard_map.60.refs_0_ = bf16[64,8192]{1,0:T(8,128)(2,1)} custom-call(bf16[64,2048]{1,0:T(8,128)(2,1)S(1)} %get-tuple-element.44.refs_0_, bf16[64,2048]{1,0:T(8,128)(2,1)S(1)} %get-tuple-element.48.refs_1_, bf16[64,2048]{1,0:T(8,128)(2,1)S(1)} %collective-permute-done.10.refs_2_), custom_call_target="tpu_custom_call" | custom-call | tf_op jit(solution)/shard_map/pallas_call | solution.py:369
  63.5 5.7 %collective-permute-done.11.refs_1_ = bf16[64,2048]{1,0:T(8,128)(2,1)S(1)} collective-permute-done((bf16[64,2048]{1,0:T(8,128)(2,1)S(1)}, bf16[64,2048]{1,0:T(8,128)(2,1)S(1)}, u32[]{:S(2)}, u32[]{:S(2)}) %collective-permute-start.11) | collective-permute-done | bytes 262176 | tf_op jit(solution)/shard_map/ppermute | solution.py:454
  69.2 0.7 %shard_map.61 = bf16[64,8192]{1,0:T(8,128)(2,1)} custom-call(bf16[64,8192]{1,0:T(8,128)(2,1)} %shard_map.60.refs_0_, bf16[64,2048]{1,0:T(8,128)(2,1)S(1)} %collective-permute-done.11.refs_1_), custom_call_target="tpu_custom_call", output_to_operand_aliasing={{}: (0, {})} | custom-call | tf_op jit(solution)/shard_map/pallas_call | solution.py:369
  (12 shorter events, 0.2 us)
Async XLA Ops:
  0.0 24.5 %copy-start = (bf16[128,4096]{1,0:T(8,128)(2,1)S(1)}, bf16[128,4096]{1,0:T(8,128)(2,1)}, u32[]{:S(2)}) copy-start(bf16[128,4096]{1,0:T(8,128)(2,1)} %q_ref.5) | copy-start | bytes 3145732
  0.0 12.8 %collective-permute-start = (bf16[128,1024]{1,0:T(8,128)(2,1)}, bf16[128,1024]{1,0:T(8,128)(2,1)S(1)}, u32[]{:S(2)}, u32[]{:S(2)}) collective-permute-start(bf16[128,1024]{1,0:T(8,128)(2,1)} %param.6), channel_id=1, source_target_pairs={{0,4},{2,10},{4,0},{6,14},{8,12},{10,2},{12,8},{14,6},{16,20},{18,... | collective-permute-start | bytes 786440 | tf_op jit(solution)/shard_map/ppermute | solution.py:28
  2.9 0.9 %copy-start.1 = (bf16[2,64,1024]{2,1,0:T(8,128)(2,1)S(1)}, bf16[2,64,1024]{2,1,0:T(8,128)(2,1)}, u32[]{:S(2)}) copy-start(bf16[2,64,1024]{2,1,0:T(8,128)(2,1)} %cache_ref.1) | copy-start | bytes 786436
  3.9 8.9 %collective-permute-start.1 = (bf16[64,1024]{1,0:T(8,128)(2,1)S(1)}, bf16[64,1024]{1,0:T(8,128)(2,1)S(1)}, u32[]{:S(2)}, u32[]{:S(2)}) collective-permute-start(bf16[64,1024]{1,0:T(8,128)(2,1)S(1)} %get-tuple-element.29), channel_id=1, source_target_pairs={{0,16},{2,18},{4,20},{6,22},{8,24},{10,26},{12,28},{14,30},{16,0},... | collective-permute-start | bytes 393224 | tf_op jit(solution)/shard_map/ppermute | solution.py:28
  6.6 8.8 %collective-permute-start.2 = (bf16[128,1024]{1,0:T(8,128)(2,1)}, bf16[128,1024]{1,0:T(8,128)(2,1)S(1)}, u32[]{:S(2)}, u32[]{:S(2)}) collective-permute-start(bf16[128,1024]{1,0:T(8,128)(2,1)} %param.6), channel_id=1, source_target_pairs={{0,8},{2,6},{4,12},{6,2},{8,0},{10,14},{12,4},{14,10},{16,24},{18,... | collective-permute-start | bytes 786440 | tf_op jit(solution)/shard_map/ppermute | solution.py:28
  8.1 0.7 copy-start.2
  8.8 0.7 copy-start.3
  12.8 8.9 %collective-permute-start.3 = (bf16[128,1024]{1,0:T(8,128)(2,1)S(1)}, bf16[128,1024]{1,0:T(8,128)(2,1)S(1)}, u32[]{:S(2)}, u32[]{:S(2)}) collective-permute-start(bf16[128,1024]{1,0:T(8,128)(2,1)S(1)} %collective-permute-done), channel_id=1, source_target_pairs={{0,8},{2,6},{4,12},{6,2},{8,0},{10,14},{12,4},{14,10},{16,24},{18,... | collective-permute-start | bytes 786440 | tf_op jit(solution)/shard_map/ppermute | solution.py:28
  12.9 8.9 %collective-permute-start.4 = (bf16[128,1024]{1,0:T(8,128)(2,1)S(1)}, bf16[128,1024]{1,0:T(8,128)(2,1)S(1)}, u32[]{:S(2)}, u32[]{:S(2)}) collective-permute-start(bf16[128,1024]{1,0:T(8,128)(2,1)S(1)} %constant_dynamic-update-slice_fusion), channel_id=1, source_target_pairs={{0,4},{2,10},{4,0},{6,14},{8,12},{10,2},{12,8},{14,6},{16,20},{18,... | collective-permute-start | bytes 786440 | tf_op jit(solution)/shard_map/ppermute | solution.py:28
  21.8 2.7 %collective-permute-start.5 = (bf16[512,1024]{1,0:T(8,128)(2,1)S(1)}, bf16[512,1024]{1,0:T(8,128)(2,1)S(1)}, u32[]{:S(2)}, u32[]{:S(2)}) collective-permute-start(bf16[512,1024]{1,0:T(8,128)(2,1)S(1)} %constant_dynamic-update-slice_fusion.2.refs_1_), channel_id=1, source_target_pairs={{0,2},{2,0},{4,6},{6,4},{8,10},{10,8},{12,14},{14,12},{16,18},{18,... | collective-permute-start | bytes 3145736 | tf_op jit(solution)/shard_map/ppermute | solution.py:28
  22.0 8.0 %collective-permute-start.6 = (bf16[256,512]{1,0:T(8,128)(2,1)S(1)}, bf16[256,512]{1,0:T(8,128)(2,1)S(1)}, u32[]{:S(2)}, u32[]{:S(2)}) collective-permute-start(bf16[256,512]{1,0:T(8,128)(2,1)S(1)} %pad_maximum_fusion.2.refs_4_), channel_id=1, source_target_pairs={{0,8},{2,6},{4,12},{6,2},{8,0},{10,14},{12,4},{14,10},{16,24},{18,... | collective-permute-start | bytes 786440 | tf_op jit(solution)/shard_map/ppermute | solution.py:28
  22.2 9.1 %collective-permute-start.8 = (bf16[256,512]{1,0:T(8,128)(2,1)S(1)}, bf16[256,512]{1,0:T(8,128)(2,1)S(1)}, u32[]{:S(2)}, u32[]{:S(2)}) collective-permute-start(bf16[256,512]{1,0:T(8,128)(2,1)S(1)} %pad_maximum_fusion.3.refs_4_), channel_id=1, source_target_pairs={{0,8},{2,6},{4,12},{6,2},{8,0},{10,14},{12,4},{14,10},{16,24},{18,... | collective-permute-start | bytes 786440 | tf_op jit(solution)/shard_map/ppermute | solution.py:28
  30.1 2.0 %collective-permute-start.7 = (bf16[512,512]{1,0:T(8,128)(2,1)S(1)}, bf16[512,512]{1,0:T(8,128)(2,1)S(1)}, u32[]{:S(2)}, u32[]{:S(2)}) collective-permute-start(bf16[512,512]{1,0:T(8,128)(2,1)S(1)} %pad_maximum_fusion), channel_id=1, source_target_pairs={{0,2},{2,0},{4,6},{6,4},{8,10},{10,8},{12,14},{14,12},{16,18},{18,... | collective-permute-start | bytes 1572872 | tf_op jit(solution)/shard_map/ppermute | solution.py:28
  31.3 17.0 %collective-permute-start.9 = (bf16[512,512]{1,0:T(8,128)(2,1)S(1)}, bf16[512,512]{1,0:T(8,128)(2,1)S(1)}, u32[]{:S(2)}, u32[]{:S(2)}) collective-permute-start(bf16[512,512]{1,0:T(8,128)(2,1)S(1)} %pad_maximum_fusion.1), channel_id=1, source_target_pairs={{0,2},{2,0},{4,6},{6,4},{8,10},{10,8},{12,14},{14,12},{16,18},{18,... | collective-permute-start | bytes 1572872 | tf_op jit(solution)/shard_map/ppermute | solution.py:28
  34.9 27.7 %collective-permute-start.10 = (bf16[64,2048]{1,0:T(8,128)(2,1)S(1)}, bf16[64,2048]{1,0:T(8,128)(2,1)S(1)}, u32[]{:S(2)}, u32[]{:S(2)}) collective-permute-start(bf16[64,2048]{1,0:T(8,128)(2,1)S(1)} %get-tuple-element.49), channel_id=1, source_target_pairs={{0,1},{1,0},{2,3},{3,2},{4,5},{5,4},{6,7},{7,6},{8,9},{9,8},{10,11... | collective-permute-start | bytes 786440 | tf_op jit(solution)/shard_map/ppermute | solution.py:454
  51.0 18.3 %collective-permute-start.11 = (bf16[64,2048]{1,0:T(8,128)(2,1)S(1)}, bf16[64,2048]{1,0:T(8,128)(2,1)S(1)}, u32[]{:S(2)}, u32[]{:S(2)}) collective-permute-start(bf16[64,2048]{1,0:T(8,128)(2,1)S(1)} %get-tuple-element.50), channel_id=1, source_target_pairs={{0,1},{1,0},{2,3},{3,2},{4,5},{5,4},{6,7},{7,6},{8,9},{9,8},{10,11... | collective-permute-start | bytes 786440 | tf_op jit(solution)/shard_map/ppermute | solution.py:454

commit v17 on v16

--- a/solution.py
+++ b/solution.py
@@ -16,7 +16,7 @@
 EXP2_SCALE = HD ** (-0.5) * math.log2(math.e)
 MASKED = -1e30
 KEY_CHUNK = 256
-HEADS_A_BLOCK = (2, 4, 2)
+HEADS_A_BLOCK = (2, 2, 2, 2)
 SHIFT_STEP = 32.0
 LOWEST_TOTAL = 1e-20
 HIGHEST_TOTAL = 1e30

time: 70.3 us -> 71.7 us (1.020)
  Pallas kernels: 13.4 us -> 36.5 us
  starting transfers between devices: 36.4 us -> 13.5 us
  waiting for transfers between devices: 16.5 us -> 17.7 us
    pallas_call x3, Pallas kernels: 11 us -> 34.1 us  [attend(): pl.pallas_call(functools.partial(attend_kernel, spec, sizes, part, groups...]
    ppermute x2, starting transfers between devices: 25.1 us -> 2.16 us  [body(): lax.ppermute(pair[1], 'head', [(0, 1), (1, 0)])]
    ppermute x2, waiting for transfers between devices: 5.7 us -> 6.9 us  [body(): lax.ppermute(pair[1], 'head', [(0, 1), (1, 0)])]
  transfers between devices with their start and end apart: 12 -> 12, of which waited for: 6 -> 6; matrix products, arithmetic and copies ran while one was open for 2% -> 2% of each run, Pallas kernels for 18% -> 50%
where the time goes in v17:
time: 71.7 us; the launch traced here: 71.5 us
  Pallas kernels  36.5 us (51%)
  waiting for transfers between devices  17.7 us (25%)
  starting transfers between devices  13.5 us (19%)
  local copies, waits for them, and re-layouts  3.37 us (5%)
    pallas_call x3, Pallas kernels, attend(): pl.pallas_call(functools.partial(attend_kernel, spec, sizes, part, groups...  34.1 us
    ppermute x10, starting transfers between devices, hop(): lax.ppermute(value, 'seq', [(source, source ^ bit_of_core[source % 2]) fo...  11.3 us
    ppermute x10, waiting for transfers between devices, hop(): lax.ppermute(value, 'seq', [(source, source ^ bit_of_core[source % 2]) fo...  10.8 us
    ppermute x2, waiting for transfers between devices, body(): lax.ppermute(pair[1], 'head', [(0, 1), (1, 0)])  6.9 us
    unnamed x12, local copies, waits for them, and re-layouts  3.3 us
    ppermute x2, starting transfers between devices, body(): lax.ppermute(pair[1], 'head', [(0, 1), (1, 0)])  2.16 us
    pallas_call x2, Pallas kernels, join(): pl.pallas_call(functools.partial(join_kernel, spots, len(pieces)), out_sh...  1.61 us
  transfers between devices with their start and end apart: 12, of which 6 were waited for; matrix products, arithmetic and copies ran while one was open for 2% of the time, Pallas kernels for 50%

profile of v17, /device:TPU:0, one launch (start us, length us, event | category | flops | bytes accessed | tf_op | source)
XLA Modules:
  0.0 71.5 jit_solution(12280802055615273683)
XLA Ops:
  0.0 0.0 copy-start
  0.0 2.9 %collective-permute-start = (bf16[128,1024]{1,0:T(8,128)(2,1)}, bf16[128,1024]{1,0:T(8,128)(2,1)S(1)}, u32[]{:S(2)}, u32[]{:S(2)}) collective-permute-start(bf16[128,1024]{1,0:T(8,128)(2,1)} %param.6), channel_id=1, source_target_pairs={{0,4},{2,10},{4,0},{6,14},{8,12},{10,2},{12,8},{14,6},{16,20},{18,... | collective-permute-start | bytes 786440 | tf_op jit(solution)/shard_map/ppermute | solution.py:28
  2.9 0.0 copy-start.1
  2.9 0.9 %copy-done.1 = bf16[2,64,1024]{2,1,0:T(8,128)(2,1)S(1)} copy-done((bf16[2,64,1024]{2,1,0:T(8,128)(2,1)S(1)}, bf16[2,64,1024]{2,1,0:T(8,128)(2,1)}, u32[]{:S(2)}) %copy-start.1) | copy-done | bytes 262168
  3.9 2.7 %collective-permute-start.1 = (bf16[64,1024]{1,0:T(8,128)(2,1)S(1)}, bf16[64,1024]{1,0:T(8,128)(2,1)S(1)}, u32[]{:S(2)}, u32[]{:S(2)}) collective-permute-start(bf16[64,1024]{1,0:T(8,128)(2,1)S(1)} %get-tuple-element.29), channel_id=1, source_target_pairs={{0,16},{2,18},{4,20},{6,22},{8,24},{10,26},{12,28},{14,30},{16,0},... | collective-permute-start | bytes 393224 | tf_op jit(solution)/shard_map/ppermute | solution.py:28
  6.6 1.6 %collective-permute-start.2 = (bf16[128,1024]{1,0:T(8,128)(2,1)}, bf16[128,1024]{1,0:T(8,128)(2,1)S(1)}, u32[]{:S(2)}, u32[]{:S(2)}) collective-permute-start(bf16[128,1024]{1,0:T(8,128)(2,1)} %param.6), channel_id=1, source_target_pairs={{0,8},{2,6},{4,12},{6,2},{8,0},{10,14},{12,4},{14,10},{16,24},{18,... | collective-permute-start | bytes 786440 | tf_op jit(solution)/shard_map/ppermute | solution.py:28
  8.1 0.0 copy-start.2
  8.1 0.7 copy-done.2
  8.8 0.0 copy-start.3
  8.8 0.7 copy-done.3
  9.5 0.8 %shard_map.55 = (bf16[1024,128]{1,0:T(8,128)(2,1)S(1)}, bf16[1024,128]{1,0:T(8,128)(2,1)S(1)}) custom-call(s32[2]{0:T(128)S(1)} %copy-done.3, s32[2,16]{1,0:T(2,128)S(1)} %copy-done.2), custom_call_target="tpu_custom_call" | custom-call | tf_op jit(solution)/shard_map/pallas_call | solution.py:84
  10.3 2.5 %collective-permute-done.1 = bf16[64,1024]{1,0:T(8,128)(2,1)S(1)} collective-permute-done((bf16[64,1024]{1,0:T(8,128)(2,1)S(1)}, bf16[64,1024]{1,0:T(8,128)(2,1)S(1)}, u32[]{:S(2)}, u32[]{:S(2)}) %collective-permute-start.1) | collective-permute-done | bytes 131104 | tf_op jit(solution)/shard_map/ppermute | solution.py:28
  12.8 0.0 collective-permute-done
  12.8 0.0 collective-permute-start.3
  12.9 1.6 %collective-permute-start.4 = (bf16[128,1024]{1,0:T(8,128)(2,1)S(1)}, bf16[128,1024]{1,0:T(8,128)(2,1)S(1)}, u32[]{:S(2)}, u32[]{:S(2)}) collective-permute-start(bf16[128,1024]{1,0:T(8,128)(2,1)S(1)} %constant_dynamic-update-slice_fusion), channel_id=1, source_target_pairs={{0,4},{2,10},{4,0},{6,14},{8,12},{10,2},{12,8},{14,6},{16,20},{18,... | collective-permute-start | bytes 786440 | tf_op jit(solution)/shard_map/ppermute | solution.py:28
  14.4 1.0 %constant_dynamic-update-slice_fusion.5 = bf16[512,1024]{1,0:T(8,128)(2,1)S(1)} fusion(bf16[128,1024]{1,0:T(8,128)(2,1)} %param.6), kind=kLoop, calls=%fused_computation.9 | loop fusion | bytes 524288
  15.4 0.0 collective-permute-done.2
  15.4 6.3 %collective-permute-done.3 = bf16[128,1024]{1,0:T(8,128)(2,1)S(1)} collective-permute-done((bf16[128,1024]{1,0:T(8,128)(2,1)S(1)}, bf16[128,1024]{1,0:T(8,128)(2,1)S(1)}, u32[]{:S(2)}, u32[]{:S(2)}) %collective-permute-start.3) | collective-permute-done | bytes 262176 | tf_op jit(solution)/shard_map/ppermute | solution.py:28
  21.7 0.0 collective-permute-done.4
  21.8 0.2 collective-permute-start.5
  22.0 0.1 collective-permute-start.6
  22.2 2.1 %collective-permute-start.8 = (bf16[256,512]{1,0:T(8,128)(2,1)S(1)}, bf16[256,512]{1,0:T(8,128)(2,1)S(1)}, u32[]{:S(2)}, u32[]{:S(2)}) collective-permute-start(bf16[256,512]{1,0:T(8,128)(2,1)S(1)} %pad_maximum_fusion.3.refs_4_), channel_id=1, source_target_pairs={{0,8},{2,6},{4,12},{6,2},{8,0},{10,14},{12,4},{14,10},{16,24},{18,... | collective-permute-start | bytes 786440 | tf_op jit(solution)/shard_map/ppermute | solution.py:28
  24.2 0.3 collective-permute-done.5.refs_2_
  24.5 0.0 copy-done
  24.5 5.4 %shard_map.57 = (f32[4096,256]{1,0:T(8,128)S(1)}, bf16[4096,128]{1,0:T(8,128)(2,1)S(1)}) custom-call(bf16[128,4096]{1,0:T(8,128)(2,1)S(1)} %copy-done, bf16[1024,128]{1,0:T(8,128)(2,1)S(1)} %get-tuple-element.30.refs_0_, bf16[512,1024]{1,0:T(8,128)(2,1)S(1)} %constant_dynamic-update-slice_fusion.2.refs_1_, bf16[512,1024]{1,0:T(8,128)(2,1)S(1)} %collective-permute-done.5.refs_2_), custom_call_target="tpu_custom_call" | custom-call | flops 4294967296 | bytes 3145728 | tf_op jit(solution)/shard_map/pallas_call | solution.py:318
  29.9 0.0 collective-permute-done.6.refs_5_
  30.0 0.2 collective-permute-start.7
  30.2 1.1 %collective-permute-done.8.refs_5_ = bf16[256,512]{1,0:T(8,128)(2,1)S(1)} collective-permute-done((bf16[256,512]{1,0:T(8,128)(2,1)S(1)}, bf16[256,512]{1,0:T(8,128)(2,1)S(1)}, u32[]{:S(2)}, u32[]{:S(2)}) %collective-permute-start.8) | collective-permute-done | bytes 262176 | tf_op jit(solution)/shard_map/ppermute | solution.py:28
  31.3 0.1 collective-permute-start.9
  31.4 0.6 collective-permute-done.7.refs_6_
  32.0 14.4 %shard_map.58 = (bf16[64,2048]{1,0:T(8,128)(2,1)S(1)}, bf16[64,2048]{1,0:T(8,128)(2,1)S(1)}) custom-call(bf16[128,4096]{1,0:T(8,128)(2,1)S(1)} %copy-done, bf16[1024,128]{1,0:T(8,128)(2,1)S(1)} %get-tuple-element.30.refs_0_, bf16[512,1024]{1,0:T(8,128)(2,1)S(1)} %constant_dynamic-update-slice_fusion.2.refs_1_, ...), custom_call_target="tpu_custom_call" | custom-call | flops 2147483648 | bytes 1572864 | tf_op jit(solution)/shard_map/pallas_call | solution.py:318
  46.4 1.8 %collective-permute-start.10 = (bf16[64,2048]{1,0:T(8,128)(2,1)S(1)}, bf16[64,2048]{1,0:T(8,128)(2,1)S(1)}, u32[]{:S(2)}, u32[]{:S(2)}) collective-permute-start(bf16[64,2048]{1,0:T(8,128)(2,1)S(1)} %get-tuple-element.49), channel_id=1, source_target_pairs={{0,1},{1,0},{2,3},{3,2},{4,5},{5,4},{6,7},{7,6},{8,9},{9,8},{10,11... | collective-permute-start | bytes 786440 | tf_op jit(solution)/shard_map/ppermute | solution.py:454
  48.2 0.0 collective-permute-done.9.refs_6_
  48.2 14.2 %shard_map.59 = (bf16[64,2048]{1,0:T(8,128)(2,1)S(1)}, bf16[64,2048]{1,0:T(8,128)(2,1)S(1)}) custom-call(bf16[128,4096]{1,0:T(8,128)(2,1)S(1)} %copy-done, bf16[1024,128]{1,0:T(8,128)(2,1)S(1)} %get-tuple-element.30.refs_0_, bf16[512,1024]{1,0:T(8,128)(2,1)S(1)} %constant_dynamic-update-slice_fusion.2.refs_1_, ...), custom_call_target="tpu_custom_call" | custom-call | flops 2147483648 | bytes 1572864 | tf_op jit(solution)/shard_map/pallas_call | solution.py:318
  62.5 0.3 collective-permute-start.11
  62.8 0.0 collective-permute-done.10.refs_2_
  62.8 0.9 %shard_map.60.refs_0_ = bf16[64,8192]{1,0:T(8,128)(2,1)} custom-call(bf16[64,2048]{1,0:T(8,128)(2,1)S(1)} %get-tuple-element.44.refs_0_, bf16[64,2048]{1,0:T(8,128)(2,1)S(1)} %get-tuple-element.48.refs_1_, bf16[64,2048]{1,0:T(8,128)(2,1)S(1)} %collective-permute-done.10.refs_2_), custom_call_target="tpu_custom_call" | custom-call | tf_op jit(solution)/shard_map/pallas_call | solution.py:369
  63.7 6.9 %collective-permute-done.11.refs_1_ = bf16[64,2048]{1,0:T(8,128)(2,1)S(1)} collective-permute-done((bf16[64,2048]{1,0:T(8,128)(2,1)S(1)}, bf16[64,2048]{1,0:T(8,128)(2,1)S(1)}, u32[]{:S(2)}, u32[]{:S(2)}) %collective-permute-start.11) | collective-permute-done | bytes 262176 | tf_op jit(solution)/shard_map/ppermute | solution.py:454
  70.6 0.7 shard_map.61
  (12 shorter events, 0.2 us)
Async XLA Ops:
  0.0 24.5 %copy-start = (bf16[128,4096]{1,0:T(8,128)(2,1)S(1)}, bf16[128,4096]{1,0:T(8,128)(2,1)}, u32[]{:S(2)}) copy-start(bf16[128,4096]{1,0:T(8,128)(2,1)} %q_ref.5) | copy-start | bytes 3145732
  0.0 12.8 %collective-permute-start = (bf16[128,1024]{1,0:T(8,128)(2,1)}, bf16[128,1024]{1,0:T(8,128)(2,1)S(1)}, u32[]{:S(2)}, u32[]{:S(2)}) collective-permute-start(bf16[128,1024]{1,0:T(8,128)(2,1)} %param.6), channel_id=1, source_target_pairs={{0,4},{2,10},{4,0},{6,14},{8,12},{10,2},{12,8},{14,6},{16,20},{18,... | collective-permute-start | bytes 786440 | tf_op jit(solution)/shard_map/ppermute | solution.py:28
  2.9 0.9 %copy-start.1 = (bf16[2,64,1024]{2,1,0:T(8,128)(2,1)S(1)}, bf16[2,64,1024]{2,1,0:T(8,128)(2,1)}, u32[]{:S(2)}) copy-start(bf16[2,64,1024]{2,1,0:T(8,128)(2,1)} %cache_ref.1) | copy-start | bytes 786436
  3.9 8.9 %collective-permute-start.1 = (bf16[64,1024]{1,0:T(8,128)(2,1)S(1)}, bf16[64,1024]{1,0:T(8,128)(2,1)S(1)}, u32[]{:S(2)}, u32[]{:S(2)}) collective-permute-start(bf16[64,1024]{1,0:T(8,128)(2,1)S(1)} %get-tuple-element.29), channel_id=1, source_target_pairs={{0,16},{2,18},{4,20},{6,22},{8,24},{10,26},{12,28},{14,30},{16,0},... | collective-permute-start | bytes 393224 | tf_op jit(solution)/shard_map/ppermute | solution.py:28
  6.6 8.8 %collective-permute-start.2 = (bf16[128,1024]{1,0:T(8,128)(2,1)}, bf16[128,1024]{1,0:T(8,128)(2,1)S(1)}, u32[]{:S(2)}, u32[]{:S(2)}) collective-permute-start(bf16[128,1024]{1,0:T(8,128)(2,1)} %param.6), channel_id=1, source_target_pairs={{0,8},{2,6},{4,12},{6,2},{8,0},{10,14},{12,4},{14,10},{16,24},{18,... | collective-permute-start | bytes 786440 | tf_op jit(solution)/shard_map/ppermute | solution.py:28
  8.1 0.7 copy-start.2
  8.8 0.7 copy-start.3
  12.8 8.9 %collective-permute-start.3 = (bf16[128,1024]{1,0:T(8,128)(2,1)S(1)}, bf16[128,1024]{1,0:T(8,128)(2,1)S(1)}, u32[]{:S(2)}, u32[]{:S(2)}) collective-permute-start(bf16[128,1024]{1,0:T(8,128)(2,1)S(1)} %collective-permute-done), channel_id=1, source_target_pairs={{0,8},{2,6},{4,12},{6,2},{8,0},{10,14},{12,4},{14,10},{16,24},{18,... | collective-permute-start | bytes 786440 | tf_op jit(solution)/shard_map/ppermute | solution.py:28
  12.9 8.9 %collective-permute-start.4 = (bf16[128,1024]{1,0:T(8,128)(2,1)S(1)}, bf16[128,1024]{1,0:T(8,128)(2,1)S(1)}, u32[]{:S(2)}, u32[]{:S(2)}) collective-permute-start(bf16[128,1024]{1,0:T(8,128)(2,1)S(1)} %constant_dynamic-update-slice_fusion), channel_id=1, source_target_pairs={{0,4},{2,10},{4,0},{6,14},{8,12},{10,2},{12,8},{14,6},{16,20},{18,... | collective-permute-start | bytes 786440 | tf_op jit(solution)/shard_map/ppermute | solution.py:28
  21.8 2.7 %collective-permute-start.5 = (bf16[512,1024]{1,0:T(8,128)(2,1)S(1)}, bf16[512,1024]{1,0:T(8,128)(2,1)S(1)}, u32[]{:S(2)}, u32[]{:S(2)}) collective-permute-start(bf16[512,1024]{1,0:T(8,128)(2,1)S(1)} %constant_dynamic-update-slice_fusion.2.refs_1_), channel_id=1, source_target_pairs={{0,2},{2,0},{4,6},{6,4},{8,10},{10,8},{12,14},{14,12},{16,18},{18,... | collective-permute-start | bytes 3145736 | tf_op jit(solution)/shard_map/ppermute | solution.py:28
  22.0 7.9 %collective-permute-start.6 = (bf16[256,512]{1,0:T(8,128)(2,1)S(1)}, bf16[256,512]{1,0:T(8,128)(2,1)S(1)}, u32[]{:S(2)}, u32[]{:S(2)}) collective-permute-start(bf16[256,512]{1,0:T(8,128)(2,1)S(1)} %pad_maximum_fusion.2.refs_4_), channel_id=1, source_target_pairs={{0,8},{2,6},{4,12},{6,2},{8,0},{10,14},{12,4},{14,10},{16,24},{18,... | collective-permute-start | bytes 786440 | tf_op jit(solution)/shard_map/ppermute | solution.py:28
  22.2 9.1 %collective-permute-start.8 = (bf16[256,512]{1,0:T(8,128)(2,1)S(1)}, bf16[256,512]{1,0:T(8,128)(2,1)S(1)}, u32[]{:S(2)}, u32[]{:S(2)}) collective-permute-start(bf16[256,512]{1,0:T(8,128)(2,1)S(1)} %pad_maximum_fusion.3.refs_4_), channel_id=1, source_target_pairs={{0,8},{2,6},{4,12},{6,2},{8,0},{10,14},{12,4},{14,10},{16,24},{18,... | collective-permute-start | bytes 786440 | tf_op jit(solution)/shard_map/ppermute | solution.py:28
  30.0 2.0 %collective-permute-start.7 = (bf16[512,512]{1,0:T(8,128)(2,1)S(1)}, bf16[512,512]{1,0:T(8,128)(2,1)S(1)}, u32[]{:S(2)}, u32[]{:S(2)}) collective-permute-start(bf16[512,512]{1,0:T(8,128)(2,1)S(1)} %pad_maximum_fusion), channel_id=1, source_target_pairs={{0,2},{2,0},{4,6},{6,4},{8,10},{10,8},{12,14},{14,12},{16,18},{18,... | collective-permute-start | bytes 1572872 | tf_op jit(solution)/shard_map/ppermute | solution.py:28
  31.3 16.9 %collective-permute-start.9 = (bf16[512,512]{1,0:T(8,128)(2,1)S(1)}, bf16[512,512]{1,0:T(8,128)(2,1)S(1)}, u32[]{:S(2)}, u32[]{:S(2)}) collective-permute-start(bf16[512,512]{1,0:T(8,128)(2,1)S(1)} %pad_maximum_fusion.1), channel_id=1, source_target_pairs={{0,2},{2,0},{4,6},{6,4},{8,10},{10,8},{12,14},{14,12},{16,18},{18,... | collective-permute-start | bytes 1572872 | tf_op jit(solution)/shard_map/ppermute | solution.py:28
  46.4 16.4 %collective-permute-start.10 = (bf16[64,2048]{1,0:T(8,128)(2,1)S(1)}, bf16[64,2048]{1,0:T(8,128)(2,1)S(1)}, u32[]{:S(2)}, u32[]{:S(2)}) collective-permute-start(bf16[64,2048]{1,0:T(8,128)(2,1)S(1)} %get-tuple-element.49), channel_id=1, source_target_pairs={{0,1},{1,0},{2,3},{3,2},{4,5},{5,4},{6,7},{7,6},{8,9},{9,8},{10,11... | collective-permute-start | bytes 786440 | tf_op jit(solution)/shard_map/ppermute | solution.py:454
  62.5 8.1 %collective-permute-start.11 = (bf16[64,2048]{1,0:T(8,128)(2,1)S(1)}, bf16[64,2048]{1,0:T(8,128)(2,1)S(1)}, u32[]{:S(2)}, u32[]{:S(2)}) collective-permute-start(bf16[64,2048]{1,0:T(8,128)(2,1)S(1)} %get-tuple-element.50), channel_id=1, source_target_pairs={{0,1},{1,0},{2,3},{3,2},{4,5},{5,4},{6,7},{7,6},{8,9},{9,8},{10,11... | collective-permute-start | bytes 786440 | tf_op jit(solution)/shard_map/ppermute | solution.py:454

commit v18 on v17

--- a/solution.py
+++ b/solution.py
@@ -15,7 +15,7 @@
 PER_GROUP = QH // KVH
 EXP2_SCALE = HD ** (-0.5) * math.log2(math.e)
 MASKED = -1e30
-KEY_CHUNK = 256
+KEY_CHUNK = 512
 HEADS_A_BLOCK = (2, 2, 2, 2)
 SHIFT_STEP = 32.0
 LOWEST_TOTAL = 1e-20

time: 71.7 us -> 71 us (level); the launches traced: 71.5 us -> 70.1 us
  Pallas kernels: 36.5 us -> 13.4 us
  starting transfers between devices: 13.5 us -> 36.4 us
  waiting for transfers between devices: 17.7 us -> 16.5 us
    pallas_call x3, Pallas kernels: 34.1 us -> 10.9 us  [attend(): pl.pallas_call(functools.partial(attend_kernel, spec, sizes, part, groups...]
    ppermute x2, starting transfers between devices: 2.16 us -> 25.1 us  [body(): lax.ppermute(pair[1], 'head', [(0, 1), (1, 0)])]
    ppermute x2, waiting for transfers between devices: 6.9 us -> 5.7 us  [body(): lax.ppermute(pair[1], 'head', [(0, 1), (1, 0)])]
  transfers between devices with their start and end apart: 12 -> 12, of which waited for: 6 -> 6; matrix products, arithmetic and copies ran while one was open for 2% -> 2% of each run, Pallas kernels for 50% -> 18%
where the time goes in v18:
time: 71 us; the launch traced here: 70.1 us
  starting transfers between devices  36.4 us (51%)
  waiting for transfers between devices  16.5 us (23%)
  Pallas kernels  13.4 us (19%)
  local copies, waits for them, and re-layouts  3.37 us (5%)
    ppermute x2, starting transfers between devices, body(): lax.ppermute(pair[1], 'head', [(0, 1), (1, 0)])  25.1 us
    ppermute x10, starting transfers between devices, hop(): lax.ppermute(value, 'seq', [(source, source ^ bit_of_core[source % 2]) fo...  11.3 us
    pallas_call x3, Pallas kernels, attend(): pl.pallas_call(functools.partial(attend_kernel, spec, sizes, part, groups...  10.9 us
    ppermute x10, waiting for transfers between devices, hop(): lax.ppermute(value, 'seq', [(source, source ^ bit_of_core[source % 2]) fo...  10.8 us
    ppermute x2, waiting for transfers between devices, body(): lax.ppermute(pair[1], 'head', [(0, 1), (1, 0)])  5.7 us
    unnamed x12, local copies, waits for them, and re-layouts  3.3 us
    pallas_call x2, Pallas kernels, join(): pl.pallas_call(functools.partial(join_kernel, spots, len(pieces)), out_sh...  1.61 us
  transfers between devices with their start and end apart: 12, of which 6 were waited for; matrix products, arithmetic and copies ran while one was open for 2% of the time, Pallas kernels for 18%

profile of v18, /device:TPU:0, one launch (start us, length us, event | category | flops | bytes accessed | tf_op | source)
XLA Modules:
  0.0 70.1 jit_solution(12280802055615273683)
XLA Ops:
  0.0 0.0 copy-start
  0.0 2.9 %collective-permute-start = (bf16[128,1024]{1,0:T(8,128)(2,1)}, bf16[128,1024]{1,0:T(8,128)(2,1)S(1)}, u32[]{:S(2)}, u32[]{:S(2)}) collective-permute-start(bf16[128,1024]{1,0:T(8,128)(2,1)} %param.6), channel_id=1, source_target_pairs={{0,4},{2,10},{4,0},{6,14},{8,12},{10,2},{12,8},{14,6},{16,20},{18,... | collective-permute-start | bytes 786440 | tf_op jit(solution)/shard_map/ppermute | solution.py:28
  2.9 0.0 copy-start.1
  2.9 0.9 %copy-done.1 = bf16[2,64,1024]{2,1,0:T(8,128)(2,1)S(1)} copy-done((bf16[2,64,1024]{2,1,0:T(8,128)(2,1)S(1)}, bf16[2,64,1024]{2,1,0:T(8,128)(2,1)}, u32[]{:S(2)}) %copy-start.1) | copy-done | bytes 262168
  3.9 2.7 %collective-permute-start.1 = (bf16[64,1024]{1,0:T(8,128)(2,1)S(1)}, bf16[64,1024]{1,0:T(8,128)(2,1)S(1)}, u32[]{:S(2)}, u32[]{:S(2)}) collective-permute-start(bf16[64,1024]{1,0:T(8,128)(2,1)S(1)} %get-tuple-element.29), channel_id=1, source_target_pairs={{0,16},{2,18},{4,20},{6,22},{8,24},{10,26},{12,28},{14,30},{16,0},... | collective-permute-start | bytes 393224 | tf_op jit(solution)/shard_map/ppermute | solution.py:28
  6.6 1.6 %collective-permute-start.2 = (bf16[128,1024]{1,0:T(8,128)(2,1)}, bf16[128,1024]{1,0:T(8,128)(2,1)S(1)}, u32[]{:S(2)}, u32[]{:S(2)}) collective-permute-start(bf16[128,1024]{1,0:T(8,128)(2,1)} %param.6), channel_id=1, source_target_pairs={{0,8},{2,6},{4,12},{6,2},{8,0},{10,14},{12,4},{14,10},{16,24},{18,... | collective-permute-start | bytes 786440 | tf_op jit(solution)/shard_map/ppermute | solution.py:28
  8.1 0.0 copy-start.2
  8.1 0.7 copy-done.2
  8.8 0.0 copy-start.3
  8.8 0.7 copy-done.3
  9.5 0.8 %shard_map.55 = (bf16[1024,128]{1,0:T(8,128)(2,1)S(1)}, bf16[1024,128]{1,0:T(8,128)(2,1)S(1)}) custom-call(s32[2]{0:T(128)S(1)} %copy-done.3, s32[2,16]{1,0:T(2,128)S(1)} %copy-done.2), custom_call_target="tpu_custom_call" | custom-call | tf_op jit(solution)/shard_map/pallas_call | solution.py:84
  10.3 2.5 %collective-permute-done.1 = bf16[64,1024]{1,0:T(8,128)(2,1)S(1)} collective-permute-done((bf16[64,1024]{1,0:T(8,128)(2,1)S(1)}, bf16[64,1024]{1,0:T(8,128)(2,1)S(1)}, u32[]{:S(2)}, u32[]{:S(2)}) %collective-permute-start.1) | collective-permute-done | bytes 131104 | tf_op jit(solution)/shard_map/ppermute | solution.py:28
  12.8 0.0 collective-permute-done
  12.8 0.0 collective-permute-start.3
  12.9 1.6 %collective-permute-start.4 = (bf16[128,1024]{1,0:T(8,128)(2,1)S(1)}, bf16[128,1024]{1,0:T(8,128)(2,1)S(1)}, u32[]{:S(2)}, u32[]{:S(2)}) collective-permute-start(bf16[128,1024]{1,0:T(8,128)(2,1)S(1)} %constant_dynamic-update-slice_fusion), channel_id=1, source_target_pairs={{0,4},{2,10},{4,0},{6,14},{8,12},{10,2},{12,8},{14,6},{16,20},{18,... | collective-permute-start | bytes 786440 | tf_op jit(solution)/shard_map/ppermute | solution.py:28
  14.4 1.0 %constant_dynamic-update-slice_fusion.5 = bf16[512,1024]{1,0:T(8,128)(2,1)S(1)} fusion(bf16[128,1024]{1,0:T(8,128)(2,1)} %param.6), kind=kLoop, calls=%fused_computation.9 | loop fusion | bytes 524288
  15.4 0.0 collective-permute-done.2
  15.4 6.3 %collective-permute-done.3 = bf16[128,1024]{1,0:T(8,128)(2,1)S(1)} collective-permute-done((bf16[128,1024]{1,0:T(8,128)(2,1)S(1)}, bf16[128,1024]{1,0:T(8,128)(2,1)S(1)}, u32[]{:S(2)}, u32[]{:S(2)}) %collective-permute-start.3) | collective-permute-done | bytes 262176 | tf_op jit(solution)/shard_map/ppermute | solution.py:28
  21.7 0.0 collective-permute-done.4
  21.8 0.2 collective-permute-start.5
  22.0 0.1 collective-permute-start.6
  22.2 2.1 %collective-permute-start.8 = (bf16[256,512]{1,0:T(8,128)(2,1)S(1)}, bf16[256,512]{1,0:T(8,128)(2,1)S(1)}, u32[]{:S(2)}, u32[]{:S(2)}) collective-permute-start(bf16[256,512]{1,0:T(8,128)(2,1)S(1)} %pad_maximum_fusion.3.refs_4_), channel_id=1, source_target_pairs={{0,8},{2,6},{4,12},{6,2},{8,0},{10,14},{12,4},{14,10},{16,24},{18,... | collective-permute-start | bytes 786440 | tf_op jit(solution)/shard_map/ppermute | solution.py:28
  24.2 0.3 collective-permute-done.5.refs_2_
  24.5 0.0 copy-done
  24.5 5.4 %shard_map.57 = (f32[4096,256]{1,0:T(8,128)S(1)}, bf16[4096,128]{1,0:T(8,128)(2,1)S(1)}) custom-call(bf16[128,4096]{1,0:T(8,128)(2,1)S(1)} %copy-done, bf16[1024,128]{1,0:T(8,128)(2,1)S(1)} %get-tuple-element.30.refs_0_, bf16[512,1024]{1,0:T(8,128)(2,1)S(1)} %constant_dynamic-update-slice_fusion.2.refs_1_, bf16[512,1024]{1,0:T(8,128)(2,1)S(1)} %collective-permute-done.5.refs_2_), custom_call_target="tpu_custom_call" | custom-call | flops 4294967296 | bytes 3145728 | tf_op jit(solution)/shard_map/pallas_call | solution.py:318
  29.9 0.0 collective-permute-done.6.refs_5_
  30.0 0.2 collective-permute-start.7
  30.2 1.1 %collective-permute-done.8.refs_5_ = bf16[256,512]{1,0:T(8,128)(2,1)S(1)} collective-permute-done((bf16[256,512]{1,0:T(8,128)(2,1)S(1)}, bf16[256,512]{1,0:T(8,128)(2,1)S(1)}, u32[]{:S(2)}, u32[]{:S(2)}) %collective-permute-start.8) | collective-permute-done | bytes 262176 | tf_op jit(solution)/shard_map/ppermute | solution.py:28
  31.3 0.1 collective-permute-start.9
  31.4 0.6 collective-permute-done.7.refs_6_
  32.0 2.8 %shard_map.58 = (bf16[64,2048]{1,0:T(8,128)(2,1)S(1)}, bf16[64,2048]{1,0:T(8,128)(2,1)S(1)}) custom-call(bf16[128,4096]{1,0:T(8,128)(2,1)S(1)} %copy-done, bf16[1024,128]{1,0:T(8,128)(2,1)S(1)} %get-tuple-element.30.refs_0_, bf16[512,1024]{1,0:T(8,128)(2,1)S(1)} %constant_dynamic-update-slice_fusion.2.refs_1_, ...), custom_call_target="tpu_custom_call" | custom-call | flops 2147483648 | bytes 1572864 | tf_op jit(solution)/shard_map/pallas_call | solution.py:318
  34.8 13.4 %collective-permute-start.10 = (bf16[64,2048]{1,0:T(8,128)(2,1)S(1)}, bf16[64,2048]{1,0:T(8,128)(2,1)S(1)}, u32[]{:S(2)}, u32[]{:S(2)}) collective-permute-start(bf16[64,2048]{1,0:T(8,128)(2,1)S(1)} %get-tuple-element.49), channel_id=1, source_target_pairs={{0,1},{1,0},{2,3},{3,2},{4,5},{5,4},{6,7},{7,6},{8,9},{9,8},{10,11... | collective-permute-start | bytes 786440 | tf_op jit(solution)/shard_map/ppermute | solution.py:454
  48.2 0.0 collective-permute-done.9.refs_6_
  48.2 2.7 %shard_map.59 = (bf16[64,2048]{1,0:T(8,128)(2,1)S(1)}, bf16[64,2048]{1,0:T(8,128)(2,1)S(1)}) custom-call(bf16[128,4096]{1,0:T(8,128)(2,1)S(1)} %copy-done, bf16[1024,128]{1,0:T(8,128)(2,1)S(1)} %get-tuple-element.30.refs_0_, bf16[512,1024]{1,0:T(8,128)(2,1)S(1)} %constant_dynamic-update-slice_fusion.2.refs_1_, ...), custom_call_target="tpu_custom_call" | custom-call | flops 2147483648 | bytes 1572864 | tf_op jit(solution)/shard_map/pallas_call | solution.py:318
  50.9 11.7 %collective-permute-start.11 = (bf16[64,2048]{1,0:T(8,128)(2,1)S(1)}, bf16[64,2048]{1,0:T(8,128)(2,1)S(1)}, u32[]{:S(2)}, u32[]{:S(2)}) collective-permute-start(bf16[64,2048]{1,0:T(8,128)(2,1)S(1)} %get-tuple-element.50), channel_id=1, source_target_pairs={{0,1},{1,0},{2,3},{3,2},{4,5},{5,4},{6,7},{7,6},{8,9},{9,8},{10,11... | collective-permute-start | bytes 786440 | tf_op jit(solution)/shard_map/ppermute | solution.py:454
  62.6 0.0 collective-permute-done.10.refs_2_
  62.6 0.9 %shard_map.60.refs_0_ = bf16[64,8192]{1,0:T(8,128)(2,1)} custom-call(bf16[64,2048]{1,0:T(8,128)(2,1)S(1)} %get-tuple-element.44.refs_0_, bf16[64,2048]{1,0:T(8,128)(2,1)S(1)} %get-tuple-element.48.refs_1_, bf16[64,2048]{1,0:T(8,128)(2,1)S(1)} %collective-permute-done.10.refs_2_), custom_call_target="tpu_custom_call" | custom-call | tf_op jit(solution)/shard_map/pallas_call | solution.py:369
  63.5 5.7 %collective-permute-done.11.refs_1_ = bf16[64,2048]{1,0:T(8,128)(2,1)S(1)} collective-permute-done((bf16[64,2048]{1,0:T(8,128)(2,1)S(1)}, bf16[64,2048]{1,0:T(8,128)(2,1)S(1)}, u32[]{:S(2)}, u32[]{:S(2)}) %collective-permute-start.11) | collective-permute-done | bytes 262176 | tf_op jit(solution)/shard_map/ppermute | solution.py:454
  69.2 0.7 %shard_map.61 = bf16[64,8192]{1,0:T(8,128)(2,1)} custom-call(bf16[64,8192]{1,0:T(8,128)(2,1)} %shard_map.60.refs_0_, bf16[64,2048]{1,0:T(8,128)(2,1)S(1)} %collective-permute-done.11.refs_1_), custom_call_target="tpu_custom_call", output_to_operand_aliasing={{}: (0, {})} | custom-call | tf_op jit(solution)/shard_map/pallas_call | solution.py:369
  (12 shorter events, 0.2 us)
Async XLA Ops:
  0.0 24.5 %copy-start = (bf16[128,4096]{1,0:T(8,128)(2,1)S(1)}, bf16[128,4096]{1,0:T(8,128)(2,1)}, u32[]{:S(2)}) copy-start(bf16[128,4096]{1,0:T(8,128)(2,1)} %q_ref.5) | copy-start | bytes 3145732
  0.0 12.8 %collective-permute-start = (bf16[128,1024]{1,0:T(8,128)(2,1)}, bf16[128,1024]{1,0:T(8,128)(2,1)S(1)}, u32[]{:S(2)}, u32[]{:S(2)}) collective-permute-start(bf16[128,1024]{1,0:T(8,128)(2,1)} %param.6), channel_id=1, source_target_pairs={{0,4},{2,10},{4,0},{6,14},{8,12},{10,2},{12,8},{14,6},{16,20},{18,... | collective-permute-start | bytes 786440 | tf_op jit(solution)/shard_map/ppermute | solution.py:28
  2.9 0.9 %copy-start.1 = (bf16[2,64,1024]{2,1,0:T(8,128)(2,1)S(1)}, bf16[2,64,1024]{2,1,0:T(8,128)(2,1)}, u32[]{:S(2)}) copy-start(bf16[2,64,1024]{2,1,0:T(8,128)(2,1)} %cache_ref.1) | copy-start | bytes 786436
  3.9 8.9 %collective-permute-start.1 = (bf16[64,1024]{1,0:T(8,128)(2,1)S(1)}, bf16[64,1024]{1,0:T(8,128)(2,1)S(1)}, u32[]{:S(2)}, u32[]{:S(2)}) collective-permute-start(bf16[64,1024]{1,0:T(8,128)(2,1)S(1)} %get-tuple-element.29), channel_id=1, source_target_pairs={{0,16},{2,18},{4,20},{6,22},{8,24},{10,26},{12,28},{14,30},{16,0},... | collective-permute-start | bytes 393224 | tf_op jit(solution)/shard_map/ppermute | solution.py:28
  6.6 8.8 %collective-permute-start.2 = (bf16[128,1024]{1,0:T(8,128)(2,1)}, bf16[128,1024]{1,0:T(8,128)(2,1)S(1)}, u32[]{:S(2)}, u32[]{:S(2)}) collective-permute-start(bf16[128,1024]{1,0:T(8,128)(2,1)} %param.6), channel_id=1, source_target_pairs={{0,8},{2,6},{4,12},{6,2},{8,0},{10,14},{12,4},{14,10},{16,24},{18,... | collective-permute-start | bytes 786440 | tf_op jit(solution)/shard_map/ppermute | solution.py:28
  8.1 0.7 copy-start.2
  8.8 0.7 copy-start.3
  12.8 8.9 %collective-permute-start.3 = (bf16[128,1024]{1,0:T(8,128)(2,1)S(1)}, bf16[128,1024]{1,0:T(8,128)(2,1)S(1)}, u32[]{:S(2)}, u32[]{:S(2)}) collective-permute-start(bf16[128,1024]{1,0:T(8,128)(2,1)S(1)} %collective-permute-done), channel_id=1, source_target_pairs={{0,8},{2,6},{4,12},{6,2},{8,0},{10,14},{12,4},{14,10},{16,24},{18,... | collective-permute-start | bytes 786440 | tf_op jit(solution)/shard_map/ppermute | solution.py:28
  12.9 8.9 %collective-permute-start.4 = (bf16[128,1024]{1,0:T(8,128)(2,1)S(1)}, bf16[128,1024]{1,0:T(8,128)(2,1)S(1)}, u32[]{:S(2)}, u32[]{:S(2)}) collective-permute-start(bf16[128,1024]{1,0:T(8,128)(2,1)S(1)} %constant_dynamic-update-slice_fusion), channel_id=1, source_target_pairs={{0,4},{2,10},{4,0},{6,14},{8,12},{10,2},{12,8},{14,6},{16,20},{18,... | collective-permute-start | bytes 786440 | tf_op jit(solution)/shard_map/ppermute | solution.py:28
  21.8 2.7 %collective-permute-start.5 = (bf16[512,1024]{1,0:T(8,128)(2,1)S(1)}, bf16[512,1024]{1,0:T(8,128)(2,1)S(1)}, u32[]{:S(2)}, u32[]{:S(2)}) collective-permute-start(bf16[512,1024]{1,0:T(8,128)(2,1)S(1)} %constant_dynamic-update-slice_fusion.2.refs_1_), channel_id=1, source_target_pairs={{0,2},{2,0},{4,6},{6,4},{8,10},{10,8},{12,14},{14,12},{16,18},{18,... | collective-permute-start | bytes 3145736 | tf_op jit(solution)/shard_map/ppermute | solution.py:28
  22.0 7.9 %collective-permute-start.6 = (bf16[256,512]{1,0:T(8,128)(2,1)S(1)}, bf16[256,512]{1,0:T(8,128)(2,1)S(1)}, u32[]{:S(2)}, u32[]{:S(2)}) collective-permute-start(bf16[256,512]{1,0:T(8,128)(2,1)S(1)} %pad_maximum_fusion.2.refs_4_), channel_id=1, source_target_pairs={{0,8},{2,6},{4,12},{6,2},{8,0},{10,14},{12,4},{14,10},{16,24},{18,... | collective-permute-start | bytes 786440 | tf_op jit(solution)/shard_map/ppermute | solution.py:28
  22.2 9.1 %collective-permute-start.8 = (bf16[256,512]{1,0:T(8,128)(2,1)S(1)}, bf16[256,512]{1,0:T(8,128)(2,1)S(1)}, u32[]{:S(2)}, u32[]{:S(2)}) collective-permute-start(bf16[256,512]{1,0:T(8,128)(2,1)S(1)} %pad_maximum_fusion.3.refs_4_), channel_id=1, source_target_pairs={{0,8},{2,6},{4,12},{6,2},{8,0},{10,14},{12,4},{14,10},{16,24},{18,... | collective-permute-start | bytes 786440 | tf_op jit(solution)/shard_map/ppermute | solution.py:28
  30.0 2.0 %collective-permute-start.7 = (bf16[512,512]{1,0:T(8,128)(2,1)S(1)}, bf16[512,512]{1,0:T(8,128)(2,1)S(1)}, u32[]{:S(2)}, u32[]{:S(2)}) collective-permute-start(bf16[512,512]{1,0:T(8,128)(2,1)S(1)} %pad_maximum_fusion), channel_id=1, source_target_pairs={{0,2},{2,0},{4,6},{6,4},{8,10},{10,8},{12,14},{14,12},{16,18},{18,... | collective-permute-start | bytes 1572872 | tf_op jit(solution)/shard_map/ppermute | solution.py:28
  31.3 16.9 %collective-permute-start.9 = (bf16[512,512]{1,0:T(8,128)(2,1)S(1)}, bf16[512,512]{1,0:T(8,128)(2,1)S(1)}, u32[]{:S(2)}, u32[]{:S(2)}) collective-permute-start(bf16[512,512]{1,0:T(8,128)(2,1)S(1)} %pad_maximum_fusion.1), channel_id=1, source_target_pairs={{0,2},{2,0},{4,6},{6,4},{8,10},{10,8},{12,14},{14,12},{16,18},{18,... | collective-permute-start | bytes 1572872 | tf_op jit(solution)/shard_map/ppermute | solution.py:28
  34.8 27.7 %collective-permute-start.10 = (bf16[64,2048]{1,0:T(8,128)(2,1)S(1)}, bf16[64,2048]{1,0:T(8,128)(2,1)S(1)}, u32[]{:S(2)}, u32[]{:S(2)}) collective-permute-start(bf16[64,2048]{1,0:T(8,128)(2,1)S(1)} %get-tuple-element.49), channel_id=1, source_target_pairs={{0,1},{1,0},{2,3},{3,2},{4,5},{5,4},{6,7},{7,6},{8,9},{9,8},{10,11... | collective-permute-start | bytes 786440 | tf_op jit(solution)/shard_map/ppermute | solution.py:454
  50.9 18.3 %collective-permute-start.11 = (bf16[64,2048]{1,0:T(8,128)(2,1)S(1)}, bf16[64,2048]{1,0:T(8,128)(2,1)S(1)}, u32[]{:S(2)}, u32[]{:S(2)}) collective-permute-start(bf16[64,2048]{1,0:T(8,128)(2,1)S(1)} %get-tuple-element.50), channel_id=1, source_target_pairs={{0,1},{1,0},{2,3},{3,2},{4,5},{5,4},{6,7},{7,6},{8,9},{9,8},{10,11... | collective-permute-start | bytes 786440 | tf_op jit(solution)/shard_map/ppermute | solution.py:454

commit v19 on v18

--- a/solution.py
+++ b/solution.py
@@ -427,10 +427,10 @@
     span_forward, span_masks, crossed = together(span_forward, span_masks, crossed)
     pages = [jnp.concatenate([own_page, crossed], axis=0)]
     pages.append(send(pages[0], 0))
-    span_early, span_late = together(span_early, span_late)
+    near = jnp.concatenate([span_kv, span_forward, span_early], axis=0)
     pages[1], span_late = together(pages[1], span_late)
-    span = [jnp.concatenate([span_kv, span_forward, span_early, span_late], axis=0)]
-    span_swapped = [swap_cores(span)]
+    span = [near, span_late]
+    span_swapped = [swap_cores(span[:1]), swap_cores(span[1:])]
 
     span_set = (span, span_swapped, span_masks)
     state = attend(span_query, 0, 1, [span_set], spec, None)

time: 71 us -> 70.9 us (level)
  Pallas kernels: 13.4 us -> 36.5 us
  starting transfers between devices: 36.4 us -> 13.8 us
    ppermute x2, starting transfers between devices: 25.1 us -> 0.14 us  [body(): lax.ppermute(pair[1], 'head', [(0, 1), (1, 0)])]
    pallas_call x3, Pallas kernels: 10.9 us -> 34.1 us  [attend(): pl.pallas_call(functools.partial(attend_kernel, spec, sizes, part, groups...]
    ppermute x10 -> x11, starting transfers between devices: 11.3 us -> 13.7 us  [hop(): lax.ppermute(value, 'seq', [(source, source ^ bit_of_core[source % 2]) fo...]
    ppermute x10 -> x11, waiting for transfers between devices: 10.8 us -> 8.5 us  [hop(): lax.ppermute(value, 'seq', [(source, source ^ bit_of_core[source % 2]) fo...]
    ppermute x2, waiting for transfers between devices: 5.7 us -> 7.5 us  [body(): lax.ppermute(pair[1], 'head', [(0, 1), (1, 0)])]
    unnamed x12 -> x11, local copies, waits for them, and re-layouts: 3.3 us -> 3.28 us
  transfers between devices with their start and end apart: 12 -> 13, of which waited for: 6 -> 6; matrix products, arithmetic and copies ran while one was open for 2% -> 2% of each run, Pallas kernels for 18% -> 51%
where the time goes in v19:
time: 70.9 us; the launch traced here: 70.1 us
  Pallas kernels  36.5 us (51%)
  waiting for transfers between devices  16 us (23%)
  starting transfers between devices  13.8 us (19%)
  local copies, waits for them, and re-layouts  3.35 us (5%)
    pallas_call x3, Pallas kernels, attend(): pl.pallas_call(functools.partial(attend_kernel, spec, sizes, part, groups...  34.1 us
    ppermute x11, starting transfers between devices, hop(): lax.ppermute(value, 'seq', [(source, source ^ bit_of_core[source % 2]) fo...  13.7 us
    ppermute x11, waiting for transfers between devices, hop(): lax.ppermute(value, 'seq', [(source, source ^ bit_of_core[source % 2]) fo...  8.5 us
    ppermute x2, waiting for transfers between devices, body(): lax.ppermute(pair[1], 'head', [(0, 1), (1, 0)])  7.5 us
    unnamed x11, local copies, waits for them, and re-layouts  3.28 us
    pallas_call x2, Pallas kernels, join(): pl.pallas_call(functools.partial(join_kernel, spots, len(pieces)), out_sh...  1.62 us
  transfers between devices with their start and end apart: 13, of which 6 were waited for; matrix products, arithmetic and copies ran while one was open for 2% of the time, Pallas kernels for 51%

profile of v19, /device:TPU:0, one launch (start us, length us, event | category | flops | bytes accessed | tf_op | source)
XLA Modules:
  0.0 70.1 jit_solution(6670407834193379372)
XLA Ops:
  0.0 0.0 copy-start
  0.0 2.9 %collective-permute-start = (bf16[128,1024]{1,0:T(8,128)(2,1)}, bf16[128,1024]{1,0:T(8,128)(2,1)S(1)}, u32[]{:S(2)}, u32[]{:S(2)}) collective-permute-start(bf16[128,1024]{1,0:T(8,128)(2,1)} %param.6), channel_id=1, source_target_pairs={{0,4},{2,10},{4,0},{6,14},{8,12},{10,2},{12,8},{14,6},{16,20},{18,... | collective-permute-start | bytes 786440 | tf_op jit(solution)/shard_map/ppermute | solution.py:28
  2.9 1.6 %collective-permute-start.2 = (bf16[128,1024]{1,0:T(8,128)(2,1)}, bf16[128,1024]{1,0:T(8,128)(2,1)S(1)}, u32[]{:S(2)}, u32[]{:S(2)}) collective-permute-start(bf16[128,1024]{1,0:T(8,128)(2,1)} %param.6), channel_id=1, source_target_pairs={{0,8},{2,6},{4,12},{6,2},{8,0},{10,14},{12,4},{14,10},{16,24},{18,... | collective-permute-start | bytes 786440 | tf_op jit(solution)/shard_map/ppermute | solution.py:28
  4.5 0.0 copy-start.1
  4.5 0.9 %copy-done.1 = bf16[2,64,1024]{2,1,0:T(8,128)(2,1)S(1)} copy-done((bf16[2,64,1024]{2,1,0:T(8,128)(2,1)S(1)}, bf16[2,64,1024]{2,1,0:T(8,128)(2,1)}, u32[]{:S(2)}) %copy-start.1) | copy-done | bytes 262168
  5.5 2.7 %collective-permute-start.1 = (bf16[64,1024]{1,0:T(8,128)(2,1)S(1)}, bf16[64,1024]{1,0:T(8,128)(2,1)S(1)}, u32[]{:S(2)}, u32[]{:S(2)}) collective-permute-start(bf16[64,1024]{1,0:T(8,128)(2,1)S(1)} %get-tuple-element.27), channel_id=1, source_target_pairs={{0,16},{2,18},{4,20},{6,22},{8,24},{10,26},{12,28},{14,30},{16,0},... | collective-permute-start | bytes 393224 | tf_op jit(solution)/shard_map/ppermute | solution.py:28
  8.2 0.0 copy-start.2
  8.2 0.7 copy-done.2
  8.8 0.0 copy-start.3
  8.8 0.7 copy-done.3
  9.5 0.8 %shard_map.55 = (bf16[1024,128]{1,0:T(8,128)(2,1)S(1)}, bf16[1024,128]{1,0:T(8,128)(2,1)S(1)}) custom-call(s32[2]{0:T(128)S(1)} %copy-done.3, s32[2,16]{1,0:T(2,128)S(1)} %copy-done.2), custom_call_target="tpu_custom_call" | custom-call | tf_op jit(solution)/shard_map/pallas_call | solution.py:84
  10.3 1.0 %constant_dynamic-update-slice_fusion.2 = bf16[384,1024]{1,0:T(8,128)(2,1)S(1)} fusion(bf16[128,1024]{1,0:T(8,128)(2,1)} %param.6), kind=kLoop, calls=%fused_computation.6 | loop fusion | bytes 524288
  11.3 1.3 %collective-permute-done.1 = bf16[64,1024]{1,0:T(8,128)(2,1)S(1)} collective-permute-done((bf16[64,1024]{1,0:T(8,128)(2,1)S(1)}, bf16[64,1024]{1,0:T(8,128)(2,1)S(1)}, u32[]{:S(2)}, u32[]{:S(2)}) %collective-permute-start.1) | collective-permute-done | bytes 131104 | tf_op jit(solution)/shard_map/ppermute | solution.py:28
  12.5 0.0 collective-permute-done
  12.6 0.0 collective-permute-done.2
  12.6 0.1 collective-permute-start.5
  12.7 1.5 %collective-permute-start.3 = (bf16[128,1024]{1,0:T(8,128)(2,1)S(1)}, bf16[128,1024]{1,0:T(8,128)(2,1)S(1)}, u32[]{:S(2)}, u32[]{:S(2)}) collective-permute-start(bf16[128,1024]{1,0:T(8,128)(2,1)S(1)} %constant_dynamic-update-slice_fusion.3), channel_id=1, source_target_pairs={{0,4},{2,10},{4,0},{6,14},{8,12},{10,2},{12,8},{14,6},{16,20},{18,... | collective-permute-start | bytes 786440 | tf_op jit(solution)/shard_map/ppermute | solution.py:28
  14.2 2.6 %collective-permute-start.4 = (bf16[128,1024]{1,0:T(8,128)(2,1)S(1)}, bf16[128,1024]{1,0:T(8,128)(2,1)S(1)}, u32[]{:S(2)}, u32[]{:S(2)}) collective-permute-start(bf16[128,1024]{1,0:T(8,128)(2,1)S(1)} %collective-permute-done), channel_id=1, source_target_pairs={{0,8},{2,6},{4,12},{6,2},{8,0},{10,14},{12,4},{14,10},{16,24},{18,... | collective-permute-start | bytes 786440 | tf_op jit(solution)/shard_map/ppermute | solution.py:28
  16.8 3.2 %collective-permute-done.3 = bf16[128,1024]{1,0:T(8,128)(2,1)S(1)} collective-permute-done((bf16[128,1024]{1,0:T(8,128)(2,1)S(1)}, bf16[128,1024]{1,0:T(8,128)(2,1)S(1)}, u32[]{:S(2)}, u32[]{:S(2)}) %collective-permute-start.3) | collective-permute-done | bytes 262176 | tf_op jit(solution)/shard_map/ppermute | solution.py:28
  20.1 2.2 %collective-permute-done.4.refs_2_ = bf16[128,1024]{1,0:T(8,128)(2,1)S(1)} collective-permute-done((bf16[128,1024]{1,0:T(8,128)(2,1)S(1)}, bf16[128,1024]{1,0:T(8,128)(2,1)S(1)}, u32[]{:S(2)}, u32[]{:S(2)}) %collective-permute-start.4) | collective-permute-done | bytes 262176 | tf_op jit(solution)/shard_map/ppermute | solution.py:28
  22.3 0.0 collective-permute-start.6
  22.3 1.9 %collective-permute-start.7 = (bf16[256,512]{1,0:T(8,128)(2,1)S(1)}, bf16[256,512]{1,0:T(8,128)(2,1)S(1)}, u32[]{:S(2)}, u32[]{:S(2)}) collective-permute-start(bf16[256,512]{1,0:T(8,128)(2,1)S(1)} %pad_maximum_fusion.2.refs_6_), channel_id=1, source_target_pairs={{0,8},{2,6},{4,12},{6,2},{8,0},{10,14},{12,4},{14,10},{16,24},{18,... | collective-permute-start | bytes 786440 | tf_op jit(solution)/shard_map/ppermute | solution.py:28
  24.3 0.3 collective-permute-start.9
  24.5 0.0 collective-permute-done.6.refs_4_
  24.5 0.0 collective-permute-done.5.refs_3_
  24.5 0.0 copy-done
  24.5 5.4 %shard_map.57 = (f32[4096,256]{1,0:T(8,128)S(1)}, bf16[4096,128]{1,0:T(8,128)(2,1)S(1)}) custom-call(bf16[128,4096]{1,0:T(8,128)(2,1)S(1)} %copy-done, bf16[1024,128]{1,0:T(8,128)(2,1)S(1)} %get-tuple-element.28.refs_0_, bf16[384,1024]{1,0:T(8,128)(2,1)S(1)} %constant_dynamic-update-slice_fusion.refs_1_, ...), custom_call_target="tpu_custom_call" | custom-call | flops 4294967296 | bytes 3145728 | tf_op jit(solution)/shard_map/pallas_call | solution.py:318
  30.0 0.0 collective-permute-done.7.refs_7_
  30.0 0.1 collective-permute-start.8
  30.1 1.5 %collective-permute-done.9.refs_7_ = bf16[256,512]{1,0:T(8,128)(2,1)S(1)} collective-permute-done((bf16[256,512]{1,0:T(8,128)(2,1)S(1)}, bf16[256,512]{1,0:T(8,128)(2,1)S(1)}, u32[]{:S(2)}, u32[]{:S(2)}) %collective-permute-start.9) | collective-permute-done | bytes 262176 | tf_op jit(solution)/shard_map/ppermute | solution.py:28
  31.6 0.1 collective-permute-start.10
  31.7 0.3 collective-permute-done.8.refs_8_
  32.0 14.4 %shard_map.58 = (bf16[64,2048]{1,0:T(8,128)(2,1)S(1)}, bf16[64,2048]{1,0:T(8,128)(2,1)S(1)}) custom-call(bf16[128,4096]{1,0:T(8,128)(2,1)S(1)} %copy-done, bf16[1024,128]{1,0:T(8,128)(2,1)S(1)} %get-tuple-element.28.refs_0_, bf16[384,1024]{1,0:T(8,128)(2,1)S(1)} %constant_dynamic-update-slice_fusion.refs_1_, ...), custom_call_target="tpu_custom_call" | custom-call | flops 2147483648 | bytes 1572864 | tf_op jit(solution)/shard_map/pallas_call | solution.py:318
  46.4 0.1 collective-permute-start.11
  46.5 0.0 collective-permute-done.10.refs_8_
  46.5 14.2 %shard_map.59 = (bf16[64,2048]{1,0:T(8,128)(2,1)S(1)}, bf16[64,2048]{1,0:T(8,128)(2,1)S(1)}) custom-call(bf16[128,4096]{1,0:T(8,128)(2,1)S(1)} %copy-done, bf16[1024,128]{1,0:T(8,128)(2,1)S(1)} %get-tuple-element.28.refs_0_, bf16[384,1024]{1,0:T(8,128)(2,1)S(1)} %constant_dynamic-update-slice_fusion.refs_1_, ...), custom_call_target="tpu_custom_call" | custom-call | flops 2147483648 | bytes 1572864 | tf_op jit(solution)/shard_map/pallas_call | solution.py:318
  60.8 0.1 collective-permute-start.12
  60.8 0.0 collective-permute-done.11.refs_2_
  60.8 0.9 %shard_map.60.refs_0_ = bf16[64,8192]{1,0:T(8,128)(2,1)} custom-call(bf16[64,2048]{1,0:T(8,128)(2,1)S(1)} %get-tuple-element.40.refs_0_, bf16[64,2048]{1,0:T(8,128)(2,1)S(1)} %get-tuple-element.44.refs_1_, bf16[64,2048]{1,0:T(8,128)(2,1)S(1)} %collective-permute-done.11.refs_2_), custom_call_target="tpu_custom_call" | custom-call | tf_op jit(solution)/shard_map/pallas_call | solution.py:369
  61.8 7.5 %collective-permute-done.12.refs_1_ = bf16[64,2048]{1,0:T(8,128)(2,1)S(1)} collective-permute-done((bf16[64,2048]{1,0:T(8,128)(2,1)S(1)}, bf16[64,2048]{1,0:T(8,128)(2,1)S(1)}, u32[]{:S(2)}, u32[]{:S(2)}) %collective-permute-start.12) | collective-permute-done | bytes 262176 | tf_op jit(solution)/shard_map/ppermute | solution.py:454
  69.3 0.7 %shard_map.61 = bf16[64,8192]{1,0:T(8,128)(2,1)} custom-call(bf16[64,8192]{1,0:T(8,128)(2,1)} %shard_map.60.refs_0_, bf16[64,2048]{1,0:T(8,128)(2,1)S(1)} %collective-permute-done.12.refs_1_), custom_call_target="tpu_custom_call", output_to_operand_aliasing={{}: (0, {})} | custom-call | tf_op jit(solution)/shard_map/pallas_call | solution.py:369
  (11 shorter events, 0.2 us)
Async XLA Ops:
  0.0 24.5 %copy-start = (bf16[128,4096]{1,0:T(8,128)(2,1)S(1)}, bf16[128,4096]{1,0:T(8,128)(2,1)}, u32[]{:S(2)}) copy-start(bf16[128,4096]{1,0:T(8,128)(2,1)} %q_ref.5) | copy-start | bytes 3145732
  0.0 12.5 %collective-permute-start = (bf16[128,1024]{1,0:T(8,128)(2,1)}, bf16[128,1024]{1,0:T(8,128)(2,1)S(1)}, u32[]{:S(2)}, u32[]{:S(2)}) collective-permute-start(bf16[128,1024]{1,0:T(8,128)(2,1)} %param.6), channel_id=1, source_target_pairs={{0,4},{2,10},{4,0},{6,14},{8,12},{10,2},{12,8},{14,6},{16,20},{18,... | collective-permute-start | bytes 786440 | tf_op jit(solution)/shard_map/ppermute | solution.py:28
  2.9 9.6 %collective-permute-start.2 = (bf16[128,1024]{1,0:T(8,128)(2,1)}, bf16[128,1024]{1,0:T(8,128)(2,1)S(1)}, u32[]{:S(2)}, u32[]{:S(2)}) collective-permute-start(bf16[128,1024]{1,0:T(8,128)(2,1)} %param.6), channel_id=1, source_target_pairs={{0,8},{2,6},{4,12},{6,2},{8,0},{10,14},{12,4},{14,10},{16,24},{18,... | collective-permute-start | bytes 786440 | tf_op jit(solution)/shard_map/ppermute | solution.py:28
  4.5 0.9 %copy-start.1 = (bf16[2,64,1024]{2,1,0:T(8,128)(2,1)S(1)}, bf16[2,64,1024]{2,1,0:T(8,128)(2,1)}, u32[]{:S(2)}) copy-start(bf16[2,64,1024]{2,1,0:T(8,128)(2,1)} %cache_ref.1) | copy-start | bytes 786436
  5.5 7.0 %collective-permute-start.1 = (bf16[64,1024]{1,0:T(8,128)(2,1)S(1)}, bf16[64,1024]{1,0:T(8,128)(2,1)S(1)}, u32[]{:S(2)}, u32[]{:S(2)}) collective-permute-start(bf16[64,1024]{1,0:T(8,128)(2,1)S(1)} %get-tuple-element.27), channel_id=1, source_target_pairs={{0,16},{2,18},{4,20},{6,22},{8,24},{10,26},{12,28},{14,30},{16,0},... | collective-permute-start | bytes 393224 | tf_op jit(solution)/shard_map/ppermute | solution.py:28
  8.2 0.7 copy-start.2
  8.8 0.7 copy-start.3
  12.6 11.9 %collective-permute-start.5 = (bf16[384,1024]{1,0:T(8,128)(2,1)S(1)}, bf16[384,1024]{1,0:T(8,128)(2,1)S(1)}, u32[]{:S(2)}, u32[]{:S(2)}) collective-permute-start(bf16[384,1024]{1,0:T(8,128)(2,1)S(1)} %constant_dynamic-update-slice_fusion.refs_1_), channel_id=1, source_target_pairs={{0,2},{2,0},{4,6},{6,4},{8,10},{10,8},{12,14},{14,12},{16,18},{18,... | collective-permute-start | bytes 2359304 | tf_op jit(solution)/shard_map/ppermute | solution.py:28
  12.7 7.4 %collective-permute-start.3 = (bf16[128,1024]{1,0:T(8,128)(2,1)S(1)}, bf16[128,1024]{1,0:T(8,128)(2,1)S(1)}, u32[]{:S(2)}, u32[]{:S(2)}) collective-permute-start(bf16[128,1024]{1,0:T(8,128)(2,1)S(1)} %constant_dynamic-update-slice_fusion.3), channel_id=1, source_target_pairs={{0,4},{2,10},{4,0},{6,14},{8,12},{10,2},{12,8},{14,6},{16,20},{18,... | collective-permute-start | bytes 786440 | tf_op jit(solution)/shard_map/ppermute | solution.py:28
  14.2 8.1 %collective-permute-start.4 = (bf16[128,1024]{1,0:T(8,128)(2,1)S(1)}, bf16[128,1024]{1,0:T(8,128)(2,1)S(1)}, u32[]{:S(2)}, u32[]{:S(2)}) collective-permute-start(bf16[128,1024]{1,0:T(8,128)(2,1)S(1)} %collective-permute-done), channel_id=1, source_target_pairs={{0,8},{2,6},{4,12},{6,2},{8,0},{10,14},{12,4},{14,10},{16,24},{18,... | collective-permute-start | bytes 786440 | tf_op jit(solution)/shard_map/ppermute | solution.py:28
  22.3 2.2 %collective-permute-start.6 = (bf16[128,1024]{1,0:T(8,128)(2,1)S(1)}, bf16[128,1024]{1,0:T(8,128)(2,1)S(1)}, u32[]{:S(2)}, u32[]{:S(2)}) collective-permute-start(bf16[128,1024]{1,0:T(8,128)(2,1)S(1)} %collective-permute-done.4.refs_2_), channel_id=1, source_target_pairs={{0,2},{2,0},{4,6},{6,4},{8,10},{10,8},{12,14},{14,12},{16,18},{18,... | collective-permute-start | bytes 786440 | tf_op jit(solution)/shard_map/ppermute | solution.py:28
  22.3 7.6 %collective-permute-start.7 = (bf16[256,512]{1,0:T(8,128)(2,1)S(1)}, bf16[256,512]{1,0:T(8,128)(2,1)S(1)}, u32[]{:S(2)}, u32[]{:S(2)}) collective-permute-start(bf16[256,512]{1,0:T(8,128)(2,1)S(1)} %pad_maximum_fusion.2.refs_6_), channel_id=1, source_target_pairs={{0,8},{2,6},{4,12},{6,2},{8,0},{10,14},{12,4},{14,10},{16,24},{18,... | collective-permute-start | bytes 786440 | tf_op jit(solution)/shard_map/ppermute | solution.py:28
  24.3 7.3 %collective-permute-start.9 = (bf16[256,512]{1,0:T(8,128)(2,1)S(1)}, bf16[256,512]{1,0:T(8,128)(2,1)S(1)}, u32[]{:S(2)}, u32[]{:S(2)}) collective-permute-start(bf16[256,512]{1,0:T(8,128)(2,1)S(1)} %pad_maximum_fusion.3.refs_6_), channel_id=1, source_target_pairs={{0,8},{2,6},{4,12},{6,2},{8,0},{10,14},{12,4},{14,10},{16,24},{18,... | collective-permute-start | bytes 786440 | tf_op jit(solution)/shard_map/ppermute | solution.py:28
  30.0 2.0 %collective-permute-start.8 = (bf16[512,512]{1,0:T(8,128)(2,1)S(1)}, bf16[512,512]{1,0:T(8,128)(2,1)S(1)}, u32[]{:S(2)}, u32[]{:S(2)}) collective-permute-start(bf16[512,512]{1,0:T(8,128)(2,1)S(1)} %pad_maximum_fusion), channel_id=1, source_target_pairs={{0,2},{2,0},{4,6},{6,4},{8,10},{10,8},{12,14},{14,12},{16,18},{18,... | collective-permute-start | bytes 1572872 | tf_op jit(solution)/shard_map/ppermute | solution.py:28
  31.6 14.9 %collective-permute-start.10 = (bf16[512,512]{1,0:T(8,128)(2,1)S(1)}, bf16[512,512]{1,0:T(8,128)(2,1)S(1)}, u32[]{:S(2)}, u32[]{:S(2)}) collective-permute-start(bf16[512,512]{1,0:T(8,128)(2,1)S(1)} %pad_maximum_fusion.1), channel_id=1, source_target_pairs={{0,2},{2,0},{4,6},{6,4},{8,10},{10,8},{12,14},{14,12},{16,18},{18,... | collective-permute-start | bytes 1572872 | tf_op jit(solution)/shard_map/ppermute | solution.py:28
  46.4 14.4 %collective-permute-start.11 = (bf16[64,2048]{1,0:T(8,128)(2,1)S(1)}, bf16[64,2048]{1,0:T(8,128)(2,1)S(1)}, u32[]{:S(2)}, u32[]{:S(2)}) collective-permute-start(bf16[64,2048]{1,0:T(8,128)(2,1)S(1)} %get-tuple-element.45), channel_id=1, source_target_pairs={{0,1},{1,0},{2,3},{3,2},{4,5},{5,4},{6,7},{7,6},{8,9},{9,8},{10,11... | collective-permute-start | bytes 786440 | tf_op jit(solution)/shard_map/ppermute | solution.py:454
  60.8 8.5 %collective-permute-start.12 = (bf16[64,2048]{1,0:T(8,128)(2,1)S(1)}, bf16[64,2048]{1,0:T(8,128)(2,1)S(1)}, u32[]{:S(2)}, u32[]{:S(2)}) collective-permute-start(bf16[64,2048]{1,0:T(8,128)(2,1)S(1)} %get-tuple-element.46), channel_id=1, source_target_pairs={{0,1},{1,0},{2,3},{3,2},{4,5},{5,4},{6,7},{7,6},{8,9},{9,8},{10,11... | collective-permute-start | bytes 786440 | tf_op jit(solution)/shard_map/ppermute | solution.py:454

commit v20 on v18

--- a/solution.py
+++ b/solution.py
@@ -443,7 +443,11 @@
     arrived = [send(rows, stages - 1) for rows in held]
     results = []
     for part in range(parts):
-        arrived[part], state = together(arrived[part], state)
+        if part:
+            first_kept, arrived[part] = together(results[-1][0], arrived[part])
+            results[-1] = (first_kept, results[-1][1])
+        else:
+            arrived[part], state = together(arrived[part], state)
         mine = [held[part], arrived[part]]
         page_set = (mine, [swap_cores(mine)], page_masks)
         results.append(attend(span_query, part, parts, [span_set, page_set], spec, state))

time: 71 us -> 72.2 us (1.017); the launches traced: 70.1 us -> 72 us
  starting transfers between devices: 36.4 us -> 13 us
  Pallas kernels: 13.4 us -> 36.5 us
  waiting for transfers between devices: 16.5 us -> 18.6 us
    pallas_call x3, Pallas kernels: 10.9 us -> 34.1 us  [attend(): pl.pallas_call(functools.partial(attend_kernel, spec, sizes, part, groups...]
    ppermute x2, starting transfers between devices: 25.1 us -> 3.6 us  [body(): lax.ppermute(pair[1], 'head', [(0, 1), (1, 0)])]
    ppermute x10, waiting for transfers between devices: 10.8 us -> 12.9 us  [hop(): lax.ppermute(value, 'seq', [(source, source ^ bit_of_core[source % 2]) fo...]
    ppermute x10, starting transfers between devices: 11.3 us -> 9.44 us  [hop(): lax.ppermute(value, 'seq', [(source, source ^ bit_of_core[source % 2]) fo...]
  transfers between devices with their start and end apart: 12 -> 12, of which waited for: 6 -> 5; matrix products, arithmetic and copies ran while one was open for 2% -> 2% of each run, Pallas kernels for 18% -> 50%
where the time goes in v20:
time: 72.2 us; the launch traced here: 72 us
  Pallas kernels  36.5 us (51%)
  waiting for transfers between devices  18.6 us (26%)
  starting transfers between devices  13 us (18%)
  local copies, waits for them, and re-layouts  3.37 us (5%)
    pallas_call x3, Pallas kernels, attend(): pl.pallas_call(functools.partial(attend_kernel, spec, sizes, part, groups...  34.1 us
    ppermute x10, waiting for transfers between devices, hop(): lax.ppermute(value, 'seq', [(source, source ^ bit_of_core[source % 2]) fo...  12.9 us
    ppermute x10, starting transfers between devices, hop(): lax.ppermute(value, 'seq', [(source, source ^ bit_of_core[source % 2]) fo...  9.44 us
    ppermute x2, waiting for transfers between devices, body(): lax.ppermute(pair[1], 'head', [(0, 1), (1, 0)])  5.7 us
    ppermute x2, starting transfers between devices, body(): lax.ppermute(pair[1], 'head', [(0, 1), (1, 0)])  3.6 us
    unnamed x12, local copies, waits for them, and re-layouts  3.3 us
    pallas_call x2, Pallas kernels, join(): pl.pallas_call(functools.partial(join_kernel, spots, len(pieces)), out_sh...  1.61 us
  transfers between devices with their start and end apart: 12, of which 5 were waited for; matrix products, arithmetic and copies ran while one was open for 2% of the time, Pallas kernels for 50%

profile of v20, /device:TPU:0, one launch (start us, length us, event | category | flops | bytes accessed | tf_op | source)
XLA Modules:
  0.0 72.0 jit_solution(2726913650204975851)
XLA Ops:
  0.0 0.0 copy-start
  0.0 2.9 %collective-permute-start = (bf16[128,1024]{1,0:T(8,128)(2,1)}, bf16[128,1024]{1,0:T(8,128)(2,1)S(1)}, u32[]{:S(2)}, u32[]{:S(2)}) collective-permute-start(bf16[128,1024]{1,0:T(8,128)(2,1)} %param.6), channel_id=1, source_target_pairs={{0,4},{2,10},{4,0},{6,14},{8,12},{10,2},{12,8},{14,6},{16,20},{18,... | collective-permute-start | bytes 786440 | tf_op jit(solution)/shard_map/ppermute | solution.py:28
  2.9 0.0 copy-start.1
  2.9 0.9 %copy-done.1 = bf16[2,64,1024]{2,1,0:T(8,128)(2,1)S(1)} copy-done((bf16[2,64,1024]{2,1,0:T(8,128)(2,1)S(1)}, bf16[2,64,1024]{2,1,0:T(8,128)(2,1)}, u32[]{:S(2)}) %copy-start.1) | copy-done | bytes 262168
  3.9 2.7 %collective-permute-start.1 = (bf16[64,1024]{1,0:T(8,128)(2,1)S(1)}, bf16[64,1024]{1,0:T(8,128)(2,1)S(1)}, u32[]{:S(2)}, u32[]{:S(2)}) collective-permute-start(bf16[64,1024]{1,0:T(8,128)(2,1)S(1)} %get-tuple-element.28), channel_id=1, source_target_pairs={{0,16},{2,18},{4,20},{6,22},{8,24},{10,26},{12,28},{14,30},{16,0},... | collective-permute-start | bytes 393224 | tf_op jit(solution)/shard_map/ppermute | solution.py:28
  6.6 1.6 %collective-permute-start.2 = (bf16[128,1024]{1,0:T(8,128)(2,1)}, bf16[128,1024]{1,0:T(8,128)(2,1)S(1)}, u32[]{:S(2)}, u32[]{:S(2)}) collective-permute-start(bf16[128,1024]{1,0:T(8,128)(2,1)} %param.6), channel_id=1, source_target_pairs={{0,8},{2,6},{4,12},{6,2},{8,0},{10,14},{12,4},{14,10},{16,24},{18,... | collective-permute-start | bytes 786440 | tf_op jit(solution)/shard_map/ppermute | solution.py:28
  8.1 0.0 copy-start.2
  8.1 0.7 copy-done.2
  8.8 0.0 copy-start.3
  8.8 0.7 copy-done.3
  9.5 0.8 %shard_map.55 = (bf16[1024,128]{1,0:T(8,128)(2,1)S(1)}, bf16[1024,128]{1,0:T(8,128)(2,1)S(1)}) custom-call(s32[2]{0:T(128)S(1)} %copy-done.3, s32[2,16]{1,0:T(2,128)S(1)} %copy-done.2), custom_call_target="tpu_custom_call" | custom-call | tf_op jit(solution)/shard_map/pallas_call | solution.py:84
  10.3 2.5 %collective-permute-done.1 = bf16[64,1024]{1,0:T(8,128)(2,1)S(1)} collective-permute-done((bf16[64,1024]{1,0:T(8,128)(2,1)S(1)}, bf16[64,1024]{1,0:T(8,128)(2,1)S(1)}, u32[]{:S(2)}, u32[]{:S(2)}) %collective-permute-start.1) | collective-permute-done | bytes 131104 | tf_op jit(solution)/shard_map/ppermute | solution.py:28
  12.8 0.0 collective-permute-done
  12.8 0.0 collective-permute-start.3
  12.9 1.6 %collective-permute-start.4 = (bf16[128,1024]{1,0:T(8,128)(2,1)S(1)}, bf16[128,1024]{1,0:T(8,128)(2,1)S(1)}, u32[]{:S(2)}, u32[]{:S(2)}) collective-permute-start(bf16[128,1024]{1,0:T(8,128)(2,1)S(1)} %constant_dynamic-update-slice_fusion), channel_id=1, source_target_pairs={{0,4},{2,10},{4,0},{6,14},{8,12},{10,2},{12,8},{14,6},{16,20},{18,... | collective-permute-start | bytes 786440 | tf_op jit(solution)/shard_map/ppermute | solution.py:28
  14.4 1.0 %constant_dynamic-update-slice_fusion.5 = bf16[512,1024]{1,0:T(8,128)(2,1)S(1)} fusion(bf16[128,1024]{1,0:T(8,128)(2,1)} %param.6), kind=kLoop, calls=%fused_computation.9 | loop fusion | bytes 524288
  15.4 0.0 collective-permute-done.2
  15.4 6.3 %collective-permute-done.3 = bf16[128,1024]{1,0:T(8,128)(2,1)S(1)} collective-permute-done((bf16[128,1024]{1,0:T(8,128)(2,1)S(1)}, bf16[128,1024]{1,0:T(8,128)(2,1)S(1)}, u32[]{:S(2)}, u32[]{:S(2)}) %collective-permute-start.3) | collective-permute-done | bytes 262176 | tf_op jit(solution)/shard_map/ppermute | solution.py:28
  21.7 0.0 collective-permute-done.4
  21.8 0.2 collective-permute-start.5
  22.0 0.1 collective-permute-start.6
  22.1 2.4 %collective-permute-done.5.refs_2_ = bf16[512,1024]{1,0:T(8,128)(2,1)S(1)} collective-permute-done((bf16[512,1024]{1,0:T(8,128)(2,1)S(1)}, bf16[512,1024]{1,0:T(8,128)(2,1)S(1)}, u32[]{:S(2)}, u32[]{:S(2)}) %collective-permute-start.5) | collective-permute-done | bytes 1048608 | tf_op jit(solution)/shard_map/ppermute | solution.py:28
  24.5 0.0 copy-done
  24.5 5.4 %shard_map.57 = (f32[4096,256]{1,0:T(8,128)S(1)}, bf16[4096,128]{1,0:T(8,128)(2,1)S(1)}) custom-call(bf16[128,4096]{1,0:T(8,128)(2,1)S(1)} %copy-done, bf16[1024,128]{1,0:T(8,128)(2,1)S(1)} %get-tuple-element.29.refs_0_, bf16[512,1024]{1,0:T(8,128)(2,1)S(1)} %constant_dynamic-update-slice_fusion.2.refs_1_, bf16[512,1024]{1,0:T(8,128)(2,1)S(1)} %collective-permute-done.5.refs_2_), custom_call_target="tpu_custom_call" | custom-call | flops 4294967296 | bytes 3145728 | tf_op jit(solution)/shard_map/pallas_call | solution.py:318
  29.9 0.0 collective-permute-done.6.refs_5_
  30.0 0.2 collective-permute-start.7
  30.2 0.1 collective-permute-start.8
  30.3 1.7 %collective-permute-done.7.refs_6_ = bf16[512,512]{1,0:T(8,128)(2,1)S(1)} collective-permute-done((bf16[512,512]{1,0:T(8,128)(2,1)S(1)}, bf16[512,512]{1,0:T(8,128)(2,1)S(1)}, u32[]{:S(2)}, u32[]{:S(2)}) %collective-permute-start.7) | collective-permute-done | bytes 524320 | tf_op jit(solution)/shard_map/ppermute | solution.py:28
  32.0 14.4 %shard_map.58 = (bf16[64,2048]{1,0:T(8,128)(2,1)S(1)}, bf16[64,2048]{1,0:T(8,128)(2,1)S(1)}) custom-call(bf16[128,4096]{1,0:T(8,128)(2,1)S(1)} %copy-done, bf16[1024,128]{1,0:T(8,128)(2,1)S(1)} %get-tuple-element.29.refs_0_, bf16[512,1024]{1,0:T(8,128)(2,1)S(1)} %constant_dynamic-update-slice_fusion.2.refs_1_, ...), custom_call_target="tpu_custom_call" | custom-call | flops 2147483648 | bytes 1572864 | tf_op jit(solution)/shard_map/pallas_call | solution.py:318
  46.4 0.0 collective-permute-done.8.refs_5_
  46.5 0.2 collective-permute-start.9
  46.7 1.8 %collective-permute-start.10 = (bf16[64,2048]{1,0:T(8,128)(2,1)S(1)}, bf16[64,2048]{1,0:T(8,128)(2,1)S(1)}, u32[]{:S(2)}, u32[]{:S(2)}) collective-permute-start(bf16[64,2048]{1,0:T(8,128)(2,1)S(1)} %get-tuple-element.47), channel_id=1, source_target_pairs={{0,1},{1,0},{2,3},{3,2},{4,5},{5,4},{6,7},{7,6},{8,9},{9,8},{10,11... | collective-permute-start | bytes 786440 | tf_op jit(solution)/shard_map/ppermute | solution.py:458
  48.4 0.0 collective-permute-done.9.refs_6_
  48.4 14.2 %shard_map.59 = (bf16[64,2048]{1,0:T(8,128)(2,1)S(1)}, bf16[64,2048]{1,0:T(8,128)(2,1)S(1)}) custom-call(bf16[128,4096]{1,0:T(8,128)(2,1)S(1)} %copy-done, bf16[1024,128]{1,0:T(8,128)(2,1)S(1)} %get-tuple-element.29.refs_0_, bf16[512,1024]{1,0:T(8,128)(2,1)S(1)} %constant_dynamic-update-slice_fusion.2.refs_1_, ...), custom_call_target="tpu_custom_call" | custom-call | flops 2147483648 | bytes 1572864 | tf_op jit(solution)/shard_map/pallas_call | solution.py:318
  62.7 1.8 %collective-permute-start.11 = (bf16[64,2048]{1,0:T(8,128)(2,1)S(1)}, bf16[64,2048]{1,0:T(8,128)(2,1)S(1)}, u32[]{:S(2)}, u32[]{:S(2)}) collective-permute-start(bf16[64,2048]{1,0:T(8,128)(2,1)S(1)} %get-tuple-element.48), channel_id=1, source_target_pairs={{0,1},{1,0},{2,3},{3,2},{4,5},{5,4},{6,7},{7,6},{8,9},{9,8},{10,11... | collective-permute-start | bytes 786440 | tf_op jit(solution)/shard_map/ppermute | solution.py:458
  64.5 0.0 collective-permute-done.10.refs_2_
  64.5 0.9 %shard_map.60.refs_0_ = bf16[64,8192]{1,0:T(8,128)(2,1)} custom-call(bf16[64,2048]{1,0:T(8,128)(2,1)S(1)} %get-tuple-element.44.refs_0_, bf16[64,2048]{1,0:T(8,128)(2,1)S(1)} %get-tuple-element.46.refs_1_, bf16[64,2048]{1,0:T(8,128)(2,1)S(1)} %collective-permute-done.10.refs_2_), custom_call_target="tpu_custom_call" | custom-call | tf_op jit(solution)/shard_map/pallas_call | solution.py:369
  65.4 5.7 %collective-permute-done.11.refs_1_ = bf16[64,2048]{1,0:T(8,128)(2,1)S(1)} collective-permute-done((bf16[64,2048]{1,0:T(8,128)(2,1)S(1)}, bf16[64,2048]{1,0:T(8,128)(2,1)S(1)}, u32[]{:S(2)}, u32[]{:S(2)}) %collective-permute-start.11) | collective-permute-done | bytes 262176 | tf_op jit(solution)/shard_map/ppermute | solution.py:458
  71.1 0.7 shard_map.61
  (12 shorter events, 0.2 us)
Async XLA Ops:
  0.0 24.5 %copy-start = (bf16[128,4096]{1,0:T(8,128)(2,1)S(1)}, bf16[128,4096]{1,0:T(8,128)(2,1)}, u32[]{:S(2)}) copy-start(bf16[128,4096]{1,0:T(8,128)(2,1)} %q_ref.5) | copy-start | bytes 3145732
  0.0 12.8 %collective-permute-start = (bf16[128,1024]{1,0:T(8,128)(2,1)}, bf16[128,1024]{1,0:T(8,128)(2,1)S(1)}, u32[]{:S(2)}, u32[]{:S(2)}) collective-permute-start(bf16[128,1024]{1,0:T(8,128)(2,1)} %param.6), channel_id=1, source_target_pairs={{0,4},{2,10},{4,0},{6,14},{8,12},{10,2},{12,8},{14,6},{16,20},{18,... | collective-permute-start | bytes 786440 | tf_op jit(solution)/shard_map/ppermute | solution.py:28
  2.9 0.9 %copy-start.1 = (bf16[2,64,1024]{2,1,0:T(8,128)(2,1)S(1)}, bf16[2,64,1024]{2,1,0:T(8,128)(2,1)}, u32[]{:S(2)}) copy-start(bf16[2,64,1024]{2,1,0:T(8,128)(2,1)} %cache_ref.1) | copy-start | bytes 786436
  3.9 8.9 %collective-permute-start.1 = (bf16[64,1024]{1,0:T(8,128)(2,1)S(1)}, bf16[64,1024]{1,0:T(8,128)(2,1)S(1)}, u32[]{:S(2)}, u32[]{:S(2)}) collective-permute-start(bf16[64,1024]{1,0:T(8,128)(2,1)S(1)} %get-tuple-element.28), channel_id=1, source_target_pairs={{0,16},{2,18},{4,20},{6,22},{8,24},{10,26},{12,28},{14,30},{16,0},... | collective-permute-start | bytes 393224 | tf_op jit(solution)/shard_map/ppermute | solution.py:28
  6.6 8.8 %collective-permute-start.2 = (bf16[128,1024]{1,0:T(8,128)(2,1)}, bf16[128,1024]{1,0:T(8,128)(2,1)S(1)}, u32[]{:S(2)}, u32[]{:S(2)}) collective-permute-start(bf16[128,1024]{1,0:T(8,128)(2,1)} %param.6), channel_id=1, source_target_pairs={{0,8},{2,6},{4,12},{6,2},{8,0},{10,14},{12,4},{14,10},{16,24},{18,... | collective-permute-start | bytes 786440 | tf_op jit(solution)/shard_map/ppermute | solution.py:28
  8.1 0.7 copy-start.2
  8.8 0.7 copy-start.3
  12.8 8.9 %collective-permute-start.3 = (bf16[128,1024]{1,0:T(8,128)(2,1)S(1)}, bf16[128,1024]{1,0:T(8,128)(2,1)S(1)}, u32[]{:S(2)}, u32[]{:S(2)}) collective-permute-start(bf16[128,1024]{1,0:T(8,128)(2,1)S(1)} %collective-permute-done), channel_id=1, source_target_pairs={{0,8},{2,6},{4,12},{6,2},{8,0},{10,14},{12,4},{14,10},{16,24},{18,... | collective-permute-start | bytes 786440 | tf_op jit(solution)/shard_map/ppermute | solution.py:28
  12.9 8.9 %collective-permute-start.4 = (bf16[128,1024]{1,0:T(8,128)(2,1)S(1)}, bf16[128,1024]{1,0:T(8,128)(2,1)S(1)}, u32[]{:S(2)}, u32[]{:S(2)}) collective-permute-start(bf16[128,1024]{1,0:T(8,128)(2,1)S(1)} %constant_dynamic-update-slice_fusion), channel_id=1, source_target_pairs={{0,4},{2,10},{4,0},{6,14},{8,12},{10,2},{12,8},{14,6},{16,20},{18,... | collective-permute-start | bytes 786440 | tf_op jit(solution)/shard_map/ppermute | solution.py:28
  21.8 2.7 %collective-permute-start.5 = (bf16[512,1024]{1,0:T(8,128)(2,1)S(1)}, bf16[512,1024]{1,0:T(8,128)(2,1)S(1)}, u32[]{:S(2)}, u32[]{:S(2)}) collective-permute-start(bf16[512,1024]{1,0:T(8,128)(2,1)S(1)} %constant_dynamic-update-slice_fusion.2.refs_1_), channel_id=1, source_target_pairs={{0,2},{2,0},{4,6},{6,4},{8,10},{10,8},{12,14},{14,12},{16,18},{18,... | collective-permute-start | bytes 3145736 | tf_op jit(solution)/shard_map/ppermute | solution.py:28
  22.0 7.9 %collective-permute-start.6 = (bf16[256,512]{1,0:T(8,128)(2,1)S(1)}, bf16[256,512]{1,0:T(8,128)(2,1)S(1)}, u32[]{:S(2)}, u32[]{:S(2)}) collective-permute-start(bf16[256,512]{1,0:T(8,128)(2,1)S(1)} %pad_maximum_fusion.2.refs_4_), channel_id=1, source_target_pairs={{0,8},{2,6},{4,12},{6,2},{8,0},{10,14},{12,4},{14,10},{16,24},{18,... | collective-permute-start | bytes 786440 | tf_op jit(solution)/shard_map/ppermute | solution.py:28
  30.0 2.0 %collective-permute-start.7 = (bf16[512,512]{1,0:T(8,128)(2,1)S(1)}, bf16[512,512]{1,0:T(8,128)(2,1)S(1)}, u32[]{:S(2)}, u32[]{:S(2)}) collective-permute-start(bf16[512,512]{1,0:T(8,128)(2,1)S(1)} %pad_maximum_fusion), channel_id=1, source_target_pairs={{0,2},{2,0},{4,6},{6,4},{8,10},{10,8},{12,14},{14,12},{16,18},{18,... | collective-permute-start | bytes 1572872 | tf_op jit(solution)/shard_map/ppermute | solution.py:28
  30.2 16.2 %collective-permute-start.8 = (bf16[256,512]{1,0:T(8,128)(2,1)S(1)}, bf16[256,512]{1,0:T(8,128)(2,1)S(1)}, u32[]{:S(2)}, u32[]{:S(2)}) collective-permute-start(bf16[256,512]{1,0:T(8,128)(2,1)S(1)} %pad_maximum_fusion.3.refs_4_), channel_id=1, source_target_pairs={{0,8},{2,6},{4,12},{6,2},{8,0},{10,14},{12,4},{14,10},{16,24},{18,... | collective-permute-start | bytes 786440 | tf_op jit(solution)/shard_map/ppermute | solution.py:28
  46.5 2.0 %collective-permute-start.9 = (bf16[512,512]{1,0:T(8,128)(2,1)S(1)}, bf16[512,512]{1,0:T(8,128)(2,1)S(1)}, u32[]{:S(2)}, u32[]{:S(2)}) collective-permute-start(bf16[512,512]{1,0:T(8,128)(2,1)S(1)} %pad_maximum_fusion.1), channel_id=1, source_target_pairs={{0,2},{2,0},{4,6},{6,4},{8,10},{10,8},{12,14},{14,12},{16,18},{18,... | collective-permute-start | bytes 1572872 | tf_op jit(solution)/shard_map/ppermute | solution.py:28
  46.7 17.9 %collective-permute-start.10 = (bf16[64,2048]{1,0:T(8,128)(2,1)S(1)}, bf16[64,2048]{1,0:T(8,128)(2,1)S(1)}, u32[]{:S(2)}, u32[]{:S(2)}) collective-permute-start(bf16[64,2048]{1,0:T(8,128)(2,1)S(1)} %get-tuple-element.47), channel_id=1, source_target_pairs={{0,1},{1,0},{2,3},{3,2},{4,5},{5,4},{6,7},{7,6},{8,9},{9,8},{10,11... | collective-permute-start | bytes 786440 | tf_op jit(solution)/shard_map/ppermute | solution.py:458
  62.7 8.4 %collective-permute-start.11 = (bf16[64,2048]{1,0:T(8,128)(2,1)S(1)}, bf16[64,2048]{1,0:T(8,128)(2,1)S(1)}, u32[]{:S(2)}, u32[]{:S(2)}) collective-permute-start(bf16[64,2048]{1,0:T(8,128)(2,1)S(1)} %get-tuple-element.48), channel_id=1, source_target_pairs={{0,1},{1,0},{2,3},{3,2},{4,5},{5,4},{6,7},{7,6},{8,9},{9,8},{10,11... | collective-permute-start | bytes 786440 | tf_op jit(solution)/shard_map/ppermute | solution.py:458
